TPU v7x, 32 devices: a whole 2x2x4 slice. The times are simulated.
32 devices in a mesh: dp: 8 (over y, x, core), tensor: 4 (over z).
Axes of the slice: x: 2, y: 2, z: 4, core: 2. Of those that a mesh axis runs over, the one named last changes fastest.
Arguments:
- layer_input: bfloat16 [2, 5120, 2048], P(None, 'dp'), may hold values from -6 to 6
- cotangent: float32 [2, 5120, 2048], P(None, 'dp'), may hold values from -6 to 6
- w_query: bfloat16 [2048, 2048], P('dp', 'tensor'), may hold values from -0.125 to 0.125
- w_key: bfloat16 [2048, 2048], P('dp', 'tensor'), may hold values from -0.125 to 0.125
- w_value: bfloat16 [2048, 2048], P('dp', 'tensor'), may hold values from -0.125 to 0.125
- w_output: bfloat16 [2048, 2048], P('tensor', 'dp'), may hold values from -0.125 to 0.125
- w_gate: bfloat16 [2048, 8192], P('dp', 'tensor'), may hold values from -0.125 to 0.125
- w_up: bfloat16 [2048, 8192], P('dp', 'tensor'), may hold values from -0.125 to 0.125
- w_down: bfloat16 [8192, 2048], P('tensor', 'dp'), may hold values from -0.0625 to 0.0625
- query_gain: float32 [2048], P('tensor'), may hold values from 0.1 to 1.9
- key_gain: float32 [2048], P('tensor'), may hold values from 0.1 to 1.9
- attn_gain: float32 [2048], replicated, may hold values from 0.1 to 1.9
- mlp_gain: float32 [2048], replicated, may hold values from 0.1 to 1.9
- slot_parent: int32 [2, 40], replicated, may hold values from 0 to 39, as said below
- slot_depth: int32 [2, 40], replicated, may hold values from 0 to 9, as said below
Outputs:
- layer_output: bfloat16 [2, 5120, 2048], P(None, 'dp')
- input_grad: float32 [2, 5120, 2048], P(None, ('dp', 'tensor'))
- w_query_grad: float32 [2048, 2048], P('dp', 'tensor')
- w_key_grad: float32 [2048, 2048], P('dp', 'tensor')
- w_value_grad: float32 [2048, 2048], P('dp', 'tensor')
- w_output_grad: float32 [2048, 2048], P('tensor', 'dp')
- w_gate_grad: float32 [2048, 8192], P('dp', 'tensor')
- w_up_grad: float32 [2048, 8192], P('dp', 'tensor')
- w_down_grad: float32 [8192, 2048], P('tensor', 'dp')
- query_gain_grad: float32 [2048], P('tensor')
- key_gain_grad: float32 [2048], P('tensor')
- attn_gain_grad: float32 [2048], replicated
- mlp_gain_grad: float32 [2048], replicated
Inputs may be any that keep to these rules, and one draw needn't show every extreme that they name: slot_parent[b, s] is the slot of micro-batch b that holds the parent block of the block in slot s; the first trunk block of a tree names its own slot. Each of the 2 trees of a micro-batch has 20 blocks: 8 trunk blocks in a chain, 4 branch blocks whose parent is the last trunk block, and 2 leaf blocks under each branch; trees and blocks lie on slots in a random order. `slot_depth`: the depth of the block in slot s: its place along the trunk, 8 for a branch block, 9 for a leaf block; consistent with slot_parent.
All inputs are finite; a program needn't handle non-finite values.
Results may differ from a plain program's by a relative error of at most 0.023.
Values may be sent and summed in bfloat16 or wider, within the bound.
No kernel may reach another device: no remote copies, remote signals or barrier semaphores. Data moves between devices by JAX's collectives and lax.ppermute only.
A program may use at most 384 MiB of HBM per device.

v0:
```python
import jax
import jax.numpy as jnp
from jax import lax
from jax.sharding import PartitionSpec as P

D = 2048
HEADS = 16
BLK = 128
TRUNK = 8
MB = 2
SEG_DEV = 5


EPSILON = 1e-06
ROPE_BASE = 500000.0


def rope_tables(depth_row):
    head_size = D // HEADS
    half_size = head_size // 2
    offsets = jnp.arange(BLK, dtype=jnp.int32)
    places = (depth_row[:, None] * BLK + offsets[None, :]).reshape(-1).astype(jnp.float32)
    frequency = ROPE_BASE ** (-2.0 * jnp.arange(half_size, dtype=jnp.float32) / head_size)
    angles = places[:, None] * frequency[None, :]
    return (jnp.cos(angles), jnp.sin(angles))


def rotate(values, cos_table, sin_table, direction):
    head_size = D // HEADS
    half_size = head_size // 2
    count = values.shape[0]
    by_head = values.reshape(count, -1, head_size)
    front_half = by_head[..., :half_size]
    back_half = by_head[..., half_size:]
    cosines = cos_table[:, None, :]
    sines = direction * sin_table[:, None, :]
    turned = jnp.concatenate(
        [front_half * cosines - back_half * sines, back_half * cosines + front_half * sines], -1
    )
    return turned.reshape(count, -1)


def ancestry(parent_row):
    blocks = parent_row.shape[0]
    slot_ids = jnp.arange(blocks, dtype=jnp.int32)
    onehot = (parent_row[:, None] == slot_ids[None, :]).astype(jnp.float32)
    reach = jnp.eye(blocks, dtype=jnp.float32)
    walker = reach
    for step_idx in range(TRUNK + 1):
        walker = jnp.dot(walker, onehot, precision=lax.Precision.HIGHEST)
        reach = jnp.maximum(reach, walker)
    return reach


def window_layout(reach_rows, depth_full, my_depth):
    blocks = depth_full.shape[0]
    span = TRUNK + 2
    levels = jnp.arange(span, dtype=jnp.int32)
    slot_ids = jnp.arange(blocks, dtype=jnp.int32).astype(jnp.float32)
    level_hot = (depth_full[:, None] == levels[None, :]).astype(jnp.float32)
    present = jnp.dot(reach_rows, level_hot, precision=lax.Precision.HIGHEST) > 0.5
    found = jnp.dot(reach_rows, slot_ids[:, None] * level_hot, precision=lax.Precision.HIGHEST)
    own_slot = jnp.dot(
        reach_rows * 0.0 + jnp.eye(reach_rows.shape[0], blocks, dtype=jnp.float32) * 0.0,
        level_hot,
        precision=lax.Precision.HIGHEST,
    )
    ancestor = jnp.where(present, found + own_slot, 0.0).astype(jnp.int32)
    offsets = jnp.arange(BLK, dtype=jnp.int32)
    row_index = (ancestor[:, :, None] * BLK + offsets[None, None, :]).reshape(-1)
    same_level = levels[None, :] == my_depth[:, None]
    causal = offsets[:, None] >= offsets[None, :]
    combined = present[:, None, :, None] & (
        jnp.logical_not(same_level)[:, None, :, None] | causal[None, :, None, :]
    )
    return (row_index, combined.reshape(reach_rows.shape[0], BLK, span * BLK))


def attend_window(query_rows, key_win, value_win, permitted, scaling):
    slots_here = key_win.shape[0]
    queries = query_rows.reshape(slots_here, BLK, -1)
    scores = (
        jnp.einsum("sqd,skd->sqk", queries, key_win, preferred_element_type=jnp.float32) * scaling
    )
    scores = jnp.where(permitted, scores, -1e30)
    maximum = jnp.max(scores, axis=-1, keepdims=True)
    expsum = jnp.exp(scores - maximum)
    totals = jnp.sum(expsum, axis=-1, keepdims=True)
    probs_low = (expsum / totals).astype(jnp.bfloat16)
    attended = jnp.einsum("sqk,skd->sqd", probs_low, value_win, preferred_element_type=jnp.float32)
    return (attended.reshape(slots_here * BLK, -1), maximum + jnp.log(totals))


def attend_window_back(query_rows, key_win, value_win, permitted, log_total, out_grad, scaling):
    slots_here = key_win.shape[0]
    queries = query_rows.reshape(slots_here, BLK, -1)
    grads_in = out_grad.reshape(slots_here, BLK, -1)
    scores = (
        jnp.einsum("sqd,skd->sqk", queries, key_win, preferred_element_type=jnp.float32) * scaling
    )
    probs_row = jnp.where(permitted, jnp.exp(scores - log_total), 0.0)
    probs_low = probs_row.astype(jnp.bfloat16)
    probs_grad = jnp.einsum("sqd,skd->sqk", grads_in, value_win, preferred_element_type=jnp.float32)
    row_inner = jnp.sum(probs_row * probs_grad, axis=-1, keepdims=True)
    score_grad = (probs_row * (probs_grad - row_inner)).astype(jnp.bfloat16)
    query_grad = (
        jnp.einsum("sqk,skd->sqd", score_grad, key_win, preferred_element_type=jnp.float32)
        * scaling
    )
    key_grad = (
        jnp.einsum("sqk,sqd->skd", score_grad, queries, preferred_element_type=jnp.float32)
        * scaling
    )
    value_grad = jnp.einsum("sqk,sqd->skd", probs_low, grads_in, preferred_element_type=jnp.float32)
    return (query_grad.reshape(slots_here * BLK, -1), key_grad, value_grad)


def norm_back(gradient, normed, inverse, gain_vec):
    weighted = gradient * gain_vec
    return inverse * (weighted - normed * jnp.mean(normed * weighted, axis=-1, keepdims=True))


def add_up(totals, parts):
    if totals is None:
        return tuple(parts)
    return tuple((left + right for left, right in zip(totals, parts)))


def shards(
    layer_input,
    cotangent,
    w_query,
    w_key,
    w_value,
    w_output,
    w_gate,
    w_up,
    w_down,
    query_gain,
    key_gain,
    attn_gain,
    mlp_gain,
    slot_parent,
    slot_depth,
):
    head_size = D // HEADS
    scaling = head_size ** (-0.5)
    dp_index = lax.axis_index("dp")
    tp_index = lax.axis_index("tensor")
    tp_count = lax.axis_size("tensor")
    local_rows = layer_input.shape[1]
    share_rows = local_rows // tp_count
    heads_here = w_query.shape[1] // head_size

    def fetch_weights():
        return (
            lax.all_gather(w_query, "dp", axis=0, tiled=True),
            lax.all_gather(w_key, "dp", axis=0, tiled=True),
            lax.all_gather(w_value, "dp", axis=0, tiled=True),
            lax.all_gather(w_output, "dp", axis=1, tiled=True),
            lax.all_gather(w_gate, "dp", axis=0, tiled=True),
            lax.all_gather(w_up, "dp", axis=0, tiled=True),
            lax.all_gather(w_down, "dp", axis=1, tiled=True),
        )

    outputs = []
    input_parts = []
    weight_total = None
    gain_total = None
    for micro_idx in range(MB):
        full_weights = fetch_weights()
        wq_full, wk_full, wv_full, wo_full, gate_full, up_full, down_full = full_weights
        tokens = layer_input[micro_idx]
        parent_row = slot_parent[micro_idx]
        first_slot = dp_index * SEG_DEV
        my_depth = lax.dynamic_slice_in_dim(slot_depth[micro_idx], first_slot, SEG_DEV, 0)
        reach_rows = lax.dynamic_slice_in_dim(ancestry(parent_row), first_slot, SEG_DEV, 0)
        cos_table, sin_table = rope_tables(my_depth)
        query_raw = jnp.dot(tokens, wq_full, preferred_element_type=jnp.float32)
        key_raw = jnp.dot(tokens, wk_full, preferred_element_type=jnp.float32)
        value_low = jnp.dot(tokens, wv_full, preferred_element_type=jnp.float32).astype(
            jnp.bfloat16
        )
        square_sums = lax.psum(
            (jnp.sum(query_raw * query_raw, axis=-1), jnp.sum(key_raw * key_raw, axis=-1)), "tensor"
        )
        query_inv = lax.rsqrt(square_sums[0] / D + EPSILON)[:, None]
        key_inv = lax.rsqrt(square_sums[1] / D + EPSILON)[:, None]
        query_hat = query_raw * query_inv
        key_hat = key_raw * key_inv
        query_low = rotate(query_hat * query_gain, cos_table, sin_table, 1.0).astype(jnp.bfloat16)
        key_low = rotate(key_hat * key_gain, cos_table, sin_table, 1.0).astype(jnp.bfloat16)
        key_all, value_all = (
            lax.all_gather(key_low, "dp", axis=0, tiled=True),
            lax.all_gather(value_low, "dp", axis=0, tiled=True),
        )
        head_outs = []
        log_totals = []
        row_index, permitted = window_layout(reach_rows, slot_depth[micro_idx], my_depth)
        key_win = jnp.take(key_all, row_index, axis=0).reshape(SEG_DEV, -1, key_all.shape[1])
        value_win = jnp.take(value_all, row_index, axis=0).reshape(SEG_DEV, -1, value_all.shape[1])
        for head_idx in range(heads_here):
            columns = slice(head_idx * head_size, (head_idx + 1) * head_size)
            attended, log_total = attend_window(
                query_low[:, columns],
                key_win[:, :, columns],
                value_win[:, :, columns],
                permitted,
                scaling,
            )
            head_outs.append(attended)
            log_totals.append(log_total)
        attn_low = jnp.concatenate(head_outs, axis=1).astype(jnp.bfloat16)
        attn_proj = lax.psum(
            jnp.dot(attn_low, wo_full, preferred_element_type=jnp.float32), "tensor"
        )
        attn_inv = lax.rsqrt(jnp.mean(attn_proj * attn_proj, axis=-1, keepdims=True) + EPSILON)
        attn_normed = attn_proj * attn_inv
        hidden = tokens.astype(jnp.float32) + attn_normed * attn_gain
        hidden_low = hidden.astype(jnp.bfloat16)
        gate_pre = jnp.dot(hidden_low, gate_full, preferred_element_type=jnp.float32)
        up_pre = jnp.dot(hidden_low, up_full, preferred_element_type=jnp.float32)
        sigmoid_gate = jax.nn.sigmoid(gate_pre)
        silu_gate = gate_pre * sigmoid_gate
        act_low = (silu_gate * up_pre).astype(jnp.bfloat16)
        mlp_proj = lax.psum(
            jnp.dot(act_low, down_full, preferred_element_type=jnp.float32), "tensor"
        )
        mlp_inv = lax.rsqrt(jnp.mean(mlp_proj * mlp_proj, axis=-1, keepdims=True) + EPSILON)
        mlp_normed = mlp_proj * mlp_inv
        outputs.append((hidden + mlp_normed * mlp_gain).astype(jnp.bfloat16))
        full_weights = fetch_weights()
        wq_full, wk_full, wv_full, wo_full, gate_full, up_full, down_full = full_weights
        out_grad = cotangent[micro_idx]
        mlp_grad = norm_back(out_grad, mlp_normed, mlp_inv, mlp_gain).astype(jnp.bfloat16)
        mlp_gain_part = jnp.sum(out_grad * mlp_normed, axis=0)
        act_grad = jnp.einsum("rd,fd->rf", mlp_grad, down_full, preferred_element_type=jnp.float32)
        down_part = jnp.einsum("rf,rd->fd", act_low, mlp_grad, preferred_element_type=jnp.float32)
        up_grad = (act_grad * silu_gate).astype(jnp.bfloat16)
        gate_grad = (
            act_grad * up_pre * sigmoid_gate * (1.0 + gate_pre * (1.0 - sigmoid_gate))
        ).astype(jnp.bfloat16)
        gate_part = jnp.einsum(
            "rd,rf->df", hidden_low, gate_grad, preferred_element_type=jnp.float32
        )
        up_part = jnp.einsum("rd,rf->df", hidden_low, up_grad, preferred_element_type=jnp.float32)
        branch_term = jnp.einsum(
            "rf,df->rd", gate_grad, gate_full, preferred_element_type=jnp.float32
        ) + jnp.einsum("rf,df->rd", up_grad, up_full, preferred_element_type=jnp.float32)
        hidden_grad = out_grad + lax.psum(branch_term, "tensor")
        proj_grad = norm_back(hidden_grad, attn_normed, attn_inv, attn_gain).astype(jnp.bfloat16)
        attn_gain_part = jnp.sum(hidden_grad * attn_normed, axis=0)
        attn_grad = jnp.einsum(
            "rd,cd->rc", proj_grad, wo_full, preferred_element_type=jnp.float32
        ).astype(jnp.bfloat16)
        output_part = jnp.einsum(
            "rc,rd->cd", attn_low, proj_grad, preferred_element_type=jnp.float32
        )
        query_heads = []
        key_heads = []
        value_heads = []
        for head_idx in range(heads_here):
            columns = slice(head_idx * head_size, (head_idx + 1) * head_size)
            head_q, head_k, head_v = attend_window_back(
                query_low[:, columns],
                key_win[:, :, columns],
                value_win[:, :, columns],
                permitted,
                log_totals[head_idx],
                attn_grad[:, columns],
                scaling,
            )
            query_heads.append(head_q)
            key_heads.append(head_k)
            value_heads.append(head_v)
        width_here = key_all.shape[1]
        key_window_grad = jnp.concatenate(key_heads, axis=2).reshape(-1, width_here)
        value_window_grad = jnp.concatenate(value_heads, axis=2).reshape(-1, width_here)
        key_full_grad = (
            jnp.zeros((key_all.shape[0], width_here), jnp.float32)
            .at[row_index]
            .add(key_window_grad)
        )
        value_full_grad = (
            jnp.zeros((value_all.shape[0], width_here), jnp.float32)
            .at[row_index]
            .add(value_window_grad)
        )
        query_rot_grad = jnp.concatenate(query_heads, axis=1)
        key_sum, value_sum = (
            lax.psum_scatter(
                key_full_grad.astype(jnp.bfloat16), "dp", scatter_dimension=0, tiled=True
            ).astype(jnp.float32),
            lax.psum_scatter(
                value_full_grad.astype(jnp.bfloat16), "dp", scatter_dimension=0, tiled=True
            ).astype(jnp.float32),
        )
        query_norm_grad = rotate(query_rot_grad, cos_table, sin_table, -1.0)
        key_norm_grad = rotate(key_sum, cos_table, sin_table, -1.0)
        query_weighted = query_norm_grad * query_gain
        key_weighted = key_norm_grad * key_gain
        inner_sums = lax.psum(
            (
                jnp.sum(query_hat * query_weighted, axis=-1),
                jnp.sum(key_hat * key_weighted, axis=-1),
            ),
            "tensor",
        )
        query_raw_grad = (
            query_inv * (query_weighted - query_hat * (inner_sums[0] / D)[:, None])
        ).astype(jnp.bfloat16)
        key_raw_grad = (key_inv * (key_weighted - key_hat * (inner_sums[1] / D)[:, None])).astype(
            jnp.bfloat16
        )
        value_raw_grad = value_sum.astype(jnp.bfloat16)
        query_gain_part = jnp.sum(query_norm_grad * query_hat, axis=0)
        key_gain_part = jnp.sum(key_norm_grad * key_hat, axis=0)

        def input_term(
            start,
            count,
            q_grad=query_raw_grad,
            k_grad=key_raw_grad,
            v_grad=value_raw_grad,
            q_full=wq_full,
            k_full=wk_full,
            v_full=wv_full,
        ):
            term = jnp.einsum("rc,dc->rd", q_grad, q_full, preferred_element_type=jnp.float32)
            term = term + jnp.einsum(
                "rc,dc->rd", k_grad, k_full, preferred_element_type=jnp.float32
            )
            return term + jnp.einsum(
                "rc,dc->rd", v_grad, v_full, preferred_element_type=jnp.float32
            )

        residual_rows = lax.dynamic_slice_in_dim(hidden_grad, tp_index * share_rows, share_rows, 0)
        input_parts.append(
            residual_rows
            + lax.psum_scatter(
                input_term(jnp.int32(0), lax.axis_size("tensor") * share_rows).astype(jnp.bfloat16),
                "tensor",
                scatter_dimension=0,
                tiled=True,
            ).astype(jnp.float32)
        )
        query_part = jnp.einsum(
            "rd,rc->dc", tokens, query_raw_grad, preferred_element_type=jnp.float32
        )
        key_part = jnp.einsum("rd,rc->dc", tokens, key_raw_grad, preferred_element_type=jnp.float32)
        value_part = jnp.einsum(
            "rd,rc->dc", tokens, value_raw_grad, preferred_element_type=jnp.float32
        )
        weight_parts = (
            query_part,
            key_part,
            value_part,
            output_part,
            gate_part,
            up_part,
            down_part,
        )
        gain_parts = (query_gain_part, key_gain_part, attn_gain_part, mlp_gain_part)
        weight_total = add_up(
            weight_total,
            (
                lax.psum_scatter(
                    weight_parts[0].astype(jnp.bfloat16), "dp", scatter_dimension=0, tiled=True
                ).astype(jnp.float32),
                lax.psum_scatter(
                    weight_parts[1].astype(jnp.bfloat16), "dp", scatter_dimension=0, tiled=True
                ).astype(jnp.float32),
                lax.psum_scatter(
                    weight_parts[2].astype(jnp.bfloat16), "dp", scatter_dimension=0, tiled=True
                ).astype(jnp.float32),
                lax.psum_scatter(
                    weight_parts[3].astype(jnp.bfloat16), "dp", scatter_dimension=1, tiled=True
                ).astype(jnp.float32),
                lax.psum_scatter(
                    weight_parts[4].astype(jnp.bfloat16), "dp", scatter_dimension=0, tiled=True
                ).astype(jnp.float32),
                lax.psum_scatter(
                    weight_parts[5].astype(jnp.bfloat16), "dp", scatter_dimension=0, tiled=True
                ).astype(jnp.float32),
                lax.psum_scatter(
                    weight_parts[6].astype(jnp.bfloat16), "dp", scatter_dimension=1, tiled=True
                ).astype(jnp.float32),
            ),
        )
        gain_total = add_up(
            gain_total, lax.psum((gain_parts[0], gain_parts[1], gain_parts[2], gain_parts[3]), "dp")
        )
    return (
        jnp.stack(outputs),
        jnp.stack(input_parts),
        weight_total[0],
        weight_total[1],
        weight_total[2],
        weight_total[3],
        weight_total[4],
        weight_total[5],
        weight_total[6],
        gain_total[0],
        gain_total[1],
        gain_total[2],
        gain_total[3],
    )


def solution(mesh):
    in_specs = (
        P(None, "dp", None),
        P(None, "dp", None),
        P("dp", "tensor"),
        P("dp", "tensor"),
        P("dp", "tensor"),
        P("tensor", "dp"),
        P("dp", "tensor"),
        P("dp", "tensor"),
        P("tensor", "dp"),
        P("tensor"),
        P("tensor"),
        P(),
        P(),
        P(),
        P(),
    )
    out_specs = (
        P(None, "dp", None),
        P(None, ("dp", "tensor"), None),
        P("dp", "tensor"),
        P("dp", "tensor"),
        P("dp", "tensor"),
        P("tensor", "dp"),
        P("dp", "tensor"),
        P("dp", "tensor"),
        P("tensor", "dp"),
        P("tensor"),
        P("tensor"),
        P(),
        P(),
    )
    return jax.shard_map(shards, mesh=mesh, in_specs=in_specs, out_specs=out_specs, check_vma=False)
```

profile of v0, /device:TPU:0, one launch (start us, length us, event | category | flops | bytes accessed | tf_op | source)
XLA Modules:
  0.0 3090.7 jit_solution(619238103119611937)
XLA Ops:
  9.5 31.1 %all-gather.18.cloned.1.call-done = bf16[2048,512]{1,0:T(8,128)(2,1)} async-done(((bf16[256,512]{1,0:T(8,128)(2,1)}), bf16[2048,512]{1,0:T(8,128)(2,1)}) %all-gather.18.cloned.1.call-update) | async-done | bytes 2097168 | tf_op jit(solution)/shard_map/all_gather | solution.py:159
  47.6 22.7 all-gather.14.cloned.1.call-done
  165.6 22.1 gather_fusion.1
  187.7 22.1 gather_fusion
  230.6 22.2 gather_fusion.3
  252.7 21.5 all-gather.30.cloned.1.call-done
  274.2 22.1 gather_fusion.2
  359.8 357.4 %all-reduce.14.cloned.1.call-done = (f32[640,2048]{1,0:T(8,128)}, f32[640,2048]{1,0:T(8,128)}) async-done(((f32[640,2048]{1,0:T(8,128)}, f32[640,2048]{1,0:T(8,128)}), (f32[640,2048]{1,0:T(8,128)}, f32[640,2048]{1,0:T(8,128)})) %all-reduce.14.cloned.1.call-update) | async-done | bytes 10485776 | tf_op jit(solution)/shard_map/psum | solution.py:214
  727.9 44.4 %all-gather.24.cloned.1.call-done = bf16[2048,2048]{1,0:T(8,128)(2,1)} async-done(((bf16[256,2048]{1,0:T(8,128)(2,1)}), bf16[2048,2048]{1,0:T(8,128)(2,1)}) %all-gather.24.cloned.1.call-update) | async-done | bytes 8388624 | tf_op jit(solution)/shard_map/all_gather | solution.py:161
  789.2 39.4 %all-gather.26.cloned.1.call-done = bf16[2048,2048]{1,0:T(8,128)(2,1)} async-done(((bf16[256,2048]{1,0:T(8,128)(2,1)}), bf16[2048,2048]{1,0:T(8,128)(2,1)}) %all-gather.26.cloned.1.call-update) | async-done | bytes 8388624 | tf_op jit(solution)/shard_map/all_gather | solution.py:162
  849.7 36.6 %all-gather.28.cloned.1.call-done = bf16[2048,2048]{1,0:T(8,128)(2,1)} async-done(((bf16[2048,256]{1,0:T(8,128)(2,1)}), bf16[2048,2048]{1,0:T(8,128)(2,1)}) %all-gather.28.cloned.1.call-update) | async-done | bytes 8388624 | tf_op jit(solution)/shard_map/all_gather | solution.py:163
  905.1 359.3 %all-reduce.12.cloned.1.call-done = (f32[640,2048]{1,0:T(8,128)}, f32[640,2048]{1,0:T(8,128)}) async-done(((f32[640,2048]{1,0:T(8,128)}, f32[640,2048]{1,0:T(8,128)}), (f32[640,2048]{1,0:T(8,128)}, f32[640,2048]{1,0:T(8,128)})) %all-reduce.12.cloned.1.call-update) | async-done | bytes 10485776 | tf_op jit(solution)/shard_map/psum | solution.py:226
  1349.2 357.3 %all-reduce.10.cloned.1.call-done = (f32[640,2048]{1,0:T(8,128)}, f32[640,2048]{1,0:T(8,128)}) async-done(((f32[640,2048]{1,0:T(8,128)}, f32[640,2048]{1,0:T(8,128)}), (f32[640,2048]{1,0:T(8,128)}, f32[640,2048]{1,0:T(8,128)})) %all-reduce.10.cloned.1.call-update) | async-done | bytes 10485776 | tf_op jit(solution)/shard_map/psum | solution.py:250
  1706.5 20.6 fusion.36
  1785.0 44.7 %scatter_custom_fusion = f32[5120,512]{1,0:T(8,128)} fusion(s32[6400]{0:T(1024)S(1)} %fusion.214, f32[6400,512]{1,0:T(8,128)} %bitcast.393, f32[]{:T(128)} %constant.72.clone.1), kind=kCustom, calls=%fused_computation.47 | custom fusion | flops 3276800 | bytes 10486272 | tf_op jit(solution)/shard_map/scatter-add | solution.py:282
  1894.2 44.8 %scatter_custom_fusion.2 = f32[5120,512]{1,0:T(8,128)} fusion(s32[6400]{0:T(1024)S(1)} %fusion.215, f32[6400,512]{1,0:T(8,128)} %bitcast.394, f32[]{:T(128)} %constant.72.clone.1), kind=kCustom, calls=%fused_computation.43 | custom fusion | flops 3276800 | bytes 10486272 | tf_op jit(solution)/shard_map/scatter-add | solution.py:282
  1975.4 44.8 %scatter_custom_fusion.1 = f32[5120,512]{1,0:T(8,128)} fusion(s32[6400]{0:T(1024)} %copy-done.158, f32[6400,512]{1,0:T(8,128)} %bitcast.392, f32[]{:T(128)} %constant.72.clone.1), kind=kCustom, calls=%fused_computation.45 | custom fusion | flops 3276800 | bytes 10486272 | tf_op jit(solution)/shard_map/scatter-add | solution.py:287
  2056.2 44.7 %scatter_custom_fusion.3 = f32[5120,512]{1,0:T(8,128)} fusion(s32[6400]{0:T(1024)S(1)} %fusion.215, f32[6400,512]{1,0:T(8,128)} %bitcast.391, f32[]{:T(128)} %constant.72.clone.1), kind=kCustom, calls=%fused_computation.41 | custom fusion | flops 3276800 | bytes 10486272 | tf_op jit(solution)/shard_map/scatter-add | solution.py:287
  2326.2 62.9 %reduce-scatter.49.cloned.1.call-done = bf16[256,2048]{1,0:T(8,128)(2,1)} async-done(((bf16[2048,2048]{1,0:T(8,128)(2,1)}), bf16[256,2048]{1,0:T(8,128)(2,1)}) %reduce-scatter.49.cloned.1.call-update) | async-done | bytes 1048592 | tf_op jit(solution)/shard_map/reduce_scatter | solution.py:379
  2389.1 75.1 %reduce-scatter.51.cloned.1.call-done = bf16[256,2048]{1,0:T(8,128)(2,1)} async-done(((bf16[2048,2048]{1,0:T(8,128)(2,1)}), bf16[256,2048]{1,0:T(8,128)(2,1)}) %reduce-scatter.51.cloned.1.call-update) | async-done | bytes 1048592 | tf_op jit(solution)/shard_map/reduce_scatter | solution.py:379
  2467.5 71.6 %reduce-scatter.59.cloned.1.call-done = bf16[2048,256]{1,0:T(8,128)(2,1)} async-done(((bf16[2048,2048]{1,0:T(8,128)(2,1)}), bf16[2048,256]{1,0:T(8,128)(2,1)}) %reduce-scatter.59.cloned.1.call-update) | async-done | bytes 1048592 | tf_op jit(solution)/shard_map/reduce_scatter | solution.py:385
  2539.1 75.0 %reduce-scatter.57.cloned.1.call-done = bf16[2048,256]{1,0:T(8,128)(2,1)} async-done(((bf16[2048,2048]{1,0:T(8,128)(2,1)}), bf16[2048,256]{1,0:T(8,128)(2,1)}) %reduce-scatter.57.cloned.1.call-update) | async-done | bytes 1048592 | tf_op jit(solution)/shard_map/reduce_scatter | solution.py:385
  2617.2 41.4 %reduce-scatter.45.cloned.1.call-done = bf16[512,256]{1,0:T(8,128)(2,1)} async-done(((bf16[512,2048]{1,0:T(8,128)(2,1)}), bf16[512,256]{1,0:T(8,128)(2,1)}) %reduce-scatter.45.cloned.1.call-update) | async-done | bytes 262160 | tf_op jit(solution)/shard_map/reduce_scatter | solution.py:376
  2658.6 44.7 %reduce-scatter.47.cloned.1.call-done = bf16[512,256]{1,0:T(8,128)(2,1)} async-done(((bf16[512,2048]{1,0:T(8,128)(2,1)}), bf16[512,256]{1,0:T(8,128)(2,1)}) %reduce-scatter.47.cloned.1.call-update) | async-done | bytes 262160 | tf_op jit(solution)/shard_map/reduce_scatter | solution.py:376
  2705.3 23.7 all-reduce
  2747.8 44.9 %reduce-scatter.39.cloned.1.call-done = bf16[256,512]{0,1:T(8,128)(2,1)} async-done(((bf16[2048,512]{0,1:T(8,128)(2,1)}), bf16[256,512]{0,1:T(8,128)(2,1)}) %reduce-scatter.39.cloned.1.call-update) | async-done | bytes 262160 | tf_op jit(solution)/shard_map/reduce_scatter | solution.py:370
  2794.7 42.5 %reduce-scatter.33.cloned.1.call-done = bf16[256,512]{0,1:T(8,128)(2,1)} async-done(((bf16[2048,512]{0,1:T(8,128)(2,1)}), bf16[256,512]{0,1:T(8,128)(2,1)}) %reduce-scatter.33.cloned.1.call-update) | async-done | bytes 262160 | tf_op jit(solution)/shard_map/reduce_scatter | solution.py:367
  2837.2 44.7 %reduce-scatter.35.cloned.1.call-done = bf16[256,512]{0,1:T(8,128)(2,1)} async-done(((bf16[2048,512]{0,1:T(8,128)(2,1)}), bf16[256,512]{0,1:T(8,128)(2,1)}) %reduce-scatter.35.cloned.1.call-update) | async-done | bytes 262160 | tf_op jit(solution)/shard_map/reduce_scatter | solution.py:367
  2884.0 42.5 %reduce-scatter.41.cloned.1.call-done = bf16[256,512]{0,1:T(8,128)(2,1)} async-done(((bf16[2048,512]{0,1:T(8,128)(2,1)}), bf16[256,512]{0,1:T(8,128)(2,1)}) %reduce-scatter.41.cloned.1.call-update) | async-done | bytes 262160 | tf_op jit(solution)/shard_map/reduce_scatter | solution.py:373
  2926.5 44.9 %reduce-scatter.43.cloned.1.call-done = bf16[256,512]{0,1:T(8,128)(2,1)} async-done(((bf16[2048,512]{0,1:T(8,128)(2,1)}), bf16[256,512]{0,1:T(8,128)(2,1)}) %reduce-scatter.43.cloned.1.call-update) | async-done | bytes 262160 | tf_op jit(solution)/shard_map/reduce_scatter | solution.py:373
  2973.4 52.8 %reduce-scatter.31.cloned.1.call-done = bf16[160,2048]{1,0:T(8,128)(2,1)} async-done(((bf16[640,2048]{1,0:T(8,128)(2,1)}), bf16[160,2048]{1,0:T(8,128)(2,1)}) %reduce-scatter.31.cloned.1.call-update) | async-done | bytes 655376 | tf_op jit(solution)/shard_map/reduce_scatter | solution.py:340
  3027.9 52.5 %reduce-scatter.25.cloned.1.call-done = bf16[160,2048]{1,0:T(8,128)(2,1)} async-done(((bf16[640,2048]{1,0:T(8,128)(2,1)}), bf16[160,2048]{1,0:T(8,128)(2,1)}) %reduce-scatter.25.cloned.1.call-update) | async-done | bytes 655376 | tf_op jit(solution)/shard_map/reduce_scatter | solution.py:340
  (793 shorter events, 796.0 us)
Async XLA Ops:
  8.7 91.5 %all-gather.12.cloned.1.call-start = ((), (), s32[]{:S(2)}) async-start(), calls=%async_computation.20 | async-start | bytes 2359296 | tf_op jit(solution)/shard_map/all_gather | solution.py:157
  9.4 156.1 %all-gather.20.cloned.1.call-start = ((), (), s32[]{:S(2)}) async-start(), calls=%async_computation.24 | async-start | bytes 5898240 | tf_op jit(solution)/shard_map/all_gather | solution.py:195
  45.3 142.4 %all-gather.16.cloned.1.call-start = ((), (), s32[]{:S(2)}) async-start(), calls=%async_computation.22 | async-start | bytes 5898240 | tf_op jit(solution)/shard_map/all_gather | solution.py:194
  134.6 96.0 %all-gather.32.cloned.1.call-start = ((), (), s32[]{:S(2)}) async-start(), calls=%async_computation.30 | async-start | bytes 5898240 | tf_op jit(solution)/shard_map/all_gather | solution.py:195
  148.4 125.8 %all-gather.30.cloned.1.call-start = ((), (), s32[]{:S(2)}) async-start(), calls=%async_computation.29 | async-start | bytes 5898240 | tf_op jit(solution)/shard_map/all_gather | solution.py:194
  151.5 196.3 %all-gather.22.cloned.1.call-start = ((), (), s32[]{:S(2)}) async-start(), calls=%async_computation.25 | async-start | bytes 2359296 | tf_op jit(solution)/shard_map/all_gather | solution.py:160
  152.2 565.0 %all-reduce.14.cloned.1.call-start = ((), (), s32[]{:S(2)}) async-start(), calls=%async_computation.53 | async-start | bytes 20971520 | tf_op jit(solution)/shard_map/psum | solution.py:214
  357.8 414.5 %all-gather.24.cloned.1.call-start = ((), (), s32[]{:S(2)}) async-start(), calls=%async_computation.26 | async-start | bytes 9437184 | tf_op jit(solution)/shard_map/all_gather | solution.py:161
  358.4 470.2 %all-gather.26.cloned.1.call-start = ((), (), s32[]{:S(2)}) async-start(), calls=%async_computation.27 | async-start | bytes 9437184 | tf_op jit(solution)/shard_map/all_gather | solution.py:162
  359.2 527.2 %all-gather.28.cloned.1.call-start = ((), (), s32[]{:S(2)}) async-start(), calls=%async_computation.28 | async-start | bytes 9437184 | tf_op jit(solution)/shard_map/all_gather | solution.py:163
  359.8 904.6 %all-reduce.12.cloned.1.call-start = ((), (), s32[]{:S(2)}) async-start(), calls=%async_computation.52 | async-start | bytes 20971520 | tf_op jit(solution)/shard_map/psum | solution.py:226
  905.0 801.4 %all-reduce.10.cloned.1.call-start = ((), (), s32[]{:S(2)}) async-start(), calls=%async_computation.51 | async-start | bytes 20971520 | tf_op jit(solution)/shard_map/psum | solution.py:250
  1348.2 881.8 %reduce-scatter.21.cloned.1.call-start = ((), (), s32[]{:S(2)}) async-start(), calls=%async_computation.31 | async-start | bytes 5898240 | tf_op jit(solution)/shard_map/reduce_scatter | solution.py:291
  1836.7 395.7 %reduce-scatter.27.cloned.1.call-start = ((), (), s32[]{:S(2)}) async-start(), calls=%async_computation.34 | async-start | bytes 5898240 | tf_op jit(solution)/shard_map/reduce_scatter | solution.py:291
  1946.0 343.6 %reduce-scatter.23.cloned.1.call-start = ((), (), s32[]{:S(2)}) async-start(), calls=%async_computation.32 | async-start | bytes 5898240 | tf_op jit(solution)/shard_map/reduce_scatter | solution.py:294
  2027.2 267.7 %reduce-scatter.29.cloned.1.call-start = ((), (), s32[]{:S(2)}) async-start(), calls=%async_computation.35 | async-start | bytes 5898240 | tf_op jit(solution)/shard_map/reduce_scatter | solution.py:294
  2108.0 214.9 %reduce-scatter.53.cloned.1.call-start = ((), (), s32[]{:S(2)}) async-start(), calls=%async_computation.47 | async-start | bytes 9437184 | tf_op jit(solution)/shard_map/reduce_scatter | solution.py:382
  2120.4 202.5 %reduce-scatter.55.cloned.1.call-start = ((), (), s32[]{:S(2)}) async-start(), calls=%async_computation.48 | async-start | bytes 9437184 | tf_op jit(solution)/shard_map/reduce_scatter | solution.py:382
  2133.1 256.0 %reduce-scatter.49.cloned.1.call-start = ((), (), s32[]{:S(2)}) async-start(), calls=%async_computation.45 | async-start | bytes 9437184 | tf_op jit(solution)/shard_map/reduce_scatter | solution.py:379
  2144.4 319.9 %reduce-scatter.51.cloned.1.call-start = ((), (), s32[]{:S(2)}) async-start(), calls=%async_computation.46 | async-start | bytes 9437184 | tf_op jit(solution)/shard_map/reduce_scatter | solution.py:379
  2155.5 383.6 %reduce-scatter.59.cloned.1.call-start = ((), (), s32[]{:S(2)}) async-start(), calls=%async_computation.50 | async-start | bytes 9437184 | tf_op jit(solution)/shard_map/reduce_scatter | solution.py:385
  2168.0 446.1 %reduce-scatter.57.cloned.1.call-start = ((), (), s32[]{:S(2)}) async-start(), calls=%async_computation.49 | async-start | bytes 9437184 | tf_op jit(solution)/shard_map/reduce_scatter | solution.py:385
  2180.7 477.9 %reduce-scatter.45.cloned.1.call-start = ((), (), s32[]{:S(2)}) async-start(), calls=%async_computation.43 | async-start | bytes 2359296 | tf_op jit(solution)/shard_map/reduce_scatter | solution.py:376
  2186.4 517.0 %reduce-scatter.47.cloned.1.call-start = ((), (), s32[]{:S(2)}) async-start(), calls=%async_computation.44 | async-start | bytes 2359296 | tf_op jit(solution)/shard_map/reduce_scatter | solution.py:376
  2227.3 520.5 %reduce-scatter.37.cloned.1.call-start = ((), (), s32[]{:S(2)}) async-start(), calls=%async_computation.39 | async-start | bytes 2359296 | tf_op jit(solution)/shard_map/reduce_scatter | solution.py:370
  2269.9 522.7 %reduce-scatter.39.cloned.1.call-start = ((), (), s32[]{:S(2)}) async-start(), calls=%async_computation.40 | async-start | bytes 2359296 | tf_op jit(solution)/shard_map/reduce_scatter | solution.py:370
  2275.1 562.1 %reduce-scatter.33.cloned.1.call-start = ((), (), s32[]{:S(2)}) async-start(), calls=%async_computation.37 | async-start | bytes 2359296 | tf_op jit(solution)/shard_map/reduce_scatter | solution.py:367
  2284.5 597.4 %reduce-scatter.35.cloned.1.call-start = ((), (), s32[]{:S(2)}) async-start(), calls=%async_computation.38 | async-start | bytes 2359296 | tf_op jit(solution)/shard_map/reduce_scatter | solution.py:367
  2289.5 637.0 %reduce-scatter.41.cloned.1.call-start = ((), (), s32[]{:S(2)}) async-start(), calls=%async_computation.41 | async-start | bytes 2359296 | tf_op jit(solution)/shard_map/reduce_scatter | solution.py:373
  2294.8 676.6 %reduce-scatter.43.cloned.1.call-start = ((), (), s32[]{:S(2)}) async-start(), calls=%async_computation.42 | async-start | bytes 2359296 | tf_op jit(solution)/shard_map/reduce_scatter | solution.py:373
  2300.1 726.1 %reduce-scatter.31.cloned.1.call-start = ((), (), s32[]{:S(2)}) async-start(), calls=%async_computation.36 | async-start | bytes 3276800 | tf_op jit(solution)/shard_map/reduce_scatter | solution.py:340
  2308.1 772.3 %reduce-scatter.25.cloned.1.call-start = ((), (), s32[]{:S(2)}) async-start(), calls=%async_computation.33 | async-start | bytes 3276800 | tf_op jit(solution)/shard_map/reduce_scatter | solution.py:340
  (224 other events, 4259.8 us)
Sparse Core Ops, SparseCore 0:
  9.9 30.5 all-gather.17
  102.5 41.1 all-gather.19
  145.9 41.1 all-gather.15
  189.4 41.1 all-gather.31
  233.0 41.1 all-gather.29
  276.0 28.1 all-gather.21
  358.0 359.1 all-reduce.13
  718.9 53.3 all-gather.23
  774.2 54.3 all-gather.25
  830.4 55.9 all-gather.27
  905.1 359.1 all-reduce.11
  1348.3 358.1 all-reduce.9
  1836.8 55.5 reduce-scatter.20
  1946.1 56.4 reduce-scatter.26
  2027.3 56.8 reduce-scatter.22
  2108.1 56.4 reduce-scatter.28
  2168.0 71.2 reduce-scatter.52
  2243.1 71.2 reduce-scatter.54
  2317.8 71.2 reduce-scatter.48
  2393.0 71.2 reduce-scatter.50
  2467.8 71.2 reduce-scatter.58
  2542.8 71.2 reduce-scatter.56
  2617.4 41.2 reduce-scatter.44
  2662.1 41.2 reduce-scatter.46
  2706.5 41.2 reduce-scatter.36
  2751.4 41.2 reduce-scatter.38
  2795.9 41.2 reduce-scatter.32
  2840.7 41.2 reduce-scatter.34
  2885.2 41.2 reduce-scatter.40
  2930.1 41.2 reduce-scatter.42
  2974.1 52.0 reduce-scatter.30
  3028.5 51.7 reduce-scatter.24
  (2 shorter events, 55.7 us)
where the time goes:
time: 3100 us; the launch traced here: 3090 us
  waiting for transfers between devices  2020 us (65%)
  matrix products  406 us (13%)
  other arithmetic  365 us (12%)
  local copies, waits for them, and re-layouts  214 us (7%)
  blocking collectives  60.4 us (2%)
    psum x1, waiting for transfers between devices, shards(): lax.psum(jnp.dot(act_low, down_full, preferred_element_type=jnp.float32),...  359 us
    psum x1, waiting for transfers between devices, shards(): lax.psum(jnp.dot(attn_low, wo_full, preferred_element_type=jnp.float32),...  357 us
    psum x1, waiting for transfers between devices, shards(): hidden_grad = out_grad + lax.psum(branch_term, 'tensor')  357 us
    reduce_scatter x2, waiting for transfers between devices, shards(): lax.psum_scatter(weight_parts[6].astype(jnp.bfloat16), 'dp', scatter_dime...  147 us
    reduce_scatter x2, waiting for transfers between devices, shards(): lax.psum_scatter(weight_parts[4].astype(jnp.bfloat16), 'dp', scatter_dime...  138 us
    reduce_scatter x2, waiting for transfers between devices, shards(): lax.psum_scatter(input_term(jnp.int32(0), lax.axis_size('tensor') * share...  105 us
    scatter-add x2, other arithmetic, shards(): value_full_grad = jnp.zeros((value_all.shape[0], width_here), jnp.float32...  89.5 us
    scatter-add x2, other arithmetic, shards(): key_full_grad = jnp.zeros((key_all.shape[0], width_here), jnp.float32).at...  89.5 us
  transfers between devices with their start and end apart: 34, of which 25 were waited for; matrix products, arithmetic and copies ran while one was open for 23% of the time, Pallas kernels for 0%

commit v1 on v0

v1 whole, which is shorter than its diff:
```python
import functools

import jax
import jax.numpy as jnp
from jax import lax
from jax.experimental import pallas as pl
from jax.experimental.pallas import tpu as pltpu
from jax.sharding import PartitionSpec as P

D = 2048
HEADS = 16
HEAD = D // HEADS
BLK = 128
TRUNK = 8
BRANCHES = 4
LEAVES = 2
TREE_BLOCKS = 20
MB = 2
SEG_DEV = 5
PAIR = 2 * BLK
TRUNK_ROWS = TRUNK * BLK

EPSILON = 1e-06
ROPE_BASE = 500000.0
SCALING = HEAD ** (-0.5)
VMEM_LIMIT = 56 * 1024 * 1024

f32 = jnp.float32
bf16 = jnp.bfloat16


def tree_order(parents, depths):
    blocks = parents.shape[1]
    ids = jnp.arange(blocks, dtype=jnp.int32)

    def follow(table, index):
        hot = index[:, :, None] == ids[None, None, :]
        return jnp.sum(jnp.where(hot, table[:, None, :], 0), axis=-1)

    up2 = follow(parents, parents)
    up4 = follow(up2, up2)
    up8 = follow(up4, up4)
    root = follow(up8, up8)
    is_leaf = depths == TRUNK + 1
    above = jnp.where(is_leaf, parents, 0)
    key = ((root * (TRUNK + 2) + depths) * blocks + above) * blocks + ids[None, :]
    rank = jnp.sum((key[:, None, :] < key[:, :, None]).astype(jnp.int32), axis=-1)
    return jnp.sum(
        jnp.where(rank[:, None, :] == ids[None, :, None], ids[None, None, :], 0), axis=-1
    ).astype(jnp.int32)


def rope_tables(depths):
    half = HEAD // 2
    offsets = jnp.arange(BLK, dtype=jnp.int32)
    places = (depths[:, :, None] * BLK + offsets).reshape(depths.shape[0], -1).astype(f32)
    frequency = ROPE_BASE ** (-2.0 * jnp.arange(half, dtype=f32) / HEAD)
    angles = places[:, :, None] * frequency
    cosines = jnp.cos(angles)
    sines = jnp.sin(angles)
    return (
        jnp.concatenate([cosines, cosines], -1),
        jnp.concatenate([-sines, sines], -1),
    )


def low_sum(*parts):
    total = parts[0].astype(f32)
    for part in parts[1:]:
        total = total + part.astype(f32)
    return total.astype(bf16)


def small_sum(values, axis, count):
    step = 1
    while step < count:
        values = values + lax.ppermute(values, axis, [(i, i ^ step) for i in range(count)])
        step *= 2
    return values


def line_all_reduce(chunks, count):
    if count != 4:
        return [lax.psum(chunk, "tensor") for chunk in chunks]
    index = lax.axis_index("tensor")
    inner = (index == 1) | (index == 2)
    sums = []
    for chunk in chunks:
        outer = lax.ppermute(chunk, "tensor", [(0, 1), (3, 2)])
        side = low_sum(chunk, outer)
        across = lax.ppermute(side, "tensor", [(1, 2), (2, 1)])
        total = low_sum(side, across)
        back = lax.ppermute(total, "tensor", [(1, 0), (2, 3)])
        sums.append(jnp.where(inner, total, back))
    return sums


def line_reduce_scatter(values, count):
    if count != 4:
        return lax.psum_scatter(values, "tensor", scatter_dimension=0, tiled=True).astype(f32)
    index = lax.axis_index("tensor")
    blocks = values.reshape(count, values.shape[0] // count, values.shape[1])

    def block(at):
        return lax.dynamic_index_in_dim(blocks, lax.rem(at + 2 * count, count), 0, keepdims=False)

    right = lax.ppermute(block(index + 3), "tensor", [(0, 1)])
    left = lax.ppermute(block(index - 3), "tensor", [(3, 2)])
    right = lax.ppermute(low_sum(block(index + 2), right), "tensor", [(0, 1), (1, 2)])
    left = lax.ppermute(low_sum(block(index - 2), left), "tensor", [(3, 2), (2, 1)])
    right = lax.ppermute(low_sum(block(index + 1), right), "tensor", [(0, 1), (1, 2), (2, 3)])
    left = lax.ppermute(low_sum(block(index - 1), left), "tensor", [(3, 2), (2, 1), (1, 0)])
    return block(index).astype(f32) + right.astype(f32) + left.astype(f32)


def line_all_gather(values, count):
    if count != 4:
        return lax.all_gather(values, "tensor", axis=1, tiled=True)
    index = lax.axis_index("tensor")
    width = values.shape[1]
    right1 = lax.ppermute(values, "tensor", [(0, 1), (1, 2), (2, 3)])
    left1 = lax.ppermute(values, "tensor", [(3, 2), (2, 1), (1, 0)])
    right2 = lax.ppermute(right1, "tensor", [(1, 2), (2, 3)])
    left2 = lax.ppermute(left1, "tensor", [(2, 1), (1, 0)])
    right3 = lax.ppermute(right2, "tensor", [(2, 3)])
    left3 = lax.ppermute(left2, "tensor", [(1, 0)])
    whole = jnp.zeros((values.shape[0], count * width), values.dtype)
    pieces = (
        values,
        jnp.where(index >= 1, right1, left3),
        jnp.where(index >= 2, right2, left2),
        jnp.where(index >= 3, right3, left1),
    )
    for back, piece in enumerate(pieces):
        place = lax.rem(index - back + count, count) * width
        whole = lax.dynamic_update_slice(whole, piece, (0, place))
    return whole


def turn(values, cosines, sines):
    return values * cosines + pltpu.roll(values, HEAD // 2, 1) * sines


def head_cols(head, group=0, heads=0):
    start = (group * heads + head) * HEAD
    return slice(start, start + HEAD)


def pack_kernel(heads, qk_ref, v_ref, inv_ref, gain_ref, cos_ref, sin_ref, out_ref):
    cosines = cos_ref[0]
    sines = sin_ref[0]
    for head in range(heads):
        for which in range(2):
            cols = head_cols(head, which, heads)
            normed = qk_ref[0, :, cols] * inv_ref[0, :, which : which + 1] * gain_ref[:, cols]
            out_ref[head, 0, which] = turn(normed, cosines, sines).astype(bf16)
        out_ref[head, 0, 2] = v_ref[0, :, head_cols(head)].astype(bf16)


def pack_heads(qk_raw, v_raw, inverse, gains, cosines, sines, heads):
    rows = qk_raw.shape[1]
    step = rows // 2
    width = heads * HEAD
    return pl.pallas_call(
        functools.partial(pack_kernel, heads),
        grid=(MB, rows // step),
        in_specs=[
            pl.BlockSpec((1, step, 2 * width), lambda b, r: (b, r, 0)),
            pl.BlockSpec((1, step, width), lambda b, r: (b, r, 0)),
            pl.BlockSpec((1, step, 2), lambda b, r: (b, r, 0)),
            pl.BlockSpec((1, 2 * width), lambda b, r: (0, 0)),
            pl.BlockSpec((1, step, HEAD), lambda b, r: (b, r, 0)),
            pl.BlockSpec((1, step, HEAD), lambda b, r: (b, r, 0)),
        ],
        out_specs=pl.BlockSpec((heads, 1, 3, step, HEAD), lambda b, r: (0, b, 0, r, 0)),
        out_shape=jax.ShapeDtypeStruct((heads, MB, 3, rows, HEAD), bf16),
        name="pack_heads",
    )(qk_raw, v_raw, inverse, gains, cosines, sines)


def inner_kernel(heads, back_ref, qk_ref, inv_ref, gain_ref, cos_ref, sin_ref, inner_ref, part_ref):
    cosines = cos_ref[0]
    sines = -sin_ref[0]

    @pl.when((pl.program_id(0) == 0) & (pl.program_id(1) == 0))
    def _():
        part_ref[...] = jnp.zeros_like(part_ref)

    for which in range(2):
        total = None
        for head in range(heads):
            cols = head_cols(head, which, heads)
            straight = turn(back_ref[head, 0, which].astype(f32), cosines, sines)
            hat = qk_ref[0, :, cols] * inv_ref[0, :, which : which + 1]
            product = straight * hat
            part_ref[:, cols] += jnp.sum(product, axis=0, keepdims=True)
            weighted = product * gain_ref[:, cols]
            total = weighted if total is None else total + weighted
        inner_ref[0, :, which : which + 1] = jnp.sum(total, axis=1, keepdims=True)


def inner_sums(back, qk_raw, inverse, gains, cosines, sines, heads):
    rows = qk_raw.shape[1]
    step = rows // 2
    width = heads * HEAD
    return pl.pallas_call(
        functools.partial(inner_kernel, heads),
        grid=(MB, rows // step),
        in_specs=[
            pl.BlockSpec((heads, 1, 2, step, HEAD), lambda b, r: (0, b, 0, r, 0)),
            pl.BlockSpec((1, step, 2 * width), lambda b, r: (b, r, 0)),
            pl.BlockSpec((1, step, 2), lambda b, r: (b, r, 0)),
            pl.BlockSpec((1, 2 * width), lambda b, r: (0, 0)),
            pl.BlockSpec((1, step, HEAD), lambda b, r: (b, r, 0)),
            pl.BlockSpec((1, step, HEAD), lambda b, r: (b, r, 0)),
        ],
        out_specs=[
            pl.BlockSpec((1, step, 2), lambda b, r: (b, r, 0)),
            pl.BlockSpec((1, 2 * width), lambda b, r: (0, 0)),
        ],
        out_shape=[
            jax.ShapeDtypeStruct((MB, rows, 2), f32),
            jax.ShapeDtypeStruct((1, 2 * width), f32),
        ],
        name="inner_sums",
    )(back, qk_raw, inverse, gains, cosines, sines)


def unpack_kernel(
    heads, back_ref, qk_ref, inv_ref, mean_ref, gain_ref, cos_ref, sin_ref, out_ref
):
    cosines = cos_ref[0]
    sines = -sin_ref[0]
    for head in range(heads):
        for which in range(2):
            cols = head_cols(head, which, heads)
            inverse = inv_ref[0, :, which : which + 1]
            straight = turn(back_ref[head, 0, which].astype(f32), cosines, sines)
            hat = qk_ref[0, :, cols] * inverse
            grad = inverse * (straight * gain_ref[:, cols] - hat * mean_ref[0, :, which : which + 1])
            out_ref[0, :, cols] = grad.astype(bf16)
        out_ref[0, :, head_cols(head, 2, heads)] = back_ref[head, 0, 2]


def unpack_heads(back, qk_raw, inverse, means, gains, cosines, sines, heads):
    rows = qk_raw.shape[1]
    step = rows // 2
    width = heads * HEAD
    return pl.pallas_call(
        functools.partial(unpack_kernel, heads),
        grid=(MB, rows // step),
        in_specs=[
            pl.BlockSpec((heads, 1, 3, step, HEAD), lambda b, r: (0, b, 0, r, 0)),
            pl.BlockSpec((1, step, 2 * width), lambda b, r: (b, r, 0)),
            pl.BlockSpec((1, step, 2), lambda b, r: (b, r, 0)),
            pl.BlockSpec((1, step, 2), lambda b, r: (b, r, 0)),
            pl.BlockSpec((1, 2 * width), lambda b, r: (0, 0)),
            pl.BlockSpec((1, step, HEAD), lambda b, r: (b, r, 0)),
            pl.BlockSpec((1, step, HEAD), lambda b, r: (b, r, 0)),
        ],
        out_specs=pl.BlockSpec((1, step, 3 * width), lambda b, r: (b, r, 0)),
        out_shape=jax.ShapeDtypeStruct((MB, rows, 3 * width), bf16),
        name="unpack_heads",
    )(back, qk_raw, inverse, means, gains, cosines, sines)


def nt(left, right):
    return lax.dot_general(left, right, (((1,), (1,)), ((), ())), preferred_element_type=f32)


def nn(left, right):
    return lax.dot_general(left, right, (((1,), (0,)), ((), ())), preferred_element_type=f32)


def key_query_iotas(keys):
    key_at = lax.broadcasted_iota(jnp.int32, (keys, PAIR), 0)
    query_at = lax.broadcasted_iota(jnp.int32, (keys, PAIR), 1)
    return key_at, query_at


def causal_mask():
    key_at, query_at = key_query_iotas(PAIR)
    return key_at <= query_at


def apart_mask(above):
    key_at, query_at = key_query_iotas(above + PAIR)
    key_at = key_at - above
    own = (key_at <= query_at) & ((key_at < BLK) == (query_at < BLK))
    return own | (key_at < 0)


def softmax_parts(queries, trunk_keys, near_keys, mask):
    near = jnp.where(mask, nt(near_keys, queries), -1e30)
    top = jnp.max(near, axis=0, keepdims=True)
    if trunk_keys is None:
        near = jnp.exp((near - top) * SCALING)
        scale = 1.0 / jnp.sum(near, axis=0, keepdims=True)
        return None, near * scale
    far = nt(trunk_keys, queries)
    top = jnp.maximum(top, jnp.max(far, axis=0, keepdims=True))
    near = jnp.exp((near - top) * SCALING)
    far = jnp.exp((far - top) * SCALING)
    scale = 1.0 / (jnp.sum(near, axis=0, keepdims=True) + jnp.sum(far, axis=0, keepdims=True))
    return far * scale, near * scale


def places(order_ref, tree):
    def at(within):
        slot = order_ref[tree * TREE_BLOCKS + within]
        return lax.div(slot, SEG_DEV), lax.rem(slot, SEG_DEV)

    return at


def load(ref, which, *spots):
    parts = [ref[group, which, row] for group, row in spots]
    return parts[0] if len(parts) == 1 else jnp.concatenate(parts, axis=0)


def across(values):
    return jnp.transpose(values.astype(f32)).astype(bf16)


def forward_kernel(trees, order_ref, x_ref, y_ref, k_ref, vt_ref):
    def one_tree(tree, carry):
        at = places(order_ref, tree)
        for within in range(TRUNK):
            rows = slice(within * BLK, (within + 1) * BLK)
            spot = at(within)
            k_ref[rows, :] = load(x_ref, 1, spot)
            vt_ref[:, rows] = across(load(x_ref, 2, spot))

        def attend(spots, far_rows, near_keys, near_values, mask):
            queries = load(x_ref, 0, *spots)
            far, near = softmax_parts(
                queries, k_ref[:far_rows, :] if far_rows else None, near_keys, mask
            )
            summed = nn(across(near_values), near.astype(bf16))
            if far_rows:
                summed = summed + nn(vt_ref[:, :far_rows], far.astype(bf16))
            rows = jnp.transpose(summed).astype(bf16)
            y_ref[spots[0][0], spots[0][1]] = rows[:BLK]
            y_ref[spots[1][0], spots[1][1]] = rows[BLK:]

        causal = causal_mask()
        for pair in range(TRUNK // 2):
            spots = (at(2 * pair), at(2 * pair + 1))
            attend(spots, pair * PAIR, load(x_ref, 1, *spots), load(x_ref, 2, *spots), causal)
        apart = apart_mask(0)
        for pair in range(BRANCHES // 2):
            spots = (at(TRUNK + 2 * pair), at(TRUNK + 2 * pair + 1))
            attend(spots, TRUNK_ROWS, load(x_ref, 1, *spots), load(x_ref, 2, *spots), apart)
        under = apart_mask(BLK)
        for branch in range(BRANCHES):
            first = TRUNK + BRANCHES + LEAVES * branch
            spots = (at(first), at(first + 1))
            near = (at(TRUNK + branch),) + spots
            attend(spots, TRUNK_ROWS, load(x_ref, 1, *near), load(x_ref, 2, *near), under)
        return carry

    lax.fori_loop(0, trees, one_tree, 0)


def attend_forward(order, packed):
    groups = packed.shape[0]
    blocks = packed.shape[2]
    trees = groups * blocks // TREE_BLOCKS
    pairs = trees * TREE_BLOCKS * BLK * 1100
    return pl.pallas_call(
        functools.partial(forward_kernel, trees),
        in_specs=[
            pl.BlockSpec(memory_space=pltpu.SMEM),
            pl.BlockSpec(memory_space=pltpu.VMEM),
        ],
        out_specs=pl.BlockSpec(memory_space=pltpu.VMEM),
        out_shape=jax.ShapeDtypeStruct((groups, blocks, BLK, HEAD), bf16),
        scratch_shapes=[
            pltpu.VMEM((TRUNK_ROWS, HEAD), bf16),
            pltpu.VMEM((HEAD, TRUNK_ROWS), bf16),
        ],
        compiler_params=pltpu.CompilerParams(vmem_limit_bytes=VMEM_LIMIT),
        cost_estimate=pl.CostEstimate(
            flops=pairs * HEAD * 4, bytes_accessed=packed.size * 3, transcendentals=pairs
        ),
        name="attend_forward",
    )(order, packed)


def backward_kernel(
    trees, order_ref, x_ref, dy_ref, out_ref, k_ref, kt_ref, v_ref, dk_ref, dv_ref, dkb_ref, dvb_ref
):
    def one_tree(tree, carry):
        at = places(order_ref, tree)
        for within in range(TRUNK):
            rows = slice(within * BLK, (within + 1) * BLK)
            spot = at(within)
            keys = load(x_ref, 1, spot)
            k_ref[rows, :] = keys
            kt_ref[:, rows] = across(keys)
            v_ref[rows, :] = load(x_ref, 2, spot)

        def attend(spots, far_rows, near_spots, mask, start):
            queries = load(x_ref, 0, *spots)
            grads = jnp.concatenate(
                [dy_ref[spots[0][0], spots[0][1]], dy_ref[spots[1][0], spots[1][1]]], axis=0
            )
            near_keys = load(x_ref, 1, *near_spots)
            near_values = load(x_ref, 2, *near_spots)
            far, near = softmax_parts(
                queries, k_ref[:far_rows, :] if far_rows else None, near_keys, mask
            )
            near_grad = nt(near_values, grads)
            inner = jnp.sum(near * near_grad, axis=0, keepdims=True)
            if far_rows:
                far_grad = nt(v_ref[:far_rows, :], grads)
                inner = inner + jnp.sum(far * far_grad, axis=0, keepdims=True)
                far_score = (far * (far_grad - inner)).astype(bf16)
                far_dk = nn(far_score, queries)
                far_dv = nn(far.astype(bf16), grads)
                if start:
                    dk_ref[:far_rows, :] = far_dk
                    dv_ref[:far_rows, :] = far_dv
                else:
                    dk_ref[:far_rows, :] += far_dk
                    dv_ref[:far_rows, :] += far_dv
            near_score = (near * (near_grad - inner)).astype(bf16)
            turned = nn(across(near_keys), near_score)
            if far_rows:
                turned = turned + nn(kt_ref[:, :far_rows], far_score)
            rows = (jnp.transpose(turned) * SCALING).astype(bf16)
            out_ref[spots[0][0], 0, spots[0][1]] = rows[:BLK]
            out_ref[spots[1][0], 0, spots[1][1]] = rows[BLK:]
            return nn(near_score, queries), nn(near.astype(bf16), grads)

        def store(spot, key_grad, value_grad):
            out_ref[spot[0], 1, spot[1]] = (key_grad * SCALING).astype(bf16)
            out_ref[spot[0], 2, spot[1]] = value_grad.astype(bf16)

        under = apart_mask(BLK)
        for branch in range(BRANCHES):
            first = TRUNK + BRANCHES + LEAVES * branch
            spots = (at(first), at(first + 1))
            key_grad, value_grad = attend(
                spots, TRUNK_ROWS, (at(TRUNK + branch),) + spots, under, branch == 0
            )
            dkb_ref[branch] = key_grad[:BLK]
            dvb_ref[branch] = value_grad[:BLK]
            store(spots[0], key_grad[BLK : 2 * BLK], value_grad[BLK : 2 * BLK])
            store(spots[1], key_grad[2 * BLK :], value_grad[2 * BLK :])
        apart = apart_mask(0)
        for pair in range(BRANCHES // 2):
            spots = (at(TRUNK + 2 * pair), at(TRUNK + 2 * pair + 1))
            key_grad, value_grad = attend(spots, TRUNK_ROWS, spots, apart, False)
            for half in range(2):
                rows = slice(half * BLK, (half + 1) * BLK)
                branch = 2 * pair + half
                store(
                    spots[half], key_grad[rows] + dkb_ref[branch], value_grad[rows] + dvb_ref[branch]
                )
        causal = causal_mask()
        for pair in reversed(range(TRUNK // 2)):
            spots = (at(2 * pair), at(2 * pair + 1))
            key_grad, value_grad = attend(spots, pair * PAIR, spots, causal, False)
            for half in range(2):
                rows = slice(half * BLK, (half + 1) * BLK)
                held = slice(pair * PAIR + half * BLK, pair * PAIR + (half + 1) * BLK)
                store(
                    spots[half],
                    key_grad[rows] + dk_ref[held, :],
                    value_grad[rows] + dv_ref[held, :],
                )
        return carry

    lax.fori_loop(0, trees, one_tree, 0)


def attend_backward(order, packed, grads):
    groups = packed.shape[0]
    blocks = packed.shape[2]
    trees = groups * blocks // TREE_BLOCKS
    pairs = trees * TREE_BLOCKS * BLK * 1100
    return pl.pallas_call(
        functools.partial(backward_kernel, trees),
        in_specs=[
            pl.BlockSpec(memory_space=pltpu.SMEM),
            pl.BlockSpec(memory_space=pltpu.VMEM),
            pl.BlockSpec(memory_space=pltpu.VMEM),
        ],
        out_specs=pl.BlockSpec(memory_space=pltpu.VMEM),
        out_shape=jax.ShapeDtypeStruct(packed.shape, bf16),
        scratch_shapes=[
            pltpu.VMEM((TRUNK_ROWS, HEAD), bf16),
            pltpu.VMEM((HEAD, TRUNK_ROWS), bf16),
            pltpu.VMEM((TRUNK_ROWS, HEAD), bf16),
            pltpu.VMEM((TRUNK_ROWS, HEAD), f32),
            pltpu.VMEM((TRUNK_ROWS, HEAD), f32),
            pltpu.VMEM((BRANCHES, BLK, HEAD), f32),
            pltpu.VMEM((BRANCHES, BLK, HEAD), f32),
        ],
        compiler_params=pltpu.CompilerParams(vmem_limit_bytes=VMEM_LIMIT),
        cost_estimate=pl.CostEstimate(
            flops=pairs * HEAD * 10, bytes_accessed=packed.size * 5, transcendentals=pairs
        ),
        name="attend_backward",
    )(order, packed, grads)


def norm_back(gradient, normed, inverse, gain_vec):
    weighted = gradient * gain_vec
    return inverse * (weighted - normed * jnp.mean(normed * weighted, axis=-1, keepdims=True))


def inverse_norm(values):
    return lax.rsqrt(jnp.mean(values * values, axis=-1, keepdims=True) + EPSILON)


def dot(left, right):
    return jnp.dot(left, right, preferred_element_type=f32)


def dot_nt(left, right):
    return lax.dot_general(left, right, (((1,), (1,)), ((), ())), preferred_element_type=f32)


def dot_tn(left, right):
    return lax.dot_general(left, right, (((0,), (0,)), ((), ())), preferred_element_type=f32)


def shards(
    layer_input,
    cotangent,
    w_query,
    w_key,
    w_value,
    w_output,
    w_gate,
    w_up,
    w_down,
    query_gain,
    key_gain,
    attn_gain,
    mlp_gain,
    slot_parent,
    slot_depth,
):
    dp_index = lax.axis_index("dp")
    tp_index = lax.axis_index("tensor")
    dp_count = lax.axis_size("dp")
    tp_count = lax.axis_size("tensor")
    rows = layer_input.shape[1]
    share = rows // tp_count
    width = w_query.shape[1]
    heads = width // HEAD
    hidden_width = w_gate.shape[1]
    items = heads * MB
    copies = dp_count // items

    def gather_rows(shard):
        return lax.all_gather(shard, "dp", axis=0, tiled=True)

    def scatter_rows(total):
        return lax.psum_scatter(
            total.astype(bf16), "dp", scatter_dimension=0, tiled=True
        ).astype(f32)

    def exchange(pieces):
        flat = pieces.reshape((items, -1, HEAD))
        if copies > 1:
            flat = jnp.tile(flat, (copies, 1, 1))
        return lax.all_to_all(flat, "dp", split_axis=0, concat_axis=0, tiled=True)

    def give_back(pieces):
        flat = pieces.reshape((dp_count, -1, HEAD))
        return lax.all_to_all(flat, "dp", split_axis=0, concat_axis=0, tiled=True)[:items]

    w_qkv = gather_rows(jnp.concatenate([w_query, w_key, w_value], axis=1))
    w_out_t = gather_rows(line_all_gather(jnp.transpose(w_output), tp_count))
    w_gate_up = gather_rows(jnp.concatenate([w_gate, w_up], axis=1))
    w_down_t = gather_rows(jnp.transpose(w_down))

    order = tree_order(slot_parent, slot_depth)
    my_batch = lax.rem(lax.rem(dp_index, items), MB)
    my_order = lax.dynamic_index_in_dim(order, my_batch, 0, keepdims=False)
    my_depth = lax.dynamic_slice_in_dim(slot_depth, dp_index * SEG_DEV, SEG_DEV, 1)
    cosines, sines = rope_tables(my_depth)

    tokens = layer_input.reshape(MB * rows, D)
    qk_raw = dot(tokens, w_qkv[:, : 2 * width])
    v_raw = dot(tokens, w_qkv[:, 2 * width :])
    squares = jnp.stack(
        [
            jnp.sum(jnp.square(qk_raw[:, :width]), axis=-1),
            jnp.sum(jnp.square(qk_raw[:, width:]), axis=-1),
        ]
    )
    squares = small_sum(squares, "tensor", tp_count)
    inverse = jnp.transpose(lax.rsqrt(squares / D + EPSILON)).reshape(MB, rows, 2)
    qk_raw = qk_raw.reshape(MB, rows, 2 * width)
    v_raw = v_raw.reshape(MB, rows, width)
    gains = jnp.concatenate([query_gain, key_gain])[None, :]
    packed = pack_heads(qk_raw, v_raw, inverse, gains, cosines, sines, heads)
    packed = exchange(packed).reshape(dp_count, 3, SEG_DEV, BLK, HEAD)

    attended = give_back(attend_forward(my_order, packed))
    attended = attended.reshape(heads, MB, rows, HEAD).transpose(1, 2, 0, 3)
    attended = attended.reshape(MB, rows, width)

    kept = []
    outputs = []
    for batch in range(MB):
        everything = line_all_gather(attended[batch], tp_count)
        attn_proj = dot_nt(everything, w_out_t)
        attn_inv = inverse_norm(attn_proj)
        hidden = layer_input[batch].astype(f32) + attn_proj * attn_inv * attn_gain
        hidden_low = hidden.astype(bf16)
        gate_pre = dot(hidden_low, w_gate_up[:, :hidden_width])
        up_pre = dot(hidden_low, w_gate_up[:, hidden_width:])
        act_low = (jax.nn.silu(gate_pre) * up_pre).astype(bf16)
        half = rows // 2
        sums = line_all_reduce(
            [
                dot_nt(act_low[:half], w_down_t).astype(bf16),
                dot_nt(act_low[half:], w_down_t).astype(bf16),
            ],
            tp_count,
        )
        mlp_proj = jnp.concatenate(sums, axis=0).astype(f32)
        mlp_inv = inverse_norm(mlp_proj)
        mlp_normed = mlp_proj * mlp_inv
        outputs.append((hidden + mlp_normed * mlp_gain).astype(bf16))
        out_grad = cotangent[batch]
        mlp_grad = norm_back(out_grad, mlp_normed, mlp_inv, mlp_gain).astype(bf16)
        mlp_gain_part = jnp.sum(out_grad * mlp_normed, axis=0)
        act_grad = dot(mlp_grad, w_down_t)
        sigmoid_gate = jax.nn.sigmoid(gate_pre)
        up_grad = (act_grad * gate_pre * sigmoid_gate).astype(bf16)
        gate_grad = (
            act_grad * up_pre * sigmoid_gate * (1.0 + gate_pre * (1.0 - sigmoid_gate))
        ).astype(bf16)
        branch_sums = line_all_reduce(
            [
                (
                    dot_nt(gate_grad[part], w_gate_up[:, :hidden_width])
                    + dot_nt(up_grad[part], w_gate_up[:, hidden_width:])
                ).astype(bf16)
                for part in (slice(0, half), slice(half, rows))
            ],
            tp_count,
        )
        hidden_grad = out_grad + jnp.concatenate(branch_sums, axis=0).astype(f32)
        attn_normed = attn_proj * attn_inv
        proj_grad = norm_back(hidden_grad, attn_normed, attn_inv, attn_gain).astype(bf16)
        attn_gain_part = jnp.sum(hidden_grad * attn_normed, axis=0)
        own_out_t = lax.dynamic_slice_in_dim(w_out_t, tp_index * width, width, 1)
        attn_grad = dot(proj_grad, own_out_t).astype(bf16)
        kept.append(
            dict(
                hidden_low=hidden_low,
                act_low=act_low,
                mlp_grad=mlp_grad,
                up_grad=up_grad,
                gate_grad=gate_grad,
                proj_grad=proj_grad,
                attn_grad=attn_grad,
                residual=lax.dynamic_slice_in_dim(hidden_grad, tp_index * share, share, 0),
                mlp_gain_part=mlp_gain_part,
                attn_gain_part=attn_gain_part,
            )
        )

    def both(name):
        return jnp.concatenate([part[name] for part in kept], axis=0)

    hidden_low = both("hidden_low")
    down_grad = scatter_rows(dot_tn(both("mlp_grad"), both("act_low")))
    gate_up_grad = scatter_rows(
        jnp.concatenate(
            [dot_tn(hidden_low, both("gate_grad")), dot_tn(hidden_low, both("up_grad"))], axis=1
        )
    )
    output_grad = scatter_rows(dot_tn(both("proj_grad"), attended.reshape(MB * rows, width)))

    attn_grad = jnp.stack([part["attn_grad"] for part in kept])
    attn_grad = attn_grad.reshape(MB, rows, heads, HEAD).transpose(2, 0, 1, 3)
    attn_grad = exchange(attn_grad).reshape(dp_count, SEG_DEV, BLK, HEAD)
    back = give_back(attend_backward(my_order, packed, attn_grad))
    back = back.reshape(heads, MB, 3, rows, HEAD)
    inner, gain_part = inner_sums(back, qk_raw, inverse, gains, cosines, sines, heads)
    means = small_sum(jnp.transpose(inner.reshape(-1, 2)), "tensor", tp_count) / D
    means = jnp.transpose(means).reshape(MB, rows, 2)
    qkv_grad = unpack_heads(back, qk_raw, inverse, means, gains, cosines, sines, heads)

    input_parts = []
    for batch in range(MB):
        term = dot_nt(qkv_grad[batch], w_qkv).astype(bf16)
        input_parts.append(kept[batch]["residual"] + line_reduce_scatter(term, tp_count))
    qkv_weight_grad = scatter_rows(dot_tn(tokens, qkv_grad.reshape(MB * rows, 3 * width)))

    gain_sums = jnp.concatenate(
        [
            gain_part[0],
            sum(part["attn_gain_part"] for part in kept),
            sum(part["mlp_gain_part"] for part in kept),
        ]
    )
    gain_sums = small_sum(gain_sums.reshape(-1, HEAD), "dp", dp_count).reshape(-1)
    return (
        jnp.stack(outputs),
        jnp.stack(input_parts),
        qkv_weight_grad[:, :width],
        qkv_weight_grad[:, width : 2 * width],
        qkv_weight_grad[:, 2 * width :],
        jnp.transpose(output_grad),
        gate_up_grad[:, :hidden_width],
        gate_up_grad[:, hidden_width:],
        jnp.transpose(down_grad),
        gain_sums[:width],
        gain_sums[width : 2 * width],
        gain_sums[2 * width : 2 * width + D],
        gain_sums[2 * width + D :],
    )


def solution(mesh):
    in_specs = (
        P(None, "dp", None),
        P(None, "dp", None),
        P("dp", "tensor"),
        P("dp", "tensor"),
        P("dp", "tensor"),
        P("tensor", "dp"),
        P("dp", "tensor"),
        P("dp", "tensor"),
        P("tensor", "dp"),
        P("tensor"),
        P("tensor"),
        P(),
        P(),
        P(),
        P(),
    )
    out_specs = (
        P(None, "dp", None),
        P(None, ("dp", "tensor"), None),
        P("dp", "tensor"),
        P("dp", "tensor"),
        P("dp", "tensor"),
        P("tensor", "dp"),
        P("dp", "tensor"),
        P("dp", "tensor"),
        P("tensor", "dp"),
        P("tensor"),
        P("tensor"),
        P(),
        P(),
    )
    return jax.shard_map(shards, mesh=mesh, in_specs=in_specs, out_specs=out_specs, check_vma=False)
```

time: 3100 us -> 1270 us (0.41)
  waiting for transfers between devices: 2020 us -> 504 us
  other arithmetic: 365 us -> 101 us
  local copies, waits for them, and re-layouts: 214 us -> 49 us
  matrix products: 406 us -> 253 us
  starting transfers between devices: 12.4 us -> 120 us
  blocking collectives: 60.4 us -> 145 us
  Pallas kernels: 0 us -> 70.2 us
    psum x3 -> x0, waiting for transfers between devices: 1070 us -> none  [the longest x1 359 us: shards(): lax.psum(jnp.dot(act_low, down_full, preferred_element_type=jnp.float32),...]
    reduce_scatter x20 -> x4, waiting for transfers between devices: 714 us -> 5.42 us  [scatter_rows(): lax.psum_scatter(total.astype(bf16), 'dp', scatter_dimension=0, tiled=True)]
    ppermute x0 -> x61, waiting for transfers between devices: none -> 432 us  [the longest x8 200 us: line_all_reduce(): back = lax.ppermute(total, 'tensor', [(1, 0), (2, 3)])]
    all_gather x11 -> x4, waiting for transfers between devices: 222 us -> 10.8 us  [gather_rows(): return lax.all_gather(shard, 'dp', axis=0, tiled=True)]
    scatter-add x4 -> x0, other arithmetic: 179 us -> none  [the longest x2 89.5 us: shards(): value_full_grad = jnp.zeros((value_all.shape[0], width_here), jnp.float32...]
    dot_general x114 -> x31, matrix products: 406 us -> 253 us  [the longest x10 95.7 us: dot(): return jnp.dot(left, right, preferred_element_type=f32)]
    all_to_all x0 -> x3, blocking collectives: none -> 145 us  [the longest x2 105 us: give_back(): lax.all_to_all(flat, 'dp', split_axis=0, concat_axis=0, tiled=True)[:items]]
    ppermute x0 -> x61, starting transfers between devices: none -> 114 us  [the longest x3 17.1 us: line_all_gather(): right1 = lax.ppermute(values, 'tensor', [(0, 1), (1, 2), (2, 3)])]
  transfers between devices with their start and end apart: 34 -> 70, of which waited for: 25 -> 37; matrix products, arithmetic and copies ran while one was open for 23% -> 25% of each run, Pallas kernels for 0% -> 6%
where the time goes in v1:
time: 1270 us; the launch traced here: 1260 us
  waiting for transfers between devices  504 us (40%)
  matrix products  253 us (20%)
  blocking collectives  145 us (11%)
  starting transfers between devices  120 us (9%)
  other arithmetic  101 us (8%)
  Pallas kernels  70.2 us (6%)
  local copies, waits for them, and re-layouts  49 us (4%)
  between operations  16.4 us (1%)
    ppermute x8, waiting for transfers between devices, line_all_reduce(): back = lax.ppermute(total, 'tensor', [(1, 0), (2, 3)])  200 us
    ppermute x8, waiting for transfers between devices, line_all_reduce(): outer = lax.ppermute(chunk, 'tensor', [(0, 1), (3, 2)])  112 us
    all_to_all x2, blocking collectives, give_back(): lax.all_to_all(flat, 'dp', split_axis=0, concat_axis=0, tiled=True)[:items]  105 us
    dot_general x10, matrix products, dot(): return jnp.dot(left, right, preferred_element_type=f32)  95.7 us
    dot_general x16, matrix products, dot_nt(): lax.dot_general(left, right, (((1,), (1,)), ((), ())), preferred_element_...  91.5 us
    dot_general x5, matrix products, dot_tn(): lax.dot_general(left, right, (((0,), (0,)), ((), ())), preferred_element_...  65.6 us
    all_to_all x1, waiting for transfers between devices, exchange(): return lax.all_to_all(flat, 'dp', split_axis=0, concat_axis=0, tiled=True)  55.7 us
    all_to_all x1, blocking collectives, exchange(): return lax.all_to_all(flat, 'dp', split_axis=0, concat_axis=0, tiled=True)  39.9 us
  transfers between devices with their start and end apart: 70, of which 37 were waited for; matrix products, arithmetic and copies ran while one was open for 25% of the time, Pallas kernels for 6%

profile of v1, /device:TPU:0, one launch (start us, length us, event | category | flops | bytes accessed | tf_op | source)
XLA Modules:
  0.0 1257.9 jit_solution(15406689744071081066)
XLA Ops:
  107.3 55.7 %all-to-all-done = bf16[8,1920,128]{2,1,0:T(8,128)(2,1)} async-done(((bf16[8,1920,128]{2,1,0:T(8,128)(2,1)}), bf16[8,1920,128]{2,1,0:T(8,128)(2,1)}, u32[]{:S(2)}, u32[]{:S(2)}) %all-to-all-start) | async-done | bytes 3932192 | tf_op jit(solution)/shard_map/all_to_all | solution.py:571
  163.1 16.4 %attend_forward.1 = bf16[8,5,128,128]{3,2,1,0:T(8,128)(2,1)} custom-call(s32[40]{0:T(128)} %fusion.146.order_ref, bf16[8,3,5,128,128]{4,3,2,1,0:T(8,128)(2,1)} %bitcast.12.x_ref), custom_call_target="tpu_custom_call" | custom-call | flops 2883584000 | bytes 5898240 | tf_op jit(solution)/shard_map/attend_forward/pallas_call | solution.py:370
  179.4 35.6 %all_to_all.20 = bf16[8,640,128]{2,1,0:T(8,128)(2,1)S(1)} all-to-all(bf16[8,640,128]{2,1,0:T(8,128)(2,1)} %bitcast.222), channel_id=1, replica_groups=mesh['dp'=8,'tensor'=4] {'dp'}, dimensions={0} | all-to-all | bytes 2621440 | tf_op jit(solution)/shard_map/all_to_all | solution.py:575
  239.0 11.1 collective-permute-done.21
  252.9 11.2 collective-permute-done.4
  280.7 11.6 collective-permute-done.5
  322.7 12.0 fusion.62
  366.9 11.7 multiply_convert_fusion.7
  388.6 21.8 %collective-permute-done.29 = bf16[320,2048]{1,0:T(8,128)(2,1)S(1)} collective-permute-done((bf16[320,2048]{1,0:T(8,128)(2,1)S(1)}, bf16[320,2048]{1,0:T(8,128)(2,1)S(1)}, u32[]{:S(2)}, u32[]{:S(2)}) %collective-permute-start.29) | collective-permute-done | bytes 1310752 | tf_op jit(solution)/shard_map/ppermute | solution.py:89
  411.6 26.8 %collective-permute-done.14 = bf16[320,2048]{1,0:T(8,128)(2,1)S(1)} collective-permute-done((bf16[320,2048]{1,0:T(8,128)(2,1)S(1)}, bf16[320,2048]{1,0:T(8,128)(2,1)S(1)}, u32[]{:S(2)}, u32[]{:S(2)}) %collective-permute-start.14) | collective-permute-done | bytes 1310752 | tf_op jit(solution)/shard_map/ppermute | solution.py:89
  439.8 18.3 %collective-permute-done.17 = bf16[320,2048]{1,0:T(8,128)(2,1)S(1)} collective-permute-done((bf16[320,2048]{1,0:T(8,128)(2,1)S(1)}, bf16[320,2048]{1,0:T(8,128)(2,1)S(1)}, u32[]{:S(2)}, u32[]{:S(2)}) %collective-permute-start.17) | collective-permute-done | bytes 1310752 | tf_op jit(solution)/shard_map/ppermute | solution.py:89
  466.9 28.1 %collective-permute-done.28 = bf16[320,2048]{1,0:T(8,128)(2,1)S(1)} collective-permute-done((bf16[320,2048]{1,0:T(8,128)(2,1)S(1)}, bf16[320,2048]{1,0:T(8,128)(2,1)S(1)}, u32[]{:S(2)}, u32[]{:S(2)}) %collective-permute-start.28) | collective-permute-done | bytes 1310752 | tf_op jit(solution)/shard_map/ppermute | solution.py:93
  495.2 27.9 %collective-permute-done.31 = bf16[320,2048]{1,0:T(8,128)(2,1)S(1)} collective-permute-done((bf16[320,2048]{1,0:T(8,128)(2,1)S(1)}, bf16[320,2048]{1,0:T(8,128)(2,1)S(1)}, u32[]{:S(2)}, u32[]{:S(2)}) %collective-permute-start.31) | collective-permute-done | bytes 1310752 | tf_op jit(solution)/shard_map/ppermute | solution.py:93
  523.8 27.3 %collective-permute-done.16 = bf16[320,2048]{1,0:T(8,128)(2,1)S(1)} collective-permute-done((bf16[320,2048]{1,0:T(8,128)(2,1)S(1)}, bf16[320,2048]{1,0:T(8,128)(2,1)S(1)}, u32[]{:S(2)}, u32[]{:S(2)}) %collective-permute-start.16) | collective-permute-done | bytes 1310752 | tf_op jit(solution)/shard_map/ppermute | solution.py:93
  551.3 18.4 %collective-permute-done.19 = bf16[320,2048]{1,0:T(8,128)(2,1)S(1)} collective-permute-done((bf16[320,2048]{1,0:T(8,128)(2,1)S(1)}, bf16[320,2048]{1,0:T(8,128)(2,1)S(1)}, u32[]{:S(2)}, u32[]{:S(2)}) %collective-permute-start.19) | collective-permute-done | bytes 1310752 | tf_op jit(solution)/shard_map/ppermute | solution.py:93
  578.7 15.2 %multiply_convert_fusion.2 = (bf16[640,2048]{1,0:T(8,128)(2,1)S(1)}, bf16[640,2048]{1,0:T(8,128)(2,1)}) fusion(f32[640,2048]{1,0:T(8,128)} %fusion.62, f32[640,2048]{1,0:T(8,128)} %get-tuple-element.127, bf16[640,2048]{1,0:T(8,128)(2,1)S(1)} %get-tuple-element.87, bf16[2048,2048]{0,1:T(8,128)(2,1)} %all-gather.11.cloned.1.call-done), kind=kOutput, calls=%fused_computation.63 | convolution fusion | flops 5385748480 | bytes 26738688 | tf_op jit(solution)/shard_map/dot_general | solution.py:519
  622.1 13.9 %multiply_convert_fusion.5 = (bf16[640,2048]{1,0:T(8,128)(2,1)}, bf16[640,2048]{1,0:T(8,128)(2,1)}) fusion(f32[640,2048]{1,0:T(8,128)} %fusion.64, f32[640,2048]{1,0:T(8,128)} %get-tuple-element.125, bf16[640,2048]{1,0:T(8,128)(2,1)S(1)} %get-tuple-element.86, bf16[2048,2048]{0,1:T(8,128)(2,1)} %all-gather.11.cloned.1.call-done), kind=kOutput, calls=%fused_computation.67 | convolution fusion | flops 5385748480 | bytes 26738688 | tf_op jit(solution)/shard_map/dot_general | solution.py:519
  667.3 26.9 %collective-permute-done.35 = bf16[320,2048]{1,0:T(8,128)(2,1)S(1)} collective-permute-done((bf16[320,2048]{1,0:T(8,128)(2,1)S(1)}, bf16[320,2048]{1,0:T(8,128)(2,1)S(1)}, u32[]{:S(2)}, u32[]{:S(2)}) %collective-permute-start.35) | collective-permute-done | bytes 1310752 | tf_op jit(solution)/shard_map/ppermute | solution.py:89
  695.4 16.4 %collective-permute-done.32 = bf16[320,2048]{1,0:T(8,128)(2,1)S(1)} collective-permute-done((bf16[320,2048]{1,0:T(8,128)(2,1)S(1)}, bf16[320,2048]{1,0:T(8,128)(2,1)S(1)}, u32[]{:S(2)}, u32[]{:S(2)}) %collective-permute-start.32) | collective-permute-done | bytes 1310752 | tf_op jit(solution)/shard_map/ppermute | solution.py:89
  721.2 28.7 %collective-permute-done.43 = bf16[320,2048]{1,0:T(8,128)(2,1)S(1)} collective-permute-done((bf16[320,2048]{1,0:T(8,128)(2,1)S(1)}, bf16[320,2048]{1,0:T(8,128)(2,1)S(1)}, u32[]{:S(2)}, u32[]{:S(2)}) %collective-permute-start.43) | collective-permute-done | bytes 1310752 | tf_op jit(solution)/shard_map/ppermute | solution.py:93
  751.1 26.9 %collective-permute-done.40 = bf16[320,2048]{1,0:T(8,128)(2,1)S(1)} collective-permute-done((bf16[320,2048]{1,0:T(8,128)(2,1)S(1)}, bf16[320,2048]{1,0:T(8,128)(2,1)S(1)}, u32[]{:S(2)}, u32[]{:S(2)}) %collective-permute-start.40) | collective-permute-done | bytes 1310752 | tf_op jit(solution)/shard_map/ppermute | solution.py:93
  779.2 26.9 %collective-permute-done.37 = bf16[320,2048]{1,0:T(8,128)(2,1)S(1)} collective-permute-done((bf16[320,2048]{1,0:T(8,128)(2,1)S(1)}, bf16[320,2048]{1,0:T(8,128)(2,1)S(1)}, u32[]{:S(2)}, u32[]{:S(2)}) %collective-permute-start.37) | collective-permute-done | bytes 1310752 | tf_op jit(solution)/shard_map/ppermute | solution.py:93
  807.3 15.7 %collective-permute-done.34 = bf16[320,2048]{1,0:T(8,128)(2,1)S(1)} collective-permute-done((bf16[320,2048]{1,0:T(8,128)(2,1)S(1)}, bf16[320,2048]{1,0:T(8,128)(2,1)S(1)}, u32[]{:S(2)}, u32[]{:S(2)}) %collective-permute-start.34) | collective-permute-done | bytes 1310752 | tf_op jit(solution)/shard_map/ppermute | solution.py:93
  832.8 14.0 %fusion.96 = (bf16[1,640,2048]{2,1,0:T(8,128)(2,1)S(1)}, bf16[1,640,2048]{2,1,0:T(8,128)(2,1)}, bf16[640,2048]{1,0:T(8,128)(2,1)S(1)}, bf16[640,2048]{1,0:T(8,128)(2,1)S(1)}) fusion(f32[640,2048]{1,0:T(8,128)S(1)} %bitcast.188, f32[2048]{0:T(1024)S(1)} %copy-done.27, f32[640]{0:T(1024)S(1)} %add_rsqrt_fusion.2, f32[2048]{0:T(1024)S(1)} %copy-done.29, ...), kind=kLoop, calls=%fused_computation.119 | loop fusion | flops 44564480 | bytes 41974784 | tf_op jit(solution)/shard_map/stack | solution.py:709
  853.6 16.8 %convolution_convert_fusion = bf16[2048,2048]{1,0:T(8,128)(2,1)} fusion(bf16[640,2048]{1,0:T(8,128)(2,1)} %copy-done.18, bf16[640,2048]{1,0:T(8,128)(2,1)} %copy-done.17, bf16[640,2048]{1,0:T(8,128)(2,1)} %get-tuple-element.126, bf16[640,2048]{1,0:T(8,128)(2,1)} %copy-done.50), kind=kOutput, calls=%fused_computation.2 | convolution fusion | flops 10762584064 | bytes 18874368 | tf_op jit(solution)/shard_map/dot_general | solution.py:527
  882.1 39.9 %all_to_all.21 = bf16[8,640,128]{2,1,0:T(8,128)(2,1)} all-to-all(bf16[8,640,128]{2,1,0:T(8,128)(2,1)} %bitcast.214), channel_id=1, replica_groups=mesh['dp'=8,'tensor'=4] {'dp'}, dimensions={0} | all-to-all | bytes 2621440 | tf_op jit(solution)/shard_map/all_to_all | solution.py:571
  922.0 30.9 %attend_backward.1 = bf16[8,3,5,128,128]{4,3,2,1,0:T(8,128)(2,1)} custom-call(s32[40]{0:T(128)} %fusion.146.order_ref, bf16[8,3,5,128,128]{4,3,2,1,0:T(8,128)(2,1)} %bitcast.12.x_ref, bf16[8,5,128,128]{3,2,1,0:T(8,128)(2,1)} %bitcast.221), custom_call_target="tpu_custom_call" | custom-call | flops 7208960000 | bytes 9830400 | tf_op jit(solution)/shard_map/attend_backward/pallas_call | solution.py:483
  952.9 69.5 %all_to_all.22 = bf16[8,1920,128]{2,1,0:T(8,128)(2,1)} all-to-all(bf16[8,1920,128]{2,1,0:T(8,128)(2,1)} %bitcast.215), channel_id=1, replica_groups=mesh['dp'=8,'tensor'=4] {'dp'}, dimensions={0} | all-to-all | bytes 7864320 | tf_op jit(solution)/shard_map/all_to_all | solution.py:575
  1048.1 13.2 %fusion.8 = bf16[2048,1536]{0,1:T(8,128)(2,1)} fusion(bf16[2,640,1536]{2,1,0:T(8,128)(2,1)} %unpack_heads.1, bf16[2,640,2048]{2,1,0:T(8,128)(2,1)} %param.15), kind=kOutput, calls=%fused_computation.17 | convolution fusion | flops 8056209408 | bytes 15466496 | tf_op jit(solution)/shard_map/dot_general | solution.py:527
  1061.4 14.7 %convolution_convert_fusion.2 = bf16[2048,2048]{0,1:T(8,128)(2,1)S(1)} fusion(bf16[640,2048]{1,0:T(8,128)(2,1)} %copy-done.44, bf16[640,2048]{1,0:T(8,128)(2,1)} %get-tuple-element.88, bf16[640,2048]{1,0:T(8,128)(2,1)} %get-tuple-element.97, bf16[640,2048]{1,0:T(8,128)(2,1)} %copy-done.14), kind=kOutput, calls=%fused_computation.4 | convolution fusion | flops 10762584064 | bytes 18874368 | tf_op jit(solution)/shard_map/dot_general | solution.py:527
  1076.1 16.8 %convolution_convert_fusion.1 = bf16[2048,2048]{0,1:T(8,128)(2,1)} fusion(bf16[640,2048]{1,0:T(8,128)(2,1)} %get-tuple-element.91, bf16[640,2048]{1,0:T(8,128)(2,1)} %get-tuple-element.89, bf16[640,2048]{1,0:T(8,128)(2,1)} %get-tuple-element.97, bf16[640,2048]{1,0:T(8,128)(2,1)} %copy-done.14), kind=kOutput, calls=%fused_computation.3 | convolution fusion | flops 10762584064 | bytes 18874368 | tf_op jit(solution)/shard_map/dot_general | solution.py:527
  1092.8 10.9 pad_maximum_fusion
  (414 shorter events, 510.5 us)
Async XLA Ops:
  7.2 51.5 %all-gather.5.cloned.1.call-start = ((), (), s32[]{:S(2)}) async-start(), calls=%async_computation.8 | async-start | bytes 7077888 | tf_op jit(solution)/shard_map/all_gather | solution.py:560
  9.4 288.1 %all-gather.7.cloned.1.call-start = ((), (), s32[]{:S(2)}) async-start(), calls=%async_computation.9 | async-start | bytes 9437184 | tf_op jit(solution)/shard_map/all_gather | solution.py:560
  42.4 280.3 %all-gather.9.cloned.1.call-start = ((), (), s32[]{:S(2)}) async-start(), calls=%async_computation.10 | async-start | bytes 18874368 | tf_op jit(solution)/shard_map/all_gather | solution.py:560
  100.2 62.8 %all-to-all-start = ((bf16[8,1920,128]{2,1,0:T(8,128)(2,1)}), bf16[8,1920,128]{2,1,0:T(8,128)(2,1)}, u32[]{:S(2)}, u32[]{:S(2)}) async-start(bf16[8,1920,128]{2,1,0:T(8,128)(2,1)} %bitcast.197), calls=%async_computation | async-start | bytes 7864320 | tf_op jit(solution)/shard_map/all_to_all | solution.py:571
  104.9 239.9 %all-gather.11.cloned.1.call-start = ((), (), s32[]{:S(2)}) async-start(), calls=%async_computation.11 | async-start | bytes 9437184 | tf_op jit(solution)/shard_map/all_gather | solution.py:560
  105.5 1055.9 %reduce-scatter.7.cloned.1.call-start = ((), (), s32[]{:S(2)}) async-start(), calls=%async_computation.13 | async-start | bytes 2359296 | tf_op jit(solution)/shard_map/reduce_scatter | solution.py:563
  237.5 33.7 %collective-permute-start.6 = (bf16[640,512]{0,1:T(8,128)(2,1)}, bf16[640,512]{0,1:T(8,128)(2,1)}, u32[]{:S(2)}, u32[]{:S(2)}) collective-permute-start(bf16[640,512]{0,1:T(8,128)(2,1)} %collective-permute-done.2), channel_id=1, source_target_pairs={{1,2},{2,3},{5,6},{6,7},{9,10},{10,11},{13,14},{14,15},{17,18},{18... | collective-permute-start | bytes 1966088 | tf_op jit(solution)/shard_map/ppermute | solution.py:123
  351.6 35.8 %collective-permute-start.26 = (bf16[320,2048]{1,0:T(8,128)(2,1)S(1)}, bf16[320,2048]{1,0:T(8,128)(2,1)S(1)}, u32[]{:S(2)}, u32[]{:S(2)}) collective-permute-start(bf16[320,2048]{1,0:T(8,128)(2,1)S(1)} %convolution_convert_fusion.6), channel_id=1, source_target_pairs={{0,1},{3,2},{4,5},{7,6},{8,9},{11,10},{12,13},{15,14},{16,17},{19,... | collective-permute-start | bytes 3932168 | tf_op jit(solution)/shard_map/ppermute | solution.py:89
  356.1 54.3 %collective-permute-start.29 = (bf16[320,2048]{1,0:T(8,128)(2,1)S(1)}, bf16[320,2048]{1,0:T(8,128)(2,1)S(1)}, u32[]{:S(2)}, u32[]{:S(2)}) collective-permute-start(bf16[320,2048]{1,0:T(8,128)(2,1)S(1)} %convolution_convert_fusion.5), channel_id=1, source_target_pairs={{0,1},{3,2},{4,5},{7,6},{8,9},{11,10},{12,13},{15,14},{16,17},{19,... | collective-permute-start | bytes 3932168 | tf_op jit(solution)/shard_map/ppermute | solution.py:89
  381.6 56.8 %collective-permute-start.14 = (bf16[320,2048]{1,0:T(8,128)(2,1)S(1)}, bf16[320,2048]{1,0:T(8,128)(2,1)S(1)}, u32[]{:S(2)}, u32[]{:S(2)}) collective-permute-start(bf16[320,2048]{1,0:T(8,128)(2,1)S(1)} %convolution_convert_fusion.8), channel_id=1, source_target_pairs={{0,1},{3,2},{4,5},{7,6},{8,9},{11,10},{12,13},{15,14},{16,17},{19,... | collective-permute-start | bytes 3932168 | tf_op jit(solution)/shard_map/ppermute | solution.py:89
  385.9 72.1 %collective-permute-start.17 = (bf16[320,2048]{1,0:T(8,128)(2,1)S(1)}, bf16[320,2048]{1,0:T(8,128)(2,1)S(1)}, u32[]{:S(2)}, u32[]{:S(2)}) collective-permute-start(bf16[320,2048]{1,0:T(8,128)(2,1)S(1)} %convolution_convert_fusion.7), channel_id=1, source_target_pairs={{0,1},{3,2},{4,5},{7,6},{8,9},{11,10},{12,13},{15,14},{16,17},{19,... | collective-permute-start | bytes 3932168 | tf_op jit(solution)/shard_map/ppermute | solution.py:89
  387.8 71.5 %collective-permute-start.27 = (bf16[320,2048]{1,0:T(8,128)(2,1)S(1)}, bf16[320,2048]{1,0:T(8,128)(2,1)S(1)}, u32[]{:S(2)}, u32[]{:S(2)}) collective-permute-start(bf16[320,2048]{1,0:T(8,128)(2,1)S(1)} %add_convert_fusion.11), channel_id=1, source_target_pairs={{1,2},{2,1},{5,6},{6,5},{9,10},{10,9},{13,14},{14,13},{17,18},{18,... | collective-permute-start | bytes 3932168 | tf_op jit(solution)/shard_map/ppermute | solution.py:91
  410.9 50.2 %collective-permute-start.30 = (bf16[320,2048]{1,0:T(8,128)(2,1)S(1)}, bf16[320,2048]{1,0:T(8,128)(2,1)S(1)}, u32[]{:S(2)}, u32[]{:S(2)}) collective-permute-start(bf16[320,2048]{1,0:T(8,128)(2,1)S(1)} %add_convert_fusion.9), channel_id=1, source_target_pairs={{1,2},{2,1},{5,6},{6,5},{9,10},{10,9},{13,14},{14,13},{17,18},{18,... | collective-permute-start | bytes 3932168 | tf_op jit(solution)/shard_map/ppermute | solution.py:91
  459.8 35.2 %collective-permute-start.28 = (bf16[320,2048]{1,0:T(8,128)(2,1)S(1)}, bf16[320,2048]{1,0:T(8,128)(2,1)S(1)}, u32[]{:S(2)}, u32[]{:S(2)}) collective-permute-start(bf16[320,2048]{1,0:T(8,128)(2,1)S(1)} %add_convert_fusion.10), channel_id=1, source_target_pairs={{1,0},{2,3},{5,4},{6,7},{9,8},{10,11},{13,12},{14,15},{17,16},{18,... | collective-permute-start | bytes 3932168 | tf_op jit(solution)/shard_map/ppermute | solution.py:93
  461.6 61.5 %collective-permute-start.31 = (bf16[320,2048]{1,0:T(8,128)(2,1)S(1)}, bf16[320,2048]{1,0:T(8,128)(2,1)S(1)}, u32[]{:S(2)}, u32[]{:S(2)}) collective-permute-start(bf16[320,2048]{1,0:T(8,128)(2,1)S(1)} %add_convert_fusion.8), channel_id=1, source_target_pairs={{1,0},{2,3},{5,4},{6,7},{9,8},{10,11},{13,12},{14,15},{17,16},{18,... | collective-permute-start | bytes 3932168 | tf_op jit(solution)/shard_map/ppermute | solution.py:93
  463.4 87.8 %collective-permute-start.16 = (bf16[320,2048]{1,0:T(8,128)(2,1)S(1)}, bf16[320,2048]{1,0:T(8,128)(2,1)S(1)}, u32[]{:S(2)}, u32[]{:S(2)}) collective-permute-start(bf16[320,2048]{1,0:T(8,128)(2,1)S(1)} %add_convert_fusion.14), channel_id=1, source_target_pairs={{1,0},{2,3},{5,4},{6,7},{9,8},{10,11},{13,12},{14,15},{17,16},{18,... | collective-permute-start | bytes 3932168 | tf_op jit(solution)/shard_map/ppermute | solution.py:93
  465.2 104.5 %collective-permute-start.19 = (bf16[320,2048]{1,0:T(8,128)(2,1)S(1)}, bf16[320,2048]{1,0:T(8,128)(2,1)S(1)}, u32[]{:S(2)}, u32[]{:S(2)}) collective-permute-start(bf16[320,2048]{1,0:T(8,128)(2,1)S(1)} %add_convert_fusion.12), channel_id=1, source_target_pairs={{1,0},{2,3},{5,4},{6,7},{9,8},{10,11},{13,12},{14,15},{17,16},{18,... | collective-permute-start | bytes 3932168 | tf_op jit(solution)/shard_map/ppermute | solution.py:93
  607.0 56.0 %collective-permute-start.41 = (bf16[320,2048]{1,0:T(8,128)(2,1)S(1)}, bf16[320,2048]{1,0:T(8,128)(2,1)S(1)}, u32[]{:S(2)}, u32[]{:S(2)}) collective-permute-start(bf16[320,2048]{1,0:T(8,128)(2,1)S(1)} %fusion.83), channel_id=1, source_target_pairs={{0,1},{3,2},{4,5},{7,6},{8,9},{11,10},{12,13},{15,14},{16,17},{19,... | collective-permute-start | bytes 3932168 | tf_op jit(solution)/shard_map/ppermute | solution.py:89
  620.7 45.4 %collective-permute-start.38 = (bf16[320,2048]{1,0:T(8,128)(2,1)S(1)}, bf16[320,2048]{1,0:T(8,128)(2,1)S(1)}, u32[]{:S(2)}, u32[]{:S(2)}) collective-permute-start(bf16[320,2048]{1,0:T(8,128)(2,1)S(1)} %fusion.86), channel_id=1, source_target_pairs={{0,1},{3,2},{4,5},{7,6},{8,9},{11,10},{12,13},{15,14},{16,17},{19,... | collective-permute-start | bytes 3932168 | tf_op jit(solution)/shard_map/ppermute | solution.py:89
  648.3 45.8 %collective-permute-start.35 = (bf16[320,2048]{1,0:T(8,128)(2,1)S(1)}, bf16[320,2048]{1,0:T(8,128)(2,1)S(1)}, u32[]{:S(2)}, u32[]{:S(2)}) collective-permute-start(bf16[320,2048]{1,0:T(8,128)(2,1)S(1)} %fusion.89), channel_id=1, source_target_pairs={{0,1},{3,2},{4,5},{7,6},{8,9},{11,10},{12,13},{15,14},{16,17},{19,... | collective-permute-start | bytes 3932168 | tf_op jit(solution)/shard_map/ppermute | solution.py:89
  661.6 50.1 %collective-permute-start.32 = (bf16[320,2048]{1,0:T(8,128)(2,1)S(1)}, bf16[320,2048]{1,0:T(8,128)(2,1)S(1)}, u32[]{:S(2)}, u32[]{:S(2)}) collective-permute-start(bf16[320,2048]{1,0:T(8,128)(2,1)S(1)} %fusion.92), channel_id=1, source_target_pairs={{0,1},{3,2},{4,5},{7,6},{8,9},{11,10},{12,13},{15,14},{16,17},{19,... | collective-permute-start | bytes 3932168 | tf_op jit(solution)/shard_map/ppermute | solution.py:89
  663.5 49.5 %collective-permute-start.42 = (bf16[320,2048]{1,0:T(8,128)(2,1)S(1)}, bf16[320,2048]{1,0:T(8,128)(2,1)S(1)}, u32[]{:S(2)}, u32[]{:S(2)}) collective-permute-start(bf16[320,2048]{1,0:T(8,128)(2,1)S(1)} %add_convert_fusion.1), channel_id=1, source_target_pairs={{1,2},{2,1},{5,6},{6,5},{9,10},{10,9},{13,14},{14,13},{17,18},{18,... | collective-permute-start | bytes 3932168 | tf_op jit(solution)/shard_map/ppermute | solution.py:91
  666.6 48.3 %collective-permute-start.39 = (bf16[320,2048]{1,0:T(8,128)(2,1)S(1)}, bf16[320,2048]{1,0:T(8,128)(2,1)S(1)}, u32[]{:S(2)}, u32[]{:S(2)}) collective-permute-start(bf16[320,2048]{1,0:T(8,128)(2,1)S(1)} %add_convert_fusion.3), channel_id=1, source_target_pairs={{1,2},{2,1},{5,6},{6,5},{9,10},{10,9},{13,14},{14,13},{17,18},{18,... | collective-permute-start | bytes 3932168 | tf_op jit(solution)/shard_map/ppermute | solution.py:91
  713.5 36.4 %collective-permute-start.43 = (bf16[320,2048]{1,0:T(8,128)(2,1)S(1)}, bf16[320,2048]{1,0:T(8,128)(2,1)S(1)}, u32[]{:S(2)}, u32[]{:S(2)}) collective-permute-start(bf16[320,2048]{1,0:T(8,128)(2,1)S(1)} %add_convert_fusion), channel_id=1, source_target_pairs={{1,0},{2,3},{5,4},{6,7},{9,8},{10,11},{13,12},{14,15},{17,16},{18,... | collective-permute-start | bytes 3932168 | tf_op jit(solution)/shard_map/ppermute | solution.py:93
  715.3 62.7 %collective-permute-start.40 = (bf16[320,2048]{1,0:T(8,128)(2,1)S(1)}, bf16[320,2048]{1,0:T(8,128)(2,1)S(1)}, u32[]{:S(2)}, u32[]{:S(2)}) collective-permute-start(bf16[320,2048]{1,0:T(8,128)(2,1)S(1)} %add_convert_fusion.2), channel_id=1, source_target_pairs={{1,0},{2,3},{5,4},{6,7},{9,8},{10,11},{13,12},{14,15},{17,16},{18,... | collective-permute-start | bytes 3932168 | tf_op jit(solution)/shard_map/ppermute | solution.py:93
  717.1 89.0 %collective-permute-start.37 = (bf16[320,2048]{1,0:T(8,128)(2,1)S(1)}, bf16[320,2048]{1,0:T(8,128)(2,1)S(1)}, u32[]{:S(2)}, u32[]{:S(2)}) collective-permute-start(bf16[320,2048]{1,0:T(8,128)(2,1)S(1)} %add_convert_fusion.4), channel_id=1, source_target_pairs={{1,0},{2,3},{5,4},{6,7},{9,8},{10,11},{13,12},{14,15},{17,16},{18,... | collective-permute-start | bytes 3932168 | tf_op jit(solution)/shard_map/ppermute | solution.py:93
  719.2 103.7 %collective-permute-start.34 = (bf16[320,2048]{1,0:T(8,128)(2,1)S(1)}, bf16[320,2048]{1,0:T(8,128)(2,1)S(1)}, u32[]{:S(2)}, u32[]{:S(2)}) collective-permute-start(bf16[320,2048]{1,0:T(8,128)(2,1)S(1)} %add_convert_fusion.6), channel_id=1, source_target_pairs={{1,0},{2,3},{5,4},{6,7},{9,8},{10,11},{13,12},{14,15},{17,16},{18,... | collective-permute-start | bytes 3932168 | tf_op jit(solution)/shard_map/ppermute | solution.py:93
  853.4 376.5 %reduce-scatter.11.cloned.1.call-start = ((), (), s32[]{:S(2)}) async-start(), calls=%async_computation.15 | async-start | bytes 9437184 | tf_op jit(solution)/shard_map/reduce_scatter | solution.py:563
  870.4 362.8 %reduce-scatter.5.cloned.1.call-start = ((), (), s32[]{:S(2)}) async-start(), calls=%async_computation.12 | async-start | bytes 7077888 | tf_op jit(solution)/shard_map/reduce_scatter | solution.py:563
  1061.3 181.5 %reduce-scatter.9.cloned.1.call-start = ((), (), s32[]{:S(2)}) async-start(), calls=%async_computation.14 | async-start | bytes 18874368 | tf_op jit(solution)/shard_map/reduce_scatter | solution.py:563
  1126.0 37.4 %collective-permute-start.55 = (bf16[160,2048]{1,0:T(8,128)(2,1)}, bf16[160,2048]{1,0:T(8,128)(2,1)}, u32[]{:S(2)}, u32[]{:S(2)}) collective-permute-start(bf16[160,2048]{1,0:T(8,128)(2,1)} %get-tuple-element.105), channel_id=1, source_target_pairs={{3,2},{7,6},{11,10},{15,14},{19,18},{23,22},{27,26},{31,30}} | collective-permute-start | bytes 1966088 | tf_op jit(solution)/shard_map/ppermute | solution.py:108
  1134.3 38.0 %collective-permute-start.49 = (bf16[160,2048]{1,0:T(8,128)(2,1)}, bf16[160,2048]{1,0:T(8,128)(2,1)}, u32[]{:S(2)}, u32[]{:S(2)}) collective-permute-start(bf16[160,2048]{1,0:T(8,128)(2,1)} %get-tuple-element.101), channel_id=1, source_target_pairs={{3,2},{7,6},{11,10},{15,14},{19,18},{23,22},{27,26},{31,30}} | collective-permute-start | bytes 1966088 | tf_op jit(solution)/shard_map/ppermute | solution.py:108
  (103 other events, 2200.3 us)
Sparse Core Ops, SparseCore 0:
  10.5 48.2 all-gather.4
  61.2 61.5 all-gather.6
  125.2 122.1 all-gather.8
  249.2 55.9 all-gather.10
  853.5 60.5 reduce-scatter.6
  917.8 104.4 reduce-scatter.10
  1061.4 61.3 reduce-scatter.4
  1126.8 115.9 reduce-scatter.8

commit v2 on v1

--- a/solution.py
+++ b/solution.py
@@ -19,11 +19,13 @@
 SEG_DEV = 5
 PAIR = 2 * BLK
 TRUNK_ROWS = TRUNK * BLK
+TILE = 512
+LONG = 1024
 
 EPSILON = 1e-06
 ROPE_BASE = 500000.0
 SCALING = HEAD ** (-0.5)
-VMEM_LIMIT = 56 * 1024 * 1024
+VMEM_LIMIT = 50 * 1024 * 1024
 
 f32 = jnp.float32
 bf16 = jnp.bfloat16
@@ -71,6 +73,12 @@
     return total.astype(bf16)
 
 
+def follow(values, after):
+    if after is None:
+        return values
+    return lax.optimization_barrier((values, after))[0]
+
+
 def small_sum(values, axis, count):
     step = 1
     while step < count:
@@ -79,51 +87,109 @@
     return values
 
 
-def line_all_reduce(chunks, count):
+class SumLine:
+    def __init__(self, count):
+        self.count = count
+        index = lax.axis_index("tensor")
+        self.inner = (index == 1) | (index == 2)
+        self.terms = []
+        self.inward = []
+        self.sides = []
+        self.across = []
+        self.totals = []
+        self.outward = []
+        self.sums = []
+
+    def enter(self, term):
+        if self.count != 4:
+            self.sums.append(lax.psum(term, "tensor"))
+            return
+        self.terms.append(term)
+        self.inward.append(lax.ppermute(term, "tensor", [(0, 1), (3, 2)]))
+
+    def advance(self, after):
+        if self.count != 4:
+            return []
+        moved = []
+        if len(self.sides) < len(self.terms):
+            at = len(self.sides)
+            side = low_sum(follow(self.terms[at], after), self.inward[at])
+            self.sides.append(side)
+            moved.append(side)
+        at = len(self.totals)
+        if at < len(self.sides) - 1 or (at < len(self.sides) and not moved):
+            total = low_sum(follow(self.sides[at], after), self.across[at])
+            self.totals.append(total)
+            moved.append(total)
+        at = len(self.sums)
+        if at < len(self.outward):
+            self.sums.append(
+                jnp.where(self.inner, follow(self.totals[at], after), self.outward[at])
+            )
+        if len(self.across) < len(self.sides):
+            self.across.append(lax.ppermute(self.sides[-1], "tensor", [(1, 2), (2, 1)]))
+        if len(self.outward) < len(self.totals):
+            self.outward.append(lax.ppermute(self.totals[-1], "tensor", [(1, 0), (2, 3)]))
+        return moved
+
+
+def line_reduce_scatter(batches, count, late):
     if count != 4:
-        return [lax.psum(chunk, "tensor") for chunk in chunks]
+        return [
+            lax.psum_scatter(values, "tensor", scatter_dimension=0, tiled=True).astype(f32)
+            for values in batches
+        ], None
     index = lax.axis_index("tensor")
-    inner = (index == 1) | (index == 2)
-    sums = []
-    for chunk in chunks:
-        outer = lax.ppermute(chunk, "tensor", [(0, 1), (3, 2)])
-        side = low_sum(chunk, outer)
-        across = lax.ppermute(side, "tensor", [(1, 2), (2, 1)])
-        total = low_sum(side, across)
-        back = lax.ppermute(total, "tensor", [(1, 0), (2, 3)])
-        sums.append(jnp.where(inner, total, back))
-    return sums
-
-
-def line_reduce_scatter(values, count):
+    rights = []
+    lefts = []
+    blocks = [item.reshape(count, item.shape[0] // count, item.shape[1]) for item in batches]
+
+    def block(item, at):
+        return lax.dynamic_index_in_dim(item, lax.rem(at + 2 * count, count), 0, keepdims=False)
+
+    operands = []
+    for stage in range(count - 1):
+        to_right = [(i, i + 1) for i in range(stage + 1)]
+        to_left = [(count - 1 - i, count - 2 - i) for i in range(stage + 1)]
+        for at, item in enumerate(blocks):
+            right = block(item, index + count - 1 - stage)
+            left = block(item, index - count + 1 + stage)
+            if stage:
+                right = low_sum(right, rights[at])
+                left = low_sum(left, lefts[at])
+                if stage == count - 2 and at == len(blocks) - 1:
+                    right, left = follow((right, left), late)
+                rights[at] = lax.ppermute(right, "tensor", to_right)
+                lefts[at] = lax.ppermute(left, "tensor", to_left)
+            else:
+                rights.append(lax.ppermute(right, "tensor", to_right))
+                lefts.append(lax.ppermute(left, "tensor", to_left))
+            operands.append((right, left))
+    sums = [
+        block(item, index).astype(f32) + right.astype(f32) + left.astype(f32)
+        for item, right, left in zip(blocks, rights, lefts)
+    ]
+    return sums, operands[-1]
+
+
+def begin_all_gather(values, count):
     if count != 4:
-        return lax.psum_scatter(values, "tensor", scatter_dimension=0, tiled=True).astype(f32)
-    index = lax.axis_index("tensor")
-    blocks = values.reshape(count, values.shape[0] // count, values.shape[1])
-
-    def block(at):
-        return lax.dynamic_index_in_dim(blocks, lax.rem(at + 2 * count, count), 0, keepdims=False)
-
-    right = lax.ppermute(block(index + 3), "tensor", [(0, 1)])
-    left = lax.ppermute(block(index - 3), "tensor", [(3, 2)])
-    right = lax.ppermute(low_sum(block(index + 2), right), "tensor", [(0, 1), (1, 2)])
-    left = lax.ppermute(low_sum(block(index - 2), left), "tensor", [(3, 2), (2, 1)])
-    right = lax.ppermute(low_sum(block(index + 1), right), "tensor", [(0, 1), (1, 2), (2, 3)])
-    left = lax.ppermute(low_sum(block(index - 1), left), "tensor", [(3, 2), (2, 1), (1, 0)])
-    return block(index).astype(f32) + right.astype(f32) + left.astype(f32)
-
-
-def line_all_gather(values, count):
+        return values, (None,) * 4
+    right1 = lax.ppermute(values, "tensor", [(0, 1), (1, 2), (2, 3)])
+    left1 = lax.ppermute(values, "tensor", [(3, 2), (2, 1), (1, 0)])
+    right2 = lax.ppermute(right1, "tensor", [(1, 2), (2, 3)])
+    left2 = lax.ppermute(left1, "tensor", [(2, 1), (1, 0)])
+    return values, (right1, left1, right2, left2)
+
+
+def end_all_gather(begun, count, after=None):
+    values, (right1, left1, right2, left2) = begun
     if count != 4:
         return lax.all_gather(values, "tensor", axis=1, tiled=True)
     index = lax.axis_index("tensor")
     width = values.shape[1]
-    right1 = lax.ppermute(values, "tensor", [(0, 1), (1, 2), (2, 3)])
-    left1 = lax.ppermute(values, "tensor", [(3, 2), (2, 1), (1, 0)])
-    right2 = lax.ppermute(right1, "tensor", [(1, 2), (2, 3)])
-    left2 = lax.ppermute(left1, "tensor", [(2, 1), (1, 0)])
-    right3 = lax.ppermute(right2, "tensor", [(2, 3)])
-    left3 = lax.ppermute(left2, "tensor", [(1, 0)])
+    right3 = lax.ppermute(follow(right2, after), "tensor", [(2, 3)])
+    left3 = lax.ppermute(follow(left2, after), "tensor", [(1, 0)])
     whole = jnp.zeros((values.shape[0], count * width), values.dtype)
     pieces = (
         values,
@@ -137,6 +203,28 @@
     return whole
 
 
+def line_all_gather(values, count):
+    return end_all_gather(begin_all_gather(values, count), count)
+
+
+def begin_output_weight(own, after, dp_index, dp_count, count):
+    if count != 4 or dp_count % 2:
+        return own, (None,) * 4
+    half = own.shape[0] // 2
+    mine = lax.dynamic_slice_in_dim(follow(own, after), lax.rem(dp_index, 2) * half, half, 0)
+    return begin_all_gather(mine, count)
+
+
+def end_output_weight(begun, after, dp_index, dp_count, count):
+    if count != 4 or dp_count % 2:
+        whole = lax.all_gather(begun[0], "tensor", axis=1, tiled=True)
+        half = whole.shape[0] // 2
+        return jnp.zeros((1,), jnp.int32), whole[:half], whole[half:]
+    mine = end_all_gather(begun, count, after)
+    other = lax.ppermute(mine, "dp", [(i, i ^ 1) for i in range(dp_count)])
+    return lax.rem(dp_index, 2).astype(jnp.int32).reshape(1), mine, other
+
+
 def turn(values, cosines, sines):
     return values * cosines + pltpu.roll(values, HEAD // 2, 1) * sines
 
@@ -146,26 +234,65 @@
     return slice(start, start + HEAD)
 
 
-def pack_kernel(heads, qk_ref, v_ref, inv_ref, gain_ref, cos_ref, sin_ref, out_ref):
+def project_kernel(x_ref, *refs):
+    count = len(refs) // 2 if len(refs) > 2 else 1
+    weights, outs = refs[:count], refs[count:]
+    for at in range(count):
+        raw = jnp.dot(x_ref[0], weights[at][0], preferred_element_type=f32)
+        outs[at][0] = raw.astype(outs[at].dtype)
+        if len(outs) > count:
+            outs[count][0, :, at : at + 1] = jnp.sum(raw * raw, axis=1, keepdims=True)
+
+
+def project(tokens, weights, which, squares):
+    batches, rows, _ = tokens.shape
+    width = weights.shape[2]
+    step = rows // 2
+    dtype = f32 if squares else bf16
+    out_specs = [pl.BlockSpec((1, step, width), lambda b, r: (b, r, 0))] * len(which)
+    out_shape = [jax.ShapeDtypeStruct((batches, rows, width), dtype)] * len(which)
+    if squares:
+        out_specs.append(pl.BlockSpec((1, step, len(which)), lambda b, r: (b, r, 0)))
+        out_shape.append(jax.ShapeDtypeStruct((batches, rows, len(which)), f32))
+    return pl.pallas_call(
+        project_kernel,
+        grid=(batches, rows // step),
+        in_specs=[pl.BlockSpec((1, step, D), lambda b, r: (b, r, 0))]
+        + [pl.BlockSpec((1, D, width), lambda b, r, at=at: (at, 0, 0)) for at in which],
+        out_specs=out_specs,
+        out_shape=out_shape,
+        compiler_params=pltpu.CompilerParams(vmem_limit_bytes=VMEM_LIMIT),
+        cost_estimate=pl.CostEstimate(
+            flops=2 * batches * rows * D * width * len(which),
+            bytes_accessed=2 * batches * rows * D + 2 * D * width * len(which),
+            transcendentals=0,
+        ),
+        name="project",
+    )(tokens, *([weights] * len(which)))
+
+
+def pack_kernel(heads, q_ref, k_ref, v_ref, inv_ref, gain_ref, cos_ref, sin_ref, out_ref):
     cosines = cos_ref[0]
     sines = sin_ref[0]
     for head in range(heads):
         for which in range(2):
             cols = head_cols(head, which, heads)
-            normed = qk_ref[0, :, cols] * inv_ref[0, :, which : which + 1] * gain_ref[:, cols]
+            raw_ref = (q_ref, k_ref)[which]
+            normed = raw_ref[0, :, head_cols(head)] * inv_ref[0, :, which : which + 1] * gain_ref[:, cols]
             out_ref[head, 0, which] = turn(normed, cosines, sines).astype(bf16)
-        out_ref[head, 0, 2] = v_ref[0, :, head_cols(head)].astype(bf16)
-
-
-def pack_heads(qk_raw, v_raw, inverse, gains, cosines, sines, heads):
-    rows = qk_raw.shape[1]
+        out_ref[head, 0, 2] = v_ref[0, :, head_cols(head)]
+
+
+def pack_heads(q_raw, k_raw, v_raw, inverse, gains, cosines, sines, heads):
+    rows = q_raw.shape[1]
     step = rows // 2
     width = heads * HEAD
     return pl.pallas_call(
         functools.partial(pack_kernel, heads),
         grid=(MB, rows // step),
         in_specs=[
-            pl.BlockSpec((1, step, 2 * width), lambda b, r: (b, r, 0)),
+            pl.BlockSpec((1, step, width), lambda b, r: (b, r, 0)),
+            pl.BlockSpec((1, step, width), lambda b, r: (b, r, 0)),
             pl.BlockSpec((1, step, width), lambda b, r: (b, r, 0)),
             pl.BlockSpec((1, step, 2), lambda b, r: (b, r, 0)),
             pl.BlockSpec((1, 2 * width), lambda b, r: (0, 0)),
@@ -175,10 +302,10 @@
         out_specs=pl.BlockSpec((heads, 1, 3, step, HEAD), lambda b, r: (0, b, 0, r, 0)),
         out_shape=jax.ShapeDtypeStruct((heads, MB, 3, rows, HEAD), bf16),
         name="pack_heads",
-    )(qk_raw, v_raw, inverse, gains, cosines, sines)
-
-
-def inner_kernel(heads, back_ref, qk_ref, inv_ref, gain_ref, cos_ref, sin_ref, inner_ref, part_ref):
+    )(q_raw, k_raw, v_raw, inverse, gains, cosines, sines)
+
+
+def inner_kernel(heads, back_ref, q_ref, k_ref, inv_ref, gain_ref, cos_ref, sin_ref, inner_ref, part_ref):
     cosines = cos_ref[0]
     sines = -sin_ref[0]
 
@@ -191,7 +318,7 @@
         for head in range(heads):
             cols = head_cols(head, which, heads)
             straight = turn(back_ref[head, 0, which].astype(f32), cosines, sines)
-            hat = qk_ref[0, :, cols] * inv_ref[0, :, which : which + 1]
+            hat = (q_ref, k_ref)[which][0, :, head_cols(head)] * inv_ref[0, :, which : which + 1]
             product = straight * hat
             part_ref[:, cols] += jnp.sum(product, axis=0, keepdims=True)
             weighted = product * gain_ref[:, cols]
@@ -199,8 +326,8 @@
         inner_ref[0, :, which : which + 1] = jnp.sum(total, axis=1, keepdims=True)
 
 
-def inner_sums(back, qk_raw, inverse, gains, cosines, sines, heads):
-    rows = qk_raw.shape[1]
+def inner_sums(back, q_raw, k_raw, inverse, gains, cosines, sines, heads):
+    rows = q_raw.shape[1]
     step = rows // 2
     width = heads * HEAD
     return pl.pallas_call(
@@ -208,7 +335,8 @@
         grid=(MB, rows // step),
         in_specs=[
             pl.BlockSpec((heads, 1, 2, step, HEAD), lambda b, r: (0, b, 0, r, 0)),
-            pl.BlockSpec((1, step, 2 * width), lambda b, r: (b, r, 0)),
+            pl.BlockSpec((1, step, width), lambda b, r: (b, r, 0)),
+            pl.BlockSpec((1, step, width), lambda b, r: (b, r, 0)),
             pl.BlockSpec((1, step, 2), lambda b, r: (b, r, 0)),
             pl.BlockSpec((1, 2 * width), lambda b, r: (0, 0)),
             pl.BlockSpec((1, step, HEAD), lambda b, r: (b, r, 0)),
@@ -223,45 +351,81 @@
             jax.ShapeDtypeStruct((1, 2 * width), f32),
         ],
         name="inner_sums",
-    )(back, qk_raw, inverse, gains, cosines, sines)
+    )(back, q_raw, k_raw, inverse, gains, cosines, sines)
 
 
 def unpack_kernel(
-    heads, back_ref, qk_ref, inv_ref, mean_ref, gain_ref, cos_ref, sin_ref, out_ref
+    heads,
+    back_ref,
+    q_ref,
+    k_ref,
+    inv_ref,
+    mean_ref,
+    gain_ref,
+    cos_ref,
+    sin_ref,
+    wq_ref,
+    wk_ref,
+    wv_ref,
+    grad_ref,
+    term_ref,
 ):
     cosines = cos_ref[0]
     sines = -sin_ref[0]
+    width = heads * HEAD
     for head in range(heads):
         for which in range(2):
             cols = head_cols(head, which, heads)
             inverse = inv_ref[0, :, which : which + 1]
             straight = turn(back_ref[head, 0, which].astype(f32), cosines, sines)
-            hat = qk_ref[0, :, cols] * inverse
+            hat = (q_ref, k_ref)[which][0, :, head_cols(head)] * inverse
             grad = inverse * (straight * gain_ref[:, cols] - hat * mean_ref[0, :, which : which + 1])
-            out_ref[0, :, cols] = grad.astype(bf16)
-        out_ref[0, :, head_cols(head, 2, heads)] = back_ref[head, 0, 2]
-
-
-def unpack_heads(back, qk_raw, inverse, means, gains, cosines, sines, heads):
-    rows = qk_raw.shape[1]
+            grad_ref[:, cols] = grad.astype(bf16)
+        grad_ref[:, head_cols(head, 2, heads)] = back_ref[head, 0, 2]
+    term = nt(grad_ref[:, :width], wq_ref[0])
+    term = term + nt(grad_ref[:, width : 2 * width], wk_ref[0])
+    term = term + nt(grad_ref[:, 2 * width :], wv_ref[0])
+    term_ref[...] = term.astype(bf16)
+
+
+def unpack_heads(
+    batch, back, q_raw, k_raw, inverse, means, gains, cosines, sines, weights, heads, kept
+):
+    rows = q_raw.shape[1]
     step = rows // 2
     width = heads * HEAD
-    return pl.pallas_call(
+    row_spec = lambda cols: pl.BlockSpec((1, step, cols), lambda r: (batch, r, 0))
+    return chunk_call(
         functools.partial(unpack_kernel, heads),
-        grid=(MB, rows // step),
-        in_specs=[
-            pl.BlockSpec((heads, 1, 3, step, HEAD), lambda b, r: (0, b, 0, r, 0)),
-            pl.BlockSpec((1, step, 2 * width), lambda b, r: (b, r, 0)),
-            pl.BlockSpec((1, step, 2), lambda b, r: (b, r, 0)),
-            pl.BlockSpec((1, step, 2), lambda b, r: (b, r, 0)),
-            pl.BlockSpec((1, 2 * width), lambda b, r: (0, 0)),
-            pl.BlockSpec((1, step, HEAD), lambda b, r: (b, r, 0)),
-            pl.BlockSpec((1, step, HEAD), lambda b, r: (b, r, 0)),
-        ],
-        out_specs=pl.BlockSpec((1, step, 3 * width), lambda b, r: (b, r, 0)),
-        out_shape=jax.ShapeDtypeStruct((MB, rows, 3 * width), bf16),
-        name="unpack_heads",
-    )(back, qk_raw, inverse, means, gains, cosines, sines)
+        [
+            (pl.BlockSpec((heads, 1, 3, step, HEAD), lambda r: (0, batch, 0, r, 0)), back),
+            (row_spec(width), q_raw),
+            (row_spec(width), k_raw),
+            (row_spec(2), inverse),
+            (row_spec(2), means),
+            (pl.BlockSpec((1, 2 * width), lambda r: (0, 0)), gains),
+            (row_spec(HEAD), cosines),
+            (row_spec(HEAD), sines),
+        ]
+        + [(pl.BlockSpec((1, D, width), lambda r, at=at: (at, 0, 0)), weights) for at in range(3)],
+        [
+            (
+                pl.BlockSpec((step, 3 * width), lambda r: (batch * 2 + r, 0)),
+                jax.ShapeDtypeStruct((MB * rows, 3 * width), bf16),
+                True,
+            ),
+            (
+                pl.BlockSpec((step, D), lambda r: (r, 0)),
+                jax.ShapeDtypeStruct((rows, D), bf16),
+                False,
+            ),
+        ],
+        kept,
+        (2,),
+        [],
+        pl.CostEstimate(flops=6 * rows * D * width, bytes_accessed=8 * rows * D, transcendentals=0),
+        "unpack_heads",
+    )
 
 
 def nt(left, right):
@@ -506,25 +670,361 @@
     )(order, packed, grads)
 
 
+def mean_square(values):
+    return jnp.mean(values * values, axis=-1, keepdims=True)
+
+
 def norm_back(gradient, normed, inverse, gain_vec):
     weighted = gradient * gain_vec
     return inverse * (weighted - normed * jnp.mean(normed * weighted, axis=-1, keepdims=True))
 
 
-def inverse_norm(values):
-    return lax.rsqrt(jnp.mean(values * values, axis=-1, keepdims=True) + EPSILON)
-
-
-def dot(left, right):
-    return jnp.dot(left, right, preferred_element_type=f32)
-
-
-def dot_nt(left, right):
-    return lax.dot_general(left, right, (((1,), (1,)), ((), ())), preferred_element_type=f32)
-
-
-def dot_tn(left, right):
-    return lax.dot_general(left, right, (((0,), (0,)), ((), ())), preferred_element_type=f32)
+def chunk_call(kernel, ins, outs, kept, grid, scratch, cost, name):
+    count = len(ins)
+    specs = [spec for spec, _ in ins]
+    values = [value for _, value in ins]
+    aliases = {}
+    if kept is not None:
+        whole = [at for at, out in enumerate(outs) if out[2]]
+        for at, value in zip(whole, kept):
+            aliases[len(values)] = at
+            specs.append(pl.BlockSpec(memory_space=pl.ANY))
+            values.append(value)
+    extra = len(values) - count
+
+    def body(*refs):
+        kernel(*refs[:count], *refs[count + extra :])
+
+    return pl.pallas_call(
+        body,
+        grid=grid,
+        in_specs=specs,
+        out_specs=[out[0] for out in outs],
+        out_shape=[out[1] for out in outs],
+        scratch_shapes=scratch,
+        input_output_aliases=aliases,
+        compiler_params=pltpu.CompilerParams(vmem_limit_bytes=VMEM_LIMIT),
+        cost_estimate=cost,
+        name=name,
+    )(*values)
+
+
+def clip(step, low, count):
+    return jnp.minimum(jnp.maximum(step - low, 0), count - 1)
+
+
+def forward_chunk_kernel(
+    first,
+    second,
+    core_ref,
+    y_ref,
+    x_ref,
+    gain_ref,
+    woa_ref,
+    wob_ref,
+    wg_ref,
+    wu_ref,
+    wd_ref,
+    proj_ref,
+    low_ref,
+    act_ref,
+    silu_ref,
+    slope_ref,
+    part_ref,
+    exact_ref,
+    held_ref,
+):
+    step = pl.program_id(0)
+    half = first // 2
+
+    def project_tile(weight_ref, side):
+        at = side * half + lax.rem(step, half)
+        columns = pl.ds(pl.multiple_of(at * LONG, LONG), LONG)
+        exact_ref[:, columns] = nt(y_ref[...], weight_ref[...])
+
+    @pl.when(step < half)
+    def _():
+        project_tile(woa_ref, core_ref[0])
+
+    @pl.when((step >= half) & (step < first))
+    def _():
+        project_tile(wob_ref, 1 - core_ref[0])
+
+    @pl.when(step == first)
+    def _():
+        proj = exact_ref[...]
+        inverse = lax.rsqrt(mean_square(proj) + EPSILON)
+        proj_ref[...] = proj.astype(bf16)
+        low_ref[...] = (x_ref[...].astype(f32) + proj * inverse * gain_ref[...]).astype(bf16)
+
+    @pl.when((step >= first) & (step < second))
+    def _():
+        low = low_ref[...]
+        gate = nn(low, wg_ref[...])
+        up = nn(low, wu_ref[...])
+        sigmoid = 1.0 / (1.0 + jnp.exp(-gate))
+        silu = gate * sigmoid
+        act = (silu * up).astype(bf16)
+        act_ref[...] = act
+        held_ref[:, pl.ds(pl.multiple_of((step - first) * TILE, TILE), TILE)] = act
+        silu_ref[...] = silu.astype(bf16)
+        slope_ref[...] = (up * sigmoid * (1.0 + gate * (1.0 - sigmoid))).astype(bf16)
+
+    @pl.when(step >= second)
+    def _():
+        part_ref[...] = nt(held_ref[...], wd_ref[...]).astype(bf16)
+
+
+def forward_chunk(at, batch, part, rows, y_all, tokens, gain, w_out, w_mlp, kept):
+    core, w_out_a, w_out_b = w_out
+    w_gate, w_rest = w_mlp
+    units = w_gate.shape[2]
+    total = tokens.shape[0] * tokens.shape[1]
+    tiles = D // LONG
+    unit_tiles = units // TILE
+    first = tiles
+    second = first + unit_tiles
+    half = first // 2
+    unit_tile = pl.BlockSpec((rows, TILE), lambda s: (at, clip(s, first, unit_tiles)))
+    wide = jax.ShapeDtypeStruct((total, units), bf16)
+    narrow = jax.ShapeDtypeStruct((total, D), bf16)
+    whole = pl.BlockSpec((rows, D), lambda s: (at, 0))
+
+    def weight(which):
+        return pl.BlockSpec((None, D, TILE), lambda s: (which, 0, clip(s, first, unit_tiles)))
+
+    return chunk_call(
+        functools.partial(forward_chunk_kernel, first, second),
+        [
+            (pl.BlockSpec(memory_space=pltpu.SMEM), core),
+            (pl.BlockSpec((rows, D), lambda s: (part, 0)), y_all),
+            (pl.BlockSpec((None, rows, D), lambda s: (batch, part, 0)), tokens),
+            (pl.BlockSpec((1, D), lambda s: (0, 0)), gain),
+            (pl.BlockSpec((LONG, D), lambda s: (clip(s, 0, half), 0)), w_out_a),
+            (pl.BlockSpec((LONG, D), lambda s: (clip(s, half, half), 0)), w_out_b),
+            (weight(0), w_gate),
+            (weight(0), w_rest),
+            (pl.BlockSpec((None, LONG, units), lambda s: (1, clip(s, second, tiles), 0)), w_rest),
+        ],
+        [
+            (whole, narrow, True),
+            (whole, narrow, True),
+            (unit_tile, wide, True),
+            (unit_tile, wide, True),
+            (unit_tile, wide, True),
+            (
+                pl.BlockSpec((rows, LONG), lambda s: (0, clip(s, second, tiles))),
+                jax.ShapeDtypeStruct((rows, D), bf16),
+                False,
+            ),
+        ],
+        kept,
+        (second + tiles,),
+        [pltpu.VMEM((rows, D), f32), pltpu.VMEM((rows, units), bf16)],
+        pl.CostEstimate(
+            flops=2 * rows * D * (D + 3 * units),
+            bytes_accessed=2 * D * (D + 3 * units) + 16 * rows * D,
+            transcendentals=rows * units,
+        ),
+        "forward_chunk",
+    )
+
+
+def middle_chunk_kernel(
+    first,
+    sum_ref,
+    proj_ref,
+    x_ref,
+    grad_ref,
+    attn_gain_ref,
+    gain_ref,
+    silu_ref,
+    slope_ref,
+    wd_ref,
+    wg_ref,
+    wu_ref,
+    output_ref,
+    low_ref,
+    gate_ref,
+    up_ref,
+    gain_part_ref,
+    part_ref,
+    gates_ref,
+    ups_ref,
+):
+    step = pl.program_id(0)
+
+    @pl.when(step == 0)
+    def _():
+        proj = proj_ref[...].astype(f32)
+        inverse = lax.rsqrt(mean_square(proj) + EPSILON)
+        hidden = x_ref[...].astype(f32) + proj * inverse * attn_gain_ref[...]
+        mlp = sum_ref[...].astype(f32)
+        inverse = lax.rsqrt(mean_square(mlp) + EPSILON)
+        normed = mlp * inverse
+        grad = grad_ref[...]
+        output_ref[...] = (hidden + normed * gain_ref[...]).astype(bf16)
+        gain_part_ref[...] = jnp.sum(grad * normed, axis=0, keepdims=True)
+        low_ref[...] = norm_back(grad, normed, inverse, gain_ref[...]).astype(bf16)
+
+    @pl.when(step < first)
+    def _():
+        act_grad = nn(low_ref[...], wd_ref[...])
+        up_grad = (act_grad * silu_ref[...].astype(f32)).astype(bf16)
+        gate_grad = (act_grad * slope_ref[...].astype(f32)).astype(bf16)
+        columns = pl.ds(pl.multiple_of(step * TILE, TILE), TILE)
+        up_ref[...] = up_grad
+        ups_ref[:, columns] = up_grad
+        gate_ref[...] = gate_grad
+        gates_ref[:, columns] = gate_grad
+
+    @pl.when(step >= first)
+    def _():
+        part_ref[...] = (
+            nt(gates_ref[...], wg_ref[...]) + nt(ups_ref[...], wu_ref[...])
+        ).astype(bf16)
+
+
+def middle_chunk(
+    at, batch, part, rows, mlp_sum, proj, tokens, grad, attn_gain, gain, silu, slope, w_mlp, kept
+):
+    w_gate, w_rest = w_mlp
+    units = w_gate.shape[2]
+    total = proj.shape[0]
+    tiles = D // LONG
+    first = units // TILE
+    whole = pl.BlockSpec((rows, D), lambda s: (at, 0))
+    row_block = pl.BlockSpec((None, rows, D), lambda s: (batch, part, 0))
+    line = pl.BlockSpec((1, D), lambda s: (0, 0))
+    tile = pl.BlockSpec((rows, TILE), lambda s: (at, clip(s, 0, first)))
+    wide = jax.ShapeDtypeStruct((total, units), bf16)
+    narrow = jax.ShapeDtypeStruct((total, D), bf16)
+
+    def weight(which):
+        return pl.BlockSpec((None, LONG, units), lambda s: (which, clip(s, first, tiles), 0))
+
+    return chunk_call(
+        functools.partial(middle_chunk_kernel, first),
+        [
+            (pl.BlockSpec((rows, D), lambda s: (0, 0)), mlp_sum),
+            (whole, proj),
+            (row_block, tokens),
+            (row_block, grad),
+            (line, attn_gain),
+            (line, gain),
+            (tile, silu),
+            (tile, slope),
+            (pl.BlockSpec((None, D, TILE), lambda s: (1, 0, clip(s, 0, first))), w_rest),
+            (weight(0), w_gate),
+            (weight(0), w_rest),
+        ],
+        [
+            (whole, narrow, True),
+            (whole, narrow, True),
+            (tile, wide, True),
+            (tile, wide, True),
+            (line, jax.ShapeDtypeStruct((1, D), f32), False),
+            (
+                pl.BlockSpec((rows, LONG), lambda s: (0, clip(s, first, tiles))),
+                jax.ShapeDtypeStruct((rows, D), bf16),
+                False,
+            ),
+        ],
+        kept,
+        (first + tiles,),
+        [pltpu.VMEM((rows, units), bf16), pltpu.VMEM((rows, units), bf16)],
+        pl.CostEstimate(
+            flops=2 * rows * D * 3 * units,
+            bytes_accessed=2 * D * 3 * units + 24 * rows * D,
+            transcendentals=rows,
+        ),
+        "middle_chunk",
+    )
+
+
+def backward_chunk_kernel(
+    heads, sum_ref, grad_ref, proj_ref, gain_ref, wo_ref, hidden_ref, low_ref, dy_ref, gain_part_ref
+):
+    hidden_grad = grad_ref[...] + sum_ref[...].astype(f32)
+    proj = proj_ref[...].astype(f32)
+    inverse = lax.rsqrt(mean_square(proj) + EPSILON)
+    normed = proj * inverse
+    hidden_ref[...] = hidden_grad
+    gain_part_ref[...] = jnp.sum(hidden_grad * normed, axis=0, keepdims=True)
+    low = norm_back(hidden_grad, normed, inverse, gain_ref[...]).astype(bf16)
+    low_ref[...] = low
+    grad = nn(low, wo_ref[...])
+    for head in range(heads):
+        dy_ref[head] = grad[:, head_cols(head)].astype(bf16)
+
+
+def backward_chunk(at, batch, part, rows, branch_sum, grad, proj, gain, w_attn, kept):
+    total = proj.shape[0]
+    width = w_attn.shape[2]
+    heads = width // HEAD
+    whole = pl.BlockSpec((rows, D), lambda s: (at, 0))
+    line = pl.BlockSpec((1, D), lambda s: (0, 0))
+    return chunk_call(
+        functools.partial(backward_chunk_kernel, heads),
+        [
+            (pl.BlockSpec((rows, D), lambda s: (0, 0)), branch_sum),
+            (pl.BlockSpec((None, rows, D), lambda s: (batch, part, 0)), grad),
+            (whole, proj),
+            (line, gain),
+            (pl.BlockSpec((None, D, width), lambda s: (3, 0, 0)), w_attn),
+        ],
+        [
+            (whole, jax.ShapeDtypeStruct((total, D), f32), True),
+            (whole, jax.ShapeDtypeStruct((total, D), bf16), True),
+            (
+                pl.BlockSpec((heads, rows, HEAD), lambda s: (0, at, 0)),
+                jax.ShapeDtypeStruct((heads, total, HEAD), bf16),
+                True,
+            ),
+            (line, jax.ShapeDtypeStruct((1, D), f32), False),
+        ],
+        kept,
+        (1,),
+        [],
+        pl.CostEstimate(
+            flops=2 * rows * D * width, bytes_accessed=16 * rows * D, transcendentals=rows
+        ),
+        "backward_chunk",
+    )
+
+
+def weight_sum_kernel(left_ref, right_ref, out_ref):
+    out_ref[...] = lax.dot_general(
+        left_ref[...], right_ref[...], (((0,), (0,)), ((), ())), preferred_element_type=f32
+    ).astype(bf16)
+
+
+def weight_sum(slots, count, left, right, units, kept):
+    rows, depth = left.shape
+    first = slots[0]
+    return chunk_call(
+        weight_sum_kernel,
+        [
+            (pl.BlockSpec((rows, TILE), lambda w, s: (0, s)), left),
+            (pl.BlockSpec((rows, units), lambda w, s: (0, w)), right),
+        ],
+        [
+            (
+                pl.BlockSpec((None, TILE, units), lambda w, s: (first + w, s, 0)),
+                jax.ShapeDtypeStruct((count, depth, units), bf16),
+                True,
+            )
+        ],
+        kept,
+        (len(slots), depth // TILE),
+        [],
+        pl.CostEstimate(
+            flops=2 * rows * depth * units * len(slots),
+            bytes_accessed=2 * len(slots) * (rows * depth + rows * units + depth * units),
+            transcendentals=0,
+        ),
+        "weight_sum",
+    )
 
 
 def shards(
@@ -556,13 +1056,13 @@
     items = heads * MB
     copies = dp_count // items
 
-    def gather_rows(shard):
-        return lax.all_gather(shard, "dp", axis=0, tiled=True)
-
-    def scatter_rows(total):
+    def gather_stack(*pieces):
+        return lax.all_gather(jnp.stack(pieces), "dp", axis=1, tiled=True)
+
+    def scatter_rows(total, dimension=0):
         return lax.psum_scatter(
-            total.astype(bf16), "dp", scatter_dimension=0, tiled=True
-        ).astype(f32)
+            total.astype(bf16), "dp", scatter_dimension=dimension, tiled=True
+        )
 
     def exchange(pieces):
         flat = pieces.reshape((items, -1, HEAD))
@@ -574,10 +1074,8 @@
         flat = pieces.reshape((dp_count, -1, HEAD))
         return lax.all_to_all(flat, "dp", split_axis=0, concat_axis=0, tiled=True)[:items]
 
-    w_qkv = gather_rows(jnp.concatenate([w_query, w_key, w_value], axis=1))
-    w_out_t = gather_rows(line_all_gather(jnp.transpose(w_output), tp_count))
-    w_gate_up = gather_rows(jnp.concatenate([w_gate, w_up], axis=1))
-    w_down_t = gather_rows(jnp.transpose(w_down))
+    w_attn = gather_stack(w_query, w_key, w_value, jnp.transpose(w_output))
+    w_gate_all = gather_stack(w_gate)
 
     order = tree_order(slot_parent, slot_depth)
     my_batch = lax.rem(lax.rem(dp_index, items), MB)
@@ -585,136 +1083,177 @@
     my_depth = lax.dynamic_slice_in_dim(slot_depth, dp_index * SEG_DEV, SEG_DEV, 1)
     cosines, sines = rope_tables(my_depth)
 
-    tokens = layer_input.reshape(MB * rows, D)
-    qk_raw = dot(tokens, w_qkv[:, : 2 * width])
-    v_raw = dot(tokens, w_qkv[:, 2 * width :])
-    squares = jnp.stack(
-        [
-            jnp.sum(jnp.square(qk_raw[:, :width]), axis=-1),
-            jnp.sum(jnp.square(qk_raw[:, width:]), axis=-1),
-        ]
-    )
+    q_raw, k_raw, squares = project(layer_input, w_attn, (0, 1), True)
+    squares = jnp.transpose(squares.reshape(MB * rows, 2))
+    (v_raw,) = project(layer_input, w_attn, (2,), False)
     squares = small_sum(squares, "tensor", tp_count)
     inverse = jnp.transpose(lax.rsqrt(squares / D + EPSILON)).reshape(MB, rows, 2)
-    qk_raw = qk_raw.reshape(MB, rows, 2 * width)
-    v_raw = v_raw.reshape(MB, rows, width)
     gains = jnp.concatenate([query_gain, key_gain])[None, :]
-    packed = pack_heads(qk_raw, v_raw, inverse, gains, cosines, sines, heads)
-    packed = exchange(packed).reshape(dp_count, 3, SEG_DEV, BLK, HEAD)
+    packed = pack_heads(q_raw, k_raw, v_raw, inverse, gains, cosines, sines, heads)
+    w_out_begun = begin_output_weight(w_attn[3], packed, dp_index, dp_count, tp_count)
+    packed = follow(exchange(packed), w_out_begun[1]).reshape(dp_count, 3, SEG_DEV, BLK, HEAD)
+    w_out = end_output_weight(w_out_begun, packed, dp_index, dp_count, tp_count)
+    w_mlp = (w_gate_all, gather_stack(*follow((w_up, jnp.transpose(w_down)), packed)))
 
     attended = give_back(attend_forward(my_order, packed))
     attended = attended.reshape(heads, MB, rows, HEAD).transpose(1, 2, 0, 3)
     attended = attended.reshape(MB, rows, width)
 
-    kept = []
-    outputs = []
+    parts = 2
+    step = rows // parts
+    spots = [(batch, part) for batch in range(MB) for part in range(parts)]
+    begun = []
+    everything = []
     for batch in range(MB):
-        everything = line_all_gather(attended[batch], tp_count)
-        attn_proj = dot_nt(everything, w_out_t)
-        attn_inv = inverse_norm(attn_proj)
-        hidden = layer_input[batch].astype(f32) + attn_proj * attn_inv * attn_gain
-        hidden_low = hidden.astype(bf16)
-        gate_pre = dot(hidden_low, w_gate_up[:, :hidden_width])
-        up_pre = dot(hidden_low, w_gate_up[:, hidden_width:])
-        act_low = (jax.nn.silu(gate_pre) * up_pre).astype(bf16)
-        half = rows // 2
-        sums = line_all_reduce(
-            [
-                dot_nt(act_low[:half], w_down_t).astype(bf16),
-                dot_nt(act_low[half:], w_down_t).astype(bf16),
-            ],
-            tp_count,
+        after = begun[-1][1][2:] if begun else None
+        begun.append(begin_all_gather(follow(attended[batch], after), tp_count))
+    sums = SumLine(tp_count)
+    attn_gain_row = attn_gain[None, :]
+    mlp_gain_row = mlp_gain[None, :]
+    chunks = len(spots)
+    state = dict(forward=None, middle=None, backward=None)
+    mlp_gain_parts = []
+    attn_gain_parts = []
+
+    def forward(at, after):
+        batch, part = spots[at]
+        if batch == len(everything):
+            early = sums.terms[0] if sums.terms else None
+            everything.append(end_all_gather(begun[batch], tp_count, early))
+        *state["forward"], term = forward_chunk(
+            at,
+            batch,
+            part,
+            step,
+            follow(everything[batch], after),
+            layer_input,
+            attn_gain_row,
+            w_out,
+            w_mlp,
+            state["forward"],
         )
-        mlp_proj = jnp.concatenate(sums, axis=0).astype(f32)
-        mlp_inv = inverse_norm(mlp_proj)
-        mlp_normed = mlp_proj * mlp_inv
-        outputs.append((hidden + mlp_normed * mlp_gain).astype(bf16))
-        out_grad = cotangent[batch]
-        mlp_grad = norm_back(out_grad, mlp_normed, mlp_inv, mlp_gain).astype(bf16)
-        mlp_gain_part = jnp.sum(out_grad * mlp_normed, axis=0)
-        act_grad = dot(mlp_grad, w_down_t)
-        sigmoid_gate = jax.nn.sigmoid(gate_pre)
-        up_grad = (act_grad * gate_pre * sigmoid_gate).astype(bf16)
-        gate_grad = (
-            act_grad * up_pre * sigmoid_gate * (1.0 + gate_pre * (1.0 - sigmoid_gate))
-        ).astype(bf16)
-        branch_sums = line_all_reduce(
-            [
-                (
-                    dot_nt(gate_grad[part], w_gate_up[:, :hidden_width])
-                    + dot_nt(up_grad[part], w_gate_up[:, hidden_width:])
-                ).astype(bf16)
-                for part in (slice(0, half), slice(half, rows))
-            ],
-            tp_count,
+        return term
+
+    def middle(at, after):
+        batch, part = spots[at]
+        proj, _, _, silu, slope = state["forward"]
+        *kept, gain_part, term = middle_chunk(
+            at,
+            batch,
+            part,
+            step,
+            follow(sums.sums[at], after),
+            proj,
+            layer_input,
+            cotangent,
+            attn_gain_row,
+            mlp_gain_row,
+            silu,
+            slope,
+            w_mlp,
+            state["middle"],
         )
-        hidden_grad = out_grad + jnp.concatenate(branch_sums, axis=0).astype(f32)
-        attn_normed = attn_proj * attn_inv
-        proj_grad = norm_back(hidden_grad, attn_normed, attn_inv, attn_gain).astype(bf16)
-        attn_gain_part = jnp.sum(hidden_grad * attn_normed, axis=0)
-        own_out_t = lax.dynamic_slice_in_dim(w_out_t, tp_index * width, width, 1)
-        attn_grad = dot(proj_grad, own_out_t).astype(bf16)
-        kept.append(
-            dict(
-                hidden_low=hidden_low,
-                act_low=act_low,
-                mlp_grad=mlp_grad,
-                up_grad=up_grad,
-                gate_grad=gate_grad,
-                proj_grad=proj_grad,
-                attn_grad=attn_grad,
-                residual=lax.dynamic_slice_in_dim(hidden_grad, tp_index * share, share, 0),
-                mlp_gain_part=mlp_gain_part,
-                attn_gain_part=attn_gain_part,
-            )
+        state["middle"] = kept
+        mlp_gain_parts.append(gain_part)
+        return term
+
+    def backward(at, after):
+        batch, part = spots[at]
+        *kept, gain_part = backward_chunk(
+            at,
+            batch,
+            part,
+            step,
+            follow(sums.sums[chunks + at], after),
+            cotangent,
+            state["forward"][0],
+            attn_gain_row,
+            w_attn,
+            state["backward"],
         )
-
-    def both(name):
-        return jnp.concatenate([part[name] for part in kept], axis=0)
-
-    hidden_low = both("hidden_low")
-    down_grad = scatter_rows(dot_tn(both("mlp_grad"), both("act_low")))
-    gate_up_grad = scatter_rows(
-        jnp.concatenate(
-            [dot_tn(hidden_low, both("gate_grad")), dot_tn(hidden_low, both("up_grad"))], axis=1
-        )
-    )
-    output_grad = scatter_rows(dot_tn(both("proj_grad"), attended.reshape(MB * rows, width)))
-
-    attn_grad = jnp.stack([part["attn_grad"] for part in kept])
-    attn_grad = attn_grad.reshape(MB, rows, heads, HEAD).transpose(2, 0, 1, 3)
+        state["backward"] = kept
+        attn_gain_parts.append(gain_part)
+        return gain_part
+
+    sums.enter(forward(0, None))
+    sums.enter(forward(1, None))
+    last = None
+    mlp_total = None
+    for at in range(2 * chunks + 2):
+        after = sums.terms[-1] if last is None and tp_count == 4 else last
+        moved = tuple(sums.advance(after)) or None
+        coming = at + 2
+        if coming < chunks:
+            last = forward(coming, moved)
+            sums.enter(last)
+        elif coming < 2 * chunks:
+            last = middle(coming - chunks, moved)
+            sums.enter(last)
+        else:
+            last = backward(coming - 2 * chunks, moved)
+            turn_at = coming - 2 * chunks
+            output, mlp_grad, gate_grad, up_grad = state["middle"]
+            hidden_low, act = state["forward"][1:3]
+            left, right = (
+                (hidden_low, gate_grad),
+                (hidden_low, up_grad),
+                (mlp_grad, act),
+                (None, None),
+            )[turn_at]
+            if left is not None:
+                mlp_total = weight_sum(
+                    (turn_at,), 3, follow(left, last), right, hidden_width, mlp_total
+                )
+                last = mlp_total[0]
+        if coming == 3 * chunks - 1:
+            break
+    hidden_grad, proj_grad, attn_grad = state["backward"]
+    mlp_weight_grad = scatter_rows(mlp_total[0], 1)
+    attended = attended.reshape(MB * rows, width)
+    attn_total = weight_sum((3,), 4, proj_grad, follow(attended, attn_grad), width, None)
+
     attn_grad = exchange(attn_grad).reshape(dp_count, SEG_DEV, BLK, HEAD)
     back = give_back(attend_backward(my_order, packed, attn_grad))
     back = back.reshape(heads, MB, 3, rows, HEAD)
-    inner, gain_part = inner_sums(back, qk_raw, inverse, gains, cosines, sines, heads)
+    inner, gain_part = inner_sums(back, q_raw, k_raw, inverse, gains, cosines, sines, heads)
     means = small_sum(jnp.transpose(inner.reshape(-1, 2)), "tensor", tp_count) / D
     means = jnp.transpose(means).reshape(MB, rows, 2)
-    qkv_grad = unpack_heads(back, qk_raw, inverse, means, gains, cosines, sines, heads)
-
-    input_parts = []
+    qkv_grad = None
+    terms = []
     for batch in range(MB):
-        term = dot_nt(qkv_grad[batch], w_qkv).astype(bf16)
-        input_parts.append(kept[batch]["residual"] + line_reduce_scatter(term, tp_count))
-    qkv_weight_grad = scatter_rows(dot_tn(tokens, qkv_grad.reshape(MB * rows, 3 * width)))
+        *qkv_grad, term = unpack_heads(
+            batch, back, q_raw, k_raw, inverse, means, gains, cosines, sines, w_attn, heads, qkv_grad
+        )
+        terms.append(term)
+    tokens = layer_input.reshape(MB * rows, D)
+    qkv_grad = follow(qkv_grad[0], mlp_weight_grad)
+    attn_total = weight_sum((0, 1, 2), 4, tokens, qkv_grad, width, attn_total)
+    attn_weight_grad = scatter_rows(attn_total[0], 1)
+    mlp_weight_grads = [mlp_weight_grad[at].astype(f32) for at in range(3)]
+    mlp_weight_grads[2] = jnp.transpose(mlp_weight_grads[2])
+    parts, last_operands = line_reduce_scatter(terms, tp_count, mlp_weight_grads)
+    input_parts = [
+        lax.dynamic_slice_in_dim(hidden_grad, batch * rows + tp_index * share, share, 0) + part
+        for batch, part in enumerate(parts)
+    ]
 
     gain_sums = jnp.concatenate(
         [
             gain_part[0],
-            sum(part["attn_gain_part"] for part in kept),
-            sum(part["mlp_gain_part"] for part in kept),
+            sum(attn_gain_parts)[0],
+            sum(mlp_gain_parts)[0],
         ]
     )
-    gain_sums = small_sum(gain_sums.reshape(-1, HEAD), "dp", dp_count).reshape(-1)
+    gain_sums = follow(gain_sums.reshape(-1, HEAD), last_operands)
+    gain_sums = small_sum(gain_sums, "dp", dp_count).reshape(-1)
     return (
-        jnp.stack(outputs),
+        output.reshape(MB, rows, D),
         jnp.stack(input_parts),
-        qkv_weight_grad[:, :width],
-        qkv_weight_grad[:, width : 2 * width],
-        qkv_weight_grad[:, 2 * width :],
-        jnp.transpose(output_grad),
-        gate_up_grad[:, :hidden_width],
-        gate_up_grad[:, hidden_width:],
-        jnp.transpose(down_grad),
+        attn_weight_grad[0].astype(f32),
+        attn_weight_grad[1].astype(f32),
+        attn_weight_grad[2].astype(f32),
+        jnp.transpose(attn_weight_grad[3].astype(f32)),
+        *mlp_weight_grads,
         gain_sums[:width],
         gain_sums[width : 2 * width],
         gain_sums[2 * width : 2 * width + D],

time: 1270 us -> 988 us (0.78)
  Pallas kernels: 70.2 us -> 382 us
  waiting for transfers between devices: 504 us -> 235 us
  matrix products: 253 us -> 0 us
  other arithmetic: 101 us -> 62.9 us
  blocking collectives: 145 us -> 111 us
  starting transfers between devices: 120 us -> 143 us
  local copies, waits for them, and re-layouts: 49 us -> 29.9 us
    pallas_call x1 -> x21, Pallas kernels: 8.16 us -> 319 us  [the longest x19 303 us: chunk_call(): pl.pallas_call(body, grid=grid, in_specs=specs, out_specs=[out[0] for out...]
    ppermute x54 -> x55, waiting for transfers between devices: 426 us -> 157 us  [the longest x3 36.1 us: begin_all_gather(): left2 = lax.ppermute(left1, 'tensor', [(2, 1), (1, 0)])]
    dot_general x31 -> x0, matrix products: 253 us -> none  [the longest x10 95.7 us: dot(): return jnp.dot(left, right, preferred_element_type=f32)]
    all_to_all x1, waiting for transfers between devices: 55.7 us -> 0.01 us  [exchange(): return lax.all_to_all(flat, 'dp', split_axis=0, concat_axis=0, tiled=True)]
    all_gather x4 -> x3, waiting for transfers between devices: 10.8 us -> 52.5 us  [gather_stack(): return lax.all_gather(jnp.stack(pieces), 'dp', axis=1, tiled=True)]
    all_to_all x2 -> x1, blocking collectives: 105 us -> 72.9 us  [give_back(): lax.all_to_all(flat, 'dp', split_axis=0, concat_axis=0, tiled=True)[:items]]
    ppermute x54 -> x55, starting transfers between devices: 97.6 us -> 128 us  [the longest x8 38.3 us: enter(): self.inward.append(lax.ppermute(term, 'tensor', [(0, 1), (3, 2)]))]
    convert_element_type x22, other arithmetic: 14.4 us -> 29.9 us  [low_sum(): return total.astype(bf16)]
  transfers between devices with their start and end apart: 70 -> 69, of which waited for: 37 -> 23; matrix products, arithmetic and copies ran while one was open for 25% -> 8% of each run, Pallas kernels for 6% -> 35%
where the time goes in v2:
time: 988 us; the launch traced here: 979 us
  Pallas kernels  382 us (39%)
  waiting for transfers between devices  235 us (24%)
  starting transfers between devices  143 us (14%)
  blocking collectives  111 us (11%)
  other arithmetic  62.9 us (6%)
  local copies, waits for them, and re-layouts  29.9 us (3%)
  between operations  15.3 us (2%)
    pallas_call x19, Pallas kernels, chunk_call(): pl.pallas_call(body, grid=grid, in_specs=specs, out_specs=[out[0] for out...  303 us
    all_to_all x1, blocking collectives, give_back(): lax.all_to_all(flat, 'dp', split_axis=0, concat_axis=0, tiled=True)[:items]  72.9 us
    all_gather x3, waiting for transfers between devices, gather_stack(): return lax.all_gather(jnp.stack(pieces), 'dp', axis=1, tiled=True)  52.5 us
    ppermute x8, starting transfers between devices, enter(): self.inward.append(lax.ppermute(term, 'tensor', [(0, 1), (3, 2)]))  38.3 us
    all_to_all x1, blocking collectives, exchange(): return lax.all_to_all(flat, 'dp', split_axis=0, concat_axis=0, tiled=True)  38.2 us
    ppermute x3, waiting for transfers between devices, begin_all_gather(): left2 = lax.ppermute(left1, 'tensor', [(2, 1), (1, 0)])  36.1 us
    convert_element_type x22, other arithmetic, low_sum(): return total.astype(bf16)  29.9 us
    pallas_call x1, Pallas kernels, attend_backward(): pl.pallas_call(functools.partial(backward_kernel, trees), in_specs=[pl.Bl...  29.6 us
  transfers between devices with their start and end apart: 69, of which 23 were waited for; matrix products, arithmetic and copies ran while one was open for 8% of the time, Pallas kernels for 35%

profile of v2, /device:TPU:0, one launch (start us, length us, event | category | flops | bytes accessed | tf_op | source)
XLA Modules:
  0.0 978.8 jit_solution(6714141403358836684)
XLA Ops:
  15.4 52.4 %all-gather.5.cloned.1.call-done.refs_0_.refs_1_.refs_4_.refs_8_.refs_9_.refs_10_ = bf16[4,2048,512]{2,1,0:T(8,128)(2,1)} async-done(((bf16[4,256,512]{2,1,0:T(8,128)(2,1)}), bf16[4,2048,512]{2,1,0:T(8,128)(2,1)}) %all-gather.5.cloned.1.call-update) | async-done | bytes 8388624 | tf_op jit(solution)/shard_map/all_gather | solution.py:1060
  67.8 9.8 %project.2 = (f32[2,640,512]{2,1,0:T(8,128)S(1)}, f32[2,640,512]{2,1,0:T(8,128)}, f32[2,640,2]{2,1,0:T(8,128)S(1)}) custom-call(bf16[2,640,2048]{2,1,0:T(8,128)(2,1)} %refs_2_.15, bf16[4,2048,512]{2,1,0:T(8,128)(2,1)} %all-gather.5.cloned.1.call-done.refs_0_.refs_1_.refs_4_.refs_8_.refs_9_.refs_10_, ...), custom_call_target="tpu_custom_call" | custom-call | flops 5368709120 | bytes 9437184 | tf_op jit(solution)/shard_map/project/pallas_call | solution.py:257
  93.8 8.8 pack_heads.1
  118.2 20.6 %collective-permute-done.2 = bf16[1024,512]{1,0:T(8,128)(2,1)} collective-permute-done((bf16[1024,512]{1,0:T(8,128)(2,1)S(1)}, bf16[1024,512]{1,0:T(8,128)(2,1)}, u32[]{:S(2)}, u32[]{:S(2)}) %collective-permute-start.2) | collective-permute-done | bytes 1048608 | tf_op jit(solution)/shard_map/ppermute | solution.py:178
  145.8 24.4 %collective-permute-done.5 = bf16[1024,512]{1,0:T(8,128)(2,1)} collective-permute-done((bf16[1024,512]{1,0:T(8,128)(2,1)S(1)}, bf16[1024,512]{1,0:T(8,128)(2,1)}, u32[]{:S(2)}, u32[]{:S(2)}) %collective-permute-start.5) | collective-permute-done | bytes 1048608 | tf_op jit(solution)/shard_map/ppermute | solution.py:181
  177.8 17.1 %attend_forward.1 = bf16[8,5,128,128]{3,2,1,0:T(8,128)(2,1)} custom-call(s32[40]{0:T(128)S(1)} %fusion.25.order_ref, bf16[8,3,5,128,128]{4,3,2,1,0:T(8,128)(2,1)} %bitcast.15.x_ref), custom_call_target="tpu_custom_call" | custom-call | flops 2883584000 | bytes 5898240 | tf_op jit(solution)/shard_map/attend_forward/pallas_call | solution.py:534
  205.9 14.9 %all-to-all-done.1 = bf16[8,640,128]{2,1,0:T(8,128)(2,1)S(1)} async-done(((bf16[8,640,128]{2,1,0:T(8,128)(2,1)}), bf16[8,640,128]{2,1,0:T(8,128)(2,1)S(1)}, u32[]{:S(2)}, u32[]{:S(2)}) %all-to-all-start.1) | async-done | bytes 1310752 | tf_op jit(solution)/shard_map/all_to_all | solution.py:1075
  227.7 9.8 collective-permute-done.8
  240.9 11.7 %collective-permute-done.9 = bf16[640,512]{1,0:T(8,128)(2,1)} collective-permute-done((bf16[640,512]{1,0:T(8,128)(2,1)S(1)}, bf16[640,512]{1,0:T(8,128)(2,1)}, u32[]{:S(2)}, u32[]{:S(2)}) %collective-permute-start.9) | collective-permute-done | bytes 655392 | tf_op jit(solution)/shard_map/ppermute | solution.py:181
  269.1 9.6 collective-permute-done.11
  280.2 12.5 %collective-permute-done.13 = bf16[640,512]{1,0:T(8,128)(2,1)} collective-permute-done((bf16[640,512]{1,0:T(8,128)(2,1)}, bf16[640,512]{1,0:T(8,128)(2,1)}, u32[]{:S(2)}, u32[]{:S(2)}) %collective-permute-start.13) | collective-permute-done | bytes 655392 | tf_op jit(solution)/shard_map/ppermute | solution.py:192
  298.9 24.1 %forward_chunk.4 = (bf16[1280,2048]{1,0:T(8,128)(2,1)}, bf16[1280,2048]{1,0:T(8,128)(2,1)}, bf16[1280,2048]{1,0:T(8,128)(2,1)}, bf16[1280,2048]{1,0:T(8,128)(2,1...) custom-call(s32[1]{0:T(128)} %bitcast.refs_0_, bf16[640,2048]{1,0:T(8,128)(2,1)S(1)} %copy-done.2, ...), custom_call_target="tpu_custom_call" | custom-call | flops 10737418240 | bytes 44040192 | tf_op jit(solution)/shard_map/forward_chunk/pallas_call | solution.py:698
  326.7 24.1 %forward_chunk.5 = (bf16[1280,2048]{1,0:T(8,128)(2,1)}, bf16[1280,2048]{1,0:T(8,128)(2,1)}, bf16[1280,2048]{1,0:T(8,128)(2,1)}, bf16[1280,2048]{1,0:T(8,128)(2,1...) custom-call(s32[1]{0:T(128)} %bitcast.refs_0_, ...), custom_call_target="tpu_custom_call", output_to_operand_aliasing={{0}: (9, {}), {1}: (10, {}), {2}: (11, {}), {3}: (12, {}), ... | custom-call | flops 10737418240 | bytes 44040192 | tf_op jit(solution)/shard_map/forward_chunk/pallas_call | solution.py:698
  359.0 24.2 %forward_chunk.6 = (bf16[1280,2048]{1,0:T(8,128)(2,1)}, bf16[1280,2048]{1,0:T(8,128)(2,1)}, bf16[1280,2048]{1,0:T(8,128)(2,1)}, bf16[1280,2048]{1,0:T(8,128)(2,1...) custom-call(s32[1]{0:T(128)} %bitcast.refs_0_, ...), custom_call_target="tpu_custom_call", output_to_operand_aliasing={{0}: (9, {}), {1}: (10, {}), {2}: (11, {}), {3}: (12, {}), ... | custom-call | flops 10737418240 | bytes 44040192 | tf_op jit(solution)/shard_map/forward_chunk/pallas_call | solution.py:698
  392.1 24.2 %forward_chunk.7 = (bf16[1280,2048]{1,0:T(8,128)(2,1)}, bf16[1280,2048]{1,0:T(8,128)(2,1)}, bf16[1280,2048]{1,0:T(8,128)(2,1)}, bf16[1280,2048]{1,0:T(8,128)(2,1...) custom-call(s32[1]{0:T(128)} %bitcast.refs_0_, ...), custom_call_target="tpu_custom_call", output_to_operand_aliasing={{0}: (9, {}), {1}: (10, {}), {2}: (11, {}), {3}: (12, {}), ... | custom-call | flops 10737418240 | bytes 44040192 | tf_op jit(solution)/shard_map/forward_chunk/pallas_call | solution.py:698
  428.1 22.4 %middle_chunk.4 = (bf16[1280,2048]{1,0:T(8,128)(2,1)}, bf16[1280,2048]{1,0:T(8,128)(2,1)}, bf16[1280,2048]{1,0:T(8,128)(2,1)}, bf16[1280,2048]{1,0:T(8,128)(2,1)...) custom-call(bf16[320,2048]{1,0:T(8,128)(2,1)S(1)} %broadcast_select_fusion.7.refs_0_, ...), custom_call_target="tpu_custom_call" | custom-call | flops 8053063680 | bytes 40894464 | tf_op jit(solution)/shard_map/middle_chunk/pallas_call | solution.py:698
  462.0 22.3 %middle_chunk.5 = (bf16[1280,2048]{1,0:T(8,128)(2,1)}, bf16[1280,2048]{1,0:T(8,128)(2,1)}, bf16[1280,2048]{1,0:T(8,128)(2,1)}, bf16[1280,2048]{1,0:T(8,128)(2,1)...) custom-call(bf16[320,2048]{1,0:T(8,128)(2,1)S(1)} %broadcast_select_, ...), custom_call_target="tpu_custom_call", output_to_operand_aliasing={{0}: (11, {}), {1}: (12, {}), {2}: (13, {}), {3}: (14, {})} | custom-call | flops 8053063680 | bytes 40894464 | tf_op jit(solution)/shard_map/middle_chunk/pallas_call | solution.py:698
  498.7 22.5 %middle_chunk.6 = (bf16[1280,2048]{1,0:T(8,128)(2,1)}, bf16[1280,2048]{1,0:T(8,128)(2,1)}, bf16[1280,2048]{1,0:T(8,128)(2,1)}, bf16[1280,2048]{1,0:T(8,128)(2,1)...) custom-call(bf16[320,2048]{1,0:T(8,128)(2,1)S(1)} %broadcast_select_, ...), custom_call_target="tpu_custom_call", output_to_operand_aliasing={{0}: (11, {}), {1}: (12, {}), {2}: (13, {}), {3}: (14, {})} | custom-call | flops 8053063680 | bytes 40894464 | tf_op jit(solution)/shard_map/middle_chunk/pallas_call | solution.py:698
  530.6 22.4 %middle_chunk.7 = (bf16[1280,2048]{1,0:T(8,128)(2,1)}, bf16[1280,2048]{1,0:T(8,128)(2,1)}, bf16[1280,2048]{1,0:T(8,128)(2,1)}, bf16[1280,2048]{1,0:T(8,128)(2,1)...) custom-call(bf16[320,2048]{1,0:T(8,128)(2,1)S(1)} %broadcast_select_, ...), custom_call_target="tpu_custom_call", output_to_operand_aliasing={{0}: (11, {}), {1}: (12, {}), {2}: (13, {}), {3}: (14, {})} | custom-call | flops 8053063680 | bytes 40894464 | tf_op jit(solution)/shard_map/middle_chunk/pallas_call | solution.py:698
  567.9 16.0 %weight_sum.5.refs_2_ = bf16[3,2048,2048]{2,1,0:T(8,128)(2,1)} custom-call(bf16[1280,2048]{1,0:T(8,128)(2,1)} %get-tuple-element.224.refs_0_, bf16[1280,2048]{1,0:T(8,128)(2,1)} %get-tuple-element.215.refs_1_), custom_call_target="tpu_custom_call" | custom-call | flops 10737418240 | bytes 18874368 | tf_op jit(solution)/shard_map/weight_sum/pallas_call | solution.py:698
  594.7 15.9 %weight_sum.6.refs_2_ = bf16[3,2048,2048]{2,1,0:T(8,128)(2,1)} custom-call(bf16[1280,2048]{1,0:T(8,128)(2,1)} %get-tuple-element.224.refs_0_, bf16[1280,2048]{1,0:T(8,128)(2,1)} %get-tuple-element.225.refs_1_, bf16[3,2048,2048]{2,1,0:T(8,128)(2,1)} %weight_sum.5.refs_2_), custom_call_target="tpu_custom_call", output_to_operand_aliasing={{}: (2, {})} | custom-call | flops 10737418240 | bytes 18874368 | tf_op jit(solution)/shard_map/weight_sum/pallas_call | solution.py:698
  617.2 16.0 %weight_sum.7 = bf16[3,2048,2048]{2,1,0:T(8,128)(2,1)} custom-call(bf16[1280,2048]{1,0:T(8,128)(2,1)} %get-tuple-element.234.refs_0_, bf16[1280,2048]{1,0:T(8,128)(2,1)} %get-tuple-element.235.refs_1_, bf16[3,2048,2048]{2,1,0:T(8,128)(2,1)} %weight_sum.6.refs_2_), custom_call_target="tpu_custom_call", output_to_operand_aliasing={{}: (2, {})} | custom-call | flops 10737418240 | bytes 18874368 | tf_op jit(solution)/shard_map/weight_sum/pallas_call | solution.py:698
  634.6 19.5 %collective-permute-done.44 = bf16[320,2048]{1,0:T(8,128)(2,1)S(1)} collective-permute-done((bf16[320,2048]{1,0:T(8,128)(2,1)S(1)}, bf16[320,2048]{1,0:T(8,128)(2,1)S(1)}, u32[]{:S(2)}, u32[]{:S(2)}) %collective-permute-start.44) | collective-permute-done | bytes 1310752 | tf_op jit(solution)/shard_map/ppermute | solution.py:132
  661.9 38.2 %all_to_all.20 = bf16[8,640,128]{2,1,0:T(8,128)(2,1)S(1)} all-to-all(bf16[8,640,128]{2,1,0:T(8,128)(2,1)S(1)} %bitcast.163), channel_id=1, replica_groups=mesh['dp'=8,'tensor'=4] {'dp'}, dimensions={0} | all-to-all | bytes 2621440 | tf_op jit(solution)/shard_map/all_to_all | solution.py:1071
  700.1 29.6 %attend_backward.1 = bf16[8,3,5,128,128]{4,3,2,1,0:T(8,128)(2,1)} custom-call(s32[40]{0:T(128)S(1)} %copy-done.12, bf16[8,3,5,128,128]{4,3,2,1,0:T(8,128)(2,1)} %bitcast.15.x_ref, bf16[8,5,128,128]{3,2,1,0:T(8,128)(2,1)S(1)} %bitcast.171), custom_call_target="tpu_custom_call" | custom-call | flops 7208960000 | bytes 9830400 | tf_op jit(solution)/shard_map/attend_backward/pallas_call | solution.py:647
  729.6 72.9 %all_to_all.21 = bf16[8,1920,128]{2,1,0:T(8,128)(2,1)} all-to-all(bf16[8,1920,128]{2,1,0:T(8,128)(2,1)} %bitcast.223), channel_id=1, replica_groups=mesh['dp'=8,'tensor'=4] {'dp'}, dimensions={0} | all-to-all | bytes 7864320 | tf_op jit(solution)/shard_map/all_to_all | solution.py:1075
  822.4 10.4 %unpack_heads.2 = (bf16[1280,1536]{1,0:T(8,128)(2,1)}, bf16[640,2048]{1,0:T(8,128)(2,1)}) custom-call(bf16[4,2,3,640,128]{4,3,2,1,0:T(8,128)(2,1)} %bitcast.203, f32[2,640,512]{2,1,0:T(8,128)} %copy-done, f32[2,640,512]{2,1,0:T(8,128)} %get-tuple-element.137.k_ref.refs_2_, f32[2,640,2]{2,1,0:T(8,128)S(1)} %bitcast.166, f32[2,640,2]{2,1,0:T(8,128)S(1)} %bitcast.168, ...), custom_call_target="tpu_custom_call" | custom-call | flops 4026531840 | bytes 10485760 | tf_op jit(solution)/shard_map/unpack_heads/pallas_call | solution.py:698
  832.8 10.1 %unpack_heads.3 = (bf16[1280,1536]{1,0:T(8,128)(2,1)}, bf16[640,2048]{1,0:T(8,128)(2,1)}) custom-call(bf16[4,2,3,640,128]{4,3,2,1,0:T(8,128)(2,1)} %bitcast.204, f32[2,640,512]{2,1,0:T(8,128)} %copy-done, f32[2,640,512]{2,1,0:T(8,128)} %get-tuple-element.137.k_ref.refs_2_, f32[2,640,2]{2,1,0:T(8,128)S(1)} %bitcast.167, ...), custom_call_target="tpu_custom_call", output_to_operand_aliasing={{0}: (11, {})} | custom-call | flops 4026531840 | bytes 10485760 | tf_op jit(solution)/shard_map/unpack_heads/pallas_call | solution.py:698
  846.4 16.3 %weight_sum.9 = bf16[4,2048,512]{2,1,0:T(8,128)(2,1)} custom-call(bf16[1280,2048]{1,0:T(8,128)(2,1)} %bitcast.201, bf16[1280,1536]{1,0:T(8,128)(2,1)S(1)} %copy-done.7, bf16[4,2048,512]{2,1,0:T(8,128)(2,1)} %weight_sum.8.refs_2_), custom_call_target="tpu_custom_call", output_to_operand_aliasing={{}: (2, {})} | custom-call | flops 8053063680 | bytes 25952256 | tf_op jit(solution)/shard_map/weight_sum/pallas_call | solution.py:698
  873.5 9.0 collective-permute-done.47
  895.1 8.5 collective-permute-done.48
  928.9 9.2 collective-permute-done.54
  (289 shorter events, 314.2 us)
Async XLA Ops:
  7.2 60.6 %all-gather.5.cloned.1.call-start = ((), (), s32[]{:S(2)}) async-start(), calls=%async_computation.6 | async-start | bytes 9437184 | tf_op jit(solution)/shard_map/all_gather | solution.py:1060
  10.6 286.6 %all-gather.9.cloned.1.call-start = ((), (), s32[]{:S(2)}) async-start(), calls=%async_computation.10 | async-start | bytes 9437184 | tf_op jit(solution)/shard_map/all_gather | solution.py:1060
  102.6 67.7 %all-to-all-start = ((bf16[8,1920,128]{2,1,0:T(8,128)(2,1)}), bf16[8,1920,128]{2,1,0:T(8,128)(2,1)}, u32[]{:S(2)}, u32[]{:S(2)}) async-start(bf16[8,1920,128]{2,1,0:T(8,128)(2,1)} %bitcast.206), calls=%async_computation | async-start | bytes 7864320 | tf_op jit(solution)/shard_map/all_to_all | solution.py:1071
  107.1 190.1 %all-gather.7.cloned.1.call-start = ((), (), s32[]{:S(2)}) async-start(), calls=%async_computation.7 | async-start | bytes 18874368 | tf_op jit(solution)/shard_map/all_gather | solution.py:1060
  198.6 645.7 %reduce-scatter.3.cloned.1.call-start = ((), (), s32[]{:S(2)}) async-start(), calls=%async_computation.8 | async-start | bytes 28311552 | tf_op jit(solution)/shard_map/reduce_scatter | solution.py:1063
  205.9 91.3 %collective-permute-start.17 = (bf16[1024,2048]{1,0:T(8,128)(2,1)}, bf16[1024,2048]{1,0:T(8,128)(2,1)}, u32[]{:S(2)}, u32[]{:S(2)}) collective-permute-start(bf16[1024,2048]{1,0:T(8,128)(2,1)} %select_dynamic-update-slice_fusion.refs_4_), channel_id=1, source_target_pairs={{0,4},{4,0},{8,12},{12,8},{16,20},{20,16},{24,28},{28,24},{1,5},{5... | collective-permute-start | bytes 12582920 | tf_op jit(solution)/shard_map/ppermute | solution.py:224
  260.3 32.4 %collective-permute-start.13 = (bf16[640,512]{1,0:T(8,128)(2,1)}, bf16[640,512]{1,0:T(8,128)(2,1)}, u32[]{:S(2)}, u32[]{:S(2)}) collective-permute-start(bf16[640,512]{1,0:T(8,128)(2,1)} %collective-permute-done.9), channel_id=1, source_target_pairs={{1,0},{5,4},{9,8},{13,12},{17,16},{21,20},{25,24},{29,28}} | collective-permute-start | bytes 1966088 | tf_op jit(solution)/shard_map/ppermute | solution.py:192
  262.1 33.3 %collective-permute-start.14 = (bf16[640,512]{1,0:T(8,128)(2,1)}, bf16[640,512]{1,0:T(8,128)(2,1)S(1)}, u32[]{:S(2)}, u32[]{:S(2)}) collective-permute-start(bf16[640,512]{1,0:T(8,128)(2,1)} %collective-permute-done.7), channel_id=1, source_target_pairs={{2,3},{6,7},{10,11},{14,15},{18,19},{22,23},{26,27},{30,31}} | collective-permute-start | bytes 1966088 | tf_op jit(solution)/shard_map/ppermute | solution.py:191
  267.6 56.8 %collective-permute-start.19 = (bf16[640,512]{1,0:T(8,128)(2,1)}, bf16[640,512]{1,0:T(8,128)(2,1)}, u32[]{:S(2)}, u32[]{:S(2)}) collective-permute-start(bf16[640,512]{1,0:T(8,128)(2,1)} %collective-permute-done.10), channel_id=1, source_target_pairs={{1,2},{2,3},{5,6},{6,7},{9,10},{10,11},{13,14},{14,15},{17,18},{18... | collective-permute-start | bytes 1966088 | tf_op jit(solution)/shard_map/ppermute | solution.py:180
  278.7 46.4 %collective-permute-start.12 = (bf16[640,512]{1,0:T(8,128)(2,1)}, bf16[640,512]{1,0:T(8,128)(2,1)S(1)}, u32[]{:S(2)}, u32[]{:S(2)}) collective-permute-start(bf16[640,512]{1,0:T(8,128)(2,1)} %collective-permute-done.11), channel_id=1, source_target_pairs={{2,1},{1,0},{6,5},{5,4},{10,9},{9,8},{14,13},{13,12},{18,17},{17,1... | collective-permute-start | bytes 1966088 | tf_op jit(solution)/shard_map/ppermute | solution.py:181
  323.0 34.3 %collective-permute-start.21 = (bf16[320,2048]{1,0:T(8,128)(2,1)S(1)}, bf16[320,2048]{1,0:T(8,128)(2,1)S(1)}, u32[]{:S(2)}, u32[]{:S(2)}) collective-permute-start(bf16[320,2048]{1,0:T(8,128)(2,1)S(1)} %get-tuple-element.155), channel_id=1, source_target_pairs={{0,1},{3,2},{4,5},{7,6},{8,9},{11,10},{12,13},{15,14},{16,17},{19,... | collective-permute-start | bytes 3932168 | tf_op jit(solution)/shard_map/ppermute | solution.py:108
  324.4 31.5 %collective-permute-start.20 = (bf16[640,512]{1,0:T(8,128)(2,1)}, bf16[640,512]{1,0:T(8,128)(2,1)S(1)}, u32[]{:S(2)}, u32[]{:S(2)}) collective-permute-start(bf16[640,512]{1,0:T(8,128)(2,1)} %collective-permute-done.19), channel_id=1, source_target_pairs={{2,3},{6,7},{10,11},{14,15},{18,19},{22,23},{26,27},{30,31}} | collective-permute-start | bytes 1966088 | tf_op jit(solution)/shard_map/ppermute | solution.py:191
  350.8 37.0 %collective-permute-start.22 = (bf16[320,2048]{1,0:T(8,128)(2,1)S(1)}, bf16[320,2048]{1,0:T(8,128)(2,1)S(1)}, u32[]{:S(2)}, u32[]{:S(2)}) collective-permute-start(bf16[320,2048]{1,0:T(8,128)(2,1)S(1)} %get-tuple-element.163), channel_id=1, source_target_pairs={{0,1},{3,2},{4,5},{7,6},{8,9},{11,10},{12,13},{15,14},{16,17},{19,... | collective-permute-start | bytes 3932168 | tf_op jit(solution)/shard_map/ppermute | solution.py:108
  357.8 32.2 %collective-permute-start.23 = (bf16[320,2048]{1,0:T(8,128)(2,1)S(1)}, bf16[320,2048]{1,0:T(8,128)(2,1)S(1)}, u32[]{:S(2)}, u32[]{:S(2)}) collective-permute-start(bf16[320,2048]{1,0:T(8,128)(2,1)S(1)} %add_convert_fusion.15), channel_id=1, source_target_pairs={{1,2},{2,1},{5,6},{6,5},{9,10},{10,9},{13,14},{14,13},{17,18},{18,... | collective-permute-start | bytes 3932168 | tf_op jit(solution)/shard_map/ppermute | solution.py:130
  383.2 37.7 %collective-permute-start.25 = (bf16[320,2048]{1,0:T(8,128)(2,1)S(1)}, bf16[320,2048]{1,0:T(8,128)(2,1)}, u32[]{:S(2)}, u32[]{:S(2)}) collective-permute-start(bf16[320,2048]{1,0:T(8,128)(2,1)S(1)} %get-tuple-element.173), channel_id=1, source_target_pairs={{0,1},{3,2},{4,5},{7,6},{8,9},{11,10},{12,13},{15,14},{16,17},{19,... | collective-permute-start | bytes 3932168 | tf_op jit(solution)/shard_map/ppermute | solution.py:108
  388.3 36.2 %collective-permute-start.26 = (bf16[320,2048]{1,0:T(8,128)(2,1)S(1)}, bf16[320,2048]{1,0:T(8,128)(2,1)}, u32[]{:S(2)}, u32[]{:S(2)}) collective-permute-start(bf16[320,2048]{1,0:T(8,128)(2,1)S(1)} %add_convert_fusion.14), channel_id=1, source_target_pairs={{1,2},{2,1},{5,6},{6,5},{9,10},{10,9},{13,14},{14,13},{17,18},{18,... | collective-permute-start | bytes 3932168 | tf_op jit(solution)/shard_map/ppermute | solution.py:130
  390.6 37.3 %collective-permute-start.24 = (bf16[320,2048]{1,0:T(8,128)(2,1)S(1)}, bf16[320,2048]{1,0:T(8,128)(2,1)S(1)}, u32[]{:S(2)}, u32[]{:S(2)}) collective-permute-start(bf16[320,2048]{1,0:T(8,128)(2,1)S(1)} %add_convert_fusion.13), channel_id=1, source_target_pairs={{1,0},{2,3},{5,4},{6,7},{9,8},{10,11},{13,12},{14,15},{17,16},{18,... | collective-permute-start | bytes 3932168 | tf_op jit(solution)/shard_map/ppermute | solution.py:132
  416.2 43.2 %collective-permute-start.27 = (bf16[320,2048]{1,0:T(8,128)(2,1)S(1)}, bf16[320,2048]{1,0:T(8,128)(2,1)S(1)}, u32[]{:S(2)}, u32[]{:S(2)}) collective-permute-start(bf16[320,2048]{1,0:T(8,128)(2,1)S(1)} %get-tuple-element.180), channel_id=1, source_target_pairs={{0,1},{3,2},{4,5},{7,6},{8,9},{11,10},{12,13},{15,14},{16,17},{19,... | collective-permute-start | bytes 3932168 | tf_op jit(solution)/shard_map/ppermute | solution.py:108
  422.8 33.4 %collective-permute-start.29 = (bf16[320,2048]{1,0:T(8,128)(2,1)S(1)}, bf16[320,2048]{1,0:T(8,128)(2,1)}, u32[]{:S(2)}, u32[]{:S(2)}) collective-permute-start(bf16[320,2048]{1,0:T(8,128)(2,1)S(1)} %add_convert_fusion.12), channel_id=1, source_target_pairs={{1,2},{2,1},{5,6},{6,5},{9,10},{10,9},{13,14},{14,13},{17,18},{18,... | collective-permute-start | bytes 3932168 | tf_op jit(solution)/shard_map/ppermute | solution.py:130
  426.4 35.5 %collective-permute-start.28 = (bf16[320,2048]{1,0:T(8,128)(2,1)S(1)}, bf16[320,2048]{1,0:T(8,128)(2,1)S(1)}, u32[]{:S(2)}, u32[]{:S(2)}) collective-permute-start(bf16[320,2048]{1,0:T(8,128)(2,1)S(1)} %add_convert_fusion.11), channel_id=1, source_target_pairs={{1,0},{2,3},{5,4},{6,7},{9,8},{10,11},{13,12},{14,15},{17,16},{18,... | collective-permute-start | bytes 3932168 | tf_op jit(solution)/shard_map/ppermute | solution.py:132
  450.5 40.8 %collective-permute-start.32 = (bf16[320,2048]{1,0:T(8,128)(2,1)S(1)}, bf16[320,2048]{1,0:T(8,128)(2,1)}, u32[]{:S(2)}, u32[]{:S(2)}) collective-permute-start(bf16[320,2048]{1,0:T(8,128)(2,1)S(1)} %get-tuple-element.191), channel_id=1, source_target_pairs={{0,1},{3,2},{4,5},{7,6},{8,9},{11,10},{12,13},{15,14},{16,17},{19,... | collective-permute-start | bytes 3932168 | tf_op jit(solution)/shard_map/ppermute | solution.py:108
  458.1 40.5 %collective-permute-start.31 = (bf16[320,2048]{1,0:T(8,128)(2,1)S(1)}, bf16[320,2048]{1,0:T(8,128)(2,1)S(1)}, u32[]{:S(2)}, u32[]{:S(2)}) collective-permute-start(bf16[320,2048]{1,0:T(8,128)(2,1)S(1)} %add_convert_fusion.9), channel_id=1, source_target_pairs={{1,0},{2,3},{5,4},{6,7},{9,8},{10,11},{13,12},{14,15},{17,16},{18,... | collective-permute-start | bytes 3932168 | tf_op jit(solution)/shard_map/ppermute | solution.py:132
  459.9 35.0 %collective-permute-start.30 = (bf16[320,2048]{1,0:T(8,128)(2,1)S(1)}, bf16[320,2048]{1,0:T(8,128)(2,1)}, u32[]{:S(2)}, u32[]{:S(2)}) collective-permute-start(bf16[320,2048]{1,0:T(8,128)(2,1)S(1)} %add_convert_fusion.10), channel_id=1, source_target_pairs={{1,2},{2,1},{5,6},{6,5},{9,10},{10,9},{13,14},{14,13},{17,18},{18,... | collective-permute-start | bytes 3932168 | tf_op jit(solution)/shard_map/ppermute | solution.py:130
  484.3 41.5 %collective-permute-start.34 = (bf16[320,2048]{1,0:T(8,128)(2,1)S(1)}, bf16[320,2048]{1,0:T(8,128)(2,1)S(1)}, u32[]{:S(2)}, u32[]{:S(2)}) collective-permute-start(bf16[320,2048]{1,0:T(8,128)(2,1)S(1)} %get-tuple-element.199), channel_id=1, source_target_pairs={{0,1},{3,2},{4,5},{7,6},{8,9},{11,10},{12,13},{15,14},{16,17},{19,... | collective-permute-start | bytes 3932168 | tf_op jit(solution)/shard_map/ppermute | solution.py:108
  493.1 34.0 %collective-permute-start.35 = (bf16[320,2048]{1,0:T(8,128)(2,1)S(1)}, bf16[320,2048]{1,0:T(8,128)(2,1)}, u32[]{:S(2)}, u32[]{:S(2)}) collective-permute-start(bf16[320,2048]{1,0:T(8,128)(2,1)S(1)} %add_convert_fusion.7), channel_id=1, source_target_pairs={{1,2},{2,1},{5,6},{6,5},{9,10},{10,9},{13,14},{14,13},{17,18},{18,... | collective-permute-start | bytes 3932168 | tf_op jit(solution)/shard_map/ppermute | solution.py:130
  496.8 33.7 %collective-permute-start.33 = (bf16[320,2048]{1,0:T(8,128)(2,1)S(1)}, bf16[320,2048]{1,0:T(8,128)(2,1)S(1)}, u32[]{:S(2)}, u32[]{:S(2)}) collective-permute-start(bf16[320,2048]{1,0:T(8,128)(2,1)S(1)} %add_convert_fusion.8), channel_id=1, source_target_pairs={{1,0},{2,3},{5,4},{6,7},{9,8},{10,11},{13,12},{14,15},{17,16},{18,... | collective-permute-start | bytes 3932168 | tf_op jit(solution)/shard_map/ppermute | solution.py:132
  521.1 37.5 %collective-permute-start.37 = (bf16[320,2048]{1,0:T(8,128)(2,1)S(1)}, bf16[320,2048]{1,0:T(8,128)(2,1)S(1)}, u32[]{:S(2)}, u32[]{:S(2)}) collective-permute-start(bf16[320,2048]{1,0:T(8,128)(2,1)S(1)} %get-tuple-element.210), channel_id=1, source_target_pairs={{0,1},{3,2},{4,5},{7,6},{8,9},{11,10},{12,13},{15,14},{16,17},{19,... | collective-permute-start | bytes 3932168 | tf_op jit(solution)/shard_map/ppermute | solution.py:108
  526.4 33.6 %collective-permute-start.38 = (bf16[320,2048]{1,0:T(8,128)(2,1)S(1)}, bf16[320,2048]{1,0:T(8,128)(2,1)S(1)}, u32[]{:S(2)}, u32[]{:S(2)}) collective-permute-start(bf16[320,2048]{1,0:T(8,128)(2,1)S(1)} %add_convert_fusion.6), channel_id=1, source_target_pairs={{1,2},{2,1},{5,6},{6,5},{9,10},{10,9},{13,14},{14,13},{17,18},{18,... | collective-permute-start | bytes 3932168 | tf_op jit(solution)/shard_map/ppermute | solution.py:130
  529.0 32.8 %collective-permute-start.36 = (bf16[320,2048]{1,0:T(8,128)(2,1)S(1)}, bf16[320,2048]{1,0:T(8,128)(2,1)S(1)}, u32[]{:S(2)}, u32[]{:S(2)}) collective-permute-start(bf16[320,2048]{1,0:T(8,128)(2,1)S(1)} %add_convert_fusion.5), channel_id=1, source_target_pairs={{1,0},{2,3},{5,4},{6,7},{9,8},{10,11},{13,12},{14,15},{17,16},{18,... | collective-permute-start | bytes 3932168 | tf_op jit(solution)/shard_map/ppermute | solution.py:132
  553.0 32.7 %collective-permute-start.39 = (bf16[320,2048]{1,0:T(8,128)(2,1)S(1)}, bf16[320,2048]{1,0:T(8,128)(2,1)}, u32[]{:S(2)}, u32[]{:S(2)}) collective-permute-start(bf16[320,2048]{1,0:T(8,128)(2,1)S(1)} %get-tuple-element.216), channel_id=1, source_target_pairs={{0,1},{3,2},{4,5},{7,6},{8,9},{11,10},{12,13},{15,14},{16,17},{19,... | collective-permute-start | bytes 3932168 | tf_op jit(solution)/shard_map/ppermute | solution.py:108
  633.2 335.4 %reduce-scatter.5.cloned.1.call-start = ((), (), s32[]{:S(2)}) async-start(), calls=%async_computation.9 | async-start | bytes 9437184 | tf_op jit(solution)/shard_map/reduce_scatter | solution.py:1063
  923.0 35.4 %collective-permute-start.49 = (bf16[160,2048]{1,0:T(8,128)(2,1)}, bf16[160,2048]{1,0:T(8,128)(2,1)S(1)}, u32[]{:S(2)}, u32[]{:S(2)}) collective-permute-start(bf16[160,2048]{1,0:T(8,128)(2,1)} %get-tuple-element.318), channel_id=1, source_target_pairs={{0,1},{1,2},{2,3},{4,5},{5,6},{6,7},{8,9},{9,10},{10,11},{12,13},{... | collective-permute-start | bytes 1966088 | tf_op jit(solution)/shard_map/ppermute | solution.py:162
  (64 other events, 1094.2 us)
Sparse Core Ops, SparseCore 0:
  10.7 57.0 all-gather.4
  69.7 77.0 all-gather.8
  173.1 102.3 all-gather.6
  633.3 210.8 reduce-scatter.2
  862.9 71.2 reduce-scatter.4

commit v3 on v2

--- a/solution.py
+++ b/solution.py
@@ -20,7 +20,6 @@
 PAIR = 2 * BLK
 TRUNK_ROWS = TRUNK * BLK
 TILE = 512
-LONG = 1024
 
 EPSILON = 1e-06
 ROPE_BASE = 500000.0
@@ -138,7 +137,7 @@
         return [
             lax.psum_scatter(values, "tensor", scatter_dimension=0, tiled=True).astype(f32)
             for values in batches
-        ], None
+        ], None, None
     index = lax.axis_index("tensor")
     rights = []
     lefts = []
@@ -154,6 +153,8 @@
         for at, item in enumerate(blocks):
             right = block(item, index + count - 1 - stage)
             left = block(item, index - count + 1 + stage)
+            if stage == 1 and at == 0:
+                right, left = follow((right, left), batches[-1])
             if stage:
                 right = low_sum(right, rights[at])
                 left = low_sum(left, lefts[at])
@@ -169,50 +170,54 @@
         block(item, index).astype(f32) + right.astype(f32) + left.astype(f32)
         for item, right, left in zip(blocks, rights, lefts)
     ]
-    return sums, operands[-1]
+    return sums, operands[len(blocks)], operands[-1]
 
 
 def begin_all_gather(values, count):
     if count != 4:
-        return values, (None,) * 4
-    right1 = lax.ppermute(values, "tensor", [(0, 1), (1, 2), (2, 3)])
-    left1 = lax.ppermute(values, "tensor", [(3, 2), (2, 1), (1, 0)])
-    right2 = lax.ppermute(right1, "tensor", [(1, 2), (2, 3)])
-    left2 = lax.ppermute(left1, "tensor", [(2, 1), (1, 0)])
-    return values, (right1, left1, right2, left2)
+        return values, None
+    right = lax.ppermute(values, "tensor", [(0, 1), (1, 2), (2, 3)])
+    left = lax.ppermute(values, "tensor", [(3, 2), (2, 1), (1, 0)])
+    return values, (right, left)
+
+
+def go_on_all_gather(begun, count):
+    values, first = begun
+    if count != 4:
+        return values, None, None
+    right = lax.ppermute(first[0], "tensor", [(1, 2), (2, 3)])
+    left = lax.ppermute(first[1], "tensor", [(2, 1), (1, 0)])
+    return values, first, (right, left)
 
 
 def end_all_gather(begun, count, after=None):
-    values, (right1, left1, right2, left2) = begun
+    values, first, second = begun
     if count != 4:
-        return lax.all_gather(values, "tensor", axis=1, tiled=True)
+        return lax.all_gather(values, "tensor", axis=1, tiled=True), None
     index = lax.axis_index("tensor")
     width = values.shape[1]
-    right3 = lax.ppermute(follow(right2, after), "tensor", [(2, 3)])
-    left3 = lax.ppermute(follow(left2, after), "tensor", [(1, 0)])
+    right, left = follow(second, after)
+    right = lax.ppermute(right, "tensor", [(2, 3)])
+    left = lax.ppermute(left, "tensor", [(1, 0)])
     whole = jnp.zeros((values.shape[0], count * width), values.dtype)
     pieces = (
         values,
-        jnp.where(index >= 1, right1, left3),
-        jnp.where(index >= 2, right2, left2),
-        jnp.where(index >= 3, right3, left1),
+        jnp.where(index >= 1, first[0], left),
+        jnp.where(index >= 2, second[0], second[1]),
+        jnp.where(index >= 3, right, first[1]),
     )
     for back, piece in enumerate(pieces):
         place = lax.rem(index - back + count, count) * width
         whole = lax.dynamic_update_slice(whole, piece, (0, place))
-    return whole
-
-
-def line_all_gather(values, count):
-    return end_all_gather(begin_all_gather(values, count), count)
+    return whole, (right, left)
 
 
 def begin_output_weight(own, after, dp_index, dp_count, count):
     if count != 4 or dp_count % 2:
-        return own, (None,) * 4
+        return own, None, None
     half = own.shape[0] // 2
     mine = lax.dynamic_slice_in_dim(follow(own, after), lax.rem(dp_index, 2) * half, half, 0)
-    return begin_all_gather(mine, count)
+    return go_on_all_gather(begin_all_gather(mine, count), count)
 
 
 def end_output_weight(begun, after, dp_index, dp_count, count):
@@ -220,7 +225,7 @@
         whole = lax.all_gather(begun[0], "tensor", axis=1, tiled=True)
         half = whole.shape[0] // 2
         return jnp.zeros((1,), jnp.int32), whole[:half], whole[half:]
-    mine = end_all_gather(begun, count, after)
+    mine, _ = end_all_gather(begun, count, after)
     other = lax.ppermute(mine, "dp", [(i, i ^ 1) for i in range(dp_count)])
     return lax.rem(dp_index, 2).astype(jnp.int32).reshape(1), mine, other
 
@@ -709,70 +714,167 @@
     )(*values)
 
 
-def clip(step, low, count):
-    return jnp.minimum(jnp.maximum(step - low, 0), count - 1)
-
-
 def forward_chunk_kernel(
-    first,
-    second,
+    place,
     core_ref,
+    gain_ref,
+    y_hbm,
+    x_hbm,
+    woa_hbm,
+    wob_hbm,
+    wg_hbm,
+    wr_hbm,
+    proj_hbm,
+    low_hbm,
+    act_hbm,
+    silu_hbm,
+    slope_hbm,
+    part_hbm,
     y_ref,
     x_ref,
-    gain_ref,
-    woa_ref,
-    wob_ref,
-    wg_ref,
-    wu_ref,
-    wd_ref,
+    row_ref,
+    gate_ref,
+    up_ref,
+    exact_ref,
     proj_ref,
     low_ref,
     act_ref,
     silu_ref,
     slope_ref,
     part_ref,
-    exact_ref,
-    held_ref,
+    y_sem,
+    x_sem,
+    row_sems,
+    gate_sems,
+    up_sems,
+    out_sems,
+    part_sems,
 ):
-    step = pl.program_id(0)
-    half = first // 2
-
-    def project_tile(weight_ref, side):
-        at = side * half + lax.rem(step, half)
-        columns = pl.ds(pl.multiple_of(at * LONG, LONG), LONG)
-        exact_ref[:, columns] = nt(y_ref[...], weight_ref[...])
-
-    @pl.when(step < half)
-    def _():
-        project_tile(woa_ref, core_ref[0])
-
-    @pl.when((step >= half) & (step < first))
-    def _():
-        project_tile(wob_ref, 1 - core_ref[0])
-
-    @pl.when(step == first)
-    def _():
-        proj = exact_ref[...]
-        inverse = lax.rsqrt(mean_square(proj) + EPSILON)
-        proj_ref[...] = proj.astype(bf16)
-        low_ref[...] = (x_ref[...].astype(f32) + proj * inverse * gain_ref[...]).astype(bf16)
-
-    @pl.when((step >= first) & (step < second))
-    def _():
+    at, batch, part = place
+    rows = y_ref.shape[0]
+    units = act_ref.shape[1]
+    tiles = D // TILE
+    half = tiles // 2
+    unit_tiles = units // TILE
+    here = pl.ds(at * rows, rows)
+
+    def tile(index):
+        return pl.ds(pl.multiple_of(index * TILE, TILE), TILE)
+
+    def out_tile(source, index):
+        slot = index if source is woa_hbm else index + half
+        return pltpu.make_async_copy(
+            source.at[tile(index), :], row_ref.at[slot], row_sems.at[slot]
+        )
+
+    def unit_copies(index):
+        slot = lax.rem(index, 2)
+        return (
+            pltpu.make_async_copy(wg_hbm.at[0, :, tile(index)], gate_ref.at[slot], gate_sems.at[slot]),
+            pltpu.make_async_copy(wr_hbm.at[0, :, tile(index)], up_ref.at[slot], up_sems.at[slot]),
+        )
+
+    def down_copy(index):
+        return pltpu.make_async_copy(
+            wr_hbm.at[1, tile(index), :], row_ref.at[index, :, pl.ds(0, units)], row_sems.at[index]
+        )
+
+    def row_wait(index, width):
+        pltpu.make_async_copy(
+            woa_hbm.at[pl.ds(0, TILE), pl.ds(0, width)],
+            row_ref.at[index, :, pl.ds(0, width)],
+            row_sems.at[index],
+        ).wait()
+
+    y_copy = pltpu.make_async_copy(y_hbm.at[pl.ds(part * rows, rows), :], y_ref, y_sem)
+    x_copy = pltpu.make_async_copy(x_hbm.at[batch, pl.ds(part * rows, rows), :], x_ref, x_sem)
+    y_copy.start()
+    for index in range(half):
+        out_tile(woa_hbm, index).start()
+    x_copy.start()
+    y_copy.wait()
+
+    def project_tile(index, carry):
+        row_wait(index, D)
+
+        @pl.when(index < half)
+        def _():
+            out_tile(wob_hbm, index).start()
+
+        @pl.when(index >= half)
+        def _():
+            for copy in unit_copies(index - half):
+                copy.start()
+
+        side = jnp.where(index < half, core_ref[0], 1 - core_ref[0])
+        columns = tile(side * half + lax.rem(index, half))
+        exact_ref[:, columns] = nt(y_ref[...], row_ref[index])
+        return carry
+
+    lax.fori_loop(0, tiles, project_tile, 0)
+    x_copy.wait()
+    proj = exact_ref[...]
+    inverse = lax.rsqrt(mean_square(proj) + EPSILON)
+    proj_ref[...] = proj.astype(bf16)
+    low_ref[...] = (x_ref[...].astype(f32) + proj * inverse * gain_ref[...]).astype(bf16)
+    outs = [
+        pltpu.make_async_copy(proj_ref, proj_hbm.at[here, :], out_sems.at[0]),
+        pltpu.make_async_copy(low_ref, low_hbm.at[here, :], out_sems.at[1]),
+        pltpu.make_async_copy(act_ref, act_hbm.at[here, :], out_sems.at[2]),
+        pltpu.make_async_copy(silu_ref, silu_hbm.at[here, :], out_sems.at[3]),
+        pltpu.make_async_copy(slope_ref, slope_hbm.at[here, :], out_sems.at[4]),
+    ]
+    outs[0].start()
+    outs[1].start()
+
+    def unit_tile(index, carry):
+        slot = lax.rem(index, 2)
+        for copy in unit_copies(index):
+            copy.wait()
         low = low_ref[...]
-        gate = nn(low, wg_ref[...])
-        up = nn(low, wu_ref[...])
+        gate = nn(low, gate_ref[slot])
+        up = nn(low, up_ref[slot])
+
+        @pl.when(index + 2 < unit_tiles)
+        def _():
+            for copy in unit_copies(index + 2):
+                copy.start()
+
+        @pl.when(index + 2 >= unit_tiles)
+        def _():
+            first = (index + 2 - unit_tiles) * half
+            for more in range(half):
+                down_copy(first + more).start()
+
         sigmoid = 1.0 / (1.0 + jnp.exp(-gate))
         silu = gate * sigmoid
-        act = (silu * up).astype(bf16)
-        act_ref[...] = act
-        held_ref[:, pl.ds(pl.multiple_of((step - first) * TILE, TILE), TILE)] = act
-        silu_ref[...] = silu.astype(bf16)
-        slope_ref[...] = (up * sigmoid * (1.0 + gate * (1.0 - sigmoid))).astype(bf16)
-
-    @pl.when(step >= second)
-    def _():
-        part_ref[...] = nt(held_ref[...], wd_ref[...]).astype(bf16)
+        columns = tile(index)
+        act_ref[:, columns] = (silu * up).astype(bf16)
+        silu_ref[:, columns] = silu.astype(bf16)
+        slope_ref[:, columns] = (up * sigmoid * (1.0 + gate * (1.0 - sigmoid))).astype(bf16)
+        return carry
+
+    lax.fori_loop(0, unit_tiles, unit_tile, 0)
+    for copy in outs[2:]:
+        copy.start()
+
+    def part_copy(index):
+        columns = tile(index)
+        return pltpu.make_async_copy(
+            part_ref.at[:, columns], part_hbm.at[:, columns], part_sems.at[index]
+        )
+
+    def down_tile(index, carry):
+        row_wait(index, units)
+        part_ref[:, tile(index)] = nt(act_ref[...], row_ref[index, :, :units]).astype(bf16)
+        part_copy(index).start()
+        return carry
+
+    lax.fori_loop(0, tiles, down_tile, 0)
+    for index in range(tiles):
+        part_copy(index).wait()
+    for copy in outs:
+        copy.wait()
 
 
 def forward_chunk(at, batch, part, rows, y_all, tokens, gain, w_out, w_mlp, kept):
@@ -780,47 +882,54 @@
     w_gate, w_rest = w_mlp
     units = w_gate.shape[2]
     total = tokens.shape[0] * tokens.shape[1]
-    tiles = D // LONG
-    unit_tiles = units // TILE
-    first = tiles
-    second = first + unit_tiles
-    half = first // 2
-    unit_tile = pl.BlockSpec((rows, TILE), lambda s: (at, clip(s, first, unit_tiles)))
+    tiles = D // TILE
+    anywhere = pl.BlockSpec(memory_space=pl.ANY)
     wide = jax.ShapeDtypeStruct((total, units), bf16)
     narrow = jax.ShapeDtypeStruct((total, D), bf16)
-    whole = pl.BlockSpec((rows, D), lambda s: (at, 0))
-
-    def weight(which):
-        return pl.BlockSpec((None, D, TILE), lambda s: (which, 0, clip(s, first, unit_tiles)))
-
+    dma = pltpu.SemaphoreType.DMA
     return chunk_call(
-        functools.partial(forward_chunk_kernel, first, second),
+        functools.partial(forward_chunk_kernel, (at, batch, part)),
         [
             (pl.BlockSpec(memory_space=pltpu.SMEM), core),
-            (pl.BlockSpec((rows, D), lambda s: (part, 0)), y_all),
-            (pl.BlockSpec((None, rows, D), lambda s: (batch, part, 0)), tokens),
-            (pl.BlockSpec((1, D), lambda s: (0, 0)), gain),
-            (pl.BlockSpec((LONG, D), lambda s: (clip(s, 0, half), 0)), w_out_a),
-            (pl.BlockSpec((LONG, D), lambda s: (clip(s, half, half), 0)), w_out_b),
-            (weight(0), w_gate),
-            (weight(0), w_rest),
-            (pl.BlockSpec((None, LONG, units), lambda s: (1, clip(s, second, tiles), 0)), w_rest),
+            (pl.BlockSpec(memory_space=pltpu.VMEM), gain),
+            (anywhere, y_all),
+            (anywhere, tokens),
+            (anywhere, w_out_a),
+            (anywhere, w_out_b),
+            (anywhere, w_gate),
+            (anywhere, w_rest),
         ],
         [
-            (whole, narrow, True),
-            (whole, narrow, True),
-            (unit_tile, wide, True),
-            (unit_tile, wide, True),
-            (unit_tile, wide, True),
-            (
-                pl.BlockSpec((rows, LONG), lambda s: (0, clip(s, second, tiles))),
-                jax.ShapeDtypeStruct((rows, D), bf16),
-                False,
-            ),
+            (anywhere, narrow, True),
+            (anywhere, narrow, True),
+            (anywhere, wide, True),
+            (anywhere, wide, True),
+            (anywhere, wide, True),
+            (anywhere, jax.ShapeDtypeStruct((rows, D), bf16), False),
         ],
         kept,
-        (second + tiles,),
-        [pltpu.VMEM((rows, D), f32), pltpu.VMEM((rows, units), bf16)],
+        (),
+        [
+            pltpu.VMEM((rows, D), bf16),
+            pltpu.VMEM((rows, D), bf16),
+            pltpu.VMEM((tiles, TILE, D), bf16),
+            pltpu.VMEM((2, D, TILE), bf16),
+            pltpu.VMEM((2, D, TILE), bf16),
+            pltpu.VMEM((rows, D), f32),
+            pltpu.VMEM((rows, D), bf16),
+            pltpu.VMEM((rows, D), bf16),
+            pltpu.VMEM((rows, units), bf16),
+            pltpu.VMEM((rows, units), bf16),
+            pltpu.VMEM((rows, units), bf16),
+            pltpu.VMEM((rows, D), bf16),
+            dma,
+            dma,
+            dma((tiles,)),
+            dma((2,)),
+            dma((2,)),
+            dma((5,)),
+            dma((tiles,)),
+        ],
         pl.CostEstimate(
             flops=2 * rows * D * (D + 3 * units),
             bytes_accessed=2 * D * (D + 3 * units) + 16 * rows * D,
@@ -831,58 +940,160 @@
 
 
 def middle_chunk_kernel(
-    first,
+    place,
+    attn_gain_ref,
+    gain_ref,
+    sum_hbm,
+    proj_hbm,
+    x_hbm,
+    grad_hbm,
+    silu_hbm,
+    slope_hbm,
+    wg_hbm,
+    wr_hbm,
+    output_hbm,
+    low_hbm,
+    gate_hbm,
+    up_hbm,
+    gain_part_ref,
+    part_hbm,
     sum_ref,
     proj_ref,
     x_ref,
     grad_ref,
-    attn_gain_ref,
-    gain_ref,
     silu_ref,
     slope_ref,
-    wd_ref,
+    down_ref,
     wg_ref,
     wu_ref,
     output_ref,
     low_ref,
-    gate_ref,
-    up_ref,
-    gain_part_ref,
-    part_ref,
     gates_ref,
     ups_ref,
+    part_ref,
+    in_sems,
+    down_sems,
+    wg_sems,
+    wu_sems,
+    out_sems,
+    part_sems,
 ):
-    step = pl.program_id(0)
-
-    @pl.when(step == 0)
-    def _():
-        proj = proj_ref[...].astype(f32)
-        inverse = lax.rsqrt(mean_square(proj) + EPSILON)
-        hidden = x_ref[...].astype(f32) + proj * inverse * attn_gain_ref[...]
-        mlp = sum_ref[...].astype(f32)
-        inverse = lax.rsqrt(mean_square(mlp) + EPSILON)
-        normed = mlp * inverse
-        grad = grad_ref[...]
-        output_ref[...] = (hidden + normed * gain_ref[...]).astype(bf16)
-        gain_part_ref[...] = jnp.sum(grad * normed, axis=0, keepdims=True)
-        low_ref[...] = norm_back(grad, normed, inverse, gain_ref[...]).astype(bf16)
-
-    @pl.when(step < first)
-    def _():
-        act_grad = nn(low_ref[...], wd_ref[...])
-        up_grad = (act_grad * silu_ref[...].astype(f32)).astype(bf16)
-        gate_grad = (act_grad * slope_ref[...].astype(f32)).astype(bf16)
-        columns = pl.ds(pl.multiple_of(step * TILE, TILE), TILE)
-        up_ref[...] = up_grad
-        ups_ref[:, columns] = up_grad
-        gate_ref[...] = gate_grad
-        gates_ref[:, columns] = gate_grad
-
-    @pl.when(step >= first)
-    def _():
-        part_ref[...] = (
-            nt(gates_ref[...], wg_ref[...]) + nt(ups_ref[...], wu_ref[...])
+    at, batch, part = place
+    rows = sum_ref.shape[0]
+    units = silu_ref.shape[1]
+    tiles = D // TILE
+    half = tiles // 2
+    unit_tiles = units // TILE
+    here = pl.ds(at * rows, rows)
+    inside = pl.ds(part * rows, rows)
+
+    def tile(index):
+        return pl.ds(pl.multiple_of(index * TILE, TILE), TILE)
+
+    def down_copy(index):
+        slot = lax.rem(index, 2)
+        return pltpu.make_async_copy(
+            wr_hbm.at[1, :, tile(index)], down_ref.at[slot], down_sems.at[slot]
+        )
+
+    def row_copies(index):
+        slot = lax.rem(index, half)
+        return (
+            pltpu.make_async_copy(wg_hbm.at[0, tile(index), :], wg_ref.at[slot], wg_sems.at[slot]),
+            pltpu.make_async_copy(wr_hbm.at[0, tile(index), :], wu_ref.at[slot], wu_sems.at[slot]),
+        )
+
+    ins = [
+        pltpu.make_async_copy(sum_hbm, sum_ref, in_sems.at[0]),
+        pltpu.make_async_copy(grad_hbm.at[batch, inside, :], grad_ref, in_sems.at[1]),
+        pltpu.make_async_copy(proj_hbm.at[here, :], proj_ref, in_sems.at[2]),
+        pltpu.make_async_copy(x_hbm.at[batch, inside, :], x_ref, in_sems.at[3]),
+        pltpu.make_async_copy(silu_hbm.at[here, :], silu_ref, in_sems.at[4]),
+        pltpu.make_async_copy(slope_hbm.at[here, :], slope_ref, in_sems.at[5]),
+    ]
+    ins[0].start()
+    ins[1].start()
+    down_copy(0).start()
+    ins[4].start()
+    ins[5].start()
+    down_copy(1).start()
+    ins[2].start()
+    ins[3].start()
+    ins[0].wait()
+    ins[1].wait()
+    mlp = sum_ref[...].astype(f32)
+    mlp_inverse = lax.rsqrt(mean_square(mlp) + EPSILON)
+    normed = mlp * mlp_inverse
+    grad = grad_ref[...]
+    gain_part_ref[...] = jnp.sum(grad * normed, axis=0, keepdims=True)
+    low_ref[...] = norm_back(grad, normed, mlp_inverse, gain_ref[...]).astype(bf16)
+    outs = [
+        pltpu.make_async_copy(output_ref, output_hbm.at[here, :], out_sems.at[0]),
+        pltpu.make_async_copy(low_ref, low_hbm.at[here, :], out_sems.at[1]),
+        pltpu.make_async_copy(gates_ref, gate_hbm.at[here, :], out_sems.at[2]),
+        pltpu.make_async_copy(ups_ref, up_hbm.at[here, :], out_sems.at[3]),
+    ]
+    outs[1].start()
+    ins[4].wait()
+    ins[5].wait()
+
+    def unit_tile(index, carry):
+        down_copy(index).wait()
+        act_grad = nn(low_ref[...], down_ref[lax.rem(index, 2)])
+
+        @pl.when(index + 2 < unit_tiles)
+        def _():
+            down_copy(index + 2).start()
+
+        @pl.when(index + 2 >= unit_tiles)
+        def _():
+            for copy in row_copies(index + 2 - unit_tiles):
+                copy.start()
+
+        columns = tile(index)
+        ups_ref[:, columns] = (act_grad * silu_ref[:, columns].astype(f32)).astype(bf16)
+        gates_ref[:, columns] = (act_grad * slope_ref[:, columns].astype(f32)).astype(bf16)
+        return carry
+
+    lax.fori_loop(0, unit_tiles, unit_tile, 0)
+    outs[2].start()
+    outs[3].start()
+    ins[2].wait()
+    ins[3].wait()
+    proj = proj_ref[...].astype(f32)
+    inverse = lax.rsqrt(mean_square(proj) + EPSILON)
+    hidden = x_ref[...].astype(f32) + proj * inverse * attn_gain_ref[...]
+    mlp = sum_ref[...].astype(f32)
+    output_ref[...] = (hidden + mlp * mlp_inverse * gain_ref[...]).astype(bf16)
+    outs[0].start()
+
+    def part_copy(index):
+        columns = tile(index)
+        return pltpu.make_async_copy(
+            part_ref.at[:, columns], part_hbm.at[:, columns], part_sems.at[index]
+        )
+
+    def row_tile(index, carry):
+        slot = lax.rem(index, half)
+        for copy in row_copies(index):
+            copy.wait()
+        part_ref[:, tile(index)] = (
+            nt(gates_ref[...], wg_ref[slot]) + nt(ups_ref[...], wu_ref[slot])
         ).astype(bf16)
+        part_copy(index).start()
+
+        @pl.when(index + half < tiles)
+        def _():
+            for copy in row_copies(index + half):
+                copy.start()
+
+        return carry
+
+    lax.fori_loop(0, tiles, row_tile, 0)
+    for index in range(tiles):
+        part_copy(index).wait()
+    for copy in outs:
+        copy.wait()
 
 
 def middle_chunk(
@@ -891,48 +1102,59 @@
     w_gate, w_rest = w_mlp
     units = w_gate.shape[2]
     total = proj.shape[0]
-    tiles = D // LONG
-    first = units // TILE
-    whole = pl.BlockSpec((rows, D), lambda s: (at, 0))
-    row_block = pl.BlockSpec((None, rows, D), lambda s: (batch, part, 0))
-    line = pl.BlockSpec((1, D), lambda s: (0, 0))
-    tile = pl.BlockSpec((rows, TILE), lambda s: (at, clip(s, 0, first)))
+    tiles = D // TILE
+    half = tiles // 2
+    vmem = pl.BlockSpec(memory_space=pltpu.VMEM)
+    anywhere = pl.BlockSpec(memory_space=pl.ANY)
     wide = jax.ShapeDtypeStruct((total, units), bf16)
     narrow = jax.ShapeDtypeStruct((total, D), bf16)
-
-    def weight(which):
-        return pl.BlockSpec((None, LONG, units), lambda s: (which, clip(s, first, tiles), 0))
-
+    dma = pltpu.SemaphoreType.DMA
     return chunk_call(
-        functools.partial(middle_chunk_kernel, first),
+        functools.partial(middle_chunk_kernel, (at, batch, part)),
         [
-            (pl.BlockSpec((rows, D), lambda s: (0, 0)), mlp_sum),
-            (whole, proj),
-            (row_block, tokens),
-            (row_block, grad),
-            (line, attn_gain),
-            (line, gain),
-            (tile, silu),
-            (tile, slope),
-            (pl.BlockSpec((None, D, TILE), lambda s: (1, 0, clip(s, 0, first))), w_rest),
-            (weight(0), w_gate),
-            (weight(0), w_rest),
+            (vmem, attn_gain),
+            (vmem, gain),
+            (anywhere, mlp_sum),
+            (anywhere, proj),
+            (anywhere, tokens),
+            (anywhere, grad),
+            (anywhere, silu),
+            (anywhere, slope),
+            (anywhere, w_gate),
+            (anywhere, w_rest),
         ],
         [
-            (whole, narrow, True),
-            (whole, narrow, True),
-            (tile, wide, True),
-            (tile, wide, True),
-            (line, jax.ShapeDtypeStruct((1, D), f32), False),
-            (
-                pl.BlockSpec((rows, LONG), lambda s: (0, clip(s, first, tiles))),
-                jax.ShapeDtypeStruct((rows, D), bf16),
-                False,
-            ),
+            (anywhere, narrow, True),
+            (anywhere, narrow, True),
+            (anywhere, wide, True),
+            (anywhere, wide, True),
+            (vmem, jax.ShapeDtypeStruct((1, D), f32), False),
+            (anywhere, jax.ShapeDtypeStruct((rows, D), bf16), False),
         ],
         kept,
-        (first + tiles,),
-        [pltpu.VMEM((rows, units), bf16), pltpu.VMEM((rows, units), bf16)],
+        (),
+        [
+            pltpu.VMEM((rows, D), bf16),
+            pltpu.VMEM((rows, D), bf16),
+            pltpu.VMEM((rows, D), bf16),
+            pltpu.VMEM((rows, D), f32),
+            pltpu.VMEM((rows, units), bf16),
+            pltpu.VMEM((rows, units), bf16),
+            pltpu.VMEM((2, D, TILE), bf16),
+            pltpu.VMEM((half, TILE, units), bf16),
+            pltpu.VMEM((half, TILE, units), bf16),
+            pltpu.VMEM((rows, D), bf16),
+            pltpu.VMEM((rows, D), bf16),
+            pltpu.VMEM((rows, units), bf16),
+            pltpu.VMEM((rows, units), bf16),
+            pltpu.VMEM((rows, D), bf16),
+            dma((6,)),
+            dma((2,)),
+            dma((half,)),
+            dma((half,)),
+            dma((4,)),
+            dma((tiles,)),
+        ],
         pl.CostEstimate(
             flops=2 * rows * D * 3 * units,
             bytes_accessed=2 * D * 3 * units + 24 * rows * D,
@@ -1091,7 +1313,7 @@
     gains = jnp.concatenate([query_gain, key_gain])[None, :]
     packed = pack_heads(q_raw, k_raw, v_raw, inverse, gains, cosines, sines, heads)
     w_out_begun = begin_output_weight(w_attn[3], packed, dp_index, dp_count, tp_count)
-    packed = follow(exchange(packed), w_out_begun[1]).reshape(dp_count, 3, SEG_DEV, BLK, HEAD)
+    packed = follow(exchange(packed), w_out_begun[1:]).reshape(dp_count, 3, SEG_DEV, BLK, HEAD)
     w_out = end_output_weight(w_out_begun, packed, dp_index, dp_count, tp_count)
     w_mlp = (w_gate_all, gather_stack(*follow((w_up, jnp.transpose(w_down)), packed)))
 
@@ -1102,11 +1324,12 @@
     parts = 2
     step = rows // parts
     spots = [(batch, part) for batch in range(MB) for part in range(parts)]
-    begun = []
-    everything = []
-    for batch in range(MB):
-        after = begun[-1][1][2:] if begun else None
-        begun.append(begin_all_gather(follow(attended[batch], after), tp_count))
+    begun = go_on_all_gather(begin_all_gather(attended[0], tp_count), tp_count)
+    gathered, hop = end_all_gather(begun, tp_count)
+    everything = [gathered]
+    begun = [begun]
+    for batch in range(1, MB):
+        begun.append(begin_all_gather(follow(attended[batch], hop), tp_count))
     sums = SumLine(tp_count)
     attn_gain_row = attn_gain[None, :]
     mlp_gain_row = mlp_gain[None, :]
@@ -1119,7 +1342,8 @@
         batch, part = spots[at]
         if batch == len(everything):
             early = sums.terms[0] if sums.terms else None
-            everything.append(end_all_gather(begun[batch], tp_count, early))
+            going = go_on_all_gather(begun[batch], tp_count)
+            everything.append(end_all_gather(going, tp_count, early)[0])
         *state["forward"], term = forward_chunk(
             at,
             batch,
@@ -1212,7 +1436,8 @@
     attended = attended.reshape(MB * rows, width)
     attn_total = weight_sum((3,), 4, proj_grad, follow(attended, attn_grad), width, None)
 
-    attn_grad = exchange(attn_grad).reshape(dp_count, SEG_DEV, BLK, HEAD)
+    attn_grad = follow(exchange(attn_grad), attn_total)
+    attn_grad = attn_grad.reshape(dp_count, SEG_DEV, BLK, HEAD)
     back = give_back(attend_backward(my_order, packed, attn_grad))
     back = back.reshape(heads, MB, 3, rows, HEAD)
     inner, gain_part = inner_sums(back, q_raw, k_raw, inverse, gains, cosines, sines, heads)
@@ -1225,13 +1450,13 @@
             batch, back, q_raw, k_raw, inverse, means, gains, cosines, sines, w_attn, heads, qkv_grad
         )
         terms.append(term)
+    mlp_weight_grads = [mlp_weight_grad[at].astype(f32) for at in range(3)]
+    mlp_weight_grads[2] = jnp.transpose(mlp_weight_grads[2])
+    parts, second_operands, last_operands = line_reduce_scatter(terms, tp_count, mlp_weight_grads)
     tokens = layer_input.reshape(MB * rows, D)
-    qkv_grad = follow(qkv_grad[0], mlp_weight_grad)
+    qkv_grad = follow(qkv_grad[0], (mlp_weight_grad, second_operands))
     attn_total = weight_sum((0, 1, 2), 4, tokens, qkv_grad, width, attn_total)
     attn_weight_grad = scatter_rows(attn_total[0], 1)
-    mlp_weight_grads = [mlp_weight_grad[at].astype(f32) for at in range(3)]
-    mlp_weight_grads[2] = jnp.transpose(mlp_weight_grads[2])
-    parts, last_operands = line_reduce_scatter(terms, tp_count, mlp_weight_grads)
     input_parts = [
         lax.dynamic_slice_in_dim(hidden_grad, batch * rows + tp_index * share, share, 0) + part
         for batch, part in enumerate(parts)

time: 988 us -> 937 us (0.948)
  Pallas kernels: 382 us -> 337 us
  blocking collectives: 111 us -> 71.7 us
  starting transfers between devices: 143 us -> 182 us
    pallas_call x19, Pallas kernels: 303 us -> 258 us  [chunk_call(): pl.pallas_call(body, grid=grid, in_specs=specs, out_specs=[out[0] for out...]
    all_to_all x1 -> x0, blocking collectives: 38.2 us -> none  [exchange(): return lax.all_to_all(flat, 'dp', split_axis=0, concat_axis=0, tiled=True)]
    all_to_all x1 -> x2, starting transfers between devices: 4.52 us -> 23.4 us  [exchange(): return lax.all_to_all(flat, 'dp', split_axis=0, concat_axis=0, tiled=True)]
    all_to_all x1 -> x2, waiting for transfers between devices: 0.01 us -> 18.5 us  [exchange(): return lax.all_to_all(flat, 'dp', split_axis=0, concat_axis=0, tiled=True)]
    ppermute x4, waiting for transfers between devices: 22.7 us -> 5.98 us  [line_reduce_scatter(): rights[at] = lax.ppermute(right, 'tensor', to_right)]
    ppermute x4, starting transfers between devices: 17.6 us -> 31.8 us  [line_reduce_scatter(): rights[at] = lax.ppermute(right, 'tensor', to_right)]
    ppermute x8, starting transfers between devices: 38.3 us -> 50.7 us  [enter(): self.inward.append(lax.ppermute(term, 'tensor', [(0, 1), (3, 2)]))]
  transfers between devices with their start and end apart: 69 -> 70, of which waited for: 23 -> 23; matrix products, arithmetic and copies ran while one was open for 8% -> 8% of each run, Pallas kernels for 35% -> 32%
where the time goes in v3:
time: 937 us; the launch traced here: 927 us
  Pallas kernels  337 us (36%)
  waiting for transfers between devices  230 us (25%)
  starting transfers between devices  182 us (19%)
  blocking collectives  71.7 us (8%)
  other arithmetic  58.1 us (6%)
  local copies, waits for them, and re-layouts  32.8 us (4%)
  between operations  15.4 us (2%)
    pallas_call x19, Pallas kernels, chunk_call(): pl.pallas_call(body, grid=grid, in_specs=specs, out_specs=[out[0] for out...  258 us
    all_to_all x1, blocking collectives, give_back(): lax.all_to_all(flat, 'dp', split_axis=0, concat_axis=0, tiled=True)[:items]  71.7 us
    all_gather x3, waiting for transfers between devices, gather_stack(): return lax.all_gather(jnp.stack(pieces), 'dp', axis=1, tiled=True)  52.5 us
    ppermute x8, starting transfers between devices, enter(): self.inward.append(lax.ppermute(term, 'tensor', [(0, 1), (3, 2)]))  50.7 us
    ppermute x3, waiting for transfers between devices, go_on_all_gather(): left = lax.ppermute(first[1], 'tensor', [(2, 1), (1, 0)])  37.4 us
    ppermute x4, starting transfers between devices, line_reduce_scatter(): rights[at] = lax.ppermute(right, 'tensor', to_right)  31.8 us
    pallas_call x1, Pallas kernels, attend_backward(): pl.pallas_call(functools.partial(backward_kernel, trees), in_specs=[pl.Bl...  30 us
    convert_element_type x22, other arithmetic, low_sum(): return total.astype(bf16)  26.4 us
  transfers between devices with their start and end apart: 70, of which 23 were waited for; matrix products, arithmetic and copies ran while one was open for 8% of the time, Pallas kernels for 32%

profile of v3, /device:TPU:0, one launch (start us, length us, event | category | flops | bytes accessed | tf_op | source)
XLA Modules:
  0.0 927.2 jit_solution(13124590645827508988)
XLA Ops:
  15.4 52.4 %all-gather.5.cloned.1.call-done.refs_0_.refs_1_.refs_4_.refs_8_.refs_9_.refs_10_ = bf16[4,2048,512]{2,1,0:T(8,128)(2,1)} async-done(((bf16[4,256,512]{2,1,0:T(8,128)(2,1)}), bf16[4,2048,512]{2,1,0:T(8,128)(2,1)}) %all-gather.5.cloned.1.call-update) | async-done | bytes 8388624 | tf_op jit(solution)/shard_map/all_gather | solution.py:1282
  67.8 9.8 %project.2 = (f32[2,640,512]{2,1,0:T(8,128)S(1)}, f32[2,640,512]{2,1,0:T(8,128)}, f32[2,640,2]{2,1,0:T(8,128)S(1)}) custom-call(bf16[2,640,2048]{2,1,0:T(8,128)(2,1)} %refs_4_.7, bf16[4,2048,512]{2,1,0:T(8,128)(2,1)} %all-gather.5.cloned.1.call-done.refs_0_.refs_1_.refs_4_.refs_8_.refs_9_.refs_10_, ...), custom_call_target="tpu_custom_call" | custom-call | flops 5368709120 | bytes 9437184 | tf_op jit(solution)/shard_map/project/pallas_call | solution.py:262
  93.8 8.8 pack_heads.1
  118.3 20.6 %collective-permute-done.2 = bf16[1024,512]{1,0:T(8,128)(2,1)} collective-permute-done((bf16[1024,512]{1,0:T(8,128)(2,1)S(1)}, bf16[1024,512]{1,0:T(8,128)(2,1)}, u32[]{:S(2)}, u32[]{:S(2)}) %collective-permute-start.2) | collective-permute-done | bytes 1048608 | tf_op jit(solution)/shard_map/ppermute | solution.py:179
  145.9 24.4 %collective-permute-done.5 = bf16[1024,512]{1,0:T(8,128)(2,1)} collective-permute-done((bf16[1024,512]{1,0:T(8,128)(2,1)S(1)}, bf16[1024,512]{1,0:T(8,128)(2,1)}, u32[]{:S(2)}, u32[]{:S(2)}) %collective-permute-start.5) | collective-permute-done | bytes 1048608 | tf_op jit(solution)/shard_map/ppermute | solution.py:189
  178.2 17.1 %attend_forward.1 = bf16[8,5,128,128]{3,2,1,0:T(8,128)(2,1)} custom-call(s32[40]{0:T(128)S(1)} %fusion.23.order_ref, bf16[8,3,5,128,128]{4,3,2,1,0:T(8,128)(2,1)} %bitcast.17.x_ref), custom_call_target="tpu_custom_call" | custom-call | flops 2883584000 | bytes 5898240 | tf_op jit(solution)/shard_map/attend_forward/pallas_call | solution.py:539
  205.9 14.9 %all-to-all-done.1 = bf16[8,640,128]{2,1,0:T(8,128)(2,1)S(1)} async-done(((bf16[8,640,128]{2,1,0:T(8,128)(2,1)}), bf16[8,640,128]{2,1,0:T(8,128)(2,1)S(1)}, u32[]{:S(2)}, u32[]{:S(2)}) %all-to-all-start.1) | async-done | bytes 1310752 | tf_op jit(solution)/shard_map/all_to_all | solution.py:1297
  227.8 9.8 %collective-permute-done.9 = bf16[640,512]{1,0:T(8,128)(2,1)S(1)} collective-permute-done((bf16[640,512]{1,0:T(8,128)(2,1)S(1)}, bf16[640,512]{1,0:T(8,128)(2,1)S(1)}, u32[]{:S(2)}, u32[]{:S(2)}) %collective-permute-start.9) | collective-permute-done | bytes 655392 | tf_op jit(solution)/shard_map/ppermute | solution.py:180
  240.5 13.0 %collective-permute-done.10 = bf16[640,512]{1,0:T(8,128)(2,1)S(1)} collective-permute-done((bf16[640,512]{1,0:T(8,128)(2,1)S(1)}, bf16[640,512]{1,0:T(8,128)(2,1)S(1)}, u32[]{:S(2)}, u32[]{:S(2)}) %collective-permute-start.10) | collective-permute-done | bytes 655392 | tf_op jit(solution)/shard_map/ppermute | solution.py:189
  257.4 10.4 %collective-permute-done.11 = bf16[640,512]{1,0:T(8,128)(2,1)} collective-permute-done((bf16[640,512]{1,0:T(8,128)(2,1)S(1)}, bf16[640,512]{1,0:T(8,128)(2,1)}, u32[]{:S(2)}, u32[]{:S(2)}) %collective-permute-start.11) | collective-permute-done | bytes 655392 | tf_op jit(solution)/shard_map/ppermute | solution.py:201
  287.3 18.7 %forward_chunk.4 = (bf16[1280,2048]{1,0:T(8,128)(2,1)}, bf16[1280,2048]{1,0:T(8,128)(2,1)}, bf16[1280,2048]{1,0:T(8,128)(2,1)}, bf16[1280,2048]{1,0:T(8,128)(2,1...) custom-call(s32[1]{0:T(128)} %bitcast.2.refs_0_, f32[1,2048]{1,0:T(1,128)S(1)} %bitcast.169, ...), custom_call_target="tpu_custom_call" | custom-call | flops 10737418240 | bytes 44040192 | tf_op jit(solution)/shard_map/forward_chunk/pallas_call | solution.py:703
  315.7 18.2 %forward_chunk.5 = (bf16[1280,2048]{1,0:T(8,128)(2,1)}, bf16[1280,2048]{1,0:T(8,128)(2,1)}, bf16[1280,2048]{1,0:T(8,128)(2,1)}, bf16[1280,2048]{1,0:T(8,128)(2,1...) custom-call(s32[1]{0:T(128)} %bitcast.2.refs_0_, ...), custom_call_target="tpu_custom_call", output_to_operand_aliasing={{0}: (8, {}), {1}: (9, {}), {2}: (10, {}), {3}: (11, {}), {... | custom-call | flops 10737418240 | bytes 44040192 | tf_op jit(solution)/shard_map/forward_chunk/pallas_call | solution.py:703
  341.9 18.2 %forward_chunk.6 = (bf16[1280,2048]{1,0:T(8,128)(2,1)}, bf16[1280,2048]{1,0:T(8,128)(2,1)}, bf16[1280,2048]{1,0:T(8,128)(2,1)}, bf16[1280,2048]{1,0:T(8,128)(2,1...) custom-call(s32[1]{0:T(128)} %bitcast.2.refs_0_, ...), custom_call_target="tpu_custom_call", output_to_operand_aliasing={{0}: (8, {}), {1}: (9, {}), {2}: (10, {}), {3}: (11, {}), {... | custom-call | flops 10737418240 | bytes 44040192 | tf_op jit(solution)/shard_map/forward_chunk/pallas_call | solution.py:703
  371.6 18.2 %forward_chunk.7 = (bf16[1280,2048]{1,0:T(8,128)(2,1)}, bf16[1280,2048]{1,0:T(8,128)(2,1)}, bf16[1280,2048]{1,0:T(8,128)(2,1)}, bf16[1280,2048]{1,0:T(8,128)(2,1...) custom-call(s32[1]{0:T(128)} %bitcast.2.refs_0_, ...), custom_call_target="tpu_custom_call", output_to_operand_aliasing={{0}: (8, {}), {1}: (9, {}), {2}: (10, {}), {3}: (11, {}), {... | custom-call | flops 10737418240 | bytes 44040192 | tf_op jit(solution)/shard_map/forward_chunk/pallas_call | solution.py:703
  404.7 17.1 %middle_chunk.4 = (bf16[1280,2048]{1,0:T(8,128)(2,1)}, bf16[1280,2048]{1,0:T(8,128)(2,1)}, bf16[1280,2048]{1,0:T(8,128)(2,1)}, bf16[1280,2048]{1,0:T(8,128)(2,1)...) custom-call(f32[1,2048]{1,0:T(1,128)S(1)} %bitcast.173, f32[1,2048]{1,0:T(1,128)S(1)} %bitcast.182, ...), custom_call_target="tpu_custom_call" | custom-call | flops 8053063680 | bytes 40894464 | tf_op jit(solution)/shard_map/middle_chunk/pallas_call | solution.py:703
  433.8 16.8 %middle_chunk.5 = (bf16[1280,2048]{1,0:T(8,128)(2,1)}, bf16[1280,2048]{1,0:T(8,128)(2,1)}, bf16[1280,2048]{1,0:T(8,128)(2,1)}, bf16[1280,2048]{1,0:T(8,128)(2,1)...) custom-call(f32[1,2048]{1,0:T(1,128)S(1)} %bitcast.174, ...), custom_call_target="tpu_custom_call", output_to_operand_aliasing={{0}: (10, {}), {1}: (11, {}), {2}: (12, {}), {3}: (13, {})} | custom-call | flops 8053063680 | bytes 40894464 | tf_op jit(solution)/shard_map/middle_chunk/pallas_call | solution.py:703
  463.2 16.8 %middle_chunk.6 = (bf16[1280,2048]{1,0:T(8,128)(2,1)}, bf16[1280,2048]{1,0:T(8,128)(2,1)}, bf16[1280,2048]{1,0:T(8,128)(2,1)}, bf16[1280,2048]{1,0:T(8,128)(2,1)...) custom-call(f32[1,2048]{1,0:T(1,128)S(1)} %bitcast.175, ...), custom_call_target="tpu_custom_call", output_to_operand_aliasing={{0}: (10, {}), {1}: (11, {}), {2}: (12, {}), {3}: (13, {})} | custom-call | flops 8053063680 | bytes 40894464 | tf_op jit(solution)/shard_map/middle_chunk/pallas_call | solution.py:703
  491.9 16.8 %middle_chunk.7 = (bf16[1280,2048]{1,0:T(8,128)(2,1)}, bf16[1280,2048]{1,0:T(8,128)(2,1)}, bf16[1280,2048]{1,0:T(8,128)(2,1)}, bf16[1280,2048]{1,0:T(8,128)(2,1)...) custom-call(f32[1,2048]{1,0:T(1,128)S(1)} %bitcast.176, ...), custom_call_target="tpu_custom_call", output_to_operand_aliasing={{0}: (10, {}), {1}: (11, {}), {2}: (12, {}), {3}: (13, {})} | custom-call | flops 8053063680 | bytes 40894464 | tf_op jit(solution)/shard_map/middle_chunk/pallas_call | solution.py:703
  524.1 15.9 %weight_sum.5.refs_2_ = bf16[3,2048,2048]{2,1,0:T(8,128)(2,1)} custom-call(bf16[1280,2048]{1,0:T(8,128)(2,1)} %get-tuple-element.227.refs_0_, bf16[1280,2048]{1,0:T(8,128)(2,1)} %get-tuple-element.218.refs_1_), custom_call_target="tpu_custom_call" | custom-call | flops 10737418240 | bytes 18874368 | tf_op jit(solution)/shard_map/weight_sum/pallas_call | solution.py:703
  549.7 15.9 %weight_sum.6.refs_2_ = bf16[3,2048,2048]{2,1,0:T(8,128)(2,1)} custom-call(bf16[1280,2048]{1,0:T(8,128)(2,1)} %get-tuple-element.227.refs_0_, bf16[1280,2048]{1,0:T(8,128)(2,1)} %get-tuple-element.228.refs_1_, bf16[3,2048,2048]{2,1,0:T(8,128)(2,1)} %weight_sum.5.refs_2_), custom_call_target="tpu_custom_call", output_to_operand_aliasing={{}: (2, {})} | custom-call | flops 10737418240 | bytes 18874368 | tf_op jit(solution)/shard_map/weight_sum/pallas_call | solution.py:703
  572.6 15.9 %weight_sum.7 = bf16[3,2048,2048]{2,1,0:T(8,128)(2,1)} custom-call(bf16[1280,2048]{1,0:T(8,128)(2,1)} %get-tuple-element.237.refs_0_, bf16[1280,2048]{1,0:T(8,128)(2,1)} %get-tuple-element.238.refs_1_, bf16[3,2048,2048]{2,1,0:T(8,128)(2,1)} %weight_sum.6.refs_2_), custom_call_target="tpu_custom_call", output_to_operand_aliasing={{}: (2, {})} | custom-call | flops 10737418240 | bytes 18874368 | tf_op jit(solution)/shard_map/weight_sum/pallas_call | solution.py:703
  589.8 22.1 %collective-permute-done.44 = bf16[320,2048]{1,0:T(8,128)(2,1)S(1)} collective-permute-done((bf16[320,2048]{1,0:T(8,128)(2,1)S(1)}, bf16[320,2048]{1,0:T(8,128)(2,1)S(1)}, u32[]{:S(2)}, u32[]{:S(2)}) %collective-permute-start.44) | collective-permute-done | bytes 1310752 | tf_op jit(solution)/shard_map/ppermute | solution.py:131
  612.0 8.1 backward_chunk.7
  620.1 18.9 %all-to-all-start.2 = ((bf16[8,640,128]{2,1,0:T(8,128)(2,1)}), bf16[8,640,128]{2,1,0:T(8,128)(2,1)S(1)}, u32[]{:S(2)}, u32[]{:S(2)}) async-start(bf16[8,640,128]{2,1,0:T(8,128)(2,1)} %bitcast.27), calls=%async_computation.2 | async-start | bytes 2621440 | tf_op jit(solution)/shard_map/all_to_all | solution.py:1293
  646.7 18.5 %all-to-all-done.2 = bf16[8,640,128]{2,1,0:T(8,128)(2,1)S(1)} async-done(((bf16[8,640,128]{2,1,0:T(8,128)(2,1)}), bf16[8,640,128]{2,1,0:T(8,128)(2,1)S(1)}, u32[]{:S(2)}, u32[]{:S(2)}) %all-to-all-start.2) | async-done | bytes 1310752 | tf_op jit(solution)/shard_map/all_to_all | solution.py:1293
  665.2 30.0 %attend_backward.1 = bf16[8,3,5,128,128]{4,3,2,1,0:T(8,128)(2,1)} custom-call(s32[40]{0:T(128)S(1)} %copy-done.12, bf16[8,3,5,128,128]{4,3,2,1,0:T(8,128)(2,1)} %bitcast.17.x_ref, bf16[8,5,128,128]{3,2,1,0:T(8,128)(2,1)S(1)} %bitcast.168), custom_call_target="tpu_custom_call" | custom-call | flops 7208960000 | bytes 9830400 | tf_op jit(solution)/shard_map/attend_backward/pallas_call | solution.py:652
  695.2 71.7 %all_to_all.20 = bf16[8,1920,128]{2,1,0:T(8,128)(2,1)} all-to-all(bf16[8,1920,128]{2,1,0:T(8,128)(2,1)} %bitcast.218), channel_id=1, replica_groups=mesh['dp'=8,'tensor'=4] {'dp'}, dimensions={0} | all-to-all | bytes 7864320 | tf_op jit(solution)/shard_map/all_to_all | solution.py:1297
  784.4 10.2 %unpack_heads.2 = (bf16[1280,1536]{1,0:T(8,128)(2,1)}, bf16[640,2048]{1,0:T(8,128)(2,1)}) custom-call(bf16[4,2,3,640,128]{4,3,2,1,0:T(8,128)(2,1)} %bitcast.200, f32[2,640,512]{2,1,0:T(8,128)} %copy-done, f32[2,640,512]{2,1,0:T(8,128)} %get-tuple-element.140.k_ref.refs_2_, f32[2,640,2]{2,1,0:T(8,128)S(1)} %bitcast.163, f32[2,640,2]{2,1,0:T(8,128)S(1)} %bitcast.165, ...), custom_call_target="tpu_custom_call" | custom-call | flops 4026531840 | bytes 10485760 | tf_op jit(solution)/shard_map/unpack_heads/pallas_call | solution.py:703
  799.7 10.2 %unpack_heads.3 = (bf16[1280,1536]{1,0:T(8,128)(2,1)}, bf16[640,2048]{1,0:T(8,128)(2,1)}) custom-call(bf16[4,2,3,640,128]{4,3,2,1,0:T(8,128)(2,1)} %bitcast.201, f32[2,640,512]{2,1,0:T(8,128)} %copy-done, f32[2,640,512]{2,1,0:T(8,128)} %get-tuple-element.140.k_ref.refs_2_, f32[2,640,2]{2,1,0:T(8,128)S(1)} %bitcast.164, ...), custom_call_target="tpu_custom_call", output_to_operand_aliasing={{0}: (11, {})} | custom-call | flops 4026531840 | bytes 10485760 | tf_op jit(solution)/shard_map/unpack_heads/pallas_call | solution.py:703
  814.1 16.3 %weight_sum.9 = bf16[4,2048,512]{2,1,0:T(8,128)(2,1)} custom-call(bf16[1280,2048]{1,0:T(8,128)(2,1)} %bitcast.198, bf16[1280,1536]{1,0:T(8,128)(2,1)S(1)} %copy-done.7, bf16[4,2048,512]{2,1,0:T(8,128)(2,1)} %weight_sum.8.refs_2_), custom_call_target="tpu_custom_call", output_to_operand_aliasing={{}: (2, {})} | custom-call | flops 8053063680 | bytes 25952256 | tf_op jit(solution)/shard_map/weight_sum/pallas_call | solution.py:703
  842.7 10.7 %collective-permute-done.53 = bf16[160,2048]{1,0:T(8,128)(2,1)} collective-permute-done((bf16[160,2048]{1,0:T(8,128)(2,1)}, bf16[160,2048]{1,0:T(8,128)(2,1)}, u32[]{:S(2)}, u32[]{:S(2)}) %collective-permute-start.53) | collective-permute-done | bytes 655392 | tf_op jit(solution)/shard_map/ppermute | solution.py:166
  856.4 19.3 %collective-permute-start.54 = (bf16[160,2048]{1,0:T(8,128)(2,1)S(1)}, bf16[160,2048]{1,0:T(8,128)(2,1)S(1)}, u32[]{:S(2)}, u32[]{:S(2)}) collective-permute-start(bf16[160,2048]{1,0:T(8,128)(2,1)S(1)} %get-tuple-element.331), channel_id=1, source_target_pairs={{0,1},{1,2},{4,5},{5,6},{8,9},{9,10},{12,13},{13,14},{16,17},{17,1... | collective-permute-start | bytes 1966088 | tf_op jit(solution)/shard_map/ppermute | solution.py:163
  (296 shorter events, 306.1 us)
Async XLA Ops:
  7.2 60.6 %all-gather.5.cloned.1.call-start = ((), (), s32[]{:S(2)}) async-start(), calls=%async_computation.6 | async-start | bytes 9437184 | tf_op jit(solution)/shard_map/all_gather | solution.py:1282
  10.6 274.9 %all-gather.9.cloned.1.call-start = ((), (), s32[]{:S(2)}) async-start(), calls=%async_computation.10 | async-start | bytes 9437184 | tf_op jit(solution)/shard_map/all_gather | solution.py:1282
  102.6 67.7 %all-to-all-start = ((bf16[8,1920,128]{2,1,0:T(8,128)(2,1)}), bf16[8,1920,128]{2,1,0:T(8,128)(2,1)}, u32[]{:S(2)}, u32[]{:S(2)}) async-start(bf16[8,1920,128]{2,1,0:T(8,128)(2,1)} %bitcast.203), calls=%async_computation | async-start | bytes 7864320 | tf_op jit(solution)/shard_map/all_to_all | solution.py:1293
  107.1 178.4 %all-gather.7.cloned.1.call-start = ((), (), s32[]{:S(2)}) async-start(), calls=%async_computation.7 | async-start | bytes 18874368 | tf_op jit(solution)/shard_map/all_gather | solution.py:1282
  176.0 28.7 %collective-permute-start.17 = (bf16[1024,512]{1,0:T(8,128)(2,1)}, bf16[1024,512]{1,0:T(8,128)(2,1)}, u32[]{:S(2)}, u32[]{:S(2)}) collective-permute-start(bf16[1024,512]{1,0:T(8,128)(2,1)} %collective-permute-done.4), channel_id=1, source_target_pairs={{2,3},{6,7},{10,11},{14,15},{18,19},{22,23},{26,27},{30,31}} | collective-permute-start | bytes 3145736 | tf_op jit(solution)/shard_map/ppermute | solution.py:200
  198.9 613.0 %reduce-scatter.3.cloned.1.call-start = ((), (), s32[]{:S(2)}) async-start(), calls=%async_computation.8 | async-start | bytes 28311552 | tf_op jit(solution)/shard_map/reduce_scatter | solution.py:1285
  205.9 79.6 %collective-permute-start.18 = (bf16[1024,2048]{1,0:T(8,128)(2,1)}, bf16[1024,2048]{1,0:T(8,128)(2,1)}, u32[]{:S(2)}, u32[]{:S(2)}) collective-permute-start(bf16[1024,2048]{1,0:T(8,128)(2,1)} %select_dynamic-update-slice_fusion.refs_4_), channel_id=1, source_target_pairs={{0,4},{4,0},{8,12},{12,8},{16,20},{20,16},{24,28},{28,24},{1,5},{5... | collective-permute-start | bytes 12582920 | tf_op jit(solution)/shard_map/ppermute | solution.py:229
  278.2 35.4 %collective-permute-start.13 = (bf16[640,512]{1,0:T(8,128)(2,1)}, bf16[640,512]{1,0:T(8,128)(2,1)}, u32[]{:S(2)}, u32[]{:S(2)}) collective-permute-start(bf16[640,512]{1,0:T(8,128)(2,1)} %collective-permute-done.12), channel_id=1, source_target_pairs={{1,2},{2,3},{5,6},{6,7},{9,10},{10,11},{13,14},{14,15},{17,18},{18... | collective-permute-start | bytes 1966088 | tf_op jit(solution)/shard_map/ppermute | solution.py:188
  284.0 29.6 %collective-permute-start.15 = (bf16[640,512]{1,0:T(8,128)(2,1)S(1)}, bf16[640,512]{1,0:T(8,128)(2,1)}, u32[]{:S(2)}, u32[]{:S(2)}) collective-permute-start(bf16[640,512]{1,0:T(8,128)(2,1)S(1)} %collective-permute-done.14), channel_id=1, source_target_pairs={{2,1},{1,0},{6,5},{5,4},{10,9},{9,8},{14,13},{13,12},{18,17},{17,1... | collective-permute-start | bytes 1966088 | tf_op jit(solution)/shard_map/ppermute | solution.py:189
  306.0 34.4 %collective-permute-start.21 = (bf16[320,2048]{1,0:T(8,128)(2,1)S(1)}, bf16[320,2048]{1,0:T(8,128)(2,1)S(1)}, u32[]{:S(2)}, u32[]{:S(2)}) collective-permute-start(bf16[320,2048]{1,0:T(8,128)(2,1)S(1)} %get-tuple-element.158), channel_id=1, source_target_pairs={{0,1},{3,2},{4,5},{7,6},{8,9},{11,10},{12,13},{15,14},{16,17},{19,... | collective-permute-start | bytes 3932168 | tf_op jit(solution)/shard_map/ppermute | solution.py:107
  333.8 33.6 %collective-permute-start.22 = (bf16[320,2048]{1,0:T(8,128)(2,1)S(1)}, bf16[320,2048]{1,0:T(8,128)(2,1)S(1)}, u32[]{:S(2)}, u32[]{:S(2)}) collective-permute-start(bf16[320,2048]{1,0:T(8,128)(2,1)S(1)} %get-tuple-element.166), channel_id=1, source_target_pairs={{0,1},{3,2},{4,5},{7,6},{8,9},{11,10},{12,13},{15,14},{16,17},{19,... | collective-permute-start | bytes 3932168 | tf_op jit(solution)/shard_map/ppermute | solution.py:107
  340.9 28.8 %collective-permute-start.23 = (bf16[320,2048]{1,0:T(8,128)(2,1)S(1)}, bf16[320,2048]{1,0:T(8,128)(2,1)S(1)}, u32[]{:S(2)}, u32[]{:S(2)}) collective-permute-start(bf16[320,2048]{1,0:T(8,128)(2,1)S(1)} %add_convert_fusion.15), channel_id=1, source_target_pairs={{1,2},{2,1},{5,6},{6,5},{9,10},{10,9},{13,14},{14,13},{17,18},{18,... | collective-permute-start | bytes 3932168 | tf_op jit(solution)/shard_map/ppermute | solution.py:129
  360.1 37.5 %collective-permute-start.25 = (bf16[320,2048]{1,0:T(8,128)(2,1)S(1)}, bf16[320,2048]{1,0:T(8,128)(2,1)}, u32[]{:S(2)}, u32[]{:S(2)}) collective-permute-start(bf16[320,2048]{1,0:T(8,128)(2,1)S(1)} %get-tuple-element.176), channel_id=1, source_target_pairs={{0,1},{3,2},{4,5},{7,6},{8,9},{11,10},{12,13},{15,14},{16,17},{19,... | collective-permute-start | bytes 3932168 | tf_op jit(solution)/shard_map/ppermute | solution.py:107
  368.0 33.2 %collective-permute-start.26 = (bf16[320,2048]{1,0:T(8,128)(2,1)S(1)}, bf16[320,2048]{1,0:T(8,128)(2,1)}, u32[]{:S(2)}, u32[]{:S(2)}) collective-permute-start(bf16[320,2048]{1,0:T(8,128)(2,1)S(1)} %add_convert_fusion.14), channel_id=1, source_target_pairs={{1,2},{2,1},{5,6},{6,5},{9,10},{10,9},{13,14},{14,13},{17,18},{18,... | collective-permute-start | bytes 3932168 | tf_op jit(solution)/shard_map/ppermute | solution.py:129
  370.3 34.3 %collective-permute-start.24 = (bf16[320,2048]{1,0:T(8,128)(2,1)S(1)}, bf16[320,2048]{1,0:T(8,128)(2,1)S(1)}, u32[]{:S(2)}, u32[]{:S(2)}) collective-permute-start(bf16[320,2048]{1,0:T(8,128)(2,1)S(1)} %add_convert_fusion.13), channel_id=1, source_target_pairs={{1,0},{2,3},{5,4},{6,7},{9,8},{10,11},{13,12},{14,15},{17,16},{18,... | collective-permute-start | bytes 3932168 | tf_op jit(solution)/shard_map/ppermute | solution.py:131
  389.7 42.2 %collective-permute-start.27 = (bf16[320,2048]{1,0:T(8,128)(2,1)S(1)}, bf16[320,2048]{1,0:T(8,128)(2,1)S(1)}, u32[]{:S(2)}, u32[]{:S(2)}) collective-permute-start(bf16[320,2048]{1,0:T(8,128)(2,1)S(1)} %get-tuple-element.183), channel_id=1, source_target_pairs={{0,1},{3,2},{4,5},{7,6},{8,9},{11,10},{12,13},{15,14},{16,17},{19,... | collective-permute-start | bytes 3932168 | tf_op jit(solution)/shard_map/ppermute | solution.py:107
  399.4 29.4 %collective-permute-start.29 = (bf16[320,2048]{1,0:T(8,128)(2,1)S(1)}, bf16[320,2048]{1,0:T(8,128)(2,1)}, u32[]{:S(2)}, u32[]{:S(2)}) collective-permute-start(bf16[320,2048]{1,0:T(8,128)(2,1)S(1)} %add_convert_fusion.12), channel_id=1, source_target_pairs={{1,2},{2,1},{5,6},{6,5},{9,10},{10,9},{13,14},{14,13},{17,18},{18,... | collective-permute-start | bytes 3932168 | tf_op jit(solution)/shard_map/ppermute | solution.py:129
  403.0 30.6 %collective-permute-start.28 = (bf16[320,2048]{1,0:T(8,128)(2,1)S(1)}, bf16[320,2048]{1,0:T(8,128)(2,1)S(1)}, u32[]{:S(2)}, u32[]{:S(2)}) collective-permute-start(bf16[320,2048]{1,0:T(8,128)(2,1)S(1)} %add_convert_fusion.11), channel_id=1, source_target_pairs={{1,0},{2,3},{5,4},{6,7},{9,8},{10,11},{13,12},{14,15},{17,16},{18,... | collective-permute-start | bytes 3932168 | tf_op jit(solution)/shard_map/ppermute | solution.py:131
  421.9 35.6 %collective-permute-start.32 = (bf16[320,2048]{1,0:T(8,128)(2,1)S(1)}, bf16[320,2048]{1,0:T(8,128)(2,1)}, u32[]{:S(2)}, u32[]{:S(2)}) collective-permute-start(bf16[320,2048]{1,0:T(8,128)(2,1)S(1)} %get-tuple-element.194), channel_id=1, source_target_pairs={{0,1},{3,2},{4,5},{7,6},{8,9},{11,10},{12,13},{15,14},{16,17},{19,... | collective-permute-start | bytes 3932168 | tf_op jit(solution)/shard_map/ppermute | solution.py:107
  430.6 32.5 %collective-permute-start.31 = (bf16[320,2048]{1,0:T(8,128)(2,1)S(1)}, bf16[320,2048]{1,0:T(8,128)(2,1)S(1)}, u32[]{:S(2)}, u32[]{:S(2)}) collective-permute-start(bf16[320,2048]{1,0:T(8,128)(2,1)S(1)} %add_convert_fusion.9), channel_id=1, source_target_pairs={{1,0},{2,3},{5,4},{6,7},{9,8},{10,11},{13,12},{14,15},{17,16},{18,... | collective-permute-start | bytes 3932168 | tf_op jit(solution)/shard_map/ppermute | solution.py:131
  432.4 28.7 %collective-permute-start.30 = (bf16[320,2048]{1,0:T(8,128)(2,1)S(1)}, bf16[320,2048]{1,0:T(8,128)(2,1)S(1)}, u32[]{:S(2)}, u32[]{:S(2)}) collective-permute-start(bf16[320,2048]{1,0:T(8,128)(2,1)S(1)} %add_convert_fusion.10), channel_id=1, source_target_pairs={{1,2},{2,1},{5,6},{6,5},{9,10},{10,9},{13,14},{14,13},{17,18},{18,... | collective-permute-start | bytes 3932168 | tf_op jit(solution)/shard_map/ppermute | solution.py:129
  450.6 34.2 %collective-permute-start.34 = (bf16[320,2048]{1,0:T(8,128)(2,1)S(1)}, bf16[320,2048]{1,0:T(8,128)(2,1)}, u32[]{:S(2)}, u32[]{:S(2)}) collective-permute-start(bf16[320,2048]{1,0:T(8,128)(2,1)S(1)} %get-tuple-element.202), channel_id=1, source_target_pairs={{0,1},{3,2},{4,5},{7,6},{8,9},{11,10},{12,13},{15,14},{16,17},{19,... | collective-permute-start | bytes 3932168 | tf_op jit(solution)/shard_map/ppermute | solution.py:107
  459.3 29.0 %collective-permute-start.35 = (bf16[320,2048]{1,0:T(8,128)(2,1)S(1)}, bf16[320,2048]{1,0:T(8,128)(2,1)}, u32[]{:S(2)}, u32[]{:S(2)}) collective-permute-start(bf16[320,2048]{1,0:T(8,128)(2,1)S(1)} %add_convert_fusion.7), channel_id=1, source_target_pairs={{1,2},{2,1},{5,6},{6,5},{9,10},{10,9},{13,14},{14,13},{17,18},{18,... | collective-permute-start | bytes 3932168 | tf_op jit(solution)/shard_map/ppermute | solution.py:129
  461.6 30.1 %collective-permute-start.33 = (bf16[320,2048]{1,0:T(8,128)(2,1)S(1)}, bf16[320,2048]{1,0:T(8,128)(2,1)S(1)}, u32[]{:S(2)}, u32[]{:S(2)}) collective-permute-start(bf16[320,2048]{1,0:T(8,128)(2,1)S(1)} %add_convert_fusion.8), channel_id=1, source_target_pairs={{1,0},{2,3},{5,4},{6,7},{9,8},{10,11},{13,12},{14,15},{17,16},{18,... | collective-permute-start | bytes 3932168 | tf_op jit(solution)/shard_map/ppermute | solution.py:131
  480.0 33.4 %collective-permute-start.37 = (bf16[320,2048]{1,0:T(8,128)(2,1)S(1)}, bf16[320,2048]{1,0:T(8,128)(2,1)S(1)}, u32[]{:S(2)}, u32[]{:S(2)}) collective-permute-start(bf16[320,2048]{1,0:T(8,128)(2,1)S(1)} %get-tuple-element.213), channel_id=1, source_target_pairs={{0,1},{3,2},{4,5},{7,6},{8,9},{11,10},{12,13},{15,14},{16,17},{19,... | collective-permute-start | bytes 3932168 | tf_op jit(solution)/shard_map/ppermute | solution.py:107
  508.7 33.5 %collective-permute-start.39 = (bf16[320,2048]{1,0:T(8,128)(2,1)S(1)}, bf16[320,2048]{1,0:T(8,128)(2,1)S(1)}, u32[]{:S(2)}, u32[]{:S(2)}) collective-permute-start(bf16[320,2048]{1,0:T(8,128)(2,1)S(1)} %get-tuple-element.219), channel_id=1, source_target_pairs={{0,1},{3,2},{4,5},{7,6},{8,9},{11,10},{12,13},{15,14},{16,17},{19,... | collective-permute-start | bytes 3932168 | tf_op jit(solution)/shard_map/ppermute | solution.py:107
  620.1 45.0 %all-to-all-start.2 = ((bf16[8,640,128]{2,1,0:T(8,128)(2,1)}), bf16[8,640,128]{2,1,0:T(8,128)(2,1)S(1)}, u32[]{:S(2)}, u32[]{:S(2)}) async-start(bf16[8,640,128]{2,1,0:T(8,128)(2,1)} %bitcast.27), calls=%async_computation.2 | async-start | bytes 2621440 | tf_op jit(solution)/shard_map/all_to_all | solution.py:1293
  639.0 278.0 %reduce-scatter.5.cloned.1.call-start = ((), (), s32[]{:S(2)}) async-start(), calls=%async_computation.9 | async-start | bytes 9437184 | tf_op jit(solution)/shard_map/reduce_scatter | solution.py:1285
  840.7 35.1 %collective-permute-start.51 = (bf16[160,2048]{1,0:T(8,128)(2,1)}, bf16[160,2048]{1,0:T(8,128)(2,1)S(1)}, u32[]{:S(2)}, u32[]{:S(2)}) collective-permute-start(bf16[160,2048]{1,0:T(8,128)(2,1)} %add_convert_fusion.16), channel_id=1, source_target_pairs={{3,2},{2,1},{7,6},{6,5},{11,10},{10,9},{15,14},{14,13},{19,18},{18... | collective-permute-start | bytes 1966088 | tf_op jit(solution)/shard_map/ppermute | solution.py:164
  841.3 34.4 %collective-permute-start.48 = (bf16[160,2048]{1,0:T(8,128)(2,1)}, bf16[160,2048]{1,0:T(8,128)(2,1)S(1)}, u32[]{:S(2)}, u32[]{:S(2)}) collective-permute-start(bf16[160,2048]{1,0:T(8,128)(2,1)} %add_convert_fusion.17), channel_id=1, source_target_pairs={{0,1},{1,2},{4,5},{5,6},{8,9},{9,10},{12,13},{13,14},{16,17},{17,1... | collective-permute-start | bytes 1966088 | tf_op jit(solution)/shard_map/ppermute | solution.py:163
  856.4 32.3 %collective-permute-start.54 = (bf16[160,2048]{1,0:T(8,128)(2,1)S(1)}, bf16[160,2048]{1,0:T(8,128)(2,1)S(1)}, u32[]{:S(2)}, u32[]{:S(2)}) collective-permute-start(bf16[160,2048]{1,0:T(8,128)(2,1)S(1)} %get-tuple-element.331), channel_id=1, source_target_pairs={{0,1},{1,2},{4,5},{5,6},{8,9},{9,10},{12,13},{13,14},{16,17},{17,1... | collective-permute-start | bytes 1966088 | tf_op jit(solution)/shard_map/ppermute | solution.py:163
  877.3 33.0 %collective-permute-start.49 = (bf16[160,2048]{1,0:T(8,128)(2,1)}, bf16[160,2048]{1,0:T(8,128)(2,1)S(1)}, u32[]{:S(2)}, u32[]{:S(2)}) collective-permute-start(bf16[160,2048]{1,0:T(8,128)(2,1)} %get-tuple-element.324), channel_id=1, source_target_pairs={{0,1},{1,2},{2,3},{4,5},{5,6},{6,7},{8,9},{9,10},{10,11},{12,13},{... | collective-permute-start | bytes 1966088 | tf_op jit(solution)/shard_map/ppermute | solution.py:163
  (68 other events, 1033.6 us)
Sparse Core Ops, SparseCore 0:
  10.7 57.0 all-gather.4
  69.7 76.9 all-gather.8
  173.2 102.3 all-gather.6
  588.7 221.2 reduce-scatter.2
  830.6 70.8 reduce-scatter.4

commit v4 on v3

--- a/solution.py
+++ b/solution.py
@@ -135,9 +135,9 @@
 def line_reduce_scatter(batches, count, late):
     if count != 4:
         return [
-            lax.psum_scatter(values, "tensor", scatter_dimension=0, tiled=True).astype(f32)
+            (lax.psum_scatter(values, "tensor", scatter_dimension=0, tiled=True),)
             for values in batches
-        ], None, None
+        ], (None, None), None
     index = lax.axis_index("tensor")
     rights = []
     lefts = []
@@ -167,10 +167,9 @@
                 lefts.append(lax.ppermute(left, "tensor", to_left))
             operands.append((right, left))
     sums = [
-        block(item, index).astype(f32) + right.astype(f32) + left.astype(f32)
-        for item, right, left in zip(blocks, rights, lefts)
+        (block(item, index), right, left) for item, right, left in zip(blocks, rights, lefts)
     ]
-    return sums, operands[len(blocks)], operands[-1]
+    return sums, operands[1 : len(blocks) + 1], operands[-1]
 
 
 def begin_all_gather(values, count):
@@ -1215,34 +1214,39 @@
     )
 
 
-def weight_sum_kernel(left_ref, right_ref, out_ref):
-    out_ref[...] = lax.dot_general(
-        left_ref[...], right_ref[...], (((0,), (0,)), ((), ())), preferred_element_type=f32
-    ).astype(bf16)
-
-
-def weight_sum(slots, count, left, right, units, kept):
+def weight_sum_kernel(count, left_ref, right_ref, out_ref):
+    units = out_ref.shape[2]
+    for at in range(count):
+        out_ref[at] = lax.dot_general(
+            left_ref[...],
+            right_ref[:, at * units : (at + 1) * units],
+            (((0,), (0,)), ((), ())),
+            preferred_element_type=f32,
+        ).astype(bf16)
+
+
+def weight_sum(first, slots, count, left, right, kept):
     rows, depth = left.shape
-    first = slots[0]
+    units = right.shape[1] // slots
     return chunk_call(
-        weight_sum_kernel,
+        functools.partial(weight_sum_kernel, slots),
         [
-            (pl.BlockSpec((rows, TILE), lambda w, s: (0, s)), left),
-            (pl.BlockSpec((rows, units), lambda w, s: (0, w)), right),
+            (pl.BlockSpec((rows, TILE), lambda s: (0, s)), left),
+            (pl.BlockSpec((rows, slots * units), lambda s: (0, 0)), right),
         ],
         [
             (
-                pl.BlockSpec((None, TILE, units), lambda w, s: (first + w, s, 0)),
+                pl.BlockSpec((slots, TILE, units), lambda s: (first // slots, s, 0)),
                 jax.ShapeDtypeStruct((count, depth, units), bf16),
                 True,
             )
         ],
         kept,
-        (len(slots), depth // TILE),
+        (depth // TILE,),
         [],
         pl.CostEstimate(
-            flops=2 * rows * depth * units * len(slots),
-            bytes_accessed=2 * len(slots) * (rows * depth + rows * units + depth * units),
+            flops=2 * rows * depth * units * slots,
+            bytes_accessed=2 * slots * (rows * depth + rows * units + depth * units),
             transcendentals=0,
         ),
         "weight_sum",
@@ -1425,16 +1429,14 @@
                 (None, None),
             )[turn_at]
             if left is not None:
-                mlp_total = weight_sum(
-                    (turn_at,), 3, follow(left, last), right, hidden_width, mlp_total
-                )
+                mlp_total = weight_sum(turn_at, 1, 3, follow(left, last), right, mlp_total)
                 last = mlp_total[0]
         if coming == 3 * chunks - 1:
             break
     hidden_grad, proj_grad, attn_grad = state["backward"]
-    mlp_weight_grad = scatter_rows(mlp_total[0], 1)
+    mlp_weight_grad = scatter_rows(follow(mlp_total[0], attn_grad), 1)
     attended = attended.reshape(MB * rows, width)
-    attn_total = weight_sum((3,), 4, proj_grad, follow(attended, attn_grad), width, None)
+    attn_total = weight_sum(3, 1, 4, proj_grad, follow(attended, attn_grad), None)
 
     attn_grad = follow(exchange(attn_grad), attn_total)
     attn_grad = attn_grad.reshape(dp_count, SEG_DEV, BLK, HEAD)
@@ -1450,15 +1452,23 @@
             batch, back, q_raw, k_raw, inverse, means, gains, cosines, sines, w_attn, heads, qkv_grad
         )
         terms.append(term)
-    mlp_weight_grads = [mlp_weight_grad[at].astype(f32) for at in range(3)]
-    mlp_weight_grads[2] = jnp.transpose(mlp_weight_grads[2])
-    parts, second_operands, last_operands = line_reduce_scatter(terms, tp_count, mlp_weight_grads)
+    mlp_weight_grads = [
+        mlp_weight_grad[0].astype(f32),
+        mlp_weight_grad[1].astype(f32),
+        jnp.transpose(mlp_weight_grad[2].astype(f32)),
+    ]
+    parts, early_operands, last_operands = line_reduce_scatter(terms, tp_count, mlp_weight_grads)
     tokens = layer_input.reshape(MB * rows, D)
-    qkv_grad = follow(qkv_grad[0], (mlp_weight_grad, second_operands))
-    attn_total = weight_sum((0, 1, 2), 4, tokens, qkv_grad, width, attn_total)
-    attn_weight_grad = scatter_rows(attn_total[0], 1)
+    qkv_grad = follow(qkv_grad[0], early_operands[0])
+    attn_total = weight_sum(0, 3, 4, tokens, qkv_grad, attn_total)
+    attn_total = follow(attn_total[0], (mlp_weight_grad, early_operands[1]))
+    attn_weight_grad = scatter_rows(attn_total, 1)
+    attn_weight_grads = [attn_weight_grad[at].astype(f32) for at in range(4)]
+    attn_weight_grads[3] = jnp.transpose(attn_weight_grads[3])
+    parts[-1] = (follow(parts[-1][0], attn_weight_grads),) + parts[-1][1:]
     input_parts = [
-        lax.dynamic_slice_in_dim(hidden_grad, batch * rows + tp_index * share, share, 0) + part
+        lax.dynamic_slice_in_dim(hidden_grad, batch * rows + tp_index * share, share, 0)
+        + sum(piece.astype(f32) for piece in part)
         for batch, part in enumerate(parts)
     ]
 
@@ -1474,10 +1484,7 @@
     return (
         output.reshape(MB, rows, D),
         jnp.stack(input_parts),
-        attn_weight_grad[0].astype(f32),
-        attn_weight_grad[1].astype(f32),
-        attn_weight_grad[2].astype(f32),
-        jnp.transpose(attn_weight_grad[3].astype(f32)),
+        *attn_weight_grads,
         *mlp_weight_grads,
         gain_sums[:width],
         gain_sums[width : 2 * width],

time: 937 us -> 940 us (level)
  blocking collectives: 71.7 us -> 93.2 us
  waiting for transfers between devices: 230 us -> 213 us
    all_to_all x1, blocking collectives: 71.7 us -> 93.2 us  [give_back(): lax.all_to_all(flat, 'dp', split_axis=0, concat_axis=0, tiled=True)[:items]]
    ppermute x8, waiting for transfers between devices: 22.4 us -> 2.17 us  [advance(): lax.ppermute(self.totals[-1], 'tensor', [(1, 0), (2, 3)])]
    ppermute x4, waiting for transfers between devices: 0.01 us -> 10.2 us  [line_reduce_scatter(): lefts[at] = lax.ppermute(left, 'tensor', to_left)]
    ppermute x4, waiting for transfers between devices: 5.98 us -> 15.8 us  [line_reduce_scatter(): rights[at] = lax.ppermute(right, 'tensor', to_right)]
  transfers between devices with their start and end apart: 70 -> 70, of which waited for: 23 -> 24; matrix products, arithmetic and copies ran while one was open for 8% -> 8% of each run, Pallas kernels for 32% -> 35%
where the time goes in v4:
time: 940 us; the launch traced here: 931 us
  Pallas kernels  331 us (35%)
  waiting for transfers between devices  213 us (23%)
  starting transfers between devices  186 us (20%)
  blocking collectives  93.2 us (10%)
  other arithmetic  63.3 us (7%)
  local copies, waits for them, and re-layouts  29.1 us (3%)
  between operations  15.3 us (2%)
    pallas_call x19, Pallas kernels, chunk_call(): pl.pallas_call(body, grid=grid, in_specs=specs, out_specs=[out[0] for out...  251 us
    all_to_all x1, blocking collectives, give_back(): lax.all_to_all(flat, 'dp', split_axis=0, concat_axis=0, tiled=True)[:items]  93.2 us
    all_gather x3, waiting for transfers between devices, gather_stack(): return lax.all_gather(jnp.stack(pieces), 'dp', axis=1, tiled=True)  52.5 us
    ppermute x8, starting transfers between devices, enter(): self.inward.append(lax.ppermute(term, 'tensor', [(0, 1), (3, 2)]))  51.6 us
    ppermute x3, waiting for transfers between devices, go_on_all_gather(): left = lax.ppermute(first[1], 'tensor', [(2, 1), (1, 0)])  37.4 us
    ppermute x4, starting transfers between devices, line_reduce_scatter(): rights[at] = lax.ppermute(right, 'tensor', to_right)  32.9 us
    convert_element_type x22, other arithmetic, low_sum(): return total.astype(bf16)  31.2 us
    pallas_call x1, Pallas kernels, attend_backward(): pl.pallas_call(functools.partial(backward_kernel, trees), in_specs=[pl.Bl...  30.7 us
  transfers between devices with their start and end apart: 70, of which 24 were waited for; matrix products, arithmetic and copies ran while one was open for 8% of the time, Pallas kernels for 35%

profile of v4, /device:TPU:0, one launch (start us, length us, event | category | flops | bytes accessed | tf_op | source)
XLA Modules:
  0.0 930.6 jit_solution(7629544189567121242)
XLA Ops:
  15.4 52.4 %all-gather.5.cloned.1.call-done.refs_0_.refs_1_.refs_4_.refs_8_.refs_9_.refs_10_ = bf16[4,2048,512]{2,1,0:T(8,128)(2,1)} async-done(((bf16[4,256,512]{2,1,0:T(8,128)(2,1)}), bf16[4,2048,512]{2,1,0:T(8,128)(2,1)}) %all-gather.5.cloned.1.call-update) | async-done | bytes 8388624 | tf_op jit(solution)/shard_map/all_gather | solution.py:1286
  67.8 9.8 %project.2 = (f32[2,640,512]{2,1,0:T(8,128)S(1)}, f32[2,640,512]{2,1,0:T(8,128)}, f32[2,640,2]{2,1,0:T(8,128)S(1)}) custom-call(bf16[2,640,2048]{2,1,0:T(8,128)(2,1)} %refs_4_.7, bf16[4,2048,512]{2,1,0:T(8,128)(2,1)} %all-gather.5.cloned.1.call-done.refs_0_.refs_1_.refs_4_.refs_8_.refs_9_.refs_10_, ...), custom_call_target="tpu_custom_call" | custom-call | flops 5368709120 | bytes 9437184 | tf_op jit(solution)/shard_map/project/pallas_call | solution.py:261
  93.8 8.8 pack_heads.1
  118.2 20.6 %collective-permute-done.2 = bf16[1024,512]{1,0:T(8,128)(2,1)} collective-permute-done((bf16[1024,512]{1,0:T(8,128)(2,1)S(1)}, bf16[1024,512]{1,0:T(8,128)(2,1)}, u32[]{:S(2)}, u32[]{:S(2)}) %collective-permute-start.2) | collective-permute-done | bytes 1048608 | tf_op jit(solution)/shard_map/ppermute | solution.py:178
  145.9 24.4 %collective-permute-done.5 = bf16[1024,512]{1,0:T(8,128)(2,1)} collective-permute-done((bf16[1024,512]{1,0:T(8,128)(2,1)S(1)}, bf16[1024,512]{1,0:T(8,128)(2,1)}, u32[]{:S(2)}, u32[]{:S(2)}) %collective-permute-start.5) | collective-permute-done | bytes 1048608 | tf_op jit(solution)/shard_map/ppermute | solution.py:188
  178.1 17.1 %attend_forward.1 = bf16[8,5,128,128]{3,2,1,0:T(8,128)(2,1)} custom-call(s32[40]{0:T(128)S(1)} %fusion.20.order_ref, bf16[8,3,5,128,128]{4,3,2,1,0:T(8,128)(2,1)} %bitcast.17.x_ref), custom_call_target="tpu_custom_call" | custom-call | flops 2883584000 | bytes 5898240 | tf_op jit(solution)/shard_map/attend_forward/pallas_call | solution.py:538
  205.9 14.9 %all-to-all-done.1 = bf16[8,640,128]{2,1,0:T(8,128)(2,1)S(1)} async-done(((bf16[8,640,128]{2,1,0:T(8,128)(2,1)}), bf16[8,640,128]{2,1,0:T(8,128)(2,1)S(1)}, u32[]{:S(2)}, u32[]{:S(2)}) %all-to-all-start.1) | async-done | bytes 1310752 | tf_op jit(solution)/shard_map/all_to_all | solution.py:1301
  227.7 9.8 %collective-permute-done.9 = bf16[640,512]{1,0:T(8,128)(2,1)S(1)} collective-permute-done((bf16[640,512]{1,0:T(8,128)(2,1)S(1)}, bf16[640,512]{1,0:T(8,128)(2,1)S(1)}, u32[]{:S(2)}, u32[]{:S(2)}) %collective-permute-start.9) | collective-permute-done | bytes 655392 | tf_op jit(solution)/shard_map/ppermute | solution.py:179
  240.4 13.0 %collective-permute-done.10 = bf16[640,512]{1,0:T(8,128)(2,1)S(1)} collective-permute-done((bf16[640,512]{1,0:T(8,128)(2,1)S(1)}, bf16[640,512]{1,0:T(8,128)(2,1)S(1)}, u32[]{:S(2)}, u32[]{:S(2)}) %collective-permute-start.10) | collective-permute-done | bytes 655392 | tf_op jit(solution)/shard_map/ppermute | solution.py:188
  257.3 10.4 %collective-permute-done.11 = bf16[640,512]{1,0:T(8,128)(2,1)} collective-permute-done((bf16[640,512]{1,0:T(8,128)(2,1)S(1)}, bf16[640,512]{1,0:T(8,128)(2,1)}, u32[]{:S(2)}, u32[]{:S(2)}) %collective-permute-start.11) | collective-permute-done | bytes 655392 | tf_op jit(solution)/shard_map/ppermute | solution.py:200
  287.2 18.7 %forward_chunk.4 = (bf16[1280,2048]{1,0:T(8,128)(2,1)}, bf16[1280,2048]{1,0:T(8,128)(2,1)}, bf16[1280,2048]{1,0:T(8,128)(2,1)}, bf16[1280,2048]{1,0:T(8,128)(2,1...) custom-call(s32[1]{0:T(128)} %bitcast.2.refs_0_, f32[1,2048]{1,0:T(1,128)S(1)} %bitcast.168, ...), custom_call_target="tpu_custom_call" | custom-call | flops 10737418240 | bytes 44040192 | tf_op jit(solution)/shard_map/forward_chunk/pallas_call | solution.py:702
  305.9 7.6 collective-permute-start.21
  315.6 18.2 %forward_chunk.5 = (bf16[1280,2048]{1,0:T(8,128)(2,1)}, bf16[1280,2048]{1,0:T(8,128)(2,1)}, bf16[1280,2048]{1,0:T(8,128)(2,1)}, bf16[1280,2048]{1,0:T(8,128)(2,1...) custom-call(s32[1]{0:T(128)} %bitcast.2.refs_0_, ...), custom_call_target="tpu_custom_call", output_to_operand_aliasing={{0}: (8, {}), {1}: (9, {}), {2}: (10, {}), {3}: (11, {}), {... | custom-call | flops 10737418240 | bytes 44040192 | tf_op jit(solution)/shard_map/forward_chunk/pallas_call | solution.py:702
  341.8 18.2 %forward_chunk.6 = (bf16[1280,2048]{1,0:T(8,128)(2,1)}, bf16[1280,2048]{1,0:T(8,128)(2,1)}, bf16[1280,2048]{1,0:T(8,128)(2,1)}, bf16[1280,2048]{1,0:T(8,128)(2,1...) custom-call(s32[1]{0:T(128)} %bitcast.2.refs_0_, ...), custom_call_target="tpu_custom_call", output_to_operand_aliasing={{0}: (8, {}), {1}: (9, {}), {2}: (10, {}), {3}: (11, {}), {... | custom-call | flops 10737418240 | bytes 44040192 | tf_op jit(solution)/shard_map/forward_chunk/pallas_call | solution.py:702
  371.5 18.2 %forward_chunk.7 = (bf16[1280,2048]{1,0:T(8,128)(2,1)}, bf16[1280,2048]{1,0:T(8,128)(2,1)}, bf16[1280,2048]{1,0:T(8,128)(2,1)}, bf16[1280,2048]{1,0:T(8,128)(2,1...) custom-call(s32[1]{0:T(128)} %bitcast.2.refs_0_, ...), custom_call_target="tpu_custom_call", output_to_operand_aliasing={{0}: (8, {}), {1}: (9, {}), {2}: (10, {}), {3}: (11, {}), {... | custom-call | flops 10737418240 | bytes 44040192 | tf_op jit(solution)/shard_map/forward_chunk/pallas_call | solution.py:702
  389.7 7.8 collective-permute-start.27
  404.7 17.1 %middle_chunk.4 = (bf16[1280,2048]{1,0:T(8,128)(2,1)}, bf16[1280,2048]{1,0:T(8,128)(2,1)}, bf16[1280,2048]{1,0:T(8,128)(2,1)}, bf16[1280,2048]{1,0:T(8,128)(2,1)...) custom-call(f32[1,2048]{1,0:T(1,128)S(1)} %bitcast.172, f32[1,2048]{1,0:T(1,128)S(1)} %bitcast.181, ...), custom_call_target="tpu_custom_call" | custom-call | flops 8053063680 | bytes 40894464 | tf_op jit(solution)/shard_map/middle_chunk/pallas_call | solution.py:702
  433.7 16.8 %middle_chunk.5 = (bf16[1280,2048]{1,0:T(8,128)(2,1)}, bf16[1280,2048]{1,0:T(8,128)(2,1)}, bf16[1280,2048]{1,0:T(8,128)(2,1)}, bf16[1280,2048]{1,0:T(8,128)(2,1)...) custom-call(f32[1,2048]{1,0:T(1,128)S(1)} %bitcast.173, ...), custom_call_target="tpu_custom_call", output_to_operand_aliasing={{0}: (10, {}), {1}: (11, {}), {2}: (12, {}), {3}: (13, {})} | custom-call | flops 8053063680 | bytes 40894464 | tf_op jit(solution)/shard_map/middle_chunk/pallas_call | solution.py:702
  463.2 16.8 %middle_chunk.6 = (bf16[1280,2048]{1,0:T(8,128)(2,1)}, bf16[1280,2048]{1,0:T(8,128)(2,1)}, bf16[1280,2048]{1,0:T(8,128)(2,1)}, bf16[1280,2048]{1,0:T(8,128)(2,1)...) custom-call(f32[1,2048]{1,0:T(1,128)S(1)} %bitcast.174, ...), custom_call_target="tpu_custom_call", output_to_operand_aliasing={{0}: (10, {}), {1}: (11, {}), {2}: (12, {}), {3}: (13, {})} | custom-call | flops 8053063680 | bytes 40894464 | tf_op jit(solution)/shard_map/middle_chunk/pallas_call | solution.py:702
  491.8 16.8 %middle_chunk.7 = (bf16[1280,2048]{1,0:T(8,128)(2,1)}, bf16[1280,2048]{1,0:T(8,128)(2,1)}, bf16[1280,2048]{1,0:T(8,128)(2,1)}, bf16[1280,2048]{1,0:T(8,128)(2,1)...) custom-call(f32[1,2048]{1,0:T(1,128)S(1)} %bitcast.175, ...), custom_call_target="tpu_custom_call", output_to_operand_aliasing={{0}: (10, {}), {1}: (11, {}), {2}: (12, {}), {3}: (13, {})} | custom-call | flops 8053063680 | bytes 40894464 | tf_op jit(solution)/shard_map/middle_chunk/pallas_call | solution.py:702
  525.0 16.0 %weight_sum.5.refs_2_ = bf16[3,2048,2048]{2,1,0:T(8,128)(2,1)} custom-call(bf16[1280,2048]{1,0:T(8,128)(2,1)} %get-tuple-element.230.refs_0_, bf16[1280,2048]{1,0:T(8,128)(2,1)} %get-tuple-element.221.refs_1_), custom_call_target="tpu_custom_call" | custom-call | flops 10737418240 | bytes 18874368 | tf_op jit(solution)/shard_map/weight_sum/pallas_call | solution.py:702
  552.0 15.9 %weight_sum.6.refs_2_ = bf16[3,2048,2048]{2,1,0:T(8,128)(2,1)} custom-call(bf16[1280,2048]{1,0:T(8,128)(2,1)} %get-tuple-element.230.refs_0_, bf16[1280,2048]{1,0:T(8,128)(2,1)} %get-tuple-element.231.refs_1_, bf16[3,2048,2048]{2,1,0:T(8,128)(2,1)} %weight_sum.5.refs_2_), custom_call_target="tpu_custom_call", output_to_operand_aliasing={{}: (2, {})} | custom-call | flops 10737418240 | bytes 18874368 | tf_op jit(solution)/shard_map/weight_sum/pallas_call | solution.py:702
  575.8 16.0 %weight_sum.7 = bf16[3,2048,2048]{2,1,0:T(8,128)(2,1)} custom-call(bf16[1280,2048]{1,0:T(8,128)(2,1)} %get-tuple-element.240.refs_0_, bf16[1280,2048]{1,0:T(8,128)(2,1)} %get-tuple-element.241.refs_1_, bf16[3,2048,2048]{2,1,0:T(8,128)(2,1)} %weight_sum.6.refs_2_), custom_call_target="tpu_custom_call", output_to_operand_aliasing={{}: (2, {})} | custom-call | flops 10737418240 | bytes 18874368 | tf_op jit(solution)/shard_map/weight_sum/pallas_call | solution.py:702
  600.1 17.2 %all-to-all-start.2 = ((bf16[8,640,128]{2,1,0:T(8,128)(2,1)}), bf16[8,640,128]{2,1,0:T(8,128)(2,1)S(1)}, u32[]{:S(2)}, u32[]{:S(2)}) async-start(bf16[8,640,128]{2,1,0:T(8,128)(2,1)} %bitcast.27), calls=%async_computation.2 | async-start | bytes 2621440 | tf_op jit(solution)/shard_map/all_to_all | solution.py:1297
  625.4 10.1 %all-to-all-done.2 = bf16[8,640,128]{2,1,0:T(8,128)(2,1)S(1)} async-done(((bf16[8,640,128]{2,1,0:T(8,128)(2,1)}), bf16[8,640,128]{2,1,0:T(8,128)(2,1)S(1)}, u32[]{:S(2)}, u32[]{:S(2)}) %all-to-all-start.2) | async-done | bytes 1310752 | tf_op jit(solution)/shard_map/all_to_all | solution.py:1297
  635.5 30.7 %attend_backward.1 = bf16[8,3,5,128,128]{4,3,2,1,0:T(8,128)(2,1)} custom-call(s32[40]{0:T(128)S(1)} %copy-done.12, bf16[8,3,5,128,128]{4,3,2,1,0:T(8,128)(2,1)} %bitcast.17.x_ref, bf16[8,5,128,128]{3,2,1,0:T(8,128)(2,1)S(1)} %bitcast.167), custom_call_target="tpu_custom_call" | custom-call | flops 7208960000 | bytes 9830400 | tf_op jit(solution)/shard_map/attend_backward/pallas_call | solution.py:651
  666.2 93.2 %all_to_all.20 = bf16[8,1920,128]{2,1,0:T(8,128)(2,1)} all-to-all(bf16[8,1920,128]{2,1,0:T(8,128)(2,1)} %bitcast.216), channel_id=1, replica_groups=mesh['dp'=8,'tensor'=4] {'dp'}, dimensions={0} | all-to-all | bytes 7864320 | tf_op jit(solution)/shard_map/all_to_all | solution.py:1301
  776.7 10.0 %unpack_heads.2 = (bf16[1280,1536]{1,0:T(8,128)(2,1)}, bf16[640,2048]{1,0:T(8,128)(2,1)}) custom-call(bf16[4,2,3,640,128]{4,3,2,1,0:T(8,128)(2,1)} %bitcast.199, f32[2,640,512]{2,1,0:T(8,128)} %copy-done, f32[2,640,512]{2,1,0:T(8,128)} %get-tuple-element.143.k_ref.refs_2_, f32[2,640,2]{2,1,0:T(8,128)S(1)} %bitcast.162, f32[2,640,2]{2,1,0:T(8,128)S(1)} %bitcast.164, ...), custom_call_target="tpu_custom_call" | custom-call | flops 4026531840 | bytes 10485760 | tf_op jit(solution)/shard_map/unpack_heads/pallas_call | solution.py:702
  786.8 10.2 %unpack_heads.3 = (bf16[1280,1536]{1,0:T(8,128)(2,1)}, bf16[640,2048]{1,0:T(8,128)(2,1)}) custom-call(bf16[4,2,3,640,128]{4,3,2,1,0:T(8,128)(2,1)} %bitcast.200, f32[2,640,512]{2,1,0:T(8,128)} %copy-done, f32[2,640,512]{2,1,0:T(8,128)} %get-tuple-element.143.k_ref.refs_2_, f32[2,640,2]{2,1,0:T(8,128)S(1)} %bitcast.163, ...), custom_call_target="tpu_custom_call", output_to_operand_aliasing={{0}: (11, {})} | custom-call | flops 4026531840 | bytes 10485760 | tf_op jit(solution)/shard_map/unpack_heads/pallas_call | solution.py:702
  805.0 11.4 %weight_sum.9 = bf16[4,2048,512]{2,1,0:T(8,128)(2,1)} custom-call(bf16[1280,2048]{1,0:T(8,128)(2,1)} %bitcast.197, bf16[1280,1536]{1,0:T(8,128)(2,1)S(1)} %copy-done.7, bf16[4,2048,512]{2,1,0:T(8,128)(2,1)} %weight_sum.8.refs_2_), custom_call_target="tpu_custom_call", output_to_operand_aliasing={{}: (2, {})} | custom-call | flops 8053063680 | bytes 25952256 | tf_op jit(solution)/shard_map/weight_sum/pallas_call | solution.py:702
  835.5 18.1 %collective-permute-start.54 = (bf16[160,2048]{1,0:T(8,128)(2,1)S(1)}, bf16[160,2048]{1,0:T(8,128)(2,1)S(1)}, u32[]{:S(2)}, u32[]{:S(2)}) collective-permute-start(bf16[160,2048]{1,0:T(8,128)(2,1)S(1)} %get-tuple-element.340), channel_id=1, source_target_pairs={{0,1},{1,2},{4,5},{5,6},{8,9},{9,10},{12,13},{13,14},{16,17},{17,1... | collective-permute-start | bytes 1966088 | tf_op jit(solution)/shard_map/ppermute | solution.py:163
  859.4 9.1 collective-permute-done.54
  (296 shorter events, 320.1 us)
Async XLA Ops:
  7.2 60.6 %all-gather.5.cloned.1.call-start = ((), (), s32[]{:S(2)}) async-start(), calls=%async_computation.6 | async-start | bytes 9437184 | tf_op jit(solution)/shard_map/all_gather | solution.py:1286
  10.6 274.9 %all-gather.9.cloned.1.call-start = ((), (), s32[]{:S(2)}) async-start(), calls=%async_computation.10 | async-start | bytes 9437184 | tf_op jit(solution)/shard_map/all_gather | solution.py:1286
  102.6 67.6 %all-to-all-start = ((bf16[8,1920,128]{2,1,0:T(8,128)(2,1)}), bf16[8,1920,128]{2,1,0:T(8,128)(2,1)}, u32[]{:S(2)}, u32[]{:S(2)}) async-start(bf16[8,1920,128]{2,1,0:T(8,128)(2,1)} %bitcast.202), calls=%async_computation | async-start | bytes 7864320 | tf_op jit(solution)/shard_map/all_to_all | solution.py:1297
  107.1 178.3 %all-gather.7.cloned.1.call-start = ((), (), s32[]{:S(2)}) async-start(), calls=%async_computation.7 | async-start | bytes 18874368 | tf_op jit(solution)/shard_map/all_gather | solution.py:1286
  175.9 28.7 %collective-permute-start.17 = (bf16[1024,512]{1,0:T(8,128)(2,1)}, bf16[1024,512]{1,0:T(8,128)(2,1)}, u32[]{:S(2)}, u32[]{:S(2)}) collective-permute-start(bf16[1024,512]{1,0:T(8,128)(2,1)} %collective-permute-done.4), channel_id=1, source_target_pairs={{2,3},{6,7},{10,11},{14,15},{18,19},{22,23},{26,27},{30,31}} | collective-permute-start | bytes 3145736 | tf_op jit(solution)/shard_map/ppermute | solution.py:199
  198.9 621.8 %reduce-scatter.3.cloned.1.call-start = ((), (), s32[]{:S(2)}) async-start(), calls=%async_computation.8 | async-start | bytes 28311552 | tf_op jit(solution)/shard_map/reduce_scatter | solution.py:1289
  205.9 79.6 %collective-permute-start.18 = (bf16[1024,2048]{1,0:T(8,128)(2,1)}, bf16[1024,2048]{1,0:T(8,128)(2,1)}, u32[]{:S(2)}, u32[]{:S(2)}) collective-permute-start(bf16[1024,2048]{1,0:T(8,128)(2,1)} %select_dynamic-update-slice_fusion.refs_4_), channel_id=1, source_target_pairs={{0,4},{4,0},{8,12},{12,8},{16,20},{20,16},{24,28},{28,24},{1,5},{5... | collective-permute-start | bytes 12582920 | tf_op jit(solution)/shard_map/ppermute | solution.py:228
  278.1 35.4 %collective-permute-start.13 = (bf16[640,512]{1,0:T(8,128)(2,1)}, bf16[640,512]{1,0:T(8,128)(2,1)}, u32[]{:S(2)}, u32[]{:S(2)}) collective-permute-start(bf16[640,512]{1,0:T(8,128)(2,1)} %collective-permute-done.12), channel_id=1, source_target_pairs={{1,2},{2,3},{5,6},{6,7},{9,10},{10,11},{13,14},{14,15},{17,18},{18... | collective-permute-start | bytes 1966088 | tf_op jit(solution)/shard_map/ppermute | solution.py:187
  284.0 29.6 %collective-permute-start.15 = (bf16[640,512]{1,0:T(8,128)(2,1)S(1)}, bf16[640,512]{1,0:T(8,128)(2,1)}, u32[]{:S(2)}, u32[]{:S(2)}) collective-permute-start(bf16[640,512]{1,0:T(8,128)(2,1)S(1)} %collective-permute-done.14), channel_id=1, source_target_pairs={{2,1},{1,0},{6,5},{5,4},{10,9},{9,8},{14,13},{13,12},{18,17},{17,1... | collective-permute-start | bytes 1966088 | tf_op jit(solution)/shard_map/ppermute | solution.py:188
  305.9 34.4 %collective-permute-start.21 = (bf16[320,2048]{1,0:T(8,128)(2,1)S(1)}, bf16[320,2048]{1,0:T(8,128)(2,1)S(1)}, u32[]{:S(2)}, u32[]{:S(2)}) collective-permute-start(bf16[320,2048]{1,0:T(8,128)(2,1)S(1)} %get-tuple-element.161), channel_id=1, source_target_pairs={{0,1},{3,2},{4,5},{7,6},{8,9},{11,10},{12,13},{15,14},{16,17},{19,... | collective-permute-start | bytes 3932168 | tf_op jit(solution)/shard_map/ppermute | solution.py:107
  333.8 33.6 %collective-permute-start.22 = (bf16[320,2048]{1,0:T(8,128)(2,1)S(1)}, bf16[320,2048]{1,0:T(8,128)(2,1)S(1)}, u32[]{:S(2)}, u32[]{:S(2)}) collective-permute-start(bf16[320,2048]{1,0:T(8,128)(2,1)S(1)} %get-tuple-element.169), channel_id=1, source_target_pairs={{0,1},{3,2},{4,5},{7,6},{8,9},{11,10},{12,13},{15,14},{16,17},{19,... | collective-permute-start | bytes 3932168 | tf_op jit(solution)/shard_map/ppermute | solution.py:107
  340.8 28.8 %collective-permute-start.23 = (bf16[320,2048]{1,0:T(8,128)(2,1)S(1)}, bf16[320,2048]{1,0:T(8,128)(2,1)S(1)}, u32[]{:S(2)}, u32[]{:S(2)}) collective-permute-start(bf16[320,2048]{1,0:T(8,128)(2,1)S(1)} %add_convert_fusion.15), channel_id=1, source_target_pairs={{1,2},{2,1},{5,6},{6,5},{9,10},{10,9},{13,14},{14,13},{17,18},{18,... | collective-permute-start | bytes 3932168 | tf_op jit(solution)/shard_map/ppermute | solution.py:129
  360.0 37.5 %collective-permute-start.25 = (bf16[320,2048]{1,0:T(8,128)(2,1)S(1)}, bf16[320,2048]{1,0:T(8,128)(2,1)}, u32[]{:S(2)}, u32[]{:S(2)}) collective-permute-start(bf16[320,2048]{1,0:T(8,128)(2,1)S(1)} %get-tuple-element.179), channel_id=1, source_target_pairs={{0,1},{3,2},{4,5},{7,6},{8,9},{11,10},{12,13},{15,14},{16,17},{19,... | collective-permute-start | bytes 3932168 | tf_op jit(solution)/shard_map/ppermute | solution.py:107
  367.9 33.2 %collective-permute-start.26 = (bf16[320,2048]{1,0:T(8,128)(2,1)S(1)}, bf16[320,2048]{1,0:T(8,128)(2,1)}, u32[]{:S(2)}, u32[]{:S(2)}) collective-permute-start(bf16[320,2048]{1,0:T(8,128)(2,1)S(1)} %add_convert_fusion.14), channel_id=1, source_target_pairs={{1,2},{2,1},{5,6},{6,5},{9,10},{10,9},{13,14},{14,13},{17,18},{18,... | collective-permute-start | bytes 3932168 | tf_op jit(solution)/shard_map/ppermute | solution.py:129
  370.2 34.3 %collective-permute-start.24 = (bf16[320,2048]{1,0:T(8,128)(2,1)S(1)}, bf16[320,2048]{1,0:T(8,128)(2,1)S(1)}, u32[]{:S(2)}, u32[]{:S(2)}) collective-permute-start(bf16[320,2048]{1,0:T(8,128)(2,1)S(1)} %add_convert_fusion.13), channel_id=1, source_target_pairs={{1,0},{2,3},{5,4},{6,7},{9,8},{10,11},{13,12},{14,15},{17,16},{18,... | collective-permute-start | bytes 3932168 | tf_op jit(solution)/shard_map/ppermute | solution.py:131
  389.7 42.2 %collective-permute-start.27 = (bf16[320,2048]{1,0:T(8,128)(2,1)S(1)}, bf16[320,2048]{1,0:T(8,128)(2,1)S(1)}, u32[]{:S(2)}, u32[]{:S(2)}) collective-permute-start(bf16[320,2048]{1,0:T(8,128)(2,1)S(1)} %get-tuple-element.186), channel_id=1, source_target_pairs={{0,1},{3,2},{4,5},{7,6},{8,9},{11,10},{12,13},{15,14},{16,17},{19,... | collective-permute-start | bytes 3932168 | tf_op jit(solution)/shard_map/ppermute | solution.py:107
  399.3 29.4 %collective-permute-start.29 = (bf16[320,2048]{1,0:T(8,128)(2,1)S(1)}, bf16[320,2048]{1,0:T(8,128)(2,1)}, u32[]{:S(2)}, u32[]{:S(2)}) collective-permute-start(bf16[320,2048]{1,0:T(8,128)(2,1)S(1)} %add_convert_fusion.12), channel_id=1, source_target_pairs={{1,2},{2,1},{5,6},{6,5},{9,10},{10,9},{13,14},{14,13},{17,18},{18,... | collective-permute-start | bytes 3932168 | tf_op jit(solution)/shard_map/ppermute | solution.py:129
  403.0 30.6 %collective-permute-start.28 = (bf16[320,2048]{1,0:T(8,128)(2,1)S(1)}, bf16[320,2048]{1,0:T(8,128)(2,1)S(1)}, u32[]{:S(2)}, u32[]{:S(2)}) collective-permute-start(bf16[320,2048]{1,0:T(8,128)(2,1)S(1)} %add_convert_fusion.11), channel_id=1, source_target_pairs={{1,0},{2,3},{5,4},{6,7},{9,8},{10,11},{13,12},{14,15},{17,16},{18,... | collective-permute-start | bytes 3932168 | tf_op jit(solution)/shard_map/ppermute | solution.py:131
  421.8 35.6 %collective-permute-start.32 = (bf16[320,2048]{1,0:T(8,128)(2,1)S(1)}, bf16[320,2048]{1,0:T(8,128)(2,1)}, u32[]{:S(2)}, u32[]{:S(2)}) collective-permute-start(bf16[320,2048]{1,0:T(8,128)(2,1)S(1)} %get-tuple-element.197), channel_id=1, source_target_pairs={{0,1},{3,2},{4,5},{7,6},{8,9},{11,10},{12,13},{15,14},{16,17},{19,... | collective-permute-start | bytes 3932168 | tf_op jit(solution)/shard_map/ppermute | solution.py:107
  430.6 32.5 %collective-permute-start.31 = (bf16[320,2048]{1,0:T(8,128)(2,1)S(1)}, bf16[320,2048]{1,0:T(8,128)(2,1)S(1)}, u32[]{:S(2)}, u32[]{:S(2)}) collective-permute-start(bf16[320,2048]{1,0:T(8,128)(2,1)S(1)} %add_convert_fusion.9), channel_id=1, source_target_pairs={{1,0},{2,3},{5,4},{6,7},{9,8},{10,11},{13,12},{14,15},{17,16},{18,... | collective-permute-start | bytes 3932168 | tf_op jit(solution)/shard_map/ppermute | solution.py:131
  432.4 28.7 %collective-permute-start.30 = (bf16[320,2048]{1,0:T(8,128)(2,1)S(1)}, bf16[320,2048]{1,0:T(8,128)(2,1)S(1)}, u32[]{:S(2)}, u32[]{:S(2)}) collective-permute-start(bf16[320,2048]{1,0:T(8,128)(2,1)S(1)} %add_convert_fusion.10), channel_id=1, source_target_pairs={{1,2},{2,1},{5,6},{6,5},{9,10},{10,9},{13,14},{14,13},{17,18},{18,... | collective-permute-start | bytes 3932168 | tf_op jit(solution)/shard_map/ppermute | solution.py:129
  450.5 34.2 %collective-permute-start.34 = (bf16[320,2048]{1,0:T(8,128)(2,1)S(1)}, bf16[320,2048]{1,0:T(8,128)(2,1)}, u32[]{:S(2)}, u32[]{:S(2)}) collective-permute-start(bf16[320,2048]{1,0:T(8,128)(2,1)S(1)} %get-tuple-element.205), channel_id=1, source_target_pairs={{0,1},{3,2},{4,5},{7,6},{8,9},{11,10},{12,13},{15,14},{16,17},{19,... | collective-permute-start | bytes 3932168 | tf_op jit(solution)/shard_map/ppermute | solution.py:107
  459.3 29.0 %collective-permute-start.35 = (bf16[320,2048]{1,0:T(8,128)(2,1)S(1)}, bf16[320,2048]{1,0:T(8,128)(2,1)}, u32[]{:S(2)}, u32[]{:S(2)}) collective-permute-start(bf16[320,2048]{1,0:T(8,128)(2,1)S(1)} %add_convert_fusion.7), channel_id=1, source_target_pairs={{1,2},{2,1},{5,6},{6,5},{9,10},{10,9},{13,14},{14,13},{17,18},{18,... | collective-permute-start | bytes 3932168 | tf_op jit(solution)/shard_map/ppermute | solution.py:129
  461.5 30.1 %collective-permute-start.33 = (bf16[320,2048]{1,0:T(8,128)(2,1)S(1)}, bf16[320,2048]{1,0:T(8,128)(2,1)S(1)}, u32[]{:S(2)}, u32[]{:S(2)}) collective-permute-start(bf16[320,2048]{1,0:T(8,128)(2,1)S(1)} %add_convert_fusion.8), channel_id=1, source_target_pairs={{1,0},{2,3},{5,4},{6,7},{9,8},{10,11},{13,12},{14,15},{17,16},{18,... | collective-permute-start | bytes 3932168 | tf_op jit(solution)/shard_map/ppermute | solution.py:131
  480.0 34.4 %collective-permute-start.37 = (bf16[320,2048]{1,0:T(8,128)(2,1)S(1)}, bf16[320,2048]{1,0:T(8,128)(2,1)S(1)}, u32[]{:S(2)}, u32[]{:S(2)}) collective-permute-start(bf16[320,2048]{1,0:T(8,128)(2,1)S(1)} %get-tuple-element.216), channel_id=1, source_target_pairs={{0,1},{3,2},{4,5},{7,6},{8,9},{11,10},{12,13},{15,14},{16,17},{19,... | collective-permute-start | bytes 3932168 | tf_op jit(solution)/shard_map/ppermute | solution.py:107
  486.6 29.0 %collective-permute-start.38 = (bf16[320,2048]{1,0:T(8,128)(2,1)S(1)}, bf16[320,2048]{1,0:T(8,128)(2,1)}, u32[]{:S(2)}, u32[]{:S(2)}) collective-permute-start(bf16[320,2048]{1,0:T(8,128)(2,1)S(1)} %add_convert_fusion.6), channel_id=1, source_target_pairs={{1,2},{2,1},{5,6},{6,5},{9,10},{10,9},{13,14},{14,13},{17,18},{18,... | collective-permute-start | bytes 3932168 | tf_op jit(solution)/shard_map/ppermute | solution.py:129
  490.2 28.6 %collective-permute-start.36 = (bf16[320,2048]{1,0:T(8,128)(2,1)S(1)}, bf16[320,2048]{1,0:T(8,128)(2,1)S(1)}, u32[]{:S(2)}, u32[]{:S(2)}) collective-permute-start(bf16[320,2048]{1,0:T(8,128)(2,1)S(1)} %add_convert_fusion.5), channel_id=1, source_target_pairs={{1,0},{2,3},{5,4},{6,7},{9,8},{10,11},{13,12},{14,15},{17,16},{18,... | collective-permute-start | bytes 3932168 | tf_op jit(solution)/shard_map/ppermute | solution.py:131
  508.6 34.5 %collective-permute-start.39 = (bf16[320,2048]{1,0:T(8,128)(2,1)S(1)}, bf16[320,2048]{1,0:T(8,128)(2,1)}, u32[]{:S(2)}, u32[]{:S(2)}) collective-permute-start(bf16[320,2048]{1,0:T(8,128)(2,1)S(1)} %get-tuple-element.222), channel_id=1, source_target_pairs={{0,1},{3,2},{4,5},{7,6},{8,9},{11,10},{12,13},{15,14},{16,17},{19,... | collective-permute-start | bytes 3932168 | tf_op jit(solution)/shard_map/ppermute | solution.py:107
  517.5 28.3 %collective-permute-start.40 = (bf16[320,2048]{1,0:T(8,128)(2,1)S(1)}, bf16[320,2048]{1,0:T(8,128)(2,1)S(1)}, u32[]{:S(2)}, u32[]{:S(2)}) collective-permute-start(bf16[320,2048]{1,0:T(8,128)(2,1)S(1)} %add_convert_fusion.3), channel_id=1, source_target_pairs={{1,0},{2,3},{5,4},{6,7},{9,8},{10,11},{13,12},{14,15},{17,16},{18,... | collective-permute-start | bytes 3932168 | tf_op jit(solution)/shard_map/ppermute | solution.py:131
  600.1 35.4 %all-to-all-start.2 = ((bf16[8,640,128]{2,1,0:T(8,128)(2,1)}), bf16[8,640,128]{2,1,0:T(8,128)(2,1)S(1)}, u32[]{:S(2)}, u32[]{:S(2)}) async-start(bf16[8,640,128]{2,1,0:T(8,128)(2,1)} %bitcast.27), calls=%async_computation.2 | async-start | bytes 2621440 | tf_op jit(solution)/shard_map/all_to_all | solution.py:1297
  617.3 280.9 %reduce-scatter.5.cloned.1.call-start = ((), (), s32[]{:S(2)}) async-start(), calls=%async_computation.9 | async-start | bytes 9437184 | tf_op jit(solution)/shard_map/reduce_scatter | solution.py:1289
  835.5 33.0 %collective-permute-start.54 = (bf16[160,2048]{1,0:T(8,128)(2,1)S(1)}, bf16[160,2048]{1,0:T(8,128)(2,1)S(1)}, u32[]{:S(2)}, u32[]{:S(2)}) collective-permute-start(bf16[160,2048]{1,0:T(8,128)(2,1)S(1)} %get-tuple-element.340), channel_id=1, source_target_pairs={{0,1},{1,2},{4,5},{5,6},{8,9},{9,10},{12,13},{13,14},{16,17},{17,1... | collective-permute-start | bytes 1966088 | tf_op jit(solution)/shard_map/ppermute | solution.py:163
  (68 other events, 1047.0 us)
Sparse Core Ops, SparseCore 0:
  10.7 57.0 all-gather.4
  69.7 76.9 all-gather.8
  173.1 102.3 all-gather.6
  600.2 212.0 reduce-scatter.2
  820.9 71.4 reduce-scatter.4

commit v5 on v4

--- a/solution.py
+++ b/solution.py
@@ -137,7 +137,7 @@
         return [
             (lax.psum_scatter(values, "tensor", scatter_dimension=0, tiled=True),)
             for values in batches
-        ], (None, None), None
+        ], None, None
     index = lax.axis_index("tensor")
     rights = []
     lefts = []
@@ -153,12 +153,13 @@
         for at, item in enumerate(blocks):
             right = block(item, index + count - 1 - stage)
             left = block(item, index - count + 1 + stage)
-            if stage == 1 and at == 0:
-                right, left = follow((right, left), batches[-1])
+            if at or stage:
+                before = max(at - 1, 0)
+                right, left = follow((right, left), (rights[before], lefts[before]))
             if stage:
                 right = low_sum(right, rights[at])
                 left = low_sum(left, lefts[at])
-                if stage == count - 2 and at == len(blocks) - 1:
+                if stage == 1 and at == len(blocks) - 1:
                     right, left = follow((right, left), late)
                 rights[at] = lax.ppermute(right, "tensor", to_right)
                 lefts[at] = lax.ppermute(left, "tensor", to_left)
@@ -169,7 +170,7 @@
     sums = [
         (block(item, index), right, left) for item, right, left in zip(blocks, rights, lefts)
     ]
-    return sums, operands[1 : len(blocks) + 1], operands[-1]
+    return sums, operands[1], operands[len(blocks)]
 
 
 def begin_all_gather(values, count):
@@ -1457,11 +1458,11 @@
         mlp_weight_grad[1].astype(f32),
         jnp.transpose(mlp_weight_grad[2].astype(f32)),
     ]
-    parts, early_operands, last_operands = line_reduce_scatter(terms, tp_count, mlp_weight_grads)
+    parts, first_operands, second_operands = line_reduce_scatter(terms, tp_count, mlp_weight_grads)
     tokens = layer_input.reshape(MB * rows, D)
-    qkv_grad = follow(qkv_grad[0], early_operands[0])
+    qkv_grad = qkv_grad[0]
     attn_total = weight_sum(0, 3, 4, tokens, qkv_grad, attn_total)
-    attn_total = follow(attn_total[0], (mlp_weight_grad, early_operands[1]))
+    attn_total = follow(attn_total[0], (mlp_weight_grad, first_operands))
     attn_weight_grad = scatter_rows(attn_total, 1)
     attn_weight_grads = [attn_weight_grad[at].astype(f32) for at in range(4)]
     attn_weight_grads[3] = jnp.transpose(attn_weight_grads[3])
@@ -1479,7 +1480,7 @@
             sum(mlp_gain_parts)[0],
         ]
     )
-    gain_sums = follow(gain_sums.reshape(-1, HEAD), last_operands)
+    gain_sums = follow(gain_sums.reshape(-1, HEAD), second_operands)
     gain_sums = small_sum(gain_sums, "dp", dp_count).reshape(-1)
     return (
         output.reshape(MB, rows, D),

time: 940 us -> 925 us (0.984)
  starting transfers between devices: 186 us -> 169 us
    ppermute x4, starting transfers between devices: 32.9 us -> 16.5 us  [line_reduce_scatter(): rights[at] = lax.ppermute(right, 'tensor', to_right)]
    convert_element_type x22 -> x24, other arithmetic: 31.2 us -> 30.1 us  [low_sum(): return total.astype(bf16)]
  transfers between devices with their start and end apart: 70 -> 70, of which waited for: 24 -> 24; matrix products, arithmetic and copies ran while one was open for 8% -> 9% of each run, Pallas kernels for 35% -> 35%
where the time goes in v5:
time: 925 us; the launch traced here: 915 us
  Pallas kernels  330 us (36%)
  waiting for transfers between devices  209 us (23%)
  starting transfers between devices  169 us (18%)
  blocking collectives  93.2 us (10%)
  other arithmetic  60.7 us (7%)
  local copies, waits for them, and re-layouts  37.6 us (4%)
  between operations  15.4 us (2%)
    pallas_call x19, Pallas kernels, chunk_call(): pl.pallas_call(body, grid=grid, in_specs=specs, out_specs=[out[0] for out...  251 us
    all_to_all x1, blocking collectives, give_back(): lax.all_to_all(flat, 'dp', split_axis=0, concat_axis=0, tiled=True)[:items]  93.2 us
    all_gather x3, waiting for transfers between devices, gather_stack(): return lax.all_gather(jnp.stack(pieces), 'dp', axis=1, tiled=True)  52.5 us
    ppermute x8, starting transfers between devices, enter(): self.inward.append(lax.ppermute(term, 'tensor', [(0, 1), (3, 2)]))  51.5 us
    ppermute x3, waiting for transfers between devices, go_on_all_gather(): left = lax.ppermute(first[1], 'tensor', [(2, 1), (1, 0)])  37.4 us
    pallas_call x1, Pallas kernels, attend_backward(): pl.pallas_call(functools.partial(backward_kernel, trees), in_specs=[pl.Bl...  30.6 us
    convert_element_type x24, other arithmetic, low_sum(): return total.astype(bf16)  30.1 us
    all_to_all x2, starting transfers between devices, exchange(): return lax.all_to_all(flat, 'dp', split_axis=0, concat_axis=0, tiled=True)  22.7 us
  transfers between devices with their start and end apart: 70, of which 24 were waited for; matrix products, arithmetic and copies ran while one was open for 9% of the time, Pallas kernels for 35%

profile of v5, /device:TPU:0, one launch (start us, length us, event | category | flops | bytes accessed | tf_op | source)
XLA Modules:
  0.0 915.4 jit_solution(5897464360110618367)
XLA Ops:
  15.4 52.4 %all-gather.5.cloned.1.call-done.refs_0_.refs_1_.refs_4_.refs_8_.refs_9_.refs_10_ = bf16[4,2048,512]{2,1,0:T(8,128)(2,1)} async-done(((bf16[4,256,512]{2,1,0:T(8,128)(2,1)}), bf16[4,2048,512]{2,1,0:T(8,128)(2,1)}) %all-gather.5.cloned.1.call-update) | async-done | bytes 8388624 | tf_op jit(solution)/shard_map/all_gather | solution.py:1287
  67.8 9.8 %project.2 = (f32[2,640,512]{2,1,0:T(8,128)S(1)}, f32[2,640,512]{2,1,0:T(8,128)}, f32[2,640,2]{2,1,0:T(8,128)S(1)}) custom-call(bf16[2,640,2048]{2,1,0:T(8,128)(2,1)} %refs_4_.7, bf16[4,2048,512]{2,1,0:T(8,128)(2,1)} %all-gather.5.cloned.1.call-done.refs_0_.refs_1_.refs_4_.refs_8_.refs_9_.refs_10_, ...), custom_call_target="tpu_custom_call" | custom-call | flops 5368709120 | bytes 9437184 | tf_op jit(solution)/shard_map/project/pallas_call | solution.py:262
  93.8 8.7 pack_heads.1
  118.3 20.6 %collective-permute-done.2 = bf16[1024,512]{1,0:T(8,128)(2,1)} collective-permute-done((bf16[1024,512]{1,0:T(8,128)(2,1)S(1)}, bf16[1024,512]{1,0:T(8,128)(2,1)}, u32[]{:S(2)}, u32[]{:S(2)}) %collective-permute-start.2) | collective-permute-done | bytes 1048608 | tf_op jit(solution)/shard_map/ppermute | solution.py:179
  145.9 24.4 %collective-permute-done.5 = bf16[1024,512]{1,0:T(8,128)(2,1)} collective-permute-done((bf16[1024,512]{1,0:T(8,128)(2,1)S(1)}, bf16[1024,512]{1,0:T(8,128)(2,1)}, u32[]{:S(2)}, u32[]{:S(2)}) %collective-permute-start.5) | collective-permute-done | bytes 1048608 | tf_op jit(solution)/shard_map/ppermute | solution.py:189
  178.2 17.1 %attend_forward.1 = bf16[8,5,128,128]{3,2,1,0:T(8,128)(2,1)} custom-call(s32[40]{0:T(128)S(1)} %fusion.14.order_ref, bf16[8,3,5,128,128]{4,3,2,1,0:T(8,128)(2,1)} %bitcast.17.x_ref), custom_call_target="tpu_custom_call" | custom-call | flops 2883584000 | bytes 5898240 | tf_op jit(solution)/shard_map/attend_forward/pallas_call | solution.py:539
  204.8 16.1 %all-to-all-done.1 = bf16[8,640,128]{2,1,0:T(8,128)(2,1)S(1)} async-done(((bf16[8,640,128]{2,1,0:T(8,128)(2,1)}), bf16[8,640,128]{2,1,0:T(8,128)(2,1)S(1)}, u32[]{:S(2)}, u32[]{:S(2)}) %all-to-all-start.1) | async-done | bytes 1310752 | tf_op jit(solution)/shard_map/all_to_all | solution.py:1302
  228.4 9.8 %collective-permute-done.9 = bf16[640,512]{1,0:T(8,128)(2,1)S(1)} collective-permute-done((bf16[640,512]{1,0:T(8,128)(2,1)S(1)}, bf16[640,512]{1,0:T(8,128)(2,1)S(1)}, u32[]{:S(2)}, u32[]{:S(2)}) %collective-permute-start.9) | collective-permute-done | bytes 655392 | tf_op jit(solution)/shard_map/ppermute | solution.py:180
  241.0 13.0 %collective-permute-done.10 = bf16[640,512]{1,0:T(8,128)(2,1)S(1)} collective-permute-done((bf16[640,512]{1,0:T(8,128)(2,1)S(1)}, bf16[640,512]{1,0:T(8,128)(2,1)S(1)}, u32[]{:S(2)}, u32[]{:S(2)}) %collective-permute-start.10) | collective-permute-done | bytes 655392 | tf_op jit(solution)/shard_map/ppermute | solution.py:189
  258.0 10.4 %collective-permute-done.11 = bf16[640,512]{1,0:T(8,128)(2,1)} collective-permute-done((bf16[640,512]{1,0:T(8,128)(2,1)S(1)}, bf16[640,512]{1,0:T(8,128)(2,1)}, u32[]{:S(2)}, u32[]{:S(2)}) %collective-permute-start.11) | collective-permute-done | bytes 655392 | tf_op jit(solution)/shard_map/ppermute | solution.py:201
  288.0 18.7 %forward_chunk.4 = (bf16[1280,2048]{1,0:T(8,128)(2,1)}, bf16[1280,2048]{1,0:T(8,128)(2,1)}, bf16[1280,2048]{1,0:T(8,128)(2,1)}, bf16[1280,2048]{1,0:T(8,128)(2,1...) custom-call(s32[1]{0:T(128)} %bitcast.2.refs_0_, f32[1,2048]{1,0:T(1,128)S(1)} %bitcast.162, ...), custom_call_target="tpu_custom_call" | custom-call | flops 10737418240 | bytes 44040192 | tf_op jit(solution)/shard_map/forward_chunk/pallas_call | solution.py:703
  306.7 7.5 collective-permute-start.21
  316.2 18.2 %forward_chunk.5 = (bf16[1280,2048]{1,0:T(8,128)(2,1)}, bf16[1280,2048]{1,0:T(8,128)(2,1)}, bf16[1280,2048]{1,0:T(8,128)(2,1)}, bf16[1280,2048]{1,0:T(8,128)(2,1...) custom-call(s32[1]{0:T(128)} %bitcast.2.refs_0_, ...), custom_call_target="tpu_custom_call", output_to_operand_aliasing={{0}: (8, {}), {1}: (9, {}), {2}: (10, {}), {3}: (11, {}), {... | custom-call | flops 10737418240 | bytes 44040192 | tf_op jit(solution)/shard_map/forward_chunk/pallas_call | solution.py:703
  342.4 18.2 %forward_chunk.6 = (bf16[1280,2048]{1,0:T(8,128)(2,1)}, bf16[1280,2048]{1,0:T(8,128)(2,1)}, bf16[1280,2048]{1,0:T(8,128)(2,1)}, bf16[1280,2048]{1,0:T(8,128)(2,1...) custom-call(s32[1]{0:T(128)} %bitcast.2.refs_0_, ...), custom_call_target="tpu_custom_call", output_to_operand_aliasing={{0}: (8, {}), {1}: (9, {}), {2}: (10, {}), {3}: (11, {}), {... | custom-call | flops 10737418240 | bytes 44040192 | tf_op jit(solution)/shard_map/forward_chunk/pallas_call | solution.py:703
  360.6 7.4 collective-permute-start.25
  372.1 18.2 %forward_chunk.7 = (bf16[1280,2048]{1,0:T(8,128)(2,1)}, bf16[1280,2048]{1,0:T(8,128)(2,1)}, bf16[1280,2048]{1,0:T(8,128)(2,1)}, bf16[1280,2048]{1,0:T(8,128)(2,1...) custom-call(s32[1]{0:T(128)} %bitcast.2.refs_0_, ...), custom_call_target="tpu_custom_call", output_to_operand_aliasing={{0}: (8, {}), {1}: (9, {}), {2}: (10, {}), {3}: (11, {}), {... | custom-call | flops 10737418240 | bytes 44040192 | tf_op jit(solution)/shard_map/forward_chunk/pallas_call | solution.py:703
  390.3 7.8 collective-permute-start.27
  405.2 17.1 %middle_chunk.4 = (bf16[1280,2048]{1,0:T(8,128)(2,1)}, bf16[1280,2048]{1,0:T(8,128)(2,1)}, bf16[1280,2048]{1,0:T(8,128)(2,1)}, bf16[1280,2048]{1,0:T(8,128)(2,1)...) custom-call(f32[1,2048]{1,0:T(1,128)S(1)} %bitcast.166, f32[1,2048]{1,0:T(1,128)S(1)} %bitcast.175, ...), custom_call_target="tpu_custom_call" | custom-call | flops 8053063680 | bytes 40894464 | tf_op jit(solution)/shard_map/middle_chunk/pallas_call | solution.py:703
  434.3 16.8 %middle_chunk.5 = (bf16[1280,2048]{1,0:T(8,128)(2,1)}, bf16[1280,2048]{1,0:T(8,128)(2,1)}, bf16[1280,2048]{1,0:T(8,128)(2,1)}, bf16[1280,2048]{1,0:T(8,128)(2,1)...) custom-call(f32[1,2048]{1,0:T(1,128)S(1)} %bitcast.167, ...), custom_call_target="tpu_custom_call", output_to_operand_aliasing={{0}: (10, {}), {1}: (11, {}), {2}: (12, {}), {3}: (13, {})} | custom-call | flops 8053063680 | bytes 40894464 | tf_op jit(solution)/shard_map/middle_chunk/pallas_call | solution.py:703
  463.7 16.8 %middle_chunk.6 = (bf16[1280,2048]{1,0:T(8,128)(2,1)}, bf16[1280,2048]{1,0:T(8,128)(2,1)}, bf16[1280,2048]{1,0:T(8,128)(2,1)}, bf16[1280,2048]{1,0:T(8,128)(2,1)...) custom-call(f32[1,2048]{1,0:T(1,128)S(1)} %bitcast.168, ...), custom_call_target="tpu_custom_call", output_to_operand_aliasing={{0}: (10, {}), {1}: (11, {}), {2}: (12, {}), {3}: (13, {})} | custom-call | flops 8053063680 | bytes 40894464 | tf_op jit(solution)/shard_map/middle_chunk/pallas_call | solution.py:703
  492.3 16.8 %middle_chunk.7 = (bf16[1280,2048]{1,0:T(8,128)(2,1)}, bf16[1280,2048]{1,0:T(8,128)(2,1)}, bf16[1280,2048]{1,0:T(8,128)(2,1)}, bf16[1280,2048]{1,0:T(8,128)(2,1)...) custom-call(f32[1,2048]{1,0:T(1,128)S(1)} %bitcast.169, ...), custom_call_target="tpu_custom_call", output_to_operand_aliasing={{0}: (10, {}), {1}: (11, {}), {2}: (12, {}), {3}: (13, {})} | custom-call | flops 8053063680 | bytes 40894464 | tf_op jit(solution)/shard_map/middle_chunk/pallas_call | solution.py:703
  525.5 15.9 %weight_sum.5.refs_2_ = bf16[3,2048,2048]{2,1,0:T(8,128)(2,1)} custom-call(bf16[1280,2048]{1,0:T(8,128)(2,1)} %get-tuple-element.237.refs_0_, bf16[1280,2048]{1,0:T(8,128)(2,1)} %get-tuple-element.228.refs_1_), custom_call_target="tpu_custom_call" | custom-call | flops 10737418240 | bytes 18874368 | tf_op jit(solution)/shard_map/weight_sum/pallas_call | solution.py:703
  552.5 15.9 %weight_sum.6.refs_2_ = bf16[3,2048,2048]{2,1,0:T(8,128)(2,1)} custom-call(bf16[1280,2048]{1,0:T(8,128)(2,1)} %get-tuple-element.237.refs_0_, bf16[1280,2048]{1,0:T(8,128)(2,1)} %get-tuple-element.238.refs_1_, bf16[3,2048,2048]{2,1,0:T(8,128)(2,1)} %weight_sum.5.refs_2_), custom_call_target="tpu_custom_call", output_to_operand_aliasing={{}: (2, {})} | custom-call | flops 10737418240 | bytes 18874368 | tf_op jit(solution)/shard_map/weight_sum/pallas_call | solution.py:703
  576.4 15.9 %weight_sum.7 = bf16[3,2048,2048]{2,1,0:T(8,128)(2,1)} custom-call(bf16[1280,2048]{1,0:T(8,128)(2,1)} %get-tuple-element.247.refs_0_, bf16[1280,2048]{1,0:T(8,128)(2,1)} %get-tuple-element.248.refs_1_, bf16[3,2048,2048]{2,1,0:T(8,128)(2,1)} %weight_sum.6.refs_2_), custom_call_target="tpu_custom_call", output_to_operand_aliasing={{}: (2, {})} | custom-call | flops 10737418240 | bytes 18874368 | tf_op jit(solution)/shard_map/weight_sum/pallas_call | solution.py:703
  600.6 18.2 %all-to-all-start.2 = ((bf16[8,640,128]{2,1,0:T(8,128)(2,1)}), bf16[8,640,128]{2,1,0:T(8,128)(2,1)S(1)}, u32[]{:S(2)}, u32[]{:S(2)}) async-start(bf16[8,640,128]{2,1,0:T(8,128)(2,1)} %bitcast.27), calls=%async_computation.2 | async-start | bytes 2621440 | tf_op jit(solution)/shard_map/all_to_all | solution.py:1298
  626.9 10.1 %all-to-all-done.2 = bf16[8,640,128]{2,1,0:T(8,128)(2,1)S(1)} async-done(((bf16[8,640,128]{2,1,0:T(8,128)(2,1)}), bf16[8,640,128]{2,1,0:T(8,128)(2,1)S(1)}, u32[]{:S(2)}, u32[]{:S(2)}) %all-to-all-start.2) | async-done | bytes 1310752 | tf_op jit(solution)/shard_map/all_to_all | solution.py:1298
  637.0 30.6 %attend_backward.1 = bf16[8,3,5,128,128]{4,3,2,1,0:T(8,128)(2,1)} custom-call(s32[40]{0:T(128)S(1)} %copy-done.12, bf16[8,3,5,128,128]{4,3,2,1,0:T(8,128)(2,1)} %bitcast.17.x_ref, bf16[8,5,128,128]{3,2,1,0:T(8,128)(2,1)S(1)} %bitcast.161), custom_call_target="tpu_custom_call" | custom-call | flops 7208960000 | bytes 9830400 | tf_op jit(solution)/shard_map/attend_backward/pallas_call | solution.py:652
  667.7 93.2 %all_to_all.20 = bf16[8,1920,128]{2,1,0:T(8,128)(2,1)} all-to-all(bf16[8,1920,128]{2,1,0:T(8,128)(2,1)} %bitcast.206), channel_id=1, replica_groups=mesh['dp'=8,'tensor'=4] {'dp'}, dimensions={0} | all-to-all | bytes 7864320 | tf_op jit(solution)/shard_map/all_to_all | solution.py:1302
  777.9 10.0 %unpack_heads.2 = (bf16[1280,1536]{1,0:T(8,128)(2,1)}, bf16[640,2048]{1,0:T(8,128)(2,1)}) custom-call(bf16[4,2,3,640,128]{4,3,2,1,0:T(8,128)(2,1)} %bitcast.193, f32[2,640,512]{2,1,0:T(8,128)} %copy-done, f32[2,640,512]{2,1,0:T(8,128)} %get-tuple-element.150.k_ref.refs_2_, f32[2,640,2]{2,1,0:T(8,128)S(1)} %bitcast.156, f32[2,640,2]{2,1,0:T(8,128)S(1)} %bitcast.158, ...), custom_call_target="tpu_custom_call" | custom-call | flops 4026531840 | bytes 10485760 | tf_op jit(solution)/shard_map/unpack_heads/pallas_call | solution.py:703
  796.6 10.2 %unpack_heads.3 = (bf16[1280,1536]{1,0:T(8,128)(2,1)}, bf16[640,2048]{1,0:T(8,128)(2,1)}) custom-call(bf16[4,2,3,640,128]{4,3,2,1,0:T(8,128)(2,1)} %bitcast.194, f32[2,640,512]{2,1,0:T(8,128)} %copy-done, f32[2,640,512]{2,1,0:T(8,128)} %get-tuple-element.150.k_ref.refs_2_, f32[2,640,2]{2,1,0:T(8,128)S(1)} %bitcast.157, ...), custom_call_target="tpu_custom_call", output_to_operand_aliasing={{0}: (11, {})} | custom-call | flops 4026531840 | bytes 10485760 | tf_op jit(solution)/shard_map/unpack_heads/pallas_call | solution.py:703
  811.0 11.4 %weight_sum.9 = bf16[4,2048,512]{2,1,0:T(8,128)(2,1)} custom-call(bf16[1280,2048]{1,0:T(8,128)(2,1)} %bitcast.191, bf16[1280,1536]{1,0:T(8,128)(2,1)S(1)} %copy-done.7, bf16[4,2048,512]{2,1,0:T(8,128)(2,1)} %weight_sum.8.refs_2_), custom_call_target="tpu_custom_call", output_to_operand_aliasing={{}: (2, {})} | custom-call | flops 8053063680 | bytes 25952256 | tf_op jit(solution)/shard_map/weight_sum/pallas_call | solution.py:703
  833.0 8.4 collective-permute-done.49
  (312 shorter events, 314.3 us)
Async XLA Ops:
  7.2 60.6 %all-gather.5.cloned.1.call-start = ((), (), s32[]{:S(2)}) async-start(), calls=%async_computation.6 | async-start | bytes 9437184 | tf_op jit(solution)/shard_map/all_gather | solution.py:1287
  10.6 275.6 %all-gather.9.cloned.1.call-start = ((), (), s32[]{:S(2)}) async-start(), calls=%async_computation.10 | async-start | bytes 9437184 | tf_op jit(solution)/shard_map/all_gather | solution.py:1287
  102.6 67.7 %all-to-all-start = ((bf16[8,1920,128]{2,1,0:T(8,128)(2,1)}), bf16[8,1920,128]{2,1,0:T(8,128)(2,1)}, u32[]{:S(2)}, u32[]{:S(2)}) async-start(bf16[8,1920,128]{2,1,0:T(8,128)(2,1)} %bitcast.196), calls=%async_computation | async-start | bytes 7864320 | tf_op jit(solution)/shard_map/all_to_all | solution.py:1298
  107.1 179.1 %all-gather.7.cloned.1.call-start = ((), (), s32[]{:S(2)}) async-start(), calls=%async_computation.7 | async-start | bytes 18874368 | tf_op jit(solution)/shard_map/all_gather | solution.py:1287
  199.0 623.5 %reduce-scatter.3.cloned.1.call-start = ((), (), s32[]{:S(2)}) async-start(), calls=%async_computation.8 | async-start | bytes 28311552 | tf_op jit(solution)/shard_map/reduce_scatter | solution.py:1290
  204.7 81.4 %collective-permute-start.18 = (bf16[1024,2048]{1,0:T(8,128)(2,1)}, bf16[1024,2048]{1,0:T(8,128)(2,1)}, u32[]{:S(2)}, u32[]{:S(2)}) collective-permute-start(bf16[1024,2048]{1,0:T(8,128)(2,1)} %select_dynamic-update-slice_fusion.refs_4_), channel_id=1, source_target_pairs={{0,4},{4,0},{8,12},{12,8},{16,20},{20,16},{24,28},{28,24},{1,5},{5... | collective-permute-start | bytes 12582920 | tf_op jit(solution)/shard_map/ppermute | solution.py:229
  278.8 35.4 %collective-permute-start.13 = (bf16[640,512]{1,0:T(8,128)(2,1)}, bf16[640,512]{1,0:T(8,128)(2,1)}, u32[]{:S(2)}, u32[]{:S(2)}) collective-permute-start(bf16[640,512]{1,0:T(8,128)(2,1)} %collective-permute-done.12), channel_id=1, source_target_pairs={{1,2},{2,3},{5,6},{6,7},{9,10},{10,11},{13,14},{14,15},{17,18},{18... | collective-permute-start | bytes 1966088 | tf_op jit(solution)/shard_map/ppermute | solution.py:188
  284.7 29.5 %collective-permute-start.15 = (bf16[640,512]{1,0:T(8,128)(2,1)S(1)}, bf16[640,512]{1,0:T(8,128)(2,1)}, u32[]{:S(2)}, u32[]{:S(2)}) collective-permute-start(bf16[640,512]{1,0:T(8,128)(2,1)S(1)} %collective-permute-done.14), channel_id=1, source_target_pairs={{2,1},{1,0},{6,5},{5,4},{10,9},{9,8},{14,13},{13,12},{18,17},{17,1... | collective-permute-start | bytes 1966088 | tf_op jit(solution)/shard_map/ppermute | solution.py:189
  306.7 34.2 %collective-permute-start.21 = (bf16[320,2048]{1,0:T(8,128)(2,1)S(1)}, bf16[320,2048]{1,0:T(8,128)(2,1)S(1)}, u32[]{:S(2)}, u32[]{:S(2)}) collective-permute-start(bf16[320,2048]{1,0:T(8,128)(2,1)S(1)} %get-tuple-element.168), channel_id=1, source_target_pairs={{0,1},{3,2},{4,5},{7,6},{8,9},{11,10},{12,13},{15,14},{16,17},{19,... | collective-permute-start | bytes 3932168 | tf_op jit(solution)/shard_map/ppermute | solution.py:107
  334.4 33.6 %collective-permute-start.22 = (bf16[320,2048]{1,0:T(8,128)(2,1)S(1)}, bf16[320,2048]{1,0:T(8,128)(2,1)S(1)}, u32[]{:S(2)}, u32[]{:S(2)}) collective-permute-start(bf16[320,2048]{1,0:T(8,128)(2,1)S(1)} %get-tuple-element.176), channel_id=1, source_target_pairs={{0,1},{3,2},{4,5},{7,6},{8,9},{11,10},{12,13},{15,14},{16,17},{19,... | collective-permute-start | bytes 3932168 | tf_op jit(solution)/shard_map/ppermute | solution.py:107
  341.5 28.8 %collective-permute-start.23 = (bf16[320,2048]{1,0:T(8,128)(2,1)S(1)}, bf16[320,2048]{1,0:T(8,128)(2,1)S(1)}, u32[]{:S(2)}, u32[]{:S(2)}) collective-permute-start(bf16[320,2048]{1,0:T(8,128)(2,1)S(1)} %add_convert_fusion.15), channel_id=1, source_target_pairs={{1,2},{2,1},{5,6},{6,5},{9,10},{10,9},{13,14},{14,13},{17,18},{18,... | collective-permute-start | bytes 3932168 | tf_op jit(solution)/shard_map/ppermute | solution.py:129
  360.6 37.5 %collective-permute-start.25 = (bf16[320,2048]{1,0:T(8,128)(2,1)S(1)}, bf16[320,2048]{1,0:T(8,128)(2,1)}, u32[]{:S(2)}, u32[]{:S(2)}) collective-permute-start(bf16[320,2048]{1,0:T(8,128)(2,1)S(1)} %get-tuple-element.186), channel_id=1, source_target_pairs={{0,1},{3,2},{4,5},{7,6},{8,9},{11,10},{12,13},{15,14},{16,17},{19,... | collective-permute-start | bytes 3932168 | tf_op jit(solution)/shard_map/ppermute | solution.py:107
  368.5 33.1 %collective-permute-start.26 = (bf16[320,2048]{1,0:T(8,128)(2,1)S(1)}, bf16[320,2048]{1,0:T(8,128)(2,1)}, u32[]{:S(2)}, u32[]{:S(2)}) collective-permute-start(bf16[320,2048]{1,0:T(8,128)(2,1)S(1)} %add_convert_fusion.14), channel_id=1, source_target_pairs={{1,2},{2,1},{5,6},{6,5},{9,10},{10,9},{13,14},{14,13},{17,18},{18,... | collective-permute-start | bytes 3932168 | tf_op jit(solution)/shard_map/ppermute | solution.py:129
  370.8 34.2 %collective-permute-start.24 = (bf16[320,2048]{1,0:T(8,128)(2,1)S(1)}, bf16[320,2048]{1,0:T(8,128)(2,1)S(1)}, u32[]{:S(2)}, u32[]{:S(2)}) collective-permute-start(bf16[320,2048]{1,0:T(8,128)(2,1)S(1)} %add_convert_fusion.13), channel_id=1, source_target_pairs={{1,0},{2,3},{5,4},{6,7},{9,8},{10,11},{13,12},{14,15},{17,16},{18,... | collective-permute-start | bytes 3932168 | tf_op jit(solution)/shard_map/ppermute | solution.py:131
  390.3 42.1 %collective-permute-start.27 = (bf16[320,2048]{1,0:T(8,128)(2,1)S(1)}, bf16[320,2048]{1,0:T(8,128)(2,1)S(1)}, u32[]{:S(2)}, u32[]{:S(2)}) collective-permute-start(bf16[320,2048]{1,0:T(8,128)(2,1)S(1)} %get-tuple-element.193), channel_id=1, source_target_pairs={{0,1},{3,2},{4,5},{7,6},{8,9},{11,10},{12,13},{15,14},{16,17},{19,... | collective-permute-start | bytes 3932168 | tf_op jit(solution)/shard_map/ppermute | solution.py:107
  399.9 29.3 %collective-permute-start.29 = (bf16[320,2048]{1,0:T(8,128)(2,1)S(1)}, bf16[320,2048]{1,0:T(8,128)(2,1)}, u32[]{:S(2)}, u32[]{:S(2)}) collective-permute-start(bf16[320,2048]{1,0:T(8,128)(2,1)S(1)} %add_convert_fusion.12), channel_id=1, source_target_pairs={{1,2},{2,1},{5,6},{6,5},{9,10},{10,9},{13,14},{14,13},{17,18},{18,... | collective-permute-start | bytes 3932168 | tf_op jit(solution)/shard_map/ppermute | solution.py:129
  403.5 30.6 %collective-permute-start.28 = (bf16[320,2048]{1,0:T(8,128)(2,1)S(1)}, bf16[320,2048]{1,0:T(8,128)(2,1)S(1)}, u32[]{:S(2)}, u32[]{:S(2)}) collective-permute-start(bf16[320,2048]{1,0:T(8,128)(2,1)S(1)} %add_convert_fusion.11), channel_id=1, source_target_pairs={{1,0},{2,3},{5,4},{6,7},{9,8},{10,11},{13,12},{14,15},{17,16},{18,... | collective-permute-start | bytes 3932168 | tf_op jit(solution)/shard_map/ppermute | solution.py:131
  422.3 35.6 %collective-permute-start.32 = (bf16[320,2048]{1,0:T(8,128)(2,1)S(1)}, bf16[320,2048]{1,0:T(8,128)(2,1)}, u32[]{:S(2)}, u32[]{:S(2)}) collective-permute-start(bf16[320,2048]{1,0:T(8,128)(2,1)S(1)} %get-tuple-element.204), channel_id=1, source_target_pairs={{0,1},{3,2},{4,5},{7,6},{8,9},{11,10},{12,13},{15,14},{16,17},{19,... | collective-permute-start | bytes 3932168 | tf_op jit(solution)/shard_map/ppermute | solution.py:107
  431.0 32.5 %collective-permute-start.31 = (bf16[320,2048]{1,0:T(8,128)(2,1)S(1)}, bf16[320,2048]{1,0:T(8,128)(2,1)S(1)}, u32[]{:S(2)}, u32[]{:S(2)}) collective-permute-start(bf16[320,2048]{1,0:T(8,128)(2,1)S(1)} %add_convert_fusion.9), channel_id=1, source_target_pairs={{1,0},{2,3},{5,4},{6,7},{9,8},{10,11},{13,12},{14,15},{17,16},{18,... | collective-permute-start | bytes 3932168 | tf_op jit(solution)/shard_map/ppermute | solution.py:131
  432.9 28.7 %collective-permute-start.30 = (bf16[320,2048]{1,0:T(8,128)(2,1)S(1)}, bf16[320,2048]{1,0:T(8,128)(2,1)S(1)}, u32[]{:S(2)}, u32[]{:S(2)}) collective-permute-start(bf16[320,2048]{1,0:T(8,128)(2,1)S(1)} %add_convert_fusion.10), channel_id=1, source_target_pairs={{1,2},{2,1},{5,6},{6,5},{9,10},{10,9},{13,14},{14,13},{17,18},{18,... | collective-permute-start | bytes 3932168 | tf_op jit(solution)/shard_map/ppermute | solution.py:129
  451.1 34.1 %collective-permute-start.34 = (bf16[320,2048]{1,0:T(8,128)(2,1)S(1)}, bf16[320,2048]{1,0:T(8,128)(2,1)}, u32[]{:S(2)}, u32[]{:S(2)}) collective-permute-start(bf16[320,2048]{1,0:T(8,128)(2,1)S(1)} %get-tuple-element.212), channel_id=1, source_target_pairs={{0,1},{3,2},{4,5},{7,6},{8,9},{11,10},{12,13},{15,14},{16,17},{19,... | collective-permute-start | bytes 3932168 | tf_op jit(solution)/shard_map/ppermute | solution.py:107
  459.8 29.0 %collective-permute-start.35 = (bf16[320,2048]{1,0:T(8,128)(2,1)S(1)}, bf16[320,2048]{1,0:T(8,128)(2,1)}, u32[]{:S(2)}, u32[]{:S(2)}) collective-permute-start(bf16[320,2048]{1,0:T(8,128)(2,1)S(1)} %add_convert_fusion.7), channel_id=1, source_target_pairs={{1,2},{2,1},{5,6},{6,5},{9,10},{10,9},{13,14},{14,13},{17,18},{18,... | collective-permute-start | bytes 3932168 | tf_op jit(solution)/shard_map/ppermute | solution.py:129
  462.1 30.1 %collective-permute-start.33 = (bf16[320,2048]{1,0:T(8,128)(2,1)S(1)}, bf16[320,2048]{1,0:T(8,128)(2,1)S(1)}, u32[]{:S(2)}, u32[]{:S(2)}) collective-permute-start(bf16[320,2048]{1,0:T(8,128)(2,1)S(1)} %add_convert_fusion.8), channel_id=1, source_target_pairs={{1,0},{2,3},{5,4},{6,7},{9,8},{10,11},{13,12},{14,15},{17,16},{18,... | collective-permute-start | bytes 3932168 | tf_op jit(solution)/shard_map/ppermute | solution.py:131
  480.5 34.3 %collective-permute-start.37 = (bf16[320,2048]{1,0:T(8,128)(2,1)S(1)}, bf16[320,2048]{1,0:T(8,128)(2,1)S(1)}, u32[]{:S(2)}, u32[]{:S(2)}) collective-permute-start(bf16[320,2048]{1,0:T(8,128)(2,1)S(1)} %get-tuple-element.223), channel_id=1, source_target_pairs={{0,1},{3,2},{4,5},{7,6},{8,9},{11,10},{12,13},{15,14},{16,17},{19,... | collective-permute-start | bytes 3932168 | tf_op jit(solution)/shard_map/ppermute | solution.py:107
  487.1 29.1 %collective-permute-start.38 = (bf16[320,2048]{1,0:T(8,128)(2,1)S(1)}, bf16[320,2048]{1,0:T(8,128)(2,1)}, u32[]{:S(2)}, u32[]{:S(2)}) collective-permute-start(bf16[320,2048]{1,0:T(8,128)(2,1)S(1)} %add_convert_fusion.6), channel_id=1, source_target_pairs={{1,2},{2,1},{5,6},{6,5},{9,10},{10,9},{13,14},{14,13},{17,18},{18,... | collective-permute-start | bytes 3932168 | tf_op jit(solution)/shard_map/ppermute | solution.py:129
  490.6 28.6 %collective-permute-start.36 = (bf16[320,2048]{1,0:T(8,128)(2,1)S(1)}, bf16[320,2048]{1,0:T(8,128)(2,1)S(1)}, u32[]{:S(2)}, u32[]{:S(2)}) collective-permute-start(bf16[320,2048]{1,0:T(8,128)(2,1)S(1)} %add_convert_fusion.5), channel_id=1, source_target_pairs={{1,0},{2,3},{5,4},{6,7},{9,8},{10,11},{13,12},{14,15},{17,16},{18,... | collective-permute-start | bytes 3932168 | tf_op jit(solution)/shard_map/ppermute | solution.py:131
  509.1 34.6 %collective-permute-start.39 = (bf16[320,2048]{1,0:T(8,128)(2,1)S(1)}, bf16[320,2048]{1,0:T(8,128)(2,1)}, u32[]{:S(2)}, u32[]{:S(2)}) collective-permute-start(bf16[320,2048]{1,0:T(8,128)(2,1)S(1)} %get-tuple-element.229), channel_id=1, source_target_pairs={{0,1},{3,2},{4,5},{7,6},{8,9},{11,10},{12,13},{15,14},{16,17},{19,... | collective-permute-start | bytes 3932168 | tf_op jit(solution)/shard_map/ppermute | solution.py:107
  518.0 28.4 %collective-permute-start.40 = (bf16[320,2048]{1,0:T(8,128)(2,1)S(1)}, bf16[320,2048]{1,0:T(8,128)(2,1)S(1)}, u32[]{:S(2)}, u32[]{:S(2)}) collective-permute-start(bf16[320,2048]{1,0:T(8,128)(2,1)S(1)} %add_convert_fusion.3), channel_id=1, source_target_pairs={{1,0},{2,3},{5,4},{6,7},{9,8},{10,11},{13,12},{14,15},{17,16},{18,... | collective-permute-start | bytes 3932168 | tf_op jit(solution)/shard_map/ppermute | solution.py:131
  600.6 36.4 %all-to-all-start.2 = ((bf16[8,640,128]{2,1,0:T(8,128)(2,1)}), bf16[8,640,128]{2,1,0:T(8,128)(2,1)S(1)}, u32[]{:S(2)}, u32[]{:S(2)}) async-start(bf16[8,640,128]{2,1,0:T(8,128)(2,1)} %bitcast.27), calls=%async_computation.2 | async-start | bytes 2621440 | tf_op jit(solution)/shard_map/all_to_all | solution.py:1298
  618.8 274.9 %reduce-scatter.5.cloned.1.call-start = ((), (), s32[]{:S(2)}) async-start(), calls=%async_computation.9 | async-start | bytes 9437184 | tf_op jit(solution)/shard_map/reduce_scatter | solution.py:1290
  792.1 30.4 %collective-permute-start.47 = (bf16[160,2048]{1,0:T(8,128)(2,1)}, bf16[160,2048]{1,0:T(8,128)(2,1)}, u32[]{:S(2)}, u32[]{:S(2)}) collective-permute-start(bf16[160,2048]{1,0:T(8,128)(2,1)} %get-tuple-element.353), channel_id=1, source_target_pairs={{0,1},{4,5},{8,9},{12,13},{16,17},{20,21},{24,25},{28,29}} | collective-permute-start | bytes 1966088 | tf_op jit(solution)/shard_map/ppermute | solution.py:167
  842.5 33.0 %collective-permute-start.51 = (bf16[160,2048]{1,0:T(8,128)(2,1)}, bf16[160,2048]{1,0:T(8,128)(2,1)}, u32[]{:S(2)}, u32[]{:S(2)}) collective-permute-start(bf16[160,2048]{1,0:T(8,128)(2,1)} %add_convert_fusion.21), channel_id=1, source_target_pairs={{0,1},{1,2},{2,3},{4,5},{5,6},{6,7},{8,9},{9,10},{10,11},{12,13},{... | collective-permute-start | bytes 1966088 | tf_op jit(solution)/shard_map/ppermute | solution.py:164
  (75 other events, 1094.1 us)
Sparse Core Ops, SparseCore 0:
  10.7 57.0 all-gather.4
  69.7 76.9 all-gather.8
  173.2 102.4 all-gather.6
  600.7 212.9 reduce-scatter.2
  822.6 71.0 reduce-scatter.4

commit v6 on v5

--- a/solution.py
+++ b/solution.py
@@ -153,12 +153,14 @@
         for at, item in enumerate(blocks):
             right = block(item, index + count - 1 - stage)
             left = block(item, index - count + 1 + stage)
-            if at or stage:
-                before = max(at - 1, 0)
+            before = max(at - 1, 0)
+            if stage:
+                arrived = follow((rights[at], lefts[at]), (rights[before], lefts[before]))
+                right = low_sum(right, arrived[0])
+                left = low_sum(left, arrived[1])
+            elif at:
                 right, left = follow((right, left), (rights[before], lefts[before]))
             if stage:
-                right = low_sum(right, rights[at])
-                left = low_sum(left, lefts[at])
                 if stage == 1 and at == len(blocks) - 1:
                     right, left = follow((right, left), late)
                 rights[at] = lax.ppermute(right, "tensor", to_right)
@@ -1467,11 +1469,11 @@
     attn_weight_grads = [attn_weight_grad[at].astype(f32) for at in range(4)]
     attn_weight_grads[3] = jnp.transpose(attn_weight_grads[3])
     parts[-1] = (follow(parts[-1][0], attn_weight_grads),) + parts[-1][1:]
-    input_parts = [
-        lax.dynamic_slice_in_dim(hidden_grad, batch * rows + tp_index * share, share, 0)
-        + sum(piece.astype(f32) for piece in part)
-        for batch, part in enumerate(parts)
-    ]
+    input_grad = jnp.zeros((MB, share, D), f32)
+    for batch, part in enumerate(parts):
+        mine = lax.dynamic_slice_in_dim(hidden_grad, batch * rows + tp_index * share, share, 0)
+        mine = mine + sum(piece.astype(f32) for piece in part)
+        input_grad = lax.dynamic_update_slice(input_grad, mine[None], (batch, 0, 0))
 
     gain_sums = jnp.concatenate(
         [
@@ -1484,7 +1486,7 @@
     gain_sums = small_sum(gain_sums, "dp", dp_count).reshape(-1)
     return (
         output.reshape(MB, rows, D),
-        jnp.stack(input_parts),
+        input_grad,
         *attn_weight_grads,
         *mlp_weight_grads,
         gain_sums[:width],

time: 925 us -> 923 us (level)
    convert_element_type x24 -> x20, other arithmetic: 30.1 us -> 30.9 us  [low_sum(): return total.astype(bf16)]
  transfers between devices with their start and end apart: 70 -> 70, of which waited for: 24 -> 23; matrix products, arithmetic and copies ran while one was open for 9% -> 8% of each run, Pallas kernels for 35% -> 36%
where the time goes in v6:
time: 923 us; the launch traced here: 914 us
  Pallas kernels  331 us (36%)
  waiting for transfers between devices  205 us (22%)
  starting transfers between devices  175 us (19%)
  blocking collectives  93.2 us (10%)
  other arithmetic  63.1 us (7%)
  local copies, waits for them, and re-layouts  31.6 us (3%)
  between operations  15.3 us (2%)
    pallas_call x19, Pallas kernels, chunk_call(): pl.pallas_call(body, grid=grid, in_specs=specs, out_specs=[out[0] for out...  251 us
    all_to_all x1, blocking collectives, give_back(): lax.all_to_all(flat, 'dp', split_axis=0, concat_axis=0, tiled=True)[:items]  93.2 us
    all_gather x3, waiting for transfers between devices, gather_stack(): return lax.all_gather(jnp.stack(pieces), 'dp', axis=1, tiled=True)  52.5 us
    ppermute x8, starting transfers between devices, enter(): self.inward.append(lax.ppermute(term, 'tensor', [(0, 1), (3, 2)]))  51.6 us
    ppermute x3, waiting for transfers between devices, go_on_all_gather(): left = lax.ppermute(first[1], 'tensor', [(2, 1), (1, 0)])  37.4 us
    convert_element_type x20, other arithmetic, low_sum(): return total.astype(bf16)  30.9 us
    pallas_call x1, Pallas kernels, attend_backward(): pl.pallas_call(functools.partial(backward_kernel, trees), in_specs=[pl.Bl...  30.7 us
    ppermute x3, waiting for transfers between devices, begin_all_gather(): right = lax.ppermute(values, 'tensor', [(0, 1), (1, 2), (2, 3)])  22.9 us
  transfers between devices with their start and end apart: 70, of which 23 were waited for; matrix products, arithmetic and copies ran while one was open for 8% of the time, Pallas kernels for 36%

profile of v6, /device:TPU:0, one launch (start us, length us, event | category | flops | bytes accessed | tf_op | source)
XLA Modules:
  0.0 914.0 jit_solution(6740258639900857415)
XLA Ops:
  15.4 52.4 %all-gather.5.cloned.1.call-done.refs_0_.refs_1_.refs_4_.refs_8_.refs_9_.refs_10_ = bf16[4,2048,512]{2,1,0:T(8,128)(2,1)} async-done(((bf16[4,256,512]{2,1,0:T(8,128)(2,1)}), bf16[4,2048,512]{2,1,0:T(8,128)(2,1)}) %all-gather.5.cloned.1.call-update) | async-done | bytes 8388624 | tf_op jit(solution)/shard_map/all_gather | solution.py:1289
  67.8 9.8 %project.2 = (f32[2,640,512]{2,1,0:T(8,128)S(1)}, f32[2,640,512]{2,1,0:T(8,128)}, f32[2,640,2]{2,1,0:T(8,128)S(1)}) custom-call(bf16[2,640,2048]{2,1,0:T(8,128)(2,1)} %refs_4_.7, bf16[4,2048,512]{2,1,0:T(8,128)(2,1)} %all-gather.5.cloned.1.call-done.refs_0_.refs_1_.refs_4_.refs_8_.refs_9_.refs_10_, ...), custom_call_target="tpu_custom_call" | custom-call | flops 5368709120 | bytes 9437184 | tf_op jit(solution)/shard_map/project/pallas_call | solution.py:264
  93.8 8.8 pack_heads.1
  118.1 20.6 %collective-permute-done.2 = bf16[1024,512]{1,0:T(8,128)(2,1)} collective-permute-done((bf16[1024,512]{1,0:T(8,128)(2,1)S(1)}, bf16[1024,512]{1,0:T(8,128)(2,1)}, u32[]{:S(2)}, u32[]{:S(2)}) %collective-permute-start.2) | collective-permute-done | bytes 1048608 | tf_op jit(solution)/shard_map/ppermute | solution.py:181
  145.8 24.4 %collective-permute-done.5 = bf16[1024,512]{1,0:T(8,128)(2,1)} collective-permute-done((bf16[1024,512]{1,0:T(8,128)(2,1)S(1)}, bf16[1024,512]{1,0:T(8,128)(2,1)}, u32[]{:S(2)}, u32[]{:S(2)}) %collective-permute-start.5) | collective-permute-done | bytes 1048608 | tf_op jit(solution)/shard_map/ppermute | solution.py:191
  178.0 17.1 %attend_forward.1 = bf16[8,5,128,128]{3,2,1,0:T(8,128)(2,1)} custom-call(s32[40]{0:T(128)S(1)} %fusion.22.order_ref, bf16[8,3,5,128,128]{4,3,2,1,0:T(8,128)(2,1)} %bitcast.17.x_ref), custom_call_target="tpu_custom_call" | custom-call | flops 2883584000 | bytes 5898240 | tf_op jit(solution)/shard_map/attend_forward/pallas_call | solution.py:541
  205.8 14.9 %all-to-all-done.1 = bf16[8,640,128]{2,1,0:T(8,128)(2,1)S(1)} async-done(((bf16[8,640,128]{2,1,0:T(8,128)(2,1)}), bf16[8,640,128]{2,1,0:T(8,128)(2,1)S(1)}, u32[]{:S(2)}, u32[]{:S(2)}) %all-to-all-start.1) | async-done | bytes 1310752 | tf_op jit(solution)/shard_map/all_to_all | solution.py:1304
  227.7 9.8 %collective-permute-done.9 = bf16[640,512]{1,0:T(8,128)(2,1)S(1)} collective-permute-done((bf16[640,512]{1,0:T(8,128)(2,1)S(1)}, bf16[640,512]{1,0:T(8,128)(2,1)S(1)}, u32[]{:S(2)}, u32[]{:S(2)}) %collective-permute-start.9) | collective-permute-done | bytes 655392 | tf_op jit(solution)/shard_map/ppermute | solution.py:182
  240.3 13.0 %collective-permute-done.10 = bf16[640,512]{1,0:T(8,128)(2,1)S(1)} collective-permute-done((bf16[640,512]{1,0:T(8,128)(2,1)S(1)}, bf16[640,512]{1,0:T(8,128)(2,1)S(1)}, u32[]{:S(2)}, u32[]{:S(2)}) %collective-permute-start.10) | collective-permute-done | bytes 655392 | tf_op jit(solution)/shard_map/ppermute | solution.py:191
  257.2 10.3 %collective-permute-done.11 = bf16[640,512]{1,0:T(8,128)(2,1)} collective-permute-done((bf16[640,512]{1,0:T(8,128)(2,1)S(1)}, bf16[640,512]{1,0:T(8,128)(2,1)}, u32[]{:S(2)}, u32[]{:S(2)}) %collective-permute-start.11) | collective-permute-done | bytes 655392 | tf_op jit(solution)/shard_map/ppermute | solution.py:203
  287.2 18.7 %forward_chunk.4 = (bf16[1280,2048]{1,0:T(8,128)(2,1)}, bf16[1280,2048]{1,0:T(8,128)(2,1)}, bf16[1280,2048]{1,0:T(8,128)(2,1)}, bf16[1280,2048]{1,0:T(8,128)(2,1...) custom-call(s32[1]{0:T(128)} %bitcast.2.refs_0_, f32[1,2048]{1,0:T(1,128)S(1)} %bitcast.170, ...), custom_call_target="tpu_custom_call" | custom-call | flops 10737418240 | bytes 44040192 | tf_op jit(solution)/shard_map/forward_chunk/pallas_call | solution.py:705
  305.9 7.6 collective-permute-start.21
  315.5 18.2 %forward_chunk.5 = (bf16[1280,2048]{1,0:T(8,128)(2,1)}, bf16[1280,2048]{1,0:T(8,128)(2,1)}, bf16[1280,2048]{1,0:T(8,128)(2,1)}, bf16[1280,2048]{1,0:T(8,128)(2,1...) custom-call(s32[1]{0:T(128)} %bitcast.2.refs_0_, ...), custom_call_target="tpu_custom_call", output_to_operand_aliasing={{0}: (8, {}), {1}: (9, {}), {2}: (10, {}), {3}: (11, {}), {... | custom-call | flops 10737418240 | bytes 44040192 | tf_op jit(solution)/shard_map/forward_chunk/pallas_call | solution.py:705
  341.7 18.2 %forward_chunk.6 = (bf16[1280,2048]{1,0:T(8,128)(2,1)}, bf16[1280,2048]{1,0:T(8,128)(2,1)}, bf16[1280,2048]{1,0:T(8,128)(2,1)}, bf16[1280,2048]{1,0:T(8,128)(2,1...) custom-call(s32[1]{0:T(128)} %bitcast.2.refs_0_, ...), custom_call_target="tpu_custom_call", output_to_operand_aliasing={{0}: (8, {}), {1}: (9, {}), {2}: (10, {}), {3}: (11, {}), {... | custom-call | flops 10737418240 | bytes 44040192 | tf_op jit(solution)/shard_map/forward_chunk/pallas_call | solution.py:705
  371.4 18.2 %forward_chunk.7 = (bf16[1280,2048]{1,0:T(8,128)(2,1)}, bf16[1280,2048]{1,0:T(8,128)(2,1)}, bf16[1280,2048]{1,0:T(8,128)(2,1)}, bf16[1280,2048]{1,0:T(8,128)(2,1...) custom-call(s32[1]{0:T(128)} %bitcast.2.refs_0_, ...), custom_call_target="tpu_custom_call", output_to_operand_aliasing={{0}: (8, {}), {1}: (9, {}), {2}: (10, {}), {3}: (11, {}), {... | custom-call | flops 10737418240 | bytes 44040192 | tf_op jit(solution)/shard_map/forward_chunk/pallas_call | solution.py:705
  389.6 7.8 collective-permute-start.27
  404.6 17.1 %middle_chunk.4 = (bf16[1280,2048]{1,0:T(8,128)(2,1)}, bf16[1280,2048]{1,0:T(8,128)(2,1)}, bf16[1280,2048]{1,0:T(8,128)(2,1)}, bf16[1280,2048]{1,0:T(8,128)(2,1)...) custom-call(f32[1,2048]{1,0:T(1,128)S(1)} %bitcast.174, f32[1,2048]{1,0:T(1,128)S(1)} %bitcast.183, ...), custom_call_target="tpu_custom_call" | custom-call | flops 8053063680 | bytes 40894464 | tf_op jit(solution)/shard_map/middle_chunk/pallas_call | solution.py:705
  433.7 16.8 %middle_chunk.5 = (bf16[1280,2048]{1,0:T(8,128)(2,1)}, bf16[1280,2048]{1,0:T(8,128)(2,1)}, bf16[1280,2048]{1,0:T(8,128)(2,1)}, bf16[1280,2048]{1,0:T(8,128)(2,1)...) custom-call(f32[1,2048]{1,0:T(1,128)S(1)} %bitcast.175, ...), custom_call_target="tpu_custom_call", output_to_operand_aliasing={{0}: (10, {}), {1}: (11, {}), {2}: (12, {}), {3}: (13, {})} | custom-call | flops 8053063680 | bytes 40894464 | tf_op jit(solution)/shard_map/middle_chunk/pallas_call | solution.py:705
  463.1 16.8 %middle_chunk.6 = (bf16[1280,2048]{1,0:T(8,128)(2,1)}, bf16[1280,2048]{1,0:T(8,128)(2,1)}, bf16[1280,2048]{1,0:T(8,128)(2,1)}, bf16[1280,2048]{1,0:T(8,128)(2,1)...) custom-call(f32[1,2048]{1,0:T(1,128)S(1)} %bitcast.176, ...), custom_call_target="tpu_custom_call", output_to_operand_aliasing={{0}: (10, {}), {1}: (11, {}), {2}: (12, {}), {3}: (13, {})} | custom-call | flops 8053063680 | bytes 40894464 | tf_op jit(solution)/shard_map/middle_chunk/pallas_call | solution.py:705
  491.8 16.8 %middle_chunk.7 = (bf16[1280,2048]{1,0:T(8,128)(2,1)}, bf16[1280,2048]{1,0:T(8,128)(2,1)}, bf16[1280,2048]{1,0:T(8,128)(2,1)}, bf16[1280,2048]{1,0:T(8,128)(2,1)...) custom-call(f32[1,2048]{1,0:T(1,128)S(1)} %bitcast.177, ...), custom_call_target="tpu_custom_call", output_to_operand_aliasing={{0}: (10, {}), {1}: (11, {}), {2}: (12, {}), {3}: (13, {})} | custom-call | flops 8053063680 | bytes 40894464 | tf_op jit(solution)/shard_map/middle_chunk/pallas_call | solution.py:705
  524.9 16.0 %weight_sum.5.refs_2_ = bf16[3,2048,2048]{2,1,0:T(8,128)(2,1)} custom-call(bf16[1280,2048]{1,0:T(8,128)(2,1)} %get-tuple-element.237.refs_0_, bf16[1280,2048]{1,0:T(8,128)(2,1)} %get-tuple-element.228.refs_1_), custom_call_target="tpu_custom_call" | custom-call | flops 10737418240 | bytes 18874368 | tf_op jit(solution)/shard_map/weight_sum/pallas_call | solution.py:705
  551.9 15.9 %weight_sum.6.refs_2_ = bf16[3,2048,2048]{2,1,0:T(8,128)(2,1)} custom-call(bf16[1280,2048]{1,0:T(8,128)(2,1)} %get-tuple-element.237.refs_0_, bf16[1280,2048]{1,0:T(8,128)(2,1)} %get-tuple-element.238.refs_1_, bf16[3,2048,2048]{2,1,0:T(8,128)(2,1)} %weight_sum.5.refs_2_), custom_call_target="tpu_custom_call", output_to_operand_aliasing={{}: (2, {})} | custom-call | flops 10737418240 | bytes 18874368 | tf_op jit(solution)/shard_map/weight_sum/pallas_call | solution.py:705
  575.8 16.0 %weight_sum.7 = bf16[3,2048,2048]{2,1,0:T(8,128)(2,1)} custom-call(bf16[1280,2048]{1,0:T(8,128)(2,1)} %get-tuple-element.247.refs_0_, bf16[1280,2048]{1,0:T(8,128)(2,1)} %get-tuple-element.248.refs_1_, bf16[3,2048,2048]{2,1,0:T(8,128)(2,1)} %weight_sum.6.refs_2_), custom_call_target="tpu_custom_call", output_to_operand_aliasing={{}: (2, {})} | custom-call | flops 10737418240 | bytes 18874368 | tf_op jit(solution)/shard_map/weight_sum/pallas_call | solution.py:705
  600.0 17.3 %all-to-all-start.2 = ((bf16[8,640,128]{2,1,0:T(8,128)(2,1)}), bf16[8,640,128]{2,1,0:T(8,128)(2,1)S(1)}, u32[]{:S(2)}, u32[]{:S(2)}) async-start(bf16[8,640,128]{2,1,0:T(8,128)(2,1)} %bitcast.27), calls=%async_computation.2 | async-start | bytes 2621440 | tf_op jit(solution)/shard_map/all_to_all | solution.py:1300
  625.4 10.1 %all-to-all-done.2 = bf16[8,640,128]{2,1,0:T(8,128)(2,1)S(1)} async-done(((bf16[8,640,128]{2,1,0:T(8,128)(2,1)}), bf16[8,640,128]{2,1,0:T(8,128)(2,1)S(1)}, u32[]{:S(2)}, u32[]{:S(2)}) %all-to-all-start.2) | async-done | bytes 1310752 | tf_op jit(solution)/shard_map/all_to_all | solution.py:1300
  635.5 30.7 %attend_backward.1 = bf16[8,3,5,128,128]{4,3,2,1,0:T(8,128)(2,1)} custom-call(s32[40]{0:T(128)S(1)} %copy-done.12, bf16[8,3,5,128,128]{4,3,2,1,0:T(8,128)(2,1)} %bitcast.17.x_ref, bf16[8,5,128,128]{3,2,1,0:T(8,128)(2,1)S(1)} %bitcast.169), custom_call_target="tpu_custom_call" | custom-call | flops 7208960000 | bytes 9830400 | tf_op jit(solution)/shard_map/attend_backward/pallas_call | solution.py:654
  666.2 93.2 %all_to_all.20 = bf16[8,1920,128]{2,1,0:T(8,128)(2,1)} all-to-all(bf16[8,1920,128]{2,1,0:T(8,128)(2,1)} %bitcast.218), channel_id=1, replica_groups=mesh['dp'=8,'tensor'=4] {'dp'}, dimensions={0} | all-to-all | bytes 7864320 | tf_op jit(solution)/shard_map/all_to_all | solution.py:1304
  776.6 10.1 %unpack_heads.2 = (bf16[1280,1536]{1,0:T(8,128)(2,1)}, bf16[640,2048]{1,0:T(8,128)(2,1)}) custom-call(bf16[4,2,3,640,128]{4,3,2,1,0:T(8,128)(2,1)} %bitcast.201, f32[2,640,512]{2,1,0:T(8,128)} %copy-done, f32[2,640,512]{2,1,0:T(8,128)} %get-tuple-element.150.k_ref.refs_2_, f32[2,640,2]{2,1,0:T(8,128)S(1)} %bitcast.164, f32[2,640,2]{2,1,0:T(8,128)S(1)} %bitcast.166, ...), custom_call_target="tpu_custom_call" | custom-call | flops 4026531840 | bytes 10485760 | tf_op jit(solution)/shard_map/unpack_heads/pallas_call | solution.py:705
  793.7 10.4 %unpack_heads.3 = (bf16[1280,1536]{1,0:T(8,128)(2,1)}, bf16[640,2048]{1,0:T(8,128)(2,1)}) custom-call(bf16[4,2,3,640,128]{4,3,2,1,0:T(8,128)(2,1)} %bitcast.202, f32[2,640,512]{2,1,0:T(8,128)} %copy-done, f32[2,640,512]{2,1,0:T(8,128)} %get-tuple-element.150.k_ref.refs_2_, f32[2,640,2]{2,1,0:T(8,128)S(1)} %bitcast.165, ...), custom_call_target="tpu_custom_call", output_to_operand_aliasing={{0}: (11, {})} | custom-call | flops 4026531840 | bytes 10485760 | tf_op jit(solution)/shard_map/unpack_heads/pallas_call | solution.py:705
  807.1 11.5 %weight_sum.9 = bf16[4,2048,512]{2,1,0:T(8,128)(2,1)} custom-call(bf16[1280,2048]{1,0:T(8,128)(2,1)} %bitcast.199, bf16[1280,1536]{1,0:T(8,128)(2,1)S(1)} %copy-done.7, bf16[4,2048,512]{2,1,0:T(8,128)(2,1)} %weight_sum.8.refs_2_), custom_call_target="tpu_custom_call", output_to_operand_aliasing={{}: (2, {})} | custom-call | flops 8053063680 | bytes 25952256 | tf_op jit(solution)/shard_map/weight_sum/pallas_call | solution.py:705
  835.6 8.4 collective-permute-done.49
  878.9 8.9 collective-permute-start.57
  (294 shorter events, 313.1 us)
Async XLA Ops:
  7.2 60.6 %all-gather.5.cloned.1.call-start = ((), (), s32[]{:S(2)}) async-start(), calls=%async_computation.6 | async-start | bytes 9437184 | tf_op jit(solution)/shard_map/all_gather | solution.py:1289
  10.6 274.8 %all-gather.9.cloned.1.call-start = ((), (), s32[]{:S(2)}) async-start(), calls=%async_computation.10 | async-start | bytes 9437184 | tf_op jit(solution)/shard_map/all_gather | solution.py:1289
  102.5 67.6 %all-to-all-start = ((bf16[8,1920,128]{2,1,0:T(8,128)(2,1)}), bf16[8,1920,128]{2,1,0:T(8,128)(2,1)}, u32[]{:S(2)}, u32[]{:S(2)}) async-start(bf16[8,1920,128]{2,1,0:T(8,128)(2,1)} %bitcast.204), calls=%async_computation | async-start | bytes 7864320 | tf_op jit(solution)/shard_map/all_to_all | solution.py:1300
  107.1 178.4 %all-gather.7.cloned.1.call-start = ((), (), s32[]{:S(2)}) async-start(), calls=%async_computation.7 | async-start | bytes 18874368 | tf_op jit(solution)/shard_map/all_gather | solution.py:1289
  175.8 28.7 %collective-permute-start.17 = (bf16[1024,512]{1,0:T(8,128)(2,1)}, bf16[1024,512]{1,0:T(8,128)(2,1)}, u32[]{:S(2)}, u32[]{:S(2)}) collective-permute-start(bf16[1024,512]{1,0:T(8,128)(2,1)} %collective-permute-done.4), channel_id=1, source_target_pairs={{2,3},{6,7},{10,11},{14,15},{18,19},{22,23},{26,27},{30,31}} | collective-permute-start | bytes 3145736 | tf_op jit(solution)/shard_map/ppermute | solution.py:202
  198.8 619.8 %reduce-scatter.3.cloned.1.call-start = ((), (), s32[]{:S(2)}) async-start(), calls=%async_computation.8 | async-start | bytes 28311552 | tf_op jit(solution)/shard_map/reduce_scatter | solution.py:1292
  205.8 79.6 %collective-permute-start.18 = (bf16[1024,2048]{1,0:T(8,128)(2,1)}, bf16[1024,2048]{1,0:T(8,128)(2,1)}, u32[]{:S(2)}, u32[]{:S(2)}) collective-permute-start(bf16[1024,2048]{1,0:T(8,128)(2,1)} %select_dynamic-update-slice_fusion.refs_4_), channel_id=1, source_target_pairs={{0,4},{4,0},{8,12},{12,8},{16,20},{20,16},{24,28},{28,24},{1,5},{5... | collective-permute-start | bytes 12582920 | tf_op jit(solution)/shard_map/ppermute | solution.py:231
  278.0 35.5 %collective-permute-start.13 = (bf16[640,512]{1,0:T(8,128)(2,1)}, bf16[640,512]{1,0:T(8,128)(2,1)}, u32[]{:S(2)}, u32[]{:S(2)}) collective-permute-start(bf16[640,512]{1,0:T(8,128)(2,1)} %collective-permute-done.12), channel_id=1, source_target_pairs={{1,2},{2,3},{5,6},{6,7},{9,10},{10,11},{13,14},{14,15},{17,18},{18... | collective-permute-start | bytes 1966088 | tf_op jit(solution)/shard_map/ppermute | solution.py:190
  283.9 29.6 %collective-permute-start.15 = (bf16[640,512]{1,0:T(8,128)(2,1)S(1)}, bf16[640,512]{1,0:T(8,128)(2,1)}, u32[]{:S(2)}, u32[]{:S(2)}) collective-permute-start(bf16[640,512]{1,0:T(8,128)(2,1)S(1)} %collective-permute-done.14), channel_id=1, source_target_pairs={{2,1},{1,0},{6,5},{5,4},{10,9},{9,8},{14,13},{13,12},{18,17},{17,1... | collective-permute-start | bytes 1966088 | tf_op jit(solution)/shard_map/ppermute | solution.py:191
  305.9 34.3 %collective-permute-start.21 = (bf16[320,2048]{1,0:T(8,128)(2,1)S(1)}, bf16[320,2048]{1,0:T(8,128)(2,1)S(1)}, u32[]{:S(2)}, u32[]{:S(2)}) collective-permute-start(bf16[320,2048]{1,0:T(8,128)(2,1)S(1)} %get-tuple-element.168), channel_id=1, source_target_pairs={{0,1},{3,2},{4,5},{7,6},{8,9},{11,10},{12,13},{15,14},{16,17},{19,... | collective-permute-start | bytes 3932168 | tf_op jit(solution)/shard_map/ppermute | solution.py:107
  333.7 33.6 %collective-permute-start.22 = (bf16[320,2048]{1,0:T(8,128)(2,1)S(1)}, bf16[320,2048]{1,0:T(8,128)(2,1)S(1)}, u32[]{:S(2)}, u32[]{:S(2)}) collective-permute-start(bf16[320,2048]{1,0:T(8,128)(2,1)S(1)} %get-tuple-element.176), channel_id=1, source_target_pairs={{0,1},{3,2},{4,5},{7,6},{8,9},{11,10},{12,13},{15,14},{16,17},{19,... | collective-permute-start | bytes 3932168 | tf_op jit(solution)/shard_map/ppermute | solution.py:107
  340.8 28.8 %collective-permute-start.23 = (bf16[320,2048]{1,0:T(8,128)(2,1)S(1)}, bf16[320,2048]{1,0:T(8,128)(2,1)S(1)}, u32[]{:S(2)}, u32[]{:S(2)}) collective-permute-start(bf16[320,2048]{1,0:T(8,128)(2,1)S(1)} %add_convert_fusion.15), channel_id=1, source_target_pairs={{1,2},{2,1},{5,6},{6,5},{9,10},{10,9},{13,14},{14,13},{17,18},{18,... | collective-permute-start | bytes 3932168 | tf_op jit(solution)/shard_map/ppermute | solution.py:129
  359.9 37.5 %collective-permute-start.25 = (bf16[320,2048]{1,0:T(8,128)(2,1)S(1)}, bf16[320,2048]{1,0:T(8,128)(2,1)}, u32[]{:S(2)}, u32[]{:S(2)}) collective-permute-start(bf16[320,2048]{1,0:T(8,128)(2,1)S(1)} %get-tuple-element.186), channel_id=1, source_target_pairs={{0,1},{3,2},{4,5},{7,6},{8,9},{11,10},{12,13},{15,14},{16,17},{19,... | collective-permute-start | bytes 3932168 | tf_op jit(solution)/shard_map/ppermute | solution.py:107
  367.9 33.2 %collective-permute-start.26 = (bf16[320,2048]{1,0:T(8,128)(2,1)S(1)}, bf16[320,2048]{1,0:T(8,128)(2,1)}, u32[]{:S(2)}, u32[]{:S(2)}) collective-permute-start(bf16[320,2048]{1,0:T(8,128)(2,1)S(1)} %add_convert_fusion.14), channel_id=1, source_target_pairs={{1,2},{2,1},{5,6},{6,5},{9,10},{10,9},{13,14},{14,13},{17,18},{18,... | collective-permute-start | bytes 3932168 | tf_op jit(solution)/shard_map/ppermute | solution.py:129
  370.1 34.3 %collective-permute-start.24 = (bf16[320,2048]{1,0:T(8,128)(2,1)S(1)}, bf16[320,2048]{1,0:T(8,128)(2,1)S(1)}, u32[]{:S(2)}, u32[]{:S(2)}) collective-permute-start(bf16[320,2048]{1,0:T(8,128)(2,1)S(1)} %add_convert_fusion.13), channel_id=1, source_target_pairs={{1,0},{2,3},{5,4},{6,7},{9,8},{10,11},{13,12},{14,15},{17,16},{18,... | collective-permute-start | bytes 3932168 | tf_op jit(solution)/shard_map/ppermute | solution.py:131
  389.6 42.1 %collective-permute-start.27 = (bf16[320,2048]{1,0:T(8,128)(2,1)S(1)}, bf16[320,2048]{1,0:T(8,128)(2,1)S(1)}, u32[]{:S(2)}, u32[]{:S(2)}) collective-permute-start(bf16[320,2048]{1,0:T(8,128)(2,1)S(1)} %get-tuple-element.193), channel_id=1, source_target_pairs={{0,1},{3,2},{4,5},{7,6},{8,9},{11,10},{12,13},{15,14},{16,17},{19,... | collective-permute-start | bytes 3932168 | tf_op jit(solution)/shard_map/ppermute | solution.py:107
  399.3 29.4 %collective-permute-start.29 = (bf16[320,2048]{1,0:T(8,128)(2,1)S(1)}, bf16[320,2048]{1,0:T(8,128)(2,1)}, u32[]{:S(2)}, u32[]{:S(2)}) collective-permute-start(bf16[320,2048]{1,0:T(8,128)(2,1)S(1)} %add_convert_fusion.12), channel_id=1, source_target_pairs={{1,2},{2,1},{5,6},{6,5},{9,10},{10,9},{13,14},{14,13},{17,18},{18,... | collective-permute-start | bytes 3932168 | tf_op jit(solution)/shard_map/ppermute | solution.py:129
  402.9 30.6 %collective-permute-start.28 = (bf16[320,2048]{1,0:T(8,128)(2,1)S(1)}, bf16[320,2048]{1,0:T(8,128)(2,1)S(1)}, u32[]{:S(2)}, u32[]{:S(2)}) collective-permute-start(bf16[320,2048]{1,0:T(8,128)(2,1)S(1)} %add_convert_fusion.11), channel_id=1, source_target_pairs={{1,0},{2,3},{5,4},{6,7},{9,8},{10,11},{13,12},{14,15},{17,16},{18,... | collective-permute-start | bytes 3932168 | tf_op jit(solution)/shard_map/ppermute | solution.py:131
  421.7 35.6 %collective-permute-start.32 = (bf16[320,2048]{1,0:T(8,128)(2,1)S(1)}, bf16[320,2048]{1,0:T(8,128)(2,1)}, u32[]{:S(2)}, u32[]{:S(2)}) collective-permute-start(bf16[320,2048]{1,0:T(8,128)(2,1)S(1)} %get-tuple-element.204), channel_id=1, source_target_pairs={{0,1},{3,2},{4,5},{7,6},{8,9},{11,10},{12,13},{15,14},{16,17},{19,... | collective-permute-start | bytes 3932168 | tf_op jit(solution)/shard_map/ppermute | solution.py:107
  430.5 32.5 %collective-permute-start.31 = (bf16[320,2048]{1,0:T(8,128)(2,1)S(1)}, bf16[320,2048]{1,0:T(8,128)(2,1)S(1)}, u32[]{:S(2)}, u32[]{:S(2)}) collective-permute-start(bf16[320,2048]{1,0:T(8,128)(2,1)S(1)} %add_convert_fusion.9), channel_id=1, source_target_pairs={{1,0},{2,3},{5,4},{6,7},{9,8},{10,11},{13,12},{14,15},{17,16},{18,... | collective-permute-start | bytes 3932168 | tf_op jit(solution)/shard_map/ppermute | solution.py:131
  432.3 28.7 %collective-permute-start.30 = (bf16[320,2048]{1,0:T(8,128)(2,1)S(1)}, bf16[320,2048]{1,0:T(8,128)(2,1)S(1)}, u32[]{:S(2)}, u32[]{:S(2)}) collective-permute-start(bf16[320,2048]{1,0:T(8,128)(2,1)S(1)} %add_convert_fusion.10), channel_id=1, source_target_pairs={{1,2},{2,1},{5,6},{6,5},{9,10},{10,9},{13,14},{14,13},{17,18},{18,... | collective-permute-start | bytes 3932168 | tf_op jit(solution)/shard_map/ppermute | solution.py:129
  450.5 34.1 %collective-permute-start.34 = (bf16[320,2048]{1,0:T(8,128)(2,1)S(1)}, bf16[320,2048]{1,0:T(8,128)(2,1)}, u32[]{:S(2)}, u32[]{:S(2)}) collective-permute-start(bf16[320,2048]{1,0:T(8,128)(2,1)S(1)} %get-tuple-element.212), channel_id=1, source_target_pairs={{0,1},{3,2},{4,5},{7,6},{8,9},{11,10},{12,13},{15,14},{16,17},{19,... | collective-permute-start | bytes 3932168 | tf_op jit(solution)/shard_map/ppermute | solution.py:107
  459.2 29.0 %collective-permute-start.35 = (bf16[320,2048]{1,0:T(8,128)(2,1)S(1)}, bf16[320,2048]{1,0:T(8,128)(2,1)}, u32[]{:S(2)}, u32[]{:S(2)}) collective-permute-start(bf16[320,2048]{1,0:T(8,128)(2,1)S(1)} %add_convert_fusion.7), channel_id=1, source_target_pairs={{1,2},{2,1},{5,6},{6,5},{9,10},{10,9},{13,14},{14,13},{17,18},{18,... | collective-permute-start | bytes 3932168 | tf_op jit(solution)/shard_map/ppermute | solution.py:129
  461.5 30.1 %collective-permute-start.33 = (bf16[320,2048]{1,0:T(8,128)(2,1)S(1)}, bf16[320,2048]{1,0:T(8,128)(2,1)S(1)}, u32[]{:S(2)}, u32[]{:S(2)}) collective-permute-start(bf16[320,2048]{1,0:T(8,128)(2,1)S(1)} %add_convert_fusion.8), channel_id=1, source_target_pairs={{1,0},{2,3},{5,4},{6,7},{9,8},{10,11},{13,12},{14,15},{17,16},{18,... | collective-permute-start | bytes 3932168 | tf_op jit(solution)/shard_map/ppermute | solution.py:131
  479.9 34.4 %collective-permute-start.37 = (bf16[320,2048]{1,0:T(8,128)(2,1)S(1)}, bf16[320,2048]{1,0:T(8,128)(2,1)S(1)}, u32[]{:S(2)}, u32[]{:S(2)}) collective-permute-start(bf16[320,2048]{1,0:T(8,128)(2,1)S(1)} %get-tuple-element.223), channel_id=1, source_target_pairs={{0,1},{3,2},{4,5},{7,6},{8,9},{11,10},{12,13},{15,14},{16,17},{19,... | collective-permute-start | bytes 3932168 | tf_op jit(solution)/shard_map/ppermute | solution.py:107
  486.5 29.1 %collective-permute-start.38 = (bf16[320,2048]{1,0:T(8,128)(2,1)S(1)}, bf16[320,2048]{1,0:T(8,128)(2,1)}, u32[]{:S(2)}, u32[]{:S(2)}) collective-permute-start(bf16[320,2048]{1,0:T(8,128)(2,1)S(1)} %add_convert_fusion.6), channel_id=1, source_target_pairs={{1,2},{2,1},{5,6},{6,5},{9,10},{10,9},{13,14},{14,13},{17,18},{18,... | collective-permute-start | bytes 3932168 | tf_op jit(solution)/shard_map/ppermute | solution.py:129
  490.1 28.6 %collective-permute-start.36 = (bf16[320,2048]{1,0:T(8,128)(2,1)S(1)}, bf16[320,2048]{1,0:T(8,128)(2,1)S(1)}, u32[]{:S(2)}, u32[]{:S(2)}) collective-permute-start(bf16[320,2048]{1,0:T(8,128)(2,1)S(1)} %add_convert_fusion.5), channel_id=1, source_target_pairs={{1,0},{2,3},{5,4},{6,7},{9,8},{10,11},{13,12},{14,15},{17,16},{18,... | collective-permute-start | bytes 3932168 | tf_op jit(solution)/shard_map/ppermute | solution.py:131
  508.6 34.6 %collective-permute-start.39 = (bf16[320,2048]{1,0:T(8,128)(2,1)S(1)}, bf16[320,2048]{1,0:T(8,128)(2,1)}, u32[]{:S(2)}, u32[]{:S(2)}) collective-permute-start(bf16[320,2048]{1,0:T(8,128)(2,1)S(1)} %get-tuple-element.229), channel_id=1, source_target_pairs={{0,1},{3,2},{4,5},{7,6},{8,9},{11,10},{12,13},{15,14},{16,17},{19,... | collective-permute-start | bytes 3932168 | tf_op jit(solution)/shard_map/ppermute | solution.py:107
  600.0 35.5 %all-to-all-start.2 = ((bf16[8,640,128]{2,1,0:T(8,128)(2,1)}), bf16[8,640,128]{2,1,0:T(8,128)(2,1)S(1)}, u32[]{:S(2)}, u32[]{:S(2)}) async-start(bf16[8,640,128]{2,1,0:T(8,128)(2,1)} %bitcast.27), calls=%async_computation.2 | async-start | bytes 2621440 | tf_op jit(solution)/shard_map/all_to_all | solution.py:1300
  617.3 274.8 %reduce-scatter.5.cloned.1.call-start = ((), (), s32[]{:S(2)}) async-start(), calls=%async_computation.9 | async-start | bytes 9437184 | tf_op jit(solution)/shard_map/reduce_scatter | solution.py:1292
  789.3 29.3 %collective-permute-start.47 = (bf16[160,2048]{1,0:T(8,128)(2,1)}, bf16[160,2048]{1,0:T(8,128)(2,1)}, u32[]{:S(2)}, u32[]{:S(2)}) collective-permute-start(bf16[160,2048]{1,0:T(8,128)(2,1)} %get-tuple-element.356), channel_id=1, source_target_pairs={{0,1},{4,5},{8,9},{12,13},{16,17},{20,21},{24,25},{28,29}} | collective-permute-start | bytes 1966088 | tf_op jit(solution)/shard_map/ppermute | solution.py:169
  846.8 28.8 %collective-permute-start.51 = (bf16[160,2048]{1,0:T(8,128)(2,1)}, bf16[160,2048]{1,0:T(8,128)(2,1)}, u32[]{:S(2)}, u32[]{:S(2)}) collective-permute-start(bf16[160,2048]{1,0:T(8,128)(2,1)} %get-tuple-element.350), channel_id=1, source_target_pairs={{0,1},{1,2},{2,3},{4,5},{5,6},{6,7},{8,9},{9,10},{10,11},{12,13},{... | collective-permute-start | bytes 1966088 | tf_op jit(solution)/shard_map/ppermute | solution.py:166
  (68 other events, 1008.7 us)
Sparse Core Ops, SparseCore 0:
  10.7 57.0 all-gather.4
  69.7 77.0 all-gather.8
  173.0 102.4 all-gather.6
  600.1 212.0 reduce-scatter.2
  818.8 70.6 reduce-scatter.4

commit v7 on v6

--- a/solution.py
+++ b/solution.py
@@ -24,7 +24,7 @@
 EPSILON = 1e-06
 ROPE_BASE = 500000.0
 SCALING = HEAD ** (-0.5)
-VMEM_LIMIT = 50 * 1024 * 1024
+VMEM_LIMIT = 42 * 1024 * 1024
 
 f32 = jnp.float32
 bf16 = jnp.bfloat16

time: 923 us -> 944 us (1.023)
  local copies, waits for them, and re-layouts: 31.6 us -> 63.8 us
  Pallas kernels: 331 us -> 313 us
    unnamed x68 -> x110, local copies, waits for them, and re-layouts: 13.6 us -> 48 us
    pallas_call x19, Pallas kernels: 251 us -> 238 us  [chunk_call(): pl.pallas_call(body, grid=grid, in_specs=specs, out_specs=[out[0] for out...]
  transfers between devices with their start and end apart: 70 -> 70, of which waited for: 23 -> 23; matrix products, arithmetic and copies ran while one was open for 8% -> 9% of each run, Pallas kernels for 36% -> 33%
where the time goes in v7:
time: 944 us; the launch traced here: 934 us
  Pallas kernels  313 us (33%)
  waiting for transfers between devices  201 us (21%)
  starting transfers between devices  183 us (19%)
  blocking collectives  92 us (10%)
  other arithmetic  66.4 us (7%)
  local copies, waits for them, and re-layouts  63.8 us (7%)
  between operations  15.3 us (2%)
    pallas_call x19, Pallas kernels, chunk_call(): pl.pallas_call(body, grid=grid, in_specs=specs, out_specs=[out[0] for out...  238 us
    all_to_all x1, blocking collectives, give_back(): lax.all_to_all(flat, 'dp', split_axis=0, concat_axis=0, tiled=True)[:items]  92 us
    ppermute x8, starting transfers between devices, enter(): self.inward.append(lax.ppermute(term, 'tensor', [(0, 1), (3, 2)]))  54.5 us
    all_gather x3, waiting for transfers between devices, gather_stack(): return lax.all_gather(jnp.stack(pieces), 'dp', axis=1, tiled=True)  52.5 us
    unnamed x110, local copies, waits for them, and re-layouts  48 us
    ppermute x3, waiting for transfers between devices, go_on_all_gather(): left = lax.ppermute(first[1], 'tensor', [(2, 1), (1, 0)])  37.3 us
    convert_element_type x20, other arithmetic, low_sum(): return total.astype(bf16)  31.5 us
    pallas_call x1, Pallas kernels, attend_backward(): pl.pallas_call(functools.partial(backward_kernel, trees), in_specs=[pl.Bl...  28.7 us
  transfers between devices with their start and end apart: 70, of which 23 were waited for; matrix products, arithmetic and copies ran while one was open for 9% of the time, Pallas kernels for 33%

profile of v7, /device:TPU:0, one launch (start us, length us, event | category | flops | bytes accessed | tf_op | source)
XLA Modules:
  0.0 934.1 jit_solution(2155931343386666830)
XLA Ops:
  15.3 52.5 %all-gather.5.cloned.1.call-done.refs_0_.refs_1_.refs_4_.refs_8_.refs_9_.refs_10_ = bf16[4,2048,512]{2,1,0:T(8,128)(2,1)} async-done(((bf16[4,256,512]{2,1,0:T(8,128)(2,1)}), bf16[4,2048,512]{2,1,0:T(8,128)(2,1)}) %all-gather.5.cloned.1.call-update) | async-done | bytes 8388624 | tf_op jit(solution)/shard_map/all_gather | solution.py:1289
  70.3 8.6 project.2
  98.0 8.3 pack_heads.1
  122.6 20.4 %collective-permute-done.2 = bf16[1024,512]{1,0:T(8,128)(2,1)} collective-permute-done((bf16[1024,512]{1,0:T(8,128)(2,1)S(1)}, bf16[1024,512]{1,0:T(8,128)(2,1)}, u32[]{:S(2)}, u32[]{:S(2)}) %collective-permute-start.2) | collective-permute-done | bytes 1048608 | tf_op jit(solution)/shard_map/ppermute | solution.py:181
  150.1 24.2 %collective-permute-done.5 = bf16[1024,512]{1,0:T(8,128)(2,1)} collective-permute-done((bf16[1024,512]{1,0:T(8,128)(2,1)S(1)}, bf16[1024,512]{1,0:T(8,128)(2,1)}, u32[]{:S(2)}, u32[]{:S(2)}) %collective-permute-start.5) | collective-permute-done | bytes 1048608 | tf_op jit(solution)/shard_map/ppermute | solution.py:191
  182.2 17.1 %attend_forward.1 = bf16[8,5,128,128]{3,2,1,0:T(8,128)(2,1)} custom-call(s32[40]{0:T(128)S(1)} %fusion.22.order_ref, bf16[8,3,5,128,128]{4,3,2,1,0:T(8,128)(2,1)} %bitcast.17.x_ref), custom_call_target="tpu_custom_call" | custom-call | flops 2883584000 | bytes 5898240 | tf_op jit(solution)/shard_map/attend_forward/pallas_call | solution.py:541
  209.9 15.1 %all-to-all-done.1 = bf16[8,640,128]{2,1,0:T(8,128)(2,1)S(1)} async-done(((bf16[8,640,128]{2,1,0:T(8,128)(2,1)}), bf16[8,640,128]{2,1,0:T(8,128)(2,1)S(1)}, u32[]{:S(2)}, u32[]{:S(2)}) %all-to-all-start.1) | async-done | bytes 1310752 | tf_op jit(solution)/shard_map/all_to_all | solution.py:1304
  232.1 9.8 %collective-permute-done.9 = bf16[640,512]{1,0:T(8,128)(2,1)S(1)} collective-permute-done((bf16[640,512]{1,0:T(8,128)(2,1)S(1)}, bf16[640,512]{1,0:T(8,128)(2,1)S(1)}, u32[]{:S(2)}, u32[]{:S(2)}) %collective-permute-start.9) | collective-permute-done | bytes 655392 | tf_op jit(solution)/shard_map/ppermute | solution.py:182
  244.7 13.0 %collective-permute-done.10 = bf16[640,512]{1,0:T(8,128)(2,1)S(1)} collective-permute-done((bf16[640,512]{1,0:T(8,128)(2,1)S(1)}, bf16[640,512]{1,0:T(8,128)(2,1)S(1)}, u32[]{:S(2)}, u32[]{:S(2)}) %collective-permute-start.10) | collective-permute-done | bytes 655392 | tf_op jit(solution)/shard_map/ppermute | solution.py:191
  261.7 10.4 %collective-permute-done.11 = bf16[640,512]{1,0:T(8,128)(2,1)} collective-permute-done((bf16[640,512]{1,0:T(8,128)(2,1)S(1)}, bf16[640,512]{1,0:T(8,128)(2,1)}, u32[]{:S(2)}, u32[]{:S(2)}) %collective-permute-start.11) | collective-permute-done | bytes 655392 | tf_op jit(solution)/shard_map/ppermute | solution.py:203
  291.5 18.7 %forward_chunk.4 = (bf16[1280,2048]{1,0:T(8,128)(2,1)}, bf16[1280,2048]{1,0:T(8,128)(2,1)}, bf16[1280,2048]{1,0:T(8,128)(2,1)}, bf16[1280,2048]{1,0:T(8,128)(2,1...) custom-call(s32[1]{0:T(128)} %bitcast.2.refs_0_, f32[1,2048]{1,0:T(1,128)S(1)} %bitcast.183, ...), custom_call_target="tpu_custom_call" | custom-call | flops 10737418240 | bytes 44040192 | tf_op jit(solution)/shard_map/forward_chunk/pallas_call | solution.py:705
  319.9 18.2 %forward_chunk.5 = (bf16[1280,2048]{1,0:T(8,128)(2,1)}, bf16[1280,2048]{1,0:T(8,128)(2,1)}, bf16[1280,2048]{1,0:T(8,128)(2,1)}, bf16[1280,2048]{1,0:T(8,128)(2,1...) custom-call(s32[1]{0:T(128)} %bitcast.2.refs_0_, ...), custom_call_target="tpu_custom_call", output_to_operand_aliasing={{0}: (8, {}), {1}: (9, {}), {2}: (10, {}), {3}: (11, {}), {... | custom-call | flops 10737418240 | bytes 44040192 | tf_op jit(solution)/shard_map/forward_chunk/pallas_call | solution.py:705
  347.1 18.2 %forward_chunk.6 = (bf16[1280,2048]{1,0:T(8,128)(2,1)}, bf16[1280,2048]{1,0:T(8,128)(2,1)}, bf16[1280,2048]{1,0:T(8,128)(2,1)}, bf16[1280,2048]{1,0:T(8,128)(2,1...) custom-call(s32[1]{0:T(128)} %bitcast.2.refs_0_, ...), custom_call_target="tpu_custom_call", output_to_operand_aliasing={{0}: (8, {}), {1}: (9, {}), {2}: (10, {}), {3}: (11, {}), {... | custom-call | flops 10737418240 | bytes 44040192 | tf_op jit(solution)/shard_map/forward_chunk/pallas_call | solution.py:705
  376.0 18.2 %forward_chunk.7 = (bf16[1280,2048]{1,0:T(8,128)(2,1)}, bf16[1280,2048]{1,0:T(8,128)(2,1)}, bf16[1280,2048]{1,0:T(8,128)(2,1)}, bf16[1280,2048]{1,0:T(8,128)(2,1...) custom-call(s32[1]{0:T(128)} %bitcast.2.refs_0_, ...), custom_call_target="tpu_custom_call", output_to_operand_aliasing={{0}: (8, {}), {1}: (9, {}), {2}: (10, {}), {3}: (11, {}), {... | custom-call | flops 10737418240 | bytes 44040192 | tf_op jit(solution)/shard_map/forward_chunk/pallas_call | solution.py:705
  394.2 8.8 collective-permute-start.27
  407.9 16.9 %middle_chunk.4 = (bf16[1280,2048]{1,0:T(8,128)(2,1)}, bf16[1280,2048]{1,0:T(8,128)(2,1)S(1)}, bf16[1280,2048]{1,0:T(8,128)(2,1)}, bf16[1280,2048]{1,0:T(8,128)(...) custom-call(f32[1,2048]{1,0:T(1,128)S(1)} %bitcast.187, f32[1,2048]{1,0:T(1,128)S(1)} %bitcast.196, ...), custom_call_target="tpu_custom_call" | custom-call | flops 8053063680 | bytes 40894464 | tf_op jit(solution)/shard_map/middle_chunk/pallas_call | solution.py:705
  433.7 16.6 %middle_chunk.5 = (bf16[1280,2048]{1,0:T(8,128)(2,1)}, bf16[1280,2048]{1,0:T(8,128)(2,1)S(1)}, bf16[1280,2048]{1,0:T(8,128)(2,1)}, bf16[1280,2048]{1,0:T(8,128)(...) custom-call(f32[1,2048]{1,0:T(1,128)S(1)} %bitcast.188, ...), custom_call_target="tpu_custom_call", output_to_operand_aliasing={{0}: (10, {}), {1}: (11, {}), {2}: (12, {}), {3}: (13, {})} | custom-call | flops 8053063680 | bytes 40894464 | tf_op jit(solution)/shard_map/middle_chunk/pallas_call | solution.py:705
  460.3 16.7 %middle_chunk.6 = (bf16[1280,2048]{1,0:T(8,128)(2,1)}, bf16[1280,2048]{1,0:T(8,128)(2,1)S(1)}, bf16[1280,2048]{1,0:T(8,128)(2,1)}, bf16[1280,2048]{1,0:T(8,128)(...) custom-call(f32[1,2048]{1,0:T(1,128)S(1)} %bitcast.189, ...), custom_call_target="tpu_custom_call", output_to_operand_aliasing={{0}: (10, {}), {1}: (11, {}), {2}: (12, {}), {3}: (13, {})} | custom-call | flops 8053063680 | bytes 40894464 | tf_op jit(solution)/shard_map/middle_chunk/pallas_call | solution.py:705
  488.5 16.7 %middle_chunk.7 = (bf16[1280,2048]{1,0:T(8,128)(2,1)}, bf16[1280,2048]{1,0:T(8,128)(2,1)S(1)}, bf16[1280,2048]{1,0:T(8,128)(2,1)}, bf16[1280,2048]{1,0:T(8,128)(...) custom-call(f32[1,2048]{1,0:T(1,128)S(1)} %bitcast.190, ...), custom_call_target="tpu_custom_call", output_to_operand_aliasing={{0}: (10, {}), {1}: (11, {}), {2}: (12, {}), {3}: (13, {})} | custom-call | flops 8053063680 | bytes 40894464 | tf_op jit(solution)/shard_map/middle_chunk/pallas_call | solution.py:705
  505.2 8.9 collective-permute-start.39
  531.7 13.4 %weight_sum.5.refs_2_ = bf16[3,2048,2048]{2,1,0:T(8,128)(2,1)} custom-call(bf16[1280,2048]{1,0:T(8,128)(2,1)S(1)} %copy-done.7, bf16[1280,2048]{1,0:T(8,128)(2,1)S(1)} %copy-done.9), custom_call_target="tpu_custom_call" | custom-call | flops 10737418240 | bytes 18874368 | tf_op jit(solution)/shard_map/weight_sum/pallas_call | solution.py:705
  566.0 13.4 %weight_sum.6.refs_2_ = bf16[3,2048,2048]{2,1,0:T(8,128)(2,1)} custom-call(bf16[1280,2048]{1,0:T(8,128)(2,1)S(1)} %copy-done.8, bf16[1280,2048]{1,0:T(8,128)(2,1)S(1)} %copy-done.6, bf16[3,2048,2048]{2,1,0:T(8,128)(2,1)} %weight_sum.5.refs_2_), custom_call_target="tpu_custom_call", output_to_operand_aliasing={{}: (2, {})} | custom-call | flops 10737418240 | bytes 18874368 | tf_op jit(solution)/shard_map/weight_sum/pallas_call | solution.py:705
  592.1 13.4 %weight_sum.7 = bf16[3,2048,2048]{2,1,0:T(8,128)(2,1)} custom-call(bf16[1280,2048]{1,0:T(8,128)(2,1)S(1)} %get-tuple-element.247.refs_0_, bf16[1280,2048]{1,0:T(8,128)(2,1)S(1)} %bitcast.166, bf16[3,2048,2048]{2,1,0:T(8,128)(2,1)} %weight_sum.6.refs_2_), custom_call_target="tpu_custom_call", output_to_operand_aliasing={{}: (2, {})} | custom-call | flops 10737418240 | bytes 18874368 | tf_op jit(solution)/shard_map/weight_sum/pallas_call | solution.py:705
  616.5 17.2 %all-to-all-start.2 = ((bf16[8,640,128]{2,1,0:T(8,128)(2,1)}), bf16[8,640,128]{2,1,0:T(8,128)(2,1)S(1)}, u32[]{:S(2)}, u32[]{:S(2)}) async-start(bf16[8,640,128]{2,1,0:T(8,128)(2,1)} %bitcast.27), calls=%async_computation.2 | async-start | bytes 2621440 | tf_op jit(solution)/shard_map/all_to_all | solution.py:1300
  641.0 10.9 %all-to-all-done.2 = bf16[8,640,128]{2,1,0:T(8,128)(2,1)S(1)} async-done(((bf16[8,640,128]{2,1,0:T(8,128)(2,1)}), bf16[8,640,128]{2,1,0:T(8,128)(2,1)S(1)}, u32[]{:S(2)}, u32[]{:S(2)}) %all-to-all-start.2) | async-done | bytes 1310752 | tf_op jit(solution)/shard_map/all_to_all | solution.py:1300
  651.9 28.7 %attend_backward.1 = bf16[8,3,5,128,128]{4,3,2,1,0:T(8,128)(2,1)S(1)} custom-call(s32[40]{0:T(128)S(1)} %copy-done.31, bf16[8,3,5,128,128]{4,3,2,1,0:T(8,128)(2,1)} %bitcast.17.x_ref, bf16[8,5,128,128]{3,2,1,0:T(8,128)(2,1)S(1)} %bitcast.182), custom_call_target="tpu_custom_call" | custom-call | flops 7208960000 | bytes 9830400 | tf_op jit(solution)/shard_map/attend_backward/pallas_call | solution.py:654
  680.7 92.0 %all_to_all.20 = bf16[8,1920,128]{2,1,0:T(8,128)(2,1)} all-to-all(bf16[8,1920,128]{2,1,0:T(8,128)(2,1)S(1)} %bitcast.181), channel_id=1, replica_groups=mesh['dp'=8,'tensor'=4] {'dp'}, dimensions={0} | all-to-all | bytes 7864320 | tf_op jit(solution)/shard_map/all_to_all | solution.py:1304
  796.3 9.2 unpack_heads.2
  812.3 9.7 %unpack_heads.3 = (bf16[1280,1536]{1,0:T(8,128)(2,1)}, bf16[640,2048]{1,0:T(8,128)(2,1)S(1)}) custom-call(bf16[4,2,3,640,128]{4,3,2,1,0:T(8,128)(2,1)} %bitcast.214, f32[2,640,512]{2,1,0:T(8,128)S(1)} %copy-done.11, f32[2,640,512]{2,1,0:T(8,128)S(1)} %copy-done.13, f32[2,640,2]{2,1,0:T(8,128)S(1)} %bitcast.170, ...), custom_call_target="tpu_custom_call", output_to_operand_aliasing={{0}: (11, {})} | custom-call | flops 4026531840 | bytes 10485760 | tf_op jit(solution)/shard_map/unpack_heads/pallas_call | solution.py:705
  825.6 10.5 %weight_sum.9 = bf16[4,2048,512]{2,1,0:T(8,128)(2,1)} custom-call(bf16[1280,2048]{1,0:T(8,128)(2,1)S(1)} %bitcast.164, bf16[1280,1536]{1,0:T(8,128)(2,1)S(1)} %copy-done.26, bf16[4,2048,512]{2,1,0:T(8,128)(2,1)} %weight_sum.8.refs_2_), custom_call_target="tpu_custom_call", output_to_operand_aliasing={{}: (2, {})} | custom-call | flops 8053063680 | bytes 25952256 | tf_op jit(solution)/shard_map/weight_sum/pallas_call | solution.py:705
  853.1 9.1 collective-permute-done.49
  897.8 9.6 %collective-permute-start.57 = (bf16[160,2048]{1,0:T(8,128)(2,1)}, bf16[160,2048]{1,0:T(8,128)(2,1)}, u32[]{:S(2)}, u32[]{:S(2)}) collective-permute-start(bf16[160,2048]{1,0:T(8,128)(2,1)} %get-tuple-element.347), channel_id=1, source_target_pairs={{0,1},{1,2},{2,3},{4,5},{5,6},{6,7},{8,9},{9,10},{10,11},{12,13},{... | collective-permute-start | bytes 1966088 | tf_op jit(solution)/shard_map/ppermute | solution.py:166
  (338 shorter events, 344.2 us)
Async XLA Ops:
  7.2 60.6 %all-gather.5.cloned.1.call-start = ((), (), s32[]{:S(2)}) async-start(), calls=%async_computation.6 | async-start | bytes 9437184 | tf_op jit(solution)/shard_map/all_gather | solution.py:1289
  10.6 279.2 %all-gather.9.cloned.1.call-start = ((), (), s32[]{:S(2)}) async-start(), calls=%async_computation.10 | async-start | bytes 9437184 | tf_op jit(solution)/shard_map/all_gather | solution.py:1289
  106.4 68.0 %all-to-all-start = ((bf16[8,1920,128]{2,1,0:T(8,128)(2,1)}), bf16[8,1920,128]{2,1,0:T(8,128)(2,1)}, u32[]{:S(2)}, u32[]{:S(2)}) async-start(bf16[8,1920,128]{2,1,0:T(8,128)(2,1)} %bitcast.216), calls=%async_computation | async-start | bytes 7864320 | tf_op jit(solution)/shard_map/all_to_all | solution.py:1300
  110.9 178.9 %all-gather.7.cloned.1.call-start = ((), (), s32[]{:S(2)}) async-start(), calls=%async_computation.7 | async-start | bytes 18874368 | tf_op jit(solution)/shard_map/all_gather | solution.py:1289
  180.0 28.6 %collective-permute-start.17 = (bf16[1024,512]{1,0:T(8,128)(2,1)}, bf16[1024,512]{1,0:T(8,128)(2,1)}, u32[]{:S(2)}, u32[]{:S(2)}) collective-permute-start(bf16[1024,512]{1,0:T(8,128)(2,1)} %collective-permute-done.4), channel_id=1, source_target_pairs={{2,3},{6,7},{10,11},{14,15},{18,19},{22,23},{26,27},{30,31}} | collective-permute-start | bytes 3145736 | tf_op jit(solution)/shard_map/ppermute | solution.py:202
  203.2 633.0 %reduce-scatter.3.cloned.1.call-start = ((), (), s32[]{:S(2)}) async-start(), calls=%async_computation.8 | async-start | bytes 28311552 | tf_op jit(solution)/shard_map/reduce_scatter | solution.py:1292
  209.8 80.0 %collective-permute-start.18 = (bf16[1024,2048]{1,0:T(8,128)(2,1)}, bf16[1024,2048]{1,0:T(8,128)(2,1)}, u32[]{:S(2)}, u32[]{:S(2)}) collective-permute-start(bf16[1024,2048]{1,0:T(8,128)(2,1)} %select_dynamic-update-slice_fusion.refs_4_), channel_id=1, source_target_pairs={{0,4},{4,0},{8,12},{12,8},{16,20},{20,16},{24,28},{28,24},{1,5},{5... | collective-permute-start | bytes 12582920 | tf_op jit(solution)/shard_map/ppermute | solution.py:231
  282.5 35.4 %collective-permute-start.13 = (bf16[640,512]{1,0:T(8,128)(2,1)}, bf16[640,512]{1,0:T(8,128)(2,1)}, u32[]{:S(2)}, u32[]{:S(2)}) collective-permute-start(bf16[640,512]{1,0:T(8,128)(2,1)} %collective-permute-done.12), channel_id=1, source_target_pairs={{1,2},{2,3},{5,6},{6,7},{9,10},{10,11},{13,14},{14,15},{17,18},{18... | collective-permute-start | bytes 1966088 | tf_op jit(solution)/shard_map/ppermute | solution.py:190
  288.3 29.6 %collective-permute-start.15 = (bf16[640,512]{1,0:T(8,128)(2,1)S(1)}, bf16[640,512]{1,0:T(8,128)(2,1)}, u32[]{:S(2)}, u32[]{:S(2)}) collective-permute-start(bf16[640,512]{1,0:T(8,128)(2,1)S(1)} %collective-permute-done.14), channel_id=1, source_target_pairs={{2,1},{1,0},{6,5},{5,4},{10,9},{9,8},{14,13},{13,12},{18,17},{17,1... | collective-permute-start | bytes 1966088 | tf_op jit(solution)/shard_map/ppermute | solution.py:191
  310.2 34.4 %collective-permute-start.21 = (bf16[320,2048]{1,0:T(8,128)(2,1)S(1)}, bf16[320,2048]{1,0:T(8,128)(2,1)S(1)}, u32[]{:S(2)}, u32[]{:S(2)}) collective-permute-start(bf16[320,2048]{1,0:T(8,128)(2,1)S(1)} %get-tuple-element.168), channel_id=1, source_target_pairs={{0,1},{3,2},{4,5},{7,6},{8,9},{11,10},{12,13},{15,14},{16,17},{19,... | collective-permute-start | bytes 3932168 | tf_op jit(solution)/shard_map/ppermute | solution.py:107
  338.1 32.5 %collective-permute-start.22 = (bf16[320,2048]{1,0:T(8,128)(2,1)S(1)}, bf16[320,2048]{1,0:T(8,128)(2,1)S(1)}, u32[]{:S(2)}, u32[]{:S(2)}) collective-permute-start(bf16[320,2048]{1,0:T(8,128)(2,1)S(1)} %get-tuple-element.176), channel_id=1, source_target_pairs={{0,1},{3,2},{4,5},{7,6},{8,9},{11,10},{12,13},{15,14},{16,17},{19,... | collective-permute-start | bytes 3932168 | tf_op jit(solution)/shard_map/ppermute | solution.py:107
  345.1 27.8 %collective-permute-start.23 = (bf16[320,2048]{1,0:T(8,128)(2,1)S(1)}, bf16[320,2048]{1,0:T(8,128)(2,1)}, u32[]{:S(2)}, u32[]{:S(2)}) collective-permute-start(bf16[320,2048]{1,0:T(8,128)(2,1)S(1)} %add_convert_fusion.15), channel_id=1, source_target_pairs={{1,2},{2,1},{5,6},{6,5},{9,10},{10,9},{13,14},{14,13},{17,18},{18,... | collective-permute-start | bytes 3932168 | tf_op jit(solution)/shard_map/ppermute | solution.py:129
  365.3 37.7 %collective-permute-start.25 = (bf16[320,2048]{1,0:T(8,128)(2,1)S(1)}, bf16[320,2048]{1,0:T(8,128)(2,1)S(1)}, u32[]{:S(2)}, u32[]{:S(2)}) collective-permute-start(bf16[320,2048]{1,0:T(8,128)(2,1)S(1)} %get-tuple-element.186), channel_id=1, source_target_pairs={{0,1},{3,2},{4,5},{7,6},{8,9},{11,10},{12,13},{15,14},{16,17},{19,... | collective-permute-start | bytes 3932168 | tf_op jit(solution)/shard_map/ppermute | solution.py:107
  371.1 33.2 %collective-permute-start.26 = (bf16[320,2048]{1,0:T(8,128)(2,1)S(1)}, bf16[320,2048]{1,0:T(8,128)(2,1)}, u32[]{:S(2)}, u32[]{:S(2)}) collective-permute-start(bf16[320,2048]{1,0:T(8,128)(2,1)S(1)} %add_convert_fusion.14), channel_id=1, source_target_pairs={{1,2},{2,1},{5,6},{6,5},{9,10},{10,9},{13,14},{14,13},{17,18},{18,... | collective-permute-start | bytes 3932168 | tf_op jit(solution)/shard_map/ppermute | solution.py:129
  374.7 33.0 %collective-permute-start.24 = (bf16[320,2048]{1,0:T(8,128)(2,1)S(1)}, bf16[320,2048]{1,0:T(8,128)(2,1)S(1)}, u32[]{:S(2)}, u32[]{:S(2)}) collective-permute-start(bf16[320,2048]{1,0:T(8,128)(2,1)S(1)} %add_convert_fusion.13), channel_id=1, source_target_pairs={{1,0},{2,3},{5,4},{6,7},{9,8},{10,11},{13,12},{14,15},{17,16},{18,... | collective-permute-start | bytes 3932168 | tf_op jit(solution)/shard_map/ppermute | solution.py:131
  394.2 37.6 %collective-permute-start.27 = (bf16[320,2048]{1,0:T(8,128)(2,1)S(1)}, bf16[320,2048]{1,0:T(8,128)(2,1)S(1)}, u32[]{:S(2)}, u32[]{:S(2)}) collective-permute-start(bf16[320,2048]{1,0:T(8,128)(2,1)S(1)} %get-tuple-element.193), channel_id=1, source_target_pairs={{0,1},{3,2},{4,5},{7,6},{8,9},{11,10},{12,13},{15,14},{16,17},{19,... | collective-permute-start | bytes 3932168 | tf_op jit(solution)/shard_map/ppermute | solution.py:107
  424.8 32.0 %collective-permute-start.32 = (bf16[320,2048]{1,0:T(8,128)(2,1)S(1)}, bf16[320,2048]{1,0:T(8,128)(2,1)S(1)}, u32[]{:S(2)}, u32[]{:S(2)}) collective-permute-start(bf16[320,2048]{1,0:T(8,128)(2,1)S(1)} %get-tuple-element.204), channel_id=1, source_target_pairs={{0,1},{3,2},{4,5},{7,6},{8,9},{11,10},{12,13},{15,14},{16,17},{19,... | collective-permute-start | bytes 3932168 | tf_op jit(solution)/shard_map/ppermute | solution.py:107
  430.4 29.7 %collective-permute-start.31 = (bf16[320,2048]{1,0:T(8,128)(2,1)S(1)}, bf16[320,2048]{1,0:T(8,128)(2,1)S(1)}, u32[]{:S(2)}, u32[]{:S(2)}) collective-permute-start(bf16[320,2048]{1,0:T(8,128)(2,1)S(1)} %add_convert_fusion.9), channel_id=1, source_target_pairs={{1,0},{2,3},{5,4},{6,7},{9,8},{10,11},{13,12},{14,15},{17,16},{18,... | collective-permute-start | bytes 3932168 | tf_op jit(solution)/shard_map/ppermute | solution.py:131
  450.3 34.8 %collective-permute-start.34 = (bf16[320,2048]{1,0:T(8,128)(2,1)S(1)}, bf16[320,2048]{1,0:T(8,128)(2,1)S(1)}, u32[]{:S(2)}, u32[]{:S(2)}) collective-permute-start(bf16[320,2048]{1,0:T(8,128)(2,1)S(1)} %get-tuple-element.212), channel_id=1, source_target_pairs={{0,1},{3,2},{4,5},{7,6},{8,9},{11,10},{12,13},{15,14},{16,17},{19,... | collective-permute-start | bytes 3932168 | tf_op jit(solution)/shard_map/ppermute | solution.py:107
  457.3 29.0 %collective-permute-start.35 = (bf16[320,2048]{1,0:T(8,128)(2,1)S(1)}, bf16[320,2048]{1,0:T(8,128)(2,1)S(1)}, u32[]{:S(2)}, u32[]{:S(2)}) collective-permute-start(bf16[320,2048]{1,0:T(8,128)(2,1)S(1)} %add_convert_fusion.7), channel_id=1, source_target_pairs={{1,2},{2,1},{5,6},{6,5},{9,10},{10,9},{13,14},{14,13},{17,18},{18,... | collective-permute-start | bytes 3932168 | tf_op jit(solution)/shard_map/ppermute | solution.py:129
  458.6 29.8 %collective-permute-start.33 = (bf16[320,2048]{1,0:T(8,128)(2,1)S(1)}, bf16[320,2048]{1,0:T(8,128)(2,1)S(1)}, u32[]{:S(2)}, u32[]{:S(2)}) collective-permute-start(bf16[320,2048]{1,0:T(8,128)(2,1)S(1)} %add_convert_fusion.8), channel_id=1, source_target_pairs={{1,0},{2,3},{5,4},{6,7},{9,8},{10,11},{13,12},{14,15},{17,16},{18,... | collective-permute-start | bytes 3932168 | tf_op jit(solution)/shard_map/ppermute | solution.py:131
  476.9 37.2 %collective-permute-start.37 = (bf16[320,2048]{1,0:T(8,128)(2,1)S(1)}, bf16[320,2048]{1,0:T(8,128)(2,1)S(1)}, u32[]{:S(2)}, u32[]{:S(2)}) collective-permute-start(bf16[320,2048]{1,0:T(8,128)(2,1)S(1)} %get-tuple-element.223), channel_id=1, source_target_pairs={{0,1},{3,2},{4,5},{7,6},{8,9},{11,10},{12,13},{15,14},{16,17},{19,... | collective-permute-start | bytes 3932168 | tf_op jit(solution)/shard_map/ppermute | solution.py:107
  485.6 31.9 %collective-permute-start.38 = (bf16[320,2048]{1,0:T(8,128)(2,1)S(1)}, bf16[320,2048]{1,0:T(8,128)(2,1)S(1)}, u32[]{:S(2)}, u32[]{:S(2)}) collective-permute-start(bf16[320,2048]{1,0:T(8,128)(2,1)S(1)} %add_convert_fusion.6), channel_id=1, source_target_pairs={{1,2},{2,1},{5,6},{6,5},{9,10},{10,9},{13,14},{14,13},{17,18},{18,... | collective-permute-start | bytes 3932168 | tf_op jit(solution)/shard_map/ppermute | solution.py:129
  486.9 33.5 %collective-permute-start.36 = (bf16[320,2048]{1,0:T(8,128)(2,1)S(1)}, bf16[320,2048]{1,0:T(8,128)(2,1)S(1)}, u32[]{:S(2)}, u32[]{:S(2)}) collective-permute-start(bf16[320,2048]{1,0:T(8,128)(2,1)S(1)} %add_convert_fusion.5), channel_id=1, source_target_pairs={{1,0},{2,3},{5,4},{6,7},{9,8},{10,11},{13,12},{14,15},{17,16},{18,... | collective-permute-start | bytes 3932168 | tf_op jit(solution)/shard_map/ppermute | solution.py:131
  505.2 44.5 %collective-permute-start.39 = (bf16[320,2048]{1,0:T(8,128)(2,1)S(1)}, bf16[320,2048]{1,0:T(8,128)(2,1)}, u32[]{:S(2)}, u32[]{:S(2)}) collective-permute-start(bf16[320,2048]{1,0:T(8,128)(2,1)S(1)} %get-tuple-element.229), channel_id=1, source_target_pairs={{0,1},{3,2},{4,5},{7,6},{8,9},{11,10},{12,13},{15,14},{16,17},{19,... | collective-permute-start | bytes 3932168 | tf_op jit(solution)/shard_map/ppermute | solution.py:107
  515.8 29.4 %collective-permute-start.41 = (bf16[320,2048]{1,0:T(8,128)(2,1)}, bf16[320,2048]{1,0:T(8,128)(2,1)}, u32[]{:S(2)}, u32[]{:S(2)}) collective-permute-start(bf16[320,2048]{1,0:T(8,128)(2,1)} %add_convert_fusion.4), channel_id=1, source_target_pairs={{1,2},{2,1},{5,6},{6,5},{9,10},{10,9},{13,14},{14,13},{17,18},{18,... | collective-permute-start | bytes 3932168 | tf_op jit(solution)/shard_map/ppermute | solution.py:129
  519.1 34.8 %collective-permute-start.40 = (bf16[320,2048]{1,0:T(8,128)(2,1)}, bf16[320,2048]{1,0:T(8,128)(2,1)}, u32[]{:S(2)}, u32[]{:S(2)}) collective-permute-start(bf16[320,2048]{1,0:T(8,128)(2,1)} %add_convert_fusion.3), channel_id=1, source_target_pairs={{1,0},{2,3},{5,4},{6,7},{9,8},{10,11},{13,12},{14,15},{17,16},{18,... | collective-permute-start | bytes 3932168 | tf_op jit(solution)/shard_map/ppermute | solution.py:131
  548.5 34.1 %collective-permute-start.43 = (bf16[320,2048]{1,0:T(8,128)(2,1)}, bf16[320,2048]{1,0:T(8,128)(2,1)}, u32[]{:S(2)}, u32[]{:S(2)}) collective-permute-start(bf16[320,2048]{1,0:T(8,128)(2,1)} %add_convert_fusion.1), channel_id=1, source_target_pairs={{1,0},{2,3},{5,4},{6,7},{9,8},{10,11},{13,12},{14,15},{17,16},{18,... | collective-permute-start | bytes 3932168 | tf_op jit(solution)/shard_map/ppermute | solution.py:131
  616.5 35.4 %all-to-all-start.2 = ((bf16[8,640,128]{2,1,0:T(8,128)(2,1)}), bf16[8,640,128]{2,1,0:T(8,128)(2,1)S(1)}, u32[]{:S(2)}, u32[]{:S(2)}) async-start(bf16[8,640,128]{2,1,0:T(8,128)(2,1)} %bitcast.27), calls=%async_computation.2 | async-start | bytes 2621440 | tf_op jit(solution)/shard_map/all_to_all | solution.py:1300
  633.7 279.0 %reduce-scatter.5.cloned.1.call-start = ((), (), s32[]{:S(2)}) async-start(), calls=%async_computation.9 | async-start | bytes 9437184 | tf_op jit(solution)/shard_map/reduce_scatter | solution.py:1292
  806.7 29.4 %collective-permute-start.47 = (bf16[160,2048]{1,0:T(8,128)(2,1)}, bf16[160,2048]{1,0:T(8,128)(2,1)}, u32[]{:S(2)}, u32[]{:S(2)}) collective-permute-start(bf16[160,2048]{1,0:T(8,128)(2,1)} %get-tuple-element.356), channel_id=1, source_target_pairs={{0,1},{4,5},{8,9},{12,13},{16,17},{20,21},{24,25},{28,29}} | collective-permute-start | bytes 1966088 | tf_op jit(solution)/shard_map/ppermute | solution.py:169
  865.0 29.5 %collective-permute-start.51 = (bf16[160,2048]{1,0:T(8,128)(2,1)}, bf16[160,2048]{1,0:T(8,128)(2,1)}, u32[]{:S(2)}, u32[]{:S(2)}) collective-permute-start(bf16[160,2048]{1,0:T(8,128)(2,1)} %get-tuple-element.350), channel_id=1, source_target_pairs={{0,1},{1,2},{2,3},{4,5},{5,6},{6,7},{8,9},{9,10},{10,11},{12,13},{... | collective-permute-start | bytes 1966088 | tf_op jit(solution)/shard_map/ppermute | solution.py:166
  (89 other events, 995.8 us)
Sparse Core Ops, SparseCore 0:
  10.7 57.0 all-gather.4
  69.7 62.5 all-gather.8
  177.2 102.5 all-gather.6
  616.6 213.7 reduce-scatter.2
  836.3 70.2 reduce-scatter.4
